TPU v7x, 32 devices: a whole 2x2x4 slice. The times are simulated.
32 devices in a mesh: dp: 8 (over z, x), tensor: 4 (over y, core).
Axes of the slice: x: 2, y: 2, z: 4, core: 2. Of those that a mesh axis runs over, the one named last changes fastest.
Arguments:
- tokens: bfloat16 [16384, 768], P('dp'), may hold values from -6 to 6
- pass_ids: int32 [16384], P('dp'), may hold values from 0 to 4
- doc_lengths: int32 [8, 8], P('dp'), may hold values from 1 to 1024, 2048 in all within a row
- cotangent: bfloat16 [16384, 768], P('dp'), may hold values from -6 to 6
- block_weights: float32 [4, 48, 192, 192], P('tensor', 'dp'), may hold values from -2 to 2
- vector_params: float32 [9, 768], P(None, 'dp'), may hold values from -2 to 2
- vector_moment: float32 [9, 768], P(None, 'dp'), may hold values from 4096 to 16384
- block_left: float32 [4, 48, 192, 192], P('tensor', 'dp'), may hold values from -6291456 to 6291456
- block_right: float32 [4, 48, 192, 192], P('tensor', 'dp'), may hold values from -6291456 to 6291456
- block_left_root: float32 [4, 48, 192, 192], P('tensor', 'dp'), may hold values from -2 to 2
- block_right_root: float32 [4, 48, 192, 192], P('tensor', 'dp'), may hold values from -2 to 2
Outputs:
- output: bfloat16 [16384, 768], P('dp')
- input_grad: bfloat16 [16384, 768], P('dp')
- block_left_new: float32 [4, 48, 192, 192], P('tensor', 'dp')
- block_right_new: float32 [4, 48, 192, 192], P('tensor', 'dp')
- block_step: float32 [4, 48, 192, 192], P('tensor', 'dp')
- block_new: float32 [4, 48, 192, 192], P('tensor', 'dp')
- vector_grad: float32 [9, 768], P(None, 'dp')
- vector_moment_new: float32 [9, 768], P(None, 'dp')
- vector_new: float32 [9, 768], P(None, 'dp')
All inputs are finite; a program needn't handle non-finite values.
Results may differ from a plain program's by a relative error of at most 0.014.
Values may be sent and summed in bfloat16 or wider, within the bound.
A program may use at most 192 MiB of HBM per device.

v0:
```python
import jax
import jax.numpy as jnp
from jax import lax
from jax.sharding import PartitionSpec as P

D = 768
HD = 64
FF = 3072
PASSES = 5


norm_eps = 1e-05
moment_eps = 1e-08
rate_matrix = 0.03
rate_vector = 0.2
decay = 0.5
gelu_coef = 0.7978845608028654
masked_score = -1e30
highest = lax.Precision.HIGHEST


def layer_norm(hidden, gain, shift):
    mean = jnp.mean(hidden, axis=-1, keepdims=True)
    center = hidden - mean
    spread = jnp.mean(center * center, axis=-1, keepdims=True)
    return center * lax.rsqrt(spread + norm_eps) * gain + shift


def gelu_tanh(value):
    return 0.5 * value * (1.0 + jnp.tanh(gelu_coef * (value + 0.044715 * value * value * value)))


def doc_numbers(lengths, count):
    ends = jnp.cumsum(lengths)
    places = jnp.arange(count, dtype=jnp.int32)
    return jnp.sum((ends[None, :] <= places[:, None]).astype(jnp.int32), axis=1)


def precondition(grad, weight, left, right, left_root, right_root):
    left_new = decay * left + (1.0 - decay) * jnp.einsum(
        "...ij,...kj->...ik", grad, grad, precision=highest
    )
    right_new = decay * right + (1.0 - decay) * jnp.einsum(
        "...ji,...jk->...ik", grad, grad, precision=highest
    )
    half = jnp.einsum("...ij,...jk->...ik", left_root, grad, precision=highest)
    step = jnp.einsum("...ij,...jk->...ik", half, right_root, precision=highest)
    return (left_new, right_new, step, weight - rate_matrix * step)


def block_scores(start, queries, keys, docs, width, scale):
    query_rows = lax.dynamic_slice_in_dim(queries, start, width, 0)
    query_docs = lax.dynamic_slice_in_dim(docs, start, width, 0)
    scores = (
        jnp.einsum("qhd,khd->hqk", query_rows, keys, preferred_element_type=jnp.float32) * scale
    )
    rows = start + jnp.arange(width, dtype=jnp.int32)
    cols = jnp.arange(keys.shape[0], dtype=jnp.int32)
    allowed = (query_docs[:, None] == docs[None, :]) & (cols[None, :] <= rows[:, None])
    return (query_rows, jnp.where(allowed[None], scores, masked_score))


def attend_forward(queries, keys, values, docs, width, scale):
    starts = jnp.arange(queries.shape[0] // width, dtype=jnp.int32) * width

    def one_block(start):
        unused, scores = block_scores(start, queries, keys, docs, width, scale)
        top = jnp.max(scores, axis=-1, keepdims=True)
        total = jnp.sum(jnp.exp(scores - top), axis=-1, keepdims=True)
        lse = top + jnp.log(total)
        probs = jnp.exp(scores - lse).astype(jnp.bfloat16)
        mixed = jnp.einsum("hqk,khd->qhd", probs, values, preferred_element_type=jnp.float32)
        return (mixed.astype(jnp.bfloat16), lse)

    return lax.map(one_block, starts)


def attend_backward(queries, keys, values, docs, lse, grad_mixed, width, scale):
    count = queries.shape[0] // width
    starts = jnp.arange(count, dtype=jnp.int32) * width
    grad_blocks = grad_mixed.reshape((count, width) + grad_mixed.shape[1:])

    def one_block(carry, item):
        start, block_lse, grad_rows = item
        query_rows, scores = block_scores(start, queries, keys, docs, width, scale)
        probs = jnp.exp(scores - block_lse)
        grad_probs = jnp.einsum(
            "qhd,khd->hqk", grad_rows, values, preferred_element_type=jnp.float32
        )
        inner = jnp.sum(probs * grad_probs, axis=-1, keepdims=True)
        grad_scores = (probs * (grad_probs - inner)).astype(jnp.bfloat16)
        grad_query = (
            jnp.einsum("hqk,khd->qhd", grad_scores, keys, preferred_element_type=jnp.float32)
            * scale
        )
        grad_key = (
            carry[0]
            + jnp.einsum(
                "hqk,qhd->khd", grad_scores, query_rows, preferred_element_type=jnp.float32
            )
            * scale
        )
        grad_value = carry[1] + jnp.einsum(
            "hqk,qhd->khd",
            probs.astype(jnp.bfloat16),
            grad_rows,
            preferred_element_type=jnp.float32,
        )
        return ((grad_key, grad_value), grad_query.astype(jnp.bfloat16))

    empty = jnp.zeros(keys.shape, jnp.float32)
    (grad_key, grad_value), grad_query = lax.scan(
        one_block, (empty, empty), (starts, lse, grad_blocks)
    )
    return (
        grad_query.reshape(queries.shape),
        grad_key.astype(jnp.bfloat16),
        grad_value.astype(jnp.bfloat16),
    )


def on_device(
    tokens,
    pass_ids,
    doc_lengths,
    cotangent,
    block_weights,
    vector_params,
    vector_moment,
    block_left,
    block_right,
    block_left_root,
    block_right_root,
):
    full_blocks, full_vector = (
        lax.all_gather(block_weights, "dp", axis=1, tiled=True),
        lax.all_gather(vector_params, "dp", axis=1, tiled=True),
    )
    side = block_weights.shape[-1]
    groups = D // side
    ratio = FF // D
    total_blocks = groups * (4 + 2 * ratio)
    slots = full_blocks.shape[1]
    blocks = full_blocks[0, :total_blocks]
    qkv_low = blocks[0 : 3 * groups].reshape(3, D, side).astype(jnp.bfloat16)
    out_low = (
        blocks[3 * groups : 4 * groups].transpose(1, 0, 2).reshape(side, D).astype(jnp.bfloat16)
    )
    up_low = (
        blocks[4 * groups : 4 * groups + groups * ratio]
        .reshape(groups, ratio, side, side)
        .transpose(0, 2, 1, 3)
        .reshape(D, ratio * side)
        .astype(jnp.bfloat16)
    )
    down_low = (
        blocks[4 * groups + groups * ratio :]
        .reshape(ratio, groups, side, side)
        .transpose(0, 2, 1, 3)
        .reshape(ratio * side, D)
        .astype(jnp.bfloat16)
    )
    embed = full_vector[:PASSES]
    gain_one = full_vector[PASSES]
    shift_one = full_vector[PASSES + 1]
    gain_two = full_vector[PASSES + 2]
    shift_two = full_vector[PASSES + 3]
    seq = tokens.shape[0]
    heads_here = side // HD
    scale = HD ** (-0.5)
    width = min(512, seq)
    share = seq // lax.axis_size("tensor")
    own = lax.axis_index("tensor") * share
    choose = (pass_ids[:, None] == jnp.arange(PASSES, dtype=jnp.int32)[None, :]).astype(jnp.float32)
    first = tokens.astype(jnp.float32) + jnp.dot(choose, embed, precision=highest)
    norm_low = layer_norm(first, gain_one, shift_one).astype(jnp.bfloat16)
    project = jnp.einsum(
        "sd,kde->kse", norm_low, qkv_low, preferred_element_type=jnp.float32
    ).astype(jnp.bfloat16)
    queries = project[0].reshape(seq, heads_here, HD)
    keys = project[1].reshape(seq, heads_here, HD)
    values = project[2].reshape(seq, heads_here, HD)
    docs = doc_numbers(doc_lengths[0], seq)
    mixed, lse = attend_forward(queries, keys, values, docs, width, scale)
    mixed = mixed.reshape(seq, heads_here * HD)
    attn_part = jnp.dot(mixed, out_low, preferred_element_type=jnp.float32)
    attn_rows = lax.psum_scatter(attn_part, "tensor", scatter_dimension=0, tiled=True)
    first_rows = lax.dynamic_slice_in_dim(first, own, share, 0)
    second_rows = first_rows + attn_rows
    norm2_low = lax.all_gather(
        layer_norm(second_rows, gain_two, shift_two).astype(jnp.bfloat16),
        "tensor",
        axis=0,
        tiled=True,
    )
    upper = jnp.dot(norm2_low, up_low, preferred_element_type=jnp.float32)
    act_low = gelu_tanh(upper).astype(jnp.bfloat16)
    mlp_part = jnp.dot(act_low, down_low, preferred_element_type=jnp.float32)
    mlp_rows = lax.psum_scatter(
        mlp_part.astype(jnp.bfloat16), "tensor", scatter_dimension=0, tiled=True
    ).astype(jnp.float32)
    output_rows = (second_rows + mlp_rows).astype(jnp.bfloat16)
    grad_act = jnp.einsum("sd,fd->sf", cotangent, down_low, preferred_element_type=jnp.float32)
    grad_down = jnp.einsum("sf,sd->fd", act_low, cotangent, preferred_element_type=jnp.float32)
    unused, gelu_back = jax.vjp(gelu_tanh, upper)
    grad_upper = gelu_back(grad_act)[0].astype(jnp.bfloat16)
    grad_up = jnp.einsum("sd,sf->df", norm2_low, grad_upper, preferred_element_type=jnp.float32)
    norm2_grad_part = jnp.einsum(
        "sf,df->sd", grad_upper, up_low, preferred_element_type=jnp.float32
    )
    norm2_grad_rows = lax.psum_scatter(
        norm2_grad_part.astype(jnp.bfloat16), "tensor", scatter_dimension=0, tiled=True
    ).astype(jnp.float32)
    unused, back_two = jax.vjp(layer_norm, second_rows, gain_two, shift_two)
    d_second, d_gain_two, d_shift_two = back_two(norm2_grad_rows)
    grad_second_rows = (
        lax.dynamic_slice_in_dim(cotangent, own, share, 0).astype(jnp.float32) + d_second
    )
    attn_grad_low = lax.all_gather(
        grad_second_rows.astype(jnp.bfloat16), "tensor", axis=0, tiled=True
    )
    grad_out = jnp.einsum("se,sd->ed", mixed, attn_grad_low, preferred_element_type=jnp.float32)
    grad_mixed = jnp.einsum(
        "sd,ed->se", attn_grad_low, out_low, preferred_element_type=jnp.float32
    ).astype(jnp.bfloat16)
    grad_query, grad_key, grad_value = attend_backward(
        queries, keys, values, docs, lse, grad_mixed.reshape(seq, heads_here, HD), width, scale
    )
    grad_project = jnp.stack(
        [grad_query.reshape(seq, -1), grad_key.reshape(seq, -1), grad_value.reshape(seq, -1)]
    )
    grad_qkv = jnp.einsum("sd,kse->kde", norm_low, grad_project, preferred_element_type=jnp.float32)
    norm1_grad_part = jnp.einsum(
        "kse,kde->sd", grad_project, qkv_low, preferred_element_type=jnp.float32
    )
    norm1_grad_rows = lax.psum_scatter(
        norm1_grad_part.astype(jnp.bfloat16), "tensor", scatter_dimension=0, tiled=True
    ).astype(jnp.float32)
    unused, back_one = jax.vjp(layer_norm, first_rows, gain_one, shift_one)
    d_first, d_gain_one, d_shift_one = back_one(norm1_grad_rows)
    grad_first_rows = grad_second_rows + d_first
    choose_rows = lax.dynamic_slice_in_dim(choose, own, share, 0)
    grad_embed = jnp.einsum("sp,sd->pd", choose_rows, grad_first_rows, precision=highest)
    vector_part = jnp.concatenate(
        [grad_embed, d_gain_one[None], d_shift_one[None], d_gain_two[None], d_shift_two[None]],
        axis=0,
    )
    vector_grad_all = lax.psum(vector_part, "tensor")
    output, input_grad = (
        lax.all_gather(output_rows, "tensor", axis=0, tiled=True),
        lax.all_gather(grad_first_rows.astype(jnp.bfloat16), "tensor", axis=0, tiled=True),
    )
    qkv_blocks = grad_qkv.reshape(3 * groups, side, side)
    out_blocks = grad_out.reshape(side, groups, side).transpose(1, 0, 2)
    up_blocks = (
        grad_up.reshape(groups, side, ratio, side)
        .transpose(0, 2, 1, 3)
        .reshape(groups * ratio, side, side)
    )
    down_blocks = (
        grad_down.reshape(ratio, side, groups, side)
        .transpose(0, 2, 1, 3)
        .reshape(ratio * groups, side, side)
    )
    spare = jnp.zeros((slots - total_blocks, side, side), jnp.float32)
    grad_blocks = jnp.concatenate([qkv_blocks, out_blocks, up_blocks, down_blocks, spare], axis=0)[
        None
    ]
    owned_blocks, vector_grad = (
        lax.psum_scatter(grad_blocks, "dp", scatter_dimension=1, tiled=True),
        lax.psum_scatter(vector_grad_all, "dp", scatter_dimension=1, tiled=True),
    )
    left_new, right_new, step, weight_new = precondition(
        owned_blocks, block_weights, block_left, block_right, block_left_root, block_right_root
    )
    moment_new = decay * vector_moment + (1.0 - decay) * vector_grad * vector_grad
    vector_new = vector_params - rate_vector * vector_grad / (jnp.sqrt(moment_new) + moment_eps)
    return (
        output,
        input_grad,
        left_new,
        right_new,
        step,
        weight_new,
        vector_grad,
        moment_new,
        vector_new,
    )


def solution(mesh):
    return jax.shard_map(
        on_device,
        mesh=mesh,
        in_specs=(
            P("dp", None),
            P("dp"),
            P("dp", None),
            P("dp", None),
            P("tensor", "dp", None, None),
            P(None, "dp"),
            P(None, "dp"),
            P("tensor", "dp", None, None),
            P("tensor", "dp", None, None),
            P("tensor", "dp", None, None),
            P("tensor", "dp", None, None),
        ),
        out_specs=(
            P("dp", None),
            P("dp", None),
            P("tensor", "dp", None, None),
            P("tensor", "dp", None, None),
            P("tensor", "dp", None, None),
            P("tensor", "dp", None, None),
            P(None, "dp"),
            P(None, "dp"),
            P(None, "dp"),
        ),
        check_vma=False,
    )
```

profile of v0, /device:TPU:0, one launch (start us, length us, event | category | flops | bytes accessed | tf_op | source)
XLA Modules:
  0.0 961.0 jit_solution(12283230383147087504)
XLA Ops:
  10.4 32.9 %all-gather = f32[8,96,9]{1,2,0:T(8,128)S(1)} all-gather(f32[1,96,9]{1,2,0:T(8,128)} %bitcast.221), channel_id=1, replica_groups=mesh['dp'=8,'tensor'=4] {'dp'}, dimensions={0}, use_global_device_ids=true | all-gather | bytes 31104 | tf_op jit(solution)/shard_map/all_gather | solution.py:137
  43.5 4.6 copy.94
  48.3 4.8 fusion.90
  58.4 35.3 %all-gather.7.cloned.1.call-done = bf16[1,48,192,192]{3,2,0,1:T(8,128)(2,1)} async-done(((bf16[1,6,192,192]{3,2,0,1:T(8,128)(2,1)}), bf16[1,48,192,192]{3,2,0,1:T(8,128)(2,1)}) %all-gather.7.cloned.1.call-update) | async-done | bytes 3538960 | tf_op jit(solution)/shard_map/all_gather | solution.py:136
  101.8 4.2 fusion.94
  108.8 107.7 %while.27 = (s32[]{:T(128)}, bf16[4,512,3,64]{1,3,2,0:T(8,128)(2,1)}, f32[4,3,512,1]{2,1,3,0:T(4,128)S(1)}, s32[4]{0:T(128)S(1)}, s32[2048]{0:T(1024)S(1)}, /*in...) while((s32[]{:T(128)}, ...), condition=%wide.region_7.8_spmd, body=%wide.region_4.7_spmd.sunk | while | flops 843152384 | bytes 47130832 | solution.py:75
  113.4 8.4 fusion.145
  121.9 6.8 exponential_reduce_fusion.2
  128.8 7.1 fusion.146
  140.3 8.4 fusion.145
  148.8 6.8 exponential_reduce_fusion.2
  155.6 7.1 fusion.146
  167.2 8.4 fusion.145
  175.7 6.8 exponential_reduce_fusion.2
  182.5 7.1 fusion.146
  194.1 8.4 fusion.145
  202.5 6.8 exponential_reduce_fusion.2
  209.4 7.1 fusion.146
  219.3 3.7 fusion.91
  223.1 56.6 %reduce-scatter.9.cloned.1.call-done = f32[512,768]{0,1:T(8,128)} async-done(((f32[2048,768]{0,1:T(8,128)}), f32[512,768]{0,1:T(8,128)}) %reduce-scatter.9.cloned.1.call-update) | async-done | bytes 1572880 | tf_op jit(solution)/shard_map/reduce_scatter | solution.py:187
  290.7 4.6 convert_element_type.137
  295.3 3.8 copy.142
  299.1 4.0 convert_element_type.141
  303.1 5.8 fusion.92
  308.9 4.8 all-gather.9.cloned.1.call-done
  313.6 12.9 %fusion.45 = (bf16[2048,768]{1,0:T(8,128)(2,1)S(1)}, f32[2048,768]{1,0:T(8,128)}) fusion(f32[2048,768]{1,0:T(8,128)} %fusion.92, bf16[2048,768]{0,1:T(8,128)(2,1)} %all-gather.9.cloned.1.call-done, bf16[768,768]{1,0:T(8,128)(2,1)} %convert_element_type.137), kind=kOutput, calls=%fused_computation.60 | convolution fusion | flops 2453667840 | bytes 20054016 | tf_op jit(solution)/shard_map/dot_general | solution.py:196
  328.1 4.0 convolution_convert_fusion
  335.4 34.8 %reduce-scatter.13.cloned.1.call-done = bf16[512,768]{0,1:T(8,128)(2,1)} async-done(((bf16[2048,768]{0,1:T(8,128)(2,1)}), bf16[512,768]{0,1:T(8,128)(2,1)}) %reduce-scatter.13.cloned.1.call-update) | async-done | bytes 786448 | tf_op jit(solution)/shard_map/reduce_scatter | solution.py:211
  378.0 28.6 %all-gather.13.cloned.1.call-done = bf16[2048,768]{0,1:T(8,128)(2,1)} async-done(((bf16[512,768]{0,1:T(8,128)(2,1)}), bf16[2048,768]{0,1:T(8,128)(2,1)}) %all-gather.13.cloned.1.call-update) | async-done | bytes 3145744 | tf_op jit(solution)/shard_map/all_gather | solution.py:219
  406.6 3.6 convolution_convert_fusion.2
  416.3 137.7 %while.28 = (s32[]{:T(128)}, f32[2048,3,64]{0,2,1:T(8,128)}, f32[2048,3,64]{0,2,1:T(8,128)}, bf16[4,512,3,64]{1,3,2,0:T(8,128)(2,1)}, s32[4]{0:T(128)S(1)}, /*in...) while((s32[]{:T(128)}, f32[2048,3,64]{0,2,1:T(8,128)}, ...), condition=%wide.region_17.18_spmd.clone, body=%wide.region_15.17_spmd.clone.sunk | while | flops 2065759232 | bytes 130285944 | solution.py:112
  424.5 4.7 fusion.159
  429.3 7.2 multiply_reduce_fusion.5
  436.5 6.9 multiply_convert_fusion.5
  457.8 6.2 fusion.159
  464.0 7.2 multiply_reduce_fusion.5
  471.2 6.9 multiply_convert_fusion.5
  492.5 6.2 fusion.159
  498.7 7.2 multiply_reduce_fusion.5
  505.9 6.9 multiply_convert_fusion.5
  527.2 6.2 fusion.159
  533.4 7.2 multiply_reduce_fusion.5
  540.6 6.9 multiply_convert_fusion.5
  563.8 4.0 bitcast_convert_fusion
  567.9 7.7 convolution_convert_fusion.1
  576.7 29.3 %reduce-scatter.15.cloned.1.call-done = bf16[512,768]{0,1:T(8,128)(2,1)} async-done(((bf16[2048,768]{0,1:T(8,128)(2,1)}), bf16[512,768]{0,1:T(8,128)(2,1)}) %reduce-scatter.15.cloned.1.call-update) | async-done | bytes 786448 | tf_op jit(solution)/shard_map/reduce_scatter | solution.py:236
  610.7 35.9 %reduce-scatter.11.cloned.1.call-done = bf16[512,768]{0,1:T(8,128)(2,1)} async-done(((bf16[2048,768]{0,1:T(8,128)(2,1)}), bf16[512,768]{0,1:T(8,128)(2,1)}) %reduce-scatter.11.cloned.1.call-update) | async-done | bytes 786448 | tf_op jit(solution)/shard_map/reduce_scatter | solution.py:199
  646.7 5.0 fusion.86
  658.2 6.9 fusion.93
  665.0 4.9 reshape.318
  669.9 4.8 copy.113
  674.7 7.5 fusion.84
  682.2 4.9 reshape.320
  687.1 4.9 copy.114
  692.0 4.0 convolution_bitcast_fusion.2
  698.4 5.9 fusion.58
  710.4 8.6 maximum_bitcast_fusion
  720.0 5.8 psum.8
  726.5 18.4 %all-gather.15.cloned.1.call-done = bf16[2048,768]{0,1:T(8,128)(2,1)} async-done(((bf16[512,768]{0,1:T(8,128)(2,1)}), bf16[2048,768]{0,1:T(8,128)(2,1)}) %all-gather.15.cloned.1.call-update) | async-done | bytes 3145744 | tf_op jit(solution)/shard_map/all_gather | solution.py:251
  744.9 4.6 copy.122
  749.5 26.0 %all-gather.11.cloned.1.call-done = bf16[2048,768]{0,1:T(8,128)(2,1)} async-done(((bf16[512,768]{0,1:T(8,128)(2,1)}), bf16[2048,768]{0,1:T(8,128)(2,1)}) %all-gather.11.cloned.1.call-update) | async-done | bytes 3145744 | tf_op jit(solution)/shard_map/all_gather | solution.py:250
  775.5 4.6 copy.121
  780.1 162.4 %reduce-scatter.17.cloned.1.call-done = f32[1,6,192,192]{2,3,1,0:T(8,128)} async-done(((f32[1,48,192,192]{2,3,1,0:T(8,128)}), f32[1,6,192,192]{2,3,1,0:T(8,128)}) %reduce-scatter.17.cloned.1.call-update) | async-done | bytes 884752 | tf_op jit(solution)/shard_map/reduce_scatter | solution.py:270
  950.8 3.5 fusion.62
  (266 shorter events, 151.3 us)
Async XLA Ops:
  7.2 295.9 %copy-start = (bf16[2048,768]{1,0:T(8,128)(2,1)S(1)}, bf16[2048,768]{1,0:T(8,128)(2,1)}, u32[]{:S(2)}) copy-start(bf16[2048,768]{1,0:T(8,128)(2,1)} %param.18) | copy-start | bytes 9437188
  7.2 86.6 %all-gather.7.cloned.1.call-start = ((), (), s32[]{:S(2)}) async-start(), calls=%async_computation.6 | async-start | bytes 5308416 | tf_op jit(solution)/shard_map/all_gather | solution.py:136
  9.6 270.1 %reduce-scatter.9.cloned.1.call-start = ((), (), s32[]{:S(2)}) async-start(), calls=%async_computation.7 | async-start | bytes 7864320 | tf_op jit(solution)/shard_map/reduce_scatter | solution.py:187
  43.4 4.8 copy-start.25
  48.2 5.6 copy-start.27
  48.3 327.6 %copy-start.23 = (f32[768]{0:T(1024)}, f32[768]{0:T(1024)S(1)}, u32[]{:S(2)}) copy-start(f32[768]{0:T(1024)S(1)} %get-tuple-element.241) | copy-start | bytes 9220
  53.1 2.6 copy-start.1
  121.9 6.9 copy-start.7
  148.8 6.9 copy-start.7
  175.7 6.9 copy-start.7
  202.5 6.9 copy-start.7
  223.0 90.6 %all-gather.9.cloned.1.call-start = ((), (), s32[]{:S(2)}) async-start(), calls=%async_computation.8 | async-start | bytes 3932160 | tf_op jit(solution)/shard_map/all_gather | solution.py:190
  282.6 93.2 %copy-start.29 = (f32[512]{0:T(512)}, f32[512]{0:T(512)S(1)}, u32[]{:S(2)}) copy-start(f32[512]{0:T(512)S(1)} %broadcast_multiply_fusion.2) | copy-start | bytes 6148
  282.9 93.0 %copy-start.31 = (f32[512]{0:T(512)}, f32[512]{0:T(512)S(1)}, u32[]{:S(2)}) copy-start(f32[512]{0:T(512)S(1)} %fusion.78) | copy-start | bytes 6148
  285.0 85.3 %reduce-scatter.13.cloned.1.call-start = ((), (), s32[]{:S(2)}) async-start(), calls=%async_computation.11 | async-start | bytes 3932160 | tf_op jit(solution)/shard_map/reduce_scatter | solution.py:211
  313.6 14.5 %copy-start.19 = (bf16[768,768]{1,0:T(8,128)(2,1)S(1)}, bf16[768,768]{1,0:T(8,128)(2,1)}, u32[]{:S(2)}) copy-start(bf16[768,768]{1,0:T(8,128)(2,1)} %convert_element_type.137) | copy-start | bytes 3538948
  326.5 1.6 copy-start.43
  332.1 74.5 %all-gather.13.cloned.1.call-start = ((), (), s32[]{:S(2)}) async-start(), calls=%async_computation.12 | async-start | bytes 3932160 | tf_op jit(solution)/shard_map/all_gather | solution.py:219
  370.2 3.0 copy-start.4
  370.2 6.2 copy-start.9
  370.2 6.2 copy-start.12
  373.3 2.6 copy-start.35
  377.9 228.0 %reduce-scatter.15.cloned.1.call-start = ((), (), s32[]{:S(2)}) async-start(), calls=%async_computation.13 | async-start | bytes 3932160 | tf_op jit(solution)/shard_map/reduce_scatter | solution.py:236
  421.2 3.3 copy-start.15
  424.5 4.8 copy-start.8
  436.5 6.9 copy-start.2
  443.4 2.8 copy-start.5
  448.6 1.1 copy-start.6
  454.5 3.3 copy-start.15
  457.7 6.2 copy-start.8
  471.2 6.9 copy-start.2
  478.1 2.8 copy-start.5
  483.3 1.1 copy-start.6
  489.2 3.3 copy-start.15
  492.5 6.2 copy-start.8
  505.9 6.9 copy-start.2
  512.8 2.8 copy-start.5
  518.0 1.1 copy-start.6
  523.9 3.3 copy-start.15
  527.2 6.2 copy-start.8
  540.6 6.9 copy-start.2
  547.5 2.8 copy-start.5
  559.5 4.3 copy-start.13
  559.5 4.3 copy-start.20
  561.1 1.8 copy-start.21
  567.9 78.8 %reduce-scatter.11.cloned.1.call-start = ((), (), s32[]{:S(2)}) async-start(), calls=%async_computation.9 | async-start | bytes 3932160 | tf_op jit(solution)/shard_map/reduce_scatter | solution.py:199
  575.6 30.4 %copy-start.28 = (f32[768]{0:T(1024)S(1)}, f32[768]{0:T(1024)}, u32[]{:S(2)}) copy-start(f32[768]{0:T(1024)} %copy-done.27) | copy-start | bytes 9220
  575.7 71.0 %copy-start.24 = (f32[768]{0:T(1024)S(1)}, f32[768]{0:T(1024)}, u32[]{:S(2)}) copy-start(f32[768]{0:T(1024)} %copy-done.23) | copy-start | bytes 9220
  575.7 71.0 %copy-start.30 = (f32[512]{0:T(512)S(1)}, f32[512]{0:T(512)}, u32[]{:S(2)}) copy-start(f32[512]{0:T(512)} %copy-done.29) | copy-start | bytes 6148
  575.7 71.0 %copy-start.32 = (f32[512]{0:T(512)S(1)}, f32[512]{0:T(512)}, u32[]{:S(2)}) copy-start(f32[512]{0:T(512)} %copy-done.31) | copy-start | bytes 6148
  575.7 71.0 %copy-start.36 = (f32[512]{0:T(512)S(1)}, f32[512]{0:T(512)}, u32[]{:S(2)}) copy-start(f32[512]{0:T(512)} %copy-done.35) | copy-start | bytes 6148
  575.7 71.0 %copy-start.38 = (f32[512]{0:T(512)S(1)}, f32[512]{0:T(512)}, u32[]{:S(2)}) copy-start(f32[512]{0:T(512)} %copy-done.37) | copy-start | bytes 6148
  575.7 143.4 %reduce-scatter.19.cloned.1.call-start = ((), (), s32[]{:S(2)}) async-start(), calls=%async_computation.16 | async-start | bytes 442368
  653.6 91.3 %all-gather.15.cloned.1.call-start = ((), (), s32[]{:S(2)}) async-start(), calls=%async_computation.14 | async-start | bytes 3932160 | tf_op jit(solution)/shard_map/all_gather | solution.py:251
  654.3 121.2 %all-gather.11.cloned.1.call-start = ((), (), s32[]{:S(2)}) async-start(), calls=%async_computation.10 | async-start | bytes 3932160 | tf_op jit(solution)/shard_map/all_gather | solution.py:250
  654.9 287.6 %reduce-scatter.17.cloned.1.call-start = ((), (), s32[]{:S(2)}) async-start(), calls=%async_computation.15 | async-start | bytes 10616832 | tf_op jit(solution)/shard_map/reduce_scatter | solution.py:270
  719.1 6.8 copy-start.33
  719.1 6.8 copy-start.42
  725.8 23.6 %copy-start.34 = (f32[9,96]{1,0:T(8,128)}, f32[9,96]{1,0:T(8,128)S(1)}, u32[]{:S(2)}) copy-start(f32[9,96]{1,0:T(8,128)S(1)} %psum.8) | copy-start | bytes 10372
  942.5 3.1 copy-start.14
  942.5 3.1 copy-start.18
  945.7 2.8 copy-start.10
  945.7 2.8 copy-start.16
  948.4 2.4 copy-start.17
  (9 other events, 8.5 us)
Sparse Core Ops, SparseCore 0:
  10.8 82.9 all-gather.6
  223.2 56.4 reduce-scatter.8
  285.1 28.5 all-gather.8
  332.3 37.9 reduce-scatter.12
  378.1 28.5 all-gather.12
  568.0 37.9 reduce-scatter.14
  608.7 37.9 reduce-scatter.10
  653.7 61.3 reduce-scatter.18
  717.3 27.5 all-gather.14
  746.8 28.5 all-gather.10
  779.1 163.4 reduce-scatter.16
where the time goes:
time: 970 us; the launch traced here: 961 us
  waiting for transfers between devices  433 us (45%)
  matrix products  235 us (24%)
  other arithmetic  111 us (11%)
  local copies, waits for them, and re-layouts  110 us (11%)
  blocking collectives  38.7 us (4%)
  loops' own time  17.1 us (2%)
  between operations  14.6 us (2%)
    reduce_scatter x1, waiting for transfers between devices, on_device(): lax.psum_scatter(grad_blocks, 'dp', scatter_dimension=1, tiled=True)  162 us
    reduce_scatter x1, waiting for transfers between devices, on_device(): lax.psum_scatter(attn_part, 'tensor', scatter_dimension=0, tiled=True)  56.6 us
    dot_general x8, matrix products, block_scores(): jnp.einsum('qhd,khd->hqk', query_rows, keys, preferred_element_type=jnp.f...  46.8 us
    reduce_scatter x1, waiting for transfers between devices, on_device(): lax.psum_scatter(mlp_part.astype(jnp.bfloat16), 'tensor', scatter_dimensi...  35.9 us
    all_gather x1, waiting for transfers between devices, on_device(): lax.all_gather(block_weights, 'dp', axis=1, tiled=True)  35.3 us
    reduce_scatter x1, waiting for transfers between devices, on_device(): lax.psum_scatter(norm2_grad_part.astype(jnp.bfloat16), 'tensor', scatter_...  34.8 us
    all_gather x1, blocking collectives, on_device(): lax.all_gather(vector_params, 'dp', axis=1, tiled=True)  32.9 us
    reduce_scatter x1, waiting for transfers between devices, on_device(): lax.psum_scatter(norm1_grad_part.astype(jnp.bfloat16), 'tensor', scatter_...  29.3 us
  transfers between devices with their start and end apart: 11, of which 10 were waited for; matrix products, arithmetic and copies ran while one was open for 13% of the time, Pallas kernels for 0%

commit v1 on v0

v1 whole, which is shorter than its diff:
```python
import functools

import jax
import jax.numpy as jnp
from jax import lax
from jax.experimental import pallas as pl
from jax.experimental.pallas import tpu as pltpu
from jax.sharding import PartitionSpec as P

D = 768
HD = 64
FF = 3072
PASSES = 5
SIDE = 192
PAIR = 2 * SIDE
ROWS = 256
DOCS = 8
NT = 4

norm_eps = 1e-05
moment_eps = 1e-08
rate_matrix = 0.03
rate_vector = 0.2
decay = 0.5
gelu_coef = 0.7978845608028654
masked_score = -1e30
f32 = jnp.float32
bf16 = jnp.bfloat16
VMEM_LIMIT = 56 * 1024 * 1024


def nn(a, b):
    return lax.dot_general(a, b, (((1,), (0,)), ((), ())), preferred_element_type=f32)


def nt(a, b):
    return lax.dot_general(a, b, (((1,), (1,)), ((), ())), preferred_element_type=f32)


def tn(a, b):
    return lax.dot_general(a, b, (((0,), (0,)), ((), ())), preferred_element_type=f32)


def split_three(value):
    high = value.astype(bf16)
    rest = value - high.astype(f32)
    mid = rest.astype(bf16)
    return high, mid, (rest - mid.astype(f32)).astype(bf16)


def one_hot(pass_row):
    kinds = lax.broadcasted_iota(jnp.int32, (16, pass_row.shape[1]), 0)
    return (kinds == pass_row).astype(f32).astype(bf16)


def embedded(tokens, pass_row, vec):
    chosen = one_hot(pass_row)
    high, mid, low = split_three(vec)
    return tokens.astype(f32) + (tn(chosen, high) + tn(chosen, mid) + tn(chosen, low))


def hat_of(hidden):
    mean = jnp.mean(hidden, axis=-1, keepdims=True)
    center = hidden - mean
    spread = jnp.mean(center * center, axis=-1, keepdims=True)
    root = lax.rsqrt(spread + norm_eps)
    return center * root, root


def norm_back(hat, root, grad, gain):
    scaled = grad * gain
    first = jnp.mean(scaled, axis=-1, keepdims=True)
    second = jnp.mean(scaled * hat, axis=-1, keepdims=True)
    return root * (scaled - first - hat * second)


def params(**kw):
    return pltpu.CompilerParams(vmem_limit_bytes=VMEM_LIMIT, **kw)


def full(shape):
    return pl.BlockSpec(shape, lambda *_: (0,) * len(shape))


def project_kernel(tok, pas, vec, wq, norm, q, k, v, cat):
    @pl.when(pl.program_id(0) == 0)
    def _():
        for x in range(3):
            for i in range(4):
                at = (i % 2) * SIDE
                parts = [wq[h, 2 * x + i // 2][:, at : at + SIDE] for h in range(2)]
                cat[x, i * SIDE : (i + 1) * SIDE, :] = jnp.concatenate(parts, axis=1)

    first = embedded(tok[...], pas[...], vec[...])
    hat, _ = hat_of(first)
    low = (hat * vec[PASSES : PASSES + 1] + vec[PASSES + 1 : PASSES + 2]).astype(bf16)
    norm[...] = low
    for x, out in enumerate((q, k, v)):
        out[...] = nn(low, cat[x]).astype(bf16)


def project(tokens, passes, vec, wq):
    seq = tokens.shape[0]
    row = lambda n: pl.BlockSpec((ROWS, n), lambda i: (i, 0))
    wide = jax.ShapeDtypeStruct((seq, PAIR), bf16)
    return pl.pallas_call(
        project_kernel,
        grid=(seq // ROWS,),
        in_specs=[row(D), pl.BlockSpec((1, ROWS), lambda i: (0, i)), full((16, D)), full(wq.shape)],
        out_specs=[row(D), row(PAIR), row(PAIR), row(PAIR), full((3, D, PAIR))],
        out_shape=[
            jax.ShapeDtypeStruct((seq, D), bf16),
            wide,
            wide,
            wide,
            jax.ShapeDtypeStruct((3, D, PAIR), bf16),
        ],
        compiler_params=params(),
        name="project",
    )(tokens, passes, vec, wq)


def doc_state(lens, base):
    rows = base + lax.broadcasted_iota(jnp.int32, (1, ROWS), 1)
    rows = jnp.concatenate([rows, rows], axis=1)
    begin = jnp.int32(0)
    first = jnp.int32(0)
    starts = jnp.zeros((1, 2 * ROWS), jnp.int32)
    for c in range(DOCS):
        starts = jnp.where(rows >= begin, begin, starts)
        first = jnp.where(base >= begin, begin, first)
        begin = begin + lens[c]
    return rows, starts, first


def two_heads(block):
    left = lax.broadcasted_iota(jnp.int32, block.shape, 1) < HD
    none = jnp.zeros_like(block)
    return jnp.concatenate([jnp.where(left, block, none), jnp.where(left, none, block)], axis=0)


def one_above(both):
    return jnp.concatenate([both[:HD, :ROWS], both[HD:, ROWS:]], axis=0).T


def attend_kernel(lens, q, k, v, out, lse, top, total, acc):
    i = pl.program_id(0)
    base = i * ROWS
    rows, starts, first = doc_state(lens, base)
    pairs = [two_heads(q[:, p * 128 : (p + 1) * 128] * bf16(0.125)) for p in range(3)]
    for p in range(3):
        top[p] = jnp.full((1, 2 * ROWS), masked_score, f32)
        total[p] = jnp.zeros((1, 2 * ROWS), f32)
        acc[p] = jnp.zeros((128, 2 * ROWS), f32)

    def step(j, carry):
        at = pl.multiple_of(j * ROWS, ROWS)
        keys = at + lax.broadcasted_iota(jnp.int32, (ROWS, 2 * ROWS), 0)
        seen = (keys >= starts) & (keys <= rows)
        for p in range(3):
            cols = slice(p * 128, (p + 1) * 128)
            scores = jnp.where(seen, nt(k[pl.ds(at, ROWS), cols], pairs[p]), masked_score)
            before = top[p]
            now = jnp.maximum(before, jnp.max(scores, axis=0, keepdims=True))
            probs = jnp.exp(scores - now)
            fade = jnp.exp(before - now)
            top[p] = now
            total[p] = total[p] * fade + jnp.sum(probs, axis=0, keepdims=True)
            acc[p] = acc[p] * fade + tn(v[pl.ds(at, ROWS), cols], probs.astype(bf16))
        return carry

    lax.fori_loop(first // ROWS, i + 1, step, 0)
    lines = []
    for p in range(3):
        out[:, p * 128 : (p + 1) * 128] = one_above(acc[p] / total[p]).astype(bf16)
        line = top[p] + jnp.log(total[p])
        lines += [line[:, :ROWS], line[:, ROWS:]]
    lse[...] = jnp.concatenate(lines + lines[:2], axis=0)


def attend(lens, q, k, v):
    seq = q.shape[0]
    row = pl.BlockSpec((ROWS, PAIR), lambda i, s: (i, 0))
    return pl.pallas_call(
        attend_kernel,
        grid_spec=pltpu.PrefetchScalarGridSpec(
            num_scalar_prefetch=1,
            grid=(seq // ROWS,),
            in_specs=[row, full((seq, PAIR)), full((seq, PAIR))],
            out_specs=[row, pl.BlockSpec((8, ROWS), lambda i, s: (0, i))],
            scratch_shapes=[
                pltpu.VMEM((3, 1, 2 * ROWS), f32),
                pltpu.VMEM((3, 1, 2 * ROWS), f32),
                pltpu.VMEM((3, 128, 2 * ROWS), f32),
            ],
        ),
        out_shape=[
            jax.ShapeDtypeStruct((seq, PAIR), bf16),
            jax.ShapeDtypeStruct((8, seq), f32),
        ],
        compiler_params=params(),
        name="attend",
    )(lens, q, k, v)


def attend_back_kernel(
    lens, place, q, k, v, mixed, lse, mine, other, wo, dq, dk, dv, gwo, dk_acc, dv_acc, dq_acc, gwo_acc
):
    i = pl.program_id(0)
    count = pl.num_programs(0)
    base = i * ROWS

    @pl.when(i == 0)
    def _():
        dk_acc[...] = jnp.zeros_like(dk_acc)
        dv_acc[...] = jnp.zeros_like(dv_acc)
        gwo_acc[...] = jnp.zeros_like(gwo_acc)

    half = (i >= count // 2).astype(jnp.int32)
    grad = jnp.where(half == place[0], mine[...], other[...])
    weight = jnp.concatenate(
        [jnp.concatenate([wo[h, 0], wo[h, 1]], axis=1) for h in range(2)], axis=0
    )
    grad_mixed = nt(grad, weight).astype(bf16)
    gwo_acc[...] += tn(mixed[...], grad)

    rows, starts, first = doc_state(lens, base)
    heads = lax.broadcasted_iota(jnp.int32, (8, 128), 0)
    lanes = lax.broadcasted_iota(jnp.int32, (8, 128), 1)
    pick = (lanes // HD == heads).astype(f32)
    queries, grads, inner, lines = [], [], [], []
    for p in range(3):
        cols = slice(p * 128, (p + 1) * 128)
        queries.append(two_heads(q[:, cols] * bf16(0.125)))
        grads.append(two_heads(grad_mixed[:, cols]))
        product = grad_mixed[:, cols].astype(f32) * mixed[:, cols].astype(f32)
        sums = lax.dot_general(
            pick,
            product,
            (((1,), (1,)), ((), ())),
            precision=lax.Precision.HIGHEST,
            preferred_element_type=f32,
        )
        inner.append(jnp.concatenate([sums[0:1], sums[1:2]], axis=1))
        lines.append(jnp.concatenate([lse[2 * p : 2 * p + 1], lse[2 * p + 1 : 2 * p + 2]], axis=1))
        dq_acc[p] = jnp.zeros((128, 2 * ROWS), f32)

    def step(j, carry):
        at = pl.multiple_of(j * ROWS, ROWS)
        keys = at + lax.broadcasted_iota(jnp.int32, (ROWS, 2 * ROWS), 0)
        seen = (keys >= starts) & (keys <= rows)
        here = pl.ds(at, ROWS)
        for p in range(3):
            cols = slice(p * 128, (p + 1) * 128)
            kb = k[here, cols]
            scores = jnp.where(seen, nt(kb, queries[p]) - lines[p], masked_score)
            probs = jnp.exp(scores)
            grad_probs = nt(v[here, cols], grads[p])
            grad_scores = (probs * (grad_probs - inner[p])).astype(bf16)
            dv_acc[here, cols] += nn(probs.astype(bf16), grads[p])
            dk_acc[here, cols] += nn(grad_scores, queries[p])
            dq_acc[p] += tn(kb, grad_scores)
        return carry

    lax.fori_loop(first // ROWS, i + 1, step, 0)
    for p in range(3):
        dq[:, p * 128 : (p + 1) * 128] = (one_above(dq_acc[p]) * 0.125).astype(bf16)

    @pl.when(i == count - 1)
    def _():
        dk[...] = dk_acc[...].astype(bf16)
        dv[...] = dv_acc[...].astype(bf16)
        at = pl.multiple_of(place[1] * SIDE, SIDE)
        for m in range(2):
            gwo[m] = gwo_acc[pl.ds(at, SIDE), m * PAIR : (m + 1) * PAIR].astype(bf16)


def attend_back(lens, place, q, k, v, mixed, lse, mine, other, wo):
    seq = q.shape[0]
    count = seq // ROWS
    row = pl.BlockSpec((ROWS, PAIR), lambda i, s, t: (i, 0))
    half = pl.BlockSpec((ROWS, D), lambda i, s, t: (lax.rem(i, count // 2), 0))
    wide = jax.ShapeDtypeStruct((seq, PAIR), bf16)
    return pl.pallas_call(
        attend_back_kernel,
        grid_spec=pltpu.PrefetchScalarGridSpec(
            num_scalar_prefetch=2,
            grid=(count,),
            in_specs=[
                row,
                full((seq, PAIR)),
                full((seq, PAIR)),
                row,
                pl.BlockSpec((8, ROWS), lambda i, s, t: (0, i)),
                half,
                half,
                full(wo.shape),
            ],
            out_specs=[row, full((seq, PAIR)), full((seq, PAIR)), full((2, SIDE, PAIR))],
            scratch_shapes=[
                pltpu.VMEM((seq, PAIR), f32),
                pltpu.VMEM((seq, PAIR), f32),
                pltpu.VMEM((3, 128, 2 * ROWS), f32),
                pltpu.VMEM((PAIR, D), f32),
            ],
        ),
        out_shape=[wide, wide, wide, jax.ShapeDtypeStruct((2, SIDE, PAIR), bf16)],
        compiler_params=params(),
        name="attend_back",
    )(lens, place, q, k, v, mixed, lse, mine, other, wo)


def mlp_kernel(
    place, tok, pas, vec, mine, other, cot, wo_mine, wo_other, w12,
    out_send, out_keep, gn_send, gn_keep, second_keep, grads,
    wom, woo, up, down, gup, gdown,
):
    i = pl.program_id(0)
    count = pl.num_programs(0)

    @pl.when(i == 0)
    def _():
        for h in range(2):
            for m in range(2):
                rows, cols = slice(h * SIDE, (h + 1) * SIDE), slice(m * PAIR, (m + 1) * PAIR)
                wom[rows, cols] = wo_mine[h, m]
                woo[rows, cols] = wo_other[h, m]
        for r in range(4):
            for m in range(2):
                rows, cols = slice(r * SIDE, (r + 1) * SIDE), slice(m * PAIR, (m + 1) * PAIR)
                up[rows, cols] = w12[2 * r + m]
                down[rows, cols] = w12[8 + 2 * r + m]
        gup[...] = jnp.zeros_like(gup)
        gdown[...] = jnp.zeros_like(gdown)

    first = embedded(tok[...], pas[...], vec[...])
    second = first + (nn(mine[...], wom[...]) + nn(other[...], woo[...]))
    hat, _ = hat_of(second)
    low = (hat * vec[PASSES + 2 : PASSES + 3] + vec[PASSES + 3 : PASSES + 4]).astype(bf16)
    upper = nn(low, up[...])
    square = upper * upper
    bent = jnp.tanh(gelu_coef * upper * (1.0 + 0.044715 * square))
    act = (0.5 * upper * (1.0 + bent)).astype(bf16)
    slope = 0.5 * (1.0 + bent) + (0.5 * gelu_coef) * upper * (1.0 - bent * bent) * (
        1.0 + (3 * 0.044715) * square
    )
    out_part = nn(act, down[...])
    grad_act = nt(cot[...], down[...])
    gdown[...] += tn(act, cot[...])
    grad_upper = (grad_act * slope).astype(bf16)
    gn_part = nt(grad_upper, up[...])
    gup[...] += tn(low, grad_upper)

    @pl.when(i < count // 2)
    def _():
        out_send[...] = out_part.astype(bf16)
        gn_send[...] = gn_part.astype(bf16)

    @pl.when(i >= count // 2)
    def _():
        out_keep[...] = out_part.astype(bf16)
        gn_keep[...] = gn_part
        second_keep[...] = second

    @pl.when(i == count - 1)
    def _():
        for r in range(4):
            for m in range(2):
                rows, cols = slice(r * SIDE, (r + 1) * SIDE), slice(m * PAIR, (m + 1) * PAIR)
                grads[2 * r + m] = gup[rows, cols].astype(bf16)
                grads[8 + 2 * r + m] = gdown[rows, cols].astype(bf16)


def mlp(place, tokens, passes, vec, mine, other, cotangent, wo_mine, wo_other, w12):
    seq = tokens.shape[0]
    count = seq // ROWS
    where = lambda i, s: lax.rem(i + (1 - s[0]) * (count // 2), count)
    row = lambda n: pl.BlockSpec((ROWS, n), lambda i, s: (where(i, s), 0))
    send = pl.BlockSpec((ROWS, D), lambda i, s: (jnp.minimum(i, count // 2 - 1), 0))
    keep = pl.BlockSpec((ROWS, D), lambda i, s: (jnp.maximum(i - count // 2, 0), 0))
    half = lambda kind: jax.ShapeDtypeStruct((seq // 2, D), kind)
    return pl.pallas_call(
        mlp_kernel,
        grid_spec=pltpu.PrefetchScalarGridSpec(
            num_scalar_prefetch=1,
            grid=(count,),
            in_specs=[
                row(D),
                pl.BlockSpec((1, ROWS), lambda i, s: (0, where(i, s))),
                full((16, D)),
                row(PAIR),
                row(PAIR),
                row(D),
                full(wo_mine.shape),
                full(wo_other.shape),
                full(w12.shape),
            ],
            out_specs=[send, keep, send, keep, keep, full((16, SIDE, PAIR))],
            scratch_shapes=[
                pltpu.VMEM((PAIR, D), bf16),
                pltpu.VMEM((PAIR, D), bf16),
                pltpu.VMEM((D, D), bf16),
                pltpu.VMEM((D, D), bf16),
                pltpu.VMEM((D, D), f32),
                pltpu.VMEM((D, D), f32),
            ],
        ),
        out_shape=[
            half(bf16),
            half(bf16),
            half(bf16),
            half(f32),
            half(f32),
            jax.ShapeDtypeStruct((16, SIDE, PAIR), bf16),
        ],
        compiler_params=params(),
        name="feed_forward",
    )(place, tokens, passes, vec, mine, other, cotangent, wo_mine, wo_other, w12)


def second_back_kernel(place, one, two, second, cot, vec, out, low, sums):
    @pl.when(pl.program_id(0) == 0)
    def _():
        sums[...] = jnp.zeros_like(sums)

    grad = one[...].astype(f32) + two[...].astype(f32)
    hat, root = hat_of(second[...])
    result = cot[...].astype(f32) + norm_back(hat, root, grad, vec[PASSES + 2 : PASSES + 3])
    out[...] = result
    low[...] = result.astype(bf16)
    sums[0:1] += jnp.sum(grad * hat, axis=0, keepdims=True)
    sums[1:2] += jnp.sum(grad, axis=0, keepdims=True)


def second_back(place, one, two, second, cotangent, vec):
    rows = one.shape[0]
    count = rows // ROWS
    row = pl.BlockSpec((ROWS, D), lambda i, s: (i, 0))
    mine = pl.BlockSpec((ROWS, D), lambda i, s: (i + s[0] * count, 0))
    return pl.pallas_call(
        second_back_kernel,
        grid_spec=pltpu.PrefetchScalarGridSpec(
            num_scalar_prefetch=1,
            grid=(count,),
            in_specs=[row, row, row, mine, full((16, D))],
            out_specs=[row, row, full((8, D))],
        ),
        out_shape=[
            jax.ShapeDtypeStruct((rows, D), f32),
            jax.ShapeDtypeStruct((rows, D), bf16),
            jax.ShapeDtypeStruct((8, D), f32),
        ],
        compiler_params=params(),
        name="second_back",
    )(place, one, two, second, cotangent, vec)


def project_back_kernel(place, norm, dq, dk, dv, cat, send, keep, grads, acc):
    i = pl.program_id(0)
    count = pl.num_programs(0)

    @pl.when(i == 0)
    def _():
        acc[...] = jnp.zeros_like(acc)

    total = nt(dq[...], cat[0]) + nt(dk[...], cat[1]) + nt(dv[...], cat[2])
    for x, grad in enumerate((dq, dk, dv)):
        mine = jnp.where(place[1] == 0, grad[:, :SIDE].astype(f32), grad[:, SIDE:].astype(f32))
        acc[x] += tn(norm[...], mine.astype(bf16))

    @pl.when(i < count // 2)
    def _():
        send[...] = total.astype(bf16)

    @pl.when(i >= count // 2)
    def _():
        keep[...] = total.astype(bf16)

    @pl.when(i == count - 1)
    def _():
        for x in range(3):
            for m in range(2):
                at = 2 * m * SIDE
                grads[2 * x + m] = jnp.concatenate(
                    [acc[x, at : at + SIDE], acc[x, at + SIDE : at + 2 * SIDE]], axis=1
                ).astype(bf16)


def project_back(place, norm, dq, dk, dv, cat):
    seq = norm.shape[0]
    count = seq // ROWS
    where = lambda i, s: lax.rem(i + (1 - s[0]) * (count // 2), count)
    row = lambda n: pl.BlockSpec((ROWS, n), lambda i, s: (where(i, s), 0))
    send = pl.BlockSpec((ROWS, D), lambda i, s: (jnp.minimum(i, count // 2 - 1), 0))
    keep = pl.BlockSpec((ROWS, D), lambda i, s: (jnp.maximum(i - count // 2, 0), 0))
    half = jax.ShapeDtypeStruct((seq // 2, D), bf16)
    return pl.pallas_call(
        project_back_kernel,
        grid_spec=pltpu.PrefetchScalarGridSpec(
            num_scalar_prefetch=1,
            grid=(count,),
            in_specs=[row(D), row(PAIR), row(PAIR), row(PAIR), full(cat.shape)],
            out_specs=[send, keep, full((6, SIDE, PAIR))],
            scratch_shapes=[pltpu.VMEM((3, D, SIDE), f32)],
        ),
        out_shape=[half, half, jax.ShapeDtypeStruct((6, SIDE, PAIR), bf16)],
        compiler_params=params(),
        name="project_back",
    )(place, norm, dq, dk, dv, cat)


def first_back_kernel(place, tok, pas, vec, one, two, grad_second, low, sums):
    @pl.when(pl.program_id(0) == 0)
    def _():
        sums[...] = jnp.zeros_like(sums)

    grad = one[...].astype(f32) + two[...].astype(f32)
    hat, root = hat_of(embedded(tok[...], pas[...], vec[...]))
    result = grad_second[...] + norm_back(hat, root, grad, vec[PASSES : PASSES + 1])
    low[...] = result.astype(bf16)
    chosen = one_hot(pas[...])
    high, mid, rest = split_three(result)
    sums[...] += nn(chosen, high) + nn(chosen, mid) + nn(chosen, rest)
    sums[PASSES : PASSES + 1] += jnp.sum(grad * hat, axis=0, keepdims=True)
    sums[PASSES + 1 : PASSES + 2] += jnp.sum(grad, axis=0, keepdims=True)


def first_back(place, tokens, passes, vec, one, two, grad_second):
    rows = one.shape[0]
    count = rows // ROWS
    row = pl.BlockSpec((ROWS, D), lambda i, s: (i, 0))
    mine = pl.BlockSpec((ROWS, D), lambda i, s: (i + s[0] * count, 0))
    return pl.pallas_call(
        first_back_kernel,
        grid_spec=pltpu.PrefetchScalarGridSpec(
            num_scalar_prefetch=1,
            grid=(count,),
            in_specs=[
                mine,
                pl.BlockSpec((1, ROWS), lambda i, s: (0, i + s[0] * count)),
                full((16, D)),
                row,
                row,
                row,
            ],
            out_specs=[row, full((16, D))],
        ),
        out_shape=[
            jax.ShapeDtypeStruct((rows, D), bf16),
            jax.ShapeDtypeStruct((16, D), f32),
        ],
        compiler_params=params(),
        name="first_back",
    )(place, tokens, passes, vec, one, two, grad_second)


def precondition(grad, weight, left, right, left_root, right_root):
    high = lax.Precision.HIGHEST
    left_new = decay * left + (1.0 - decay) * jnp.einsum(
        "...ij,...kj->...ik", grad, grad, precision=high
    )
    right_new = decay * right + (1.0 - decay) * jnp.einsum(
        "...ji,...jk->...ik", grad, grad, precision=high
    )
    half = jnp.einsum("...ij,...jk->...ik", left_root, grad, precision=high)
    step = jnp.einsum("...ij,...jk->...ik", half, right_root, precision=high)
    return (left_new, right_new, step, weight - rate_matrix * step)


def to_pairs(blocks):
    n = blocks.shape[0] // 2
    return blocks.reshape(n, 2, SIDE, SIDE).transpose(0, 2, 1, 3).reshape(n, SIDE, PAIR)


def from_pairs(pairs):
    n = pairs.shape[0]
    return pairs.reshape(n, SIDE, 2, SIDE).transpose(0, 2, 1, 3).reshape(2 * n, SIDE, SIDE)


def swap(value, bit):
    return lax.ppermute(value, "tensor", [(t, t ^ bit) for t in range(NT)])


def on_device(
    tokens,
    pass_ids,
    doc_lengths,
    cotangent,
    block_weights,
    vector_params,
    vector_moment,
    block_left,
    block_right,
    block_left_root,
    block_right_root,
):
    t = lax.axis_index("tensor")
    core, side = t % 2, t // 2
    place = jnp.stack([core, side]).astype(jnp.int32)
    lens = doc_lengths[0]
    seq = tokens.shape[0]
    passes = pass_ids.reshape(1, seq)
    total_blocks = (D // SIDE) * (4 + 2 * (FF // D))
    n_dp = lax.axis_size("dp")

    every = lax.all_gather(block_weights.astype(bf16), "dp", axis=1, tiled=True)[0]
    slots = every.shape[0]
    pairs = to_pairs(every[:total_blocks])
    vec = lax.all_gather(vector_params, "dp", axis=1, tiled=True)
    vec = jnp.pad(vec, ((0, 16 - vec.shape[0]), (0, 0)))
    shared = pairs[:8]
    shared_far = swap(shared, 2)
    both = jnp.where(side == 0, jnp.stack([shared, shared_far]), jnp.stack([shared_far, shared]))
    wq, wo_mine = both[:, :6], both[:, 6:]
    wo_other = swap(wo_mine, 1)
    w12 = pairs[8:]

    norm, q, k, v, cat = project(tokens, passes, vec, wq)
    mine, lse = attend(lens, q, k, v)
    other = swap(mine, 1)
    out_send, out_keep, gn_send, gn_keep, second, grads_12 = mlp(
        place, tokens, passes, vec, mine, other, cotangent, wo_mine, wo_other, w12
    )
    gn_chip = (gn_keep + swap(gn_send, 1).astype(f32)).astype(bf16)
    gn_far = swap(gn_chip, 2)
    grad_second, grad_attn, sums_two = second_back(place, gn_chip, gn_far, second, cotangent, vec)
    grad_attn_other = swap(grad_attn, 1)
    dq, dk, dv, grads_o = attend_back(
        lens, place, q, k, v, mine, lse, grad_attn, grad_attn_other, wo_mine
    )
    g1_send, g1_keep, grads_qkv = project_back(place, norm, dq, dk, dv, cat)
    low_half, sums_one = first_back(
        place, tokens, passes, vec, g1_keep, swap(g1_send, 1), grad_second
    )
    out_chip = (out_keep.astype(f32) + swap(out_send, 1).astype(f32)).astype(bf16)
    out_half = (second + (out_chip.astype(f32) + swap(out_chip, 2).astype(f32))).astype(bf16)

    def join(half):
        far = swap(half, 1)
        low = jnp.where(core == 0, half, far)
        high = jnp.where(core == 0, far, half)
        return jnp.concatenate([low, high], axis=0)

    output, input_grad = join(out_half), join(low_half)
    vector_part = jnp.concatenate([sums_one[: PASSES + 2], sums_two[:2]], axis=0)
    vector_part = vector_part + swap(vector_part, 1)
    grad_blocks = from_pairs(jnp.concatenate([grads_qkv, grads_o, grads_12], axis=0)).astype(f32)
    spare = jnp.zeros((slots - total_blocks, SIDE, SIDE), f32)
    grad_blocks = jnp.concatenate([grad_blocks, spare], axis=0)[None]
    owned = lax.psum_scatter(grad_blocks, "dp", scatter_dimension=1, tiled=True)
    vector_grad = lax.psum_scatter(vector_part, "dp", scatter_dimension=1, tiled=True)
    left_new, right_new, step, weight_new = precondition(
        owned, block_weights, block_left, block_right, block_left_root, block_right_root
    )
    moment_new = decay * vector_moment + (1.0 - decay) * vector_grad * vector_grad
    vector_new = vector_params - rate_vector * vector_grad / (jnp.sqrt(moment_new) + moment_eps)
    return (
        output,
        input_grad,
        left_new,
        right_new,
        step,
        weight_new,
        vector_grad,
        moment_new,
        vector_new,
    )


def solution(mesh):
    rows, line = P("dp", None), P(None, "dp")
    block = P("tensor", "dp", None, None)
    return jax.shard_map(
        on_device,
        mesh=mesh,
        in_specs=(rows, P("dp"), rows, rows, block, line, line, block, block, block, block),
        out_specs=(rows, rows, block, block, block, block, line, line, line),
        check_vma=False,
    )
```

time: 970 us -> 627 us (0.65)
  matrix products: 235 us -> 11.2 us
  Pallas kernels: 0 us -> 158 us
  waiting for transfers between devices: 433 us -> 327 us
  other arithmetic: 111 us -> 22.7 us
  local copies, waits for them, and re-layouts: 110 us -> 52 us
  loops' own time: 17.1 us -> 0 us
    dot_general x45 -> x4, matrix products: 231 us -> 11.2 us  [the longest x1 3.49 us: precondition(): jnp.einsum('...ij,...kj->...ik', grad, grad, precision=high)]
    reduce_scatter x5 -> x1, waiting for transfers between devices: 319 us -> 156 us  [on_device(): owned = lax.psum_scatter(grad_blocks, 'dp', scatter_dimension=1, tiled=True)]
    pallas_call x0 -> x7, Pallas kernels: none -> 158 us  [the longest x1 41 us: attend_back(): pl.pallas_call(attend_back_kernel, grid_spec=pltpu.PrefetchScalarGridSpec...]
    ppermute x0 -> x12, waiting for transfers between devices: none -> 87.7 us  [swap(): return lax.ppermute(value, 'tensor', [(t, t ^ bit) for t in range(NT)])]
    reduce_sum x12 -> x0, other arithmetic: 41.5 us -> none  [the longest x4 27.3 us: one_block(): total = jnp.sum(jnp.exp(scores - top), axis=-1, keepdims=True)]
    convert_element_type x11 -> x4, other arithmetic: 41.8 us -> 5.46 us  [the longest x1 2.29 us: on_device(): gn_chip = (gn_keep + swap(gn_send, 1).astype(f32)).astype(bf16)]
    all_gather x5 -> x1, waiting for transfers between devices: 113 us -> 83.8 us  [on_device(): lax.all_gather(block_weights.astype(bf16), 'dp', axis=1, tiled=True)[0]]
    unnamed x85 -> x43, local copies, waits for them, and re-layouts: 27.9 us -> 8.7 us
  transfers between devices with their start and end apart: 11 -> 15, of which waited for: 10 -> 9; matrix products, arithmetic and copies ran while one was open for 13% -> 7% of each run, Pallas kernels for 0% -> 0%
where the time goes in v1:
time: 627 us; the launch traced here: 621 us
  waiting for transfers between devices  327 us (52%)
  Pallas kernels  158 us (25%)
  local copies, waits for them, and re-layouts  52 us (8%)
  blocking collectives  30.7 us (5%)
  other arithmetic  22.7 us (4%)
  between operations  14.4 us (2%)
  matrix products  11.2 us (2%)
    reduce_scatter x1, waiting for transfers between devices, on_device(): owned = lax.psum_scatter(grad_blocks, 'dp', scatter_dimension=1, tiled=True)  156 us
    ppermute x12, waiting for transfers between devices, swap(): return lax.ppermute(value, 'tensor', [(t, t ^ bit) for t in range(NT)])  87.7 us
    all_gather x1, waiting for transfers between devices, on_device(): lax.all_gather(block_weights.astype(bf16), 'dp', axis=1, tiled=True)[0]  83.8 us
    pallas_call x1, Pallas kernels, attend_back(): pl.pallas_call(attend_back_kernel, grid_spec=pltpu.PrefetchScalarGridSpec...  41 us
    pallas_call x1, Pallas kernels, mlp(): pl.pallas_call(mlp_kernel, grid_spec=pltpu.PrefetchScalarGridSpec(num_sca...  37.7 us
    pallas_call x1, Pallas kernels, attend(): pl.pallas_call(attend_kernel, grid_spec=pltpu.PrefetchScalarGridSpec(num_...  32 us
    all_gather x1, blocking collectives, on_device(): vec = lax.all_gather(vector_params, 'dp', axis=1, tiled=True)  30.7 us
    pallas_call x1, Pallas kernels, project(): pl.pallas_call(project_kernel, grid=(seq // ROWS,), in_specs=[row(D), pl....  16.1 us
  transfers between devices with their start and end apart: 15, of which 9 were waited for; matrix products, arithmetic and copies ran while one was open for 7% of the time, Pallas kernels for 0%

profile of v1, /device:TPU:0, one launch (start us, length us, event | category | flops | bytes accessed | tf_op | source)
XLA Modules:
  0.0 620.9 jit_solution(13929068305597617476)
XLA Ops:
  7.2 2.2 bitcast_convert_fusion
  9.5 83.8 %all-gather.3.cloned.1.call-done = bf16[1,48,192,192]{3,2,0,1:T(8,128)(2,1)} async-done(((bf16[1,6,192,192]{3,2,0,1:T(8,128)(2,1)}), bf16[1,48,192,192]{3,2,0,1:T(8,128)(2,1)}) %all-gather.3.cloned.1.call-update) | async-done | bytes 3538960 | tf_op jit(solution)/shard_map/all_gather | solution.py:606
  93.4 9.4 %copy.39 = bf16[24,2,192,192]{3,1,2,0:T(2,128)(2,1)} copy(bf16[24,2,192,192]{3,2,1,0:T(8,128)(2,1)} %bitcast.55) | data formatting | bytes 7077888 | tf_op jit(solution)/shard_map/reshape;squeeze | solution.py:572
  102.8 2.5 slice.40
  105.3 1.7 slice.31
  107.0 1.5 collective-permute-start
  108.5 30.7 %all-gather = f32[8,96,9]{1,2,0:T(8,128)S(1)} all-gather(f32[1,96,9]{1,2,0:T(8,128)S(1)} %bitcast.63), channel_id=1, replica_groups=mesh['dp'=8,'tensor'=4] {'dp'}, dimensions={0}, use_global_device_ids=true | all-gather | bytes 31104 | tf_op jit(solution)/shard_map/all_gather | solution.py:609
  139.1 0.1 reshape.65
  139.2 0.6 pad.4.vec
  139.9 1.7 stack.26
  141.5 2.9 maximum_select_fusion
  144.5 1.4 slice.41.wq
  145.8 16.1 %project.1 = (bf16[2048,768]{1,0:T(8,128)(2,1)}, bf16[2048,384]{1,0:T(8,128)(2,1)}, bf16[2048,384]{1,0:T(8,128)(2,1)}, bf16[2048,384]{1,0:T(8,128)(2,1)}, bf16[3,768,384]{2,1,0:T(8,128)(2,1)}) custom-call(bf16[2048,768]{1,0:T(8,128)(2,1)} %tok.5, s32[1,2048]{1,0:T(1,128)} %bitcast.59, f32[16,768]{1,0:T(8,128)} %pad.4.vec, bf16[2,6,192,384]{3,2,1,0:T(8,128)(2,1)} %slice.41.wq), custom_call_target="tpu_custom_call" | custom-call | tf_op jit(solution)/shard_map/project/pallas_call | solution.py:106
  161.9 32.0 %attend.1 = (bf16[2048,384]{1,0:T(8,128)(2,1)}, f32[8,2048]{1,0:T(8,128)}) custom-call(s32[8]{0:T(128)} %bitcast.64, bf16[2048,384]{1,0:T(8,128)(2,1)} %get-tuple-element.34.q, bf16[2048,384]{1,0:T(8,128)(2,1)} %get-tuple-element.35.k, bf16[2048,384]{1,0:T(8,128)(2,1)} %get-tuple-element.36.v), custom_call_target="tpu_custom_call" | custom-call | tf_op jit(solution)/shard_map/attend/pallas_call | solution.py:184
  194.0 0.6 collective-permute-start.2
  194.6 0.6 pad_add_fusion.place
  195.2 5.9 slice.43
  201.0 7.4 %slice.35.w12 = bf16[16,192,384]{2,1,0:T(8,128)(2,1)} reshape(bf16[16,192,2,192]{3,2,1,0:T(2,128)(2,1)} %slice.43) | data formatting | bytes 4718592 | tf_op jit(solution)/shard_map/slice | solution.py:616
  208.4 1.2 copy-done.9
  209.6 37.7 %feed_forward.1 = (bf16[1024,768]{1,0:T(8,128)(2,1)}, bf16[1024,768]{1,0:T(8,128)(2,1)}, bf16[1024,768]{1,0:T(8,128)(2,1)}, f32[1024,768]{1,0:T(8,128)}, f32[102...) custom-call(s32[2]{0:T(128)} %pad_add_fusion.place, bf16[2048,768]{1,0:T(8,128)(2,1)} %tok.5, s32[1,2048]{1,0:T(1,128)} %bitcast.60, ...), custom_call_target="tpu_custom_call" | custom-call | tf_op jit(solution)/shard_map/feed_forward/pallas_call | solution.py:382
  247.3 0.1 collective-permute-start.6
  247.4 3.6 collective-permute-done.6
  251.0 2.3 add_convert_fusion.one
  253.3 0.6 collective-permute-start.7
  253.9 35.9 %collective-permute-done.7.two = bf16[1024,768]{1,0:T(8,128)(2,1)S(1)} collective-permute-done((bf16[1024,768]{1,0:T(8,128)(2,1)S(1)}, bf16[1024,768]{1,0:T(8,128)(2,1)S(1)}, u32[]{:S(2)}, u32[]{:S(2)}) %collective-permute-start.7) | collective-permute-done | bytes 1572896 | tf_op jit(solution)/shard_map/ppermute | solution.py:581
  289.8 1.2 copy-done.7
  291.0 7.5 %second_back.1 = (f32[1024,768]{1,0:T(8,128)}, bf16[1024,768]{1,0:T(8,128)(2,1)}, f32[8,768]{1,0:T(8,128)}) custom-call(s32[2]{0:T(128)} %pad_add_fusion.place, bf16[1024,768]{1,0:T(8,128)(2,1)} %copy-done.3, bf16[1024,768]{1,0:T(8,128)(2,1)} %copy-done.7, f32[1024,768]{1,0:T(8,128)} %get-tuple-element.38.second, bf16[2048,768]{1,0:T(8,128)(2,1)} %cot.3, ...), custom_call_target="tpu_custom_call" | custom-call | tf_op jit(solution)/shard_map/second_back/pallas_call | solution.py:440
  298.5 3.6 collective-permute-done.8.other
  302.1 1.2 copy-done.11
  303.3 41.0 %attend_back.1 = (bf16[2048,384]{1,0:T(8,128)(2,1)}, bf16[2048,384]{1,0:T(8,128)(2,1)}, bf16[2048,384]{1,0:T(8,128)(2,1)}, bf16[2,192,384]{2,1,0:T(8,128)(2,1)}) custom-call(s32[8]{0:T(128)} %bitcast.65, s32[2]{0:T(128)} %pad_add_fusion.place, bf16[2048,384]{1,0:T(8,128)(2,1)} %get-tuple-element.34.q, bf16[2048,384]{1,0:T(8,128)(2,1)} %get-tuple-element.35.k, ...), custom_call_target="tpu_custom_call" | custom-call | tf_op jit(solution)/shard_map/attend_back/pallas_call | solution.py:284
  344.3 14.2 %project_back.1 = (bf16[1024,768]{1,0:T(8,128)(2,1)}, bf16[1024,768]{1,0:T(8,128)(2,1)}, bf16[6,192,384]{2,1,0:T(8,128)(2,1)}) custom-call(s32[2]{0:T(128)} %pad_add_fusion.place, bf16[2048,768]{1,0:T(8,128)(2,1)} %get-tuple-element.41.norm, bf16[2048,384]{1,0:T(8,128)(2,1)} %get-tuple-element.46.dq, bf16[2048,384]{1,0:T(8,128)(2,1)} %get-tuple-element.47.dk, ...), custom_call_target="tpu_custom_call" | custom-call | tf_op jit(solution)/shard_map/project_back/pallas_call | solution.py:497
  358.5 0.2 collective-permute-start.9
  358.7 0.9 slice.39
  359.6 1.3 constant_dynamic-update-slice_fusion.2
  360.9 0.5 constant_dynamic-update-slice_fusion
  361.4 0.8 collective-permute-done.9.two
  362.2 1.1 copy-done.10
  363.3 9.2 %first_back.1 = (bf16[1024,768]{1,0:T(8,128)(2,1)}, f32[16,768]{1,0:T(8,128)}) custom-call(s32[2]{0:T(128)} %pad_add_fusion.place, bf16[2048,768]{1,0:T(8,128)(2,1)} %tok.5, s32[1,2048]{1,0:T(1,128)} %bitcast.61, f32[16,768]{1,0:T(8,128)} %pad.4.vec, bf16[1024,768]{1,0:T(8,128)(2,1)} %get-tuple-element.50.one, bf16[1024,768]{1,0:T(8,128)(2,1)} %copy-done.10, ...), custom_call_target="tpu_custom_call" | custom-call | tf_op jit(solution)/shard_map/first_back/pallas_call | solution.py:533
  372.5 0.7 slice.38
  373.3 0.2 collective-permute-start.11
  373.5 2.8 fusion.14
  376.3 0.6 fusion.12
  377.0 1.7 copy.36
  378.8 4.8 pad_maximum_fusion
  383.5 7.8 %copy.29 = f32[1,48,192,192]{2,3,1,0:T(8,128)} copy(bf16[1,48,192,192]{3,2,1,0:T(8,128)(2,1)} %bitcast.54) | data formatting | bytes 10616832 | tf_op jit(solution)/shard_map/convert_element_type | solution.py:647
  391.4 0.4 collective-permute-start.3
  391.8 3.3 collective-permute-done.3
  395.1 0.5 add_convert_fusion.2
  395.5 0.6 collective-permute-start.4
  396.2 36.1 %collective-permute-done.4 = bf16[1024,768]{1,0:T(8,128)(2,1)S(1)} collective-permute-done((bf16[1024,768]{1,0:T(8,128)(2,1)S(1)}, bf16[1024,768]{1,0:T(8,128)(2,1)S(1)}, u32[]{:S(2)}, u32[]{:S(2)}) %collective-permute-start.4) | collective-permute-done | bytes 1572896 | tf_op jit(solution)/shard_map/ppermute | solution.py:581
  432.3 0.5 add_convert_fusion.1
  432.8 0.5 collective-permute-start.10
  433.3 4.5 collective-permute-done.5
  437.8 1.6 broadcast_select_fusion.3
  439.4 1.9 pad_maximum_fusion.1
  441.3 0.9 copy.37
  442.2 0.6 divide_subtract_fusion
  442.8 2.1 broadcast_select_fusion.1
  444.9 2.1 pad_maximum_fusion.2
  447.1 155.6 %reduce-scatter.5.cloned.1.call-done = f32[1,6,192,192]{2,3,1,0:T(8,128)} async-done(((f32[1,48,192,192]{2,3,1,0:T(8,128)}), f32[1,6,192,192]{2,3,1,0:T(8,128)}) %reduce-scatter.5.cloned.1.call-update) | async-done | bytes 884752 | tf_op jit(solution)/shard_map/reduce_scatter | solution.py:650
  602.7 2.6 fusion.6
  605.4 2.7 bitcast_subtract_fusion
  608.1 2.3 fusion.3
  610.4 3.5 fusion.1
  (53 shorter events, 0.5 us)
Async XLA Ops:
  7.2 598.1 %copy-start = (f32[1,6,192,192]{3,2,1,0:T(8,128)S(1)}, f32[1,6,192,192]{3,2,1,0:T(8,128)}, u32[]{:S(2)}) copy-start(f32[1,6,192,192]{3,2,1,0:T(8,128)} %param.21) | copy-start | bytes 2654212
  7.2 86.2 %all-gather.3.cloned.1.call-start = ((), (), s32[]{:S(2)}) async-start(), calls=%async_computation.2 | async-start | bytes 5308416 | tf_op jit(solution)/shard_map/all_gather | solution.py:606
  9.5 431.8 %reduce-scatter.7.cloned.1.call-start = ((), (), s32[]{:S(2)}) async-start(), calls=%async_computation.4 | async-start | bytes 442368
  105.3 3.2 copy-start.16
  107.0 34.5 %collective-permute-start = (bf16[8,192,384]{2,1,0:T(8,128)(2,1)}, bf16[8,192,384]{2,1,0:T(8,128)(2,1)}, u32[]{:S(2)}, u32[]{:S(2)}) collective-permute-start(bf16[8,192,384]{2,1,0:T(8,128)(2,1)} %slice.31), channel_id=1, source_target_pairs={{0,2},{1,3},{2,0},{3,1},{4,6},{5,7},{6,4},{7,5},{8,10},{9,11},{10,... | collective-permute-start | bytes 3538952 | tf_op jit(solution)/shard_map/ppermute | solution.py:581
  193.9 14.5 %collective-permute-start.1 = (bf16[2048,384]{1,0:T(8,128)(2,1)}, bf16[2048,384]{1,0:T(8,128)(2,1)S(1)}, u32[]{:S(2)}, u32[]{:S(2)}) collective-permute-start(bf16[2048,384]{1,0:T(8,128)(2,1)} %get-tuple-element.37.mine.mixed), channel_id=1, source_target_pairs={{0,1},{1,0},{2,3},{3,2},{4,5},{5,4},{6,7},{7,6},{8,9},{9,8},{10,11... | collective-permute-start | bytes 4718600 | tf_op jit(solution)/shard_map/ppermute | solution.py:581
  194.0 7.0 %copy-start.4 = (bf16[2,2,192,384]{3,2,1,0:T(8,128)(2,1)}, bf16[2,2,192,384]{3,2,1,0:T(8,128)(2,1)S(1)}, u32[]{:S(2)}) copy-start(bf16[2,2,192,384]{3,2,1,0:T(8,128)(2,1)S(1)} %slice.42.wo_mine.wo) | copy-start | bytes 1769476
  194.0 14.4 %collective-permute-start.2 = (bf16[2,2,192,384]{3,2,1,0:T(8,128)(2,1)S(1)}, bf16[2,2,192,384]{3,2,1,0:T(8,128)(2,1)}, u32[]{:S(2)}, u32[]{:S(2)}) collective-permute-start(bf16[2,2,192,384]{3,2,1,0:T(8,128)(2,1)S(1)} %slice.42.wo_mine.wo), channel_id=1, source_target_pairs={{0,1},{1,0},{2,3},{3,2},{4,5},{5,4},{6,7},{7,6},{8,9},{9,8},{10,11... | collective-permute-start | bytes 1769480 | tf_op jit(solution)/shard_map/ppermute | solution.py:581
  208.4 1.2 copy-start.9
  247.3 3.7 collective-permute-start.6
  253.3 36.5 %copy-start.3 = (bf16[1024,768]{1,0:T(8,128)(2,1)}, bf16[1024,768]{1,0:T(8,128)(2,1)S(1)}, u32[]{:S(2)}) copy-start(bf16[1024,768]{1,0:T(8,128)(2,1)S(1)} %add_convert_fusion.one) | copy-start | bytes 4718596
  253.3 36.5 %collective-permute-start.7 = (bf16[1024,768]{1,0:T(8,128)(2,1)S(1)}, bf16[1024,768]{1,0:T(8,128)(2,1)S(1)}, u32[]{:S(2)}, u32[]{:S(2)}) collective-permute-start(bf16[1024,768]{1,0:T(8,128)(2,1)S(1)} %add_convert_fusion.one), channel_id=1, source_target_pairs={{0,2},{1,3},{2,0},{3,1},{4,6},{5,7},{6,4},{7,5},{8,10},{9,11},{10,... | collective-permute-start | bytes 4718600 | tf_op jit(solution)/shard_map/ppermute | solution.py:581
  289.8 1.2 copy-start.7
  298.5 3.7 collective-permute-start.8
  302.1 1.2 copy-start.11
  344.3 16.5 %copy-start.15 = (bf16[2,192,384]{2,1,0:T(8,128)(2,1)S(1)}, bf16[2,192,384]{2,1,0:T(8,128)(2,1)}, u32[]{:S(2)}) copy-start(bf16[2,192,384]{2,1,0:T(8,128)(2,1)} %get-tuple-element.55) | copy-start | bytes 884740
  358.5 2.4 copy-start.6
  358.5 3.7 collective-permute-start.9
  362.2 1.1 copy-start.10
  373.3 3.1 collective-permute-start.11
  378.7 224.0 %reduce-scatter.5.cloned.1.call-start = ((), (), s32[]{:S(2)}) async-start(), calls=%async_computation.3 | async-start | bytes 10616832 | tf_op jit(solution)/shard_map/reduce_scatter | solution.py:650
  391.4 3.7 copy-start.8
  391.4 3.7 collective-permute-start.3
  395.1 37.2 %copy-start.1 = (f32[1024,768]{1,0:T(8,128)S(1)}, f32[1024,768]{1,0:T(8,128)}, u32[]{:S(2)}) copy-start(f32[1024,768]{1,0:T(8,128)} %get-tuple-element.38.second) | copy-start | bytes 9437188
  395.5 36.7 %collective-permute-start.4 = (bf16[1024,768]{1,0:T(8,128)(2,1)S(1)}, bf16[1024,768]{1,0:T(8,128)(2,1)S(1)}, u32[]{:S(2)}, u32[]{:S(2)}) collective-permute-start(bf16[1024,768]{1,0:T(8,128)(2,1)S(1)} %add_convert_fusion.2), channel_id=1, source_target_pairs={{0,2},{1,3},{2,0},{3,1},{4,6},{5,7},{6,4},{7,5},{8,10},{9,11},{10,... | collective-permute-start | bytes 4718600 | tf_op jit(solution)/shard_map/ppermute | solution.py:581
  432.8 5.1 collective-permute-start.5
  432.8 10.0 %collective-permute-start.10 = (bf16[1024,768]{1,0:T(8,128)(2,1)}, bf16[1024,768]{1,0:T(8,128)(2,1)}, u32[]{:S(2)}, u32[]{:S(2)}) collective-permute-start(bf16[1024,768]{1,0:T(8,128)(2,1)} %get-tuple-element.53), channel_id=1, source_target_pairs={{0,1},{1,0},{2,3},{3,2},{4,5},{5,4},{6,7},{7,6},{8,9},{9,8},{10,11... | collective-permute-start | bytes 4718600 | tf_op jit(solution)/shard_map/ppermute | solution.py:581
  439.4 2.8 copy-start.18
  442.2 2.7 copy-start.17
  444.9 157.8 %copy-start.12 = (f32[1,6,192,192]{3,2,1,0:T(8,128)S(1)}, f32[1,6,192,192]{3,2,1,0:T(8,128)}, u32[]{:S(2)}) copy-start(f32[1,6,192,192]{3,2,1,0:T(8,128)} %param.20) | copy-start | bytes 2654212
  447.1 158.3 %copy-start.5 = (f32[1,6,192,192]{3,2,1,0:T(8,128)S(1)}, f32[1,6,192,192]{3,2,1,0:T(8,128)}, u32[]{:S(2)}) copy-start(f32[1,6,192,192]{3,2,1,0:T(8,128)} %param.15) | copy-start | bytes 2654212
  605.3 2.7 copy-start.2
  605.3 2.7 copy-start.13
  608.1 2.4 copy-start.14
Sparse Core Ops, SparseCore 0:
  10.8 82.5 all-gather.2
  378.8 57.7 reduce-scatter.6
  440.2 162.4 reduce-scatter.4

commit v2 on v1

--- a/solution.py
+++ b/solution.py
@@ -26,6 +26,7 @@
 masked_score = -1e30
 f32 = jnp.float32
 bf16 = jnp.bfloat16
+MESH = pl.DeviceIdType.MESH
 VMEM_LIMIT = 56 * 1024 * 1024
 
 
@@ -80,6 +81,165 @@
 
 def full(shape):
     return pl.BlockSpec(shape, lambda *_: (0,) * len(shape))
+
+
+def gather_kernel(own, vec_own, all_pairs, vec_out, pack, vec_pack, vec_land, *sems):
+    (s_z1, r_z1, s_x1, r_x1, s_y1, r_y1, s_d1, r_d1, s_l, r_l, s_r, r_r, s_x2, r_x2, s_y2, r_y2, s_v, r_v, loc) = sems
+    dp, t = lax.axis_index("dp"), lax.axis_index("tensor")
+    z, x = dp // 2, dp % 2
+    y, core = t // 2, t % 2
+    far_x, far_y = z * 2 + (1 - x), (1 - y) * 2 + core
+
+    barrier = pltpu.get_barrier_semaphore()
+    peers = [lax.rem(dp + k, 8) for k in range(1, 8)]
+    for peer in peers:
+        pl.semaphore_signal(barrier, inc=1, device_id={"dp": peer, "tensor": t}, device_id_type=MESH)
+    pl.semaphore_signal(barrier, inc=1, device_id={"dp": dp, "tensor": far_y}, device_id_type=MESH)
+
+    for m in range(3):
+        pack[m] = jnp.concatenate([own[0, 2 * m], own[0, 2 * m + 1]], axis=1).astype(bf16)
+    vec_pack[...] = jnp.zeros_like(vec_pack)
+    vec_pack[0 : PASSES + 4, 0 : D // 8] = vec_own[...]
+    pl.semaphore_wait(barrier, 8)
+
+    started = []
+
+    def send(src, dst, s_sem, r_sem, dp_to, t_to, cond=None):
+        copy = pltpu.make_async_remote_copy(
+            src_ref=src,
+            dst_ref=dst,
+            send_sem=s_sem,
+            recv_sem=r_sem,
+            device_id={"dp": dp_to, "tensor": t_to},
+            device_id_type=MESH,
+        )
+        started.append((cond, copy))
+        if cond is None:
+            copy.start()
+        else:
+            pl.when(cond)(copy.start)
+
+    def arrived(dst, r_sem, cond=None):
+        copy = pltpu.make_async_remote_copy(
+            src_ref=dst,
+            dst_ref=dst,
+            send_sem=loc,
+            recv_sem=r_sem,
+            device_id={"dp": far_x, "tensor": t},
+            device_id_type=MESH,
+        )
+        if cond is None:
+            copy.wait_recv()
+        else:
+            pl.when(cond)(copy.wait_recv)
+
+    own_copy = pltpu.make_async_copy(pack, all_pairs.at[y, pl.ds(3 * dp, 3)], loc)
+    own_copy.start()
+
+    for m in range(3):
+        send(pack.at[m], all_pairs.at[y, 3 * dp + m], s_l.at[0, m], r_l.at[0, m], dp - 2, t, z > 0)
+    for k, peer in enumerate(peers):
+        send(vec_pack, vec_land.at[dp], s_v.at[k], r_v.at[dp], peer, t)
+    for m in range(3):
+        send(pack.at[m], all_pairs.at[y, 3 * dp + m], s_x2.at[z, m], r_x2.at[z, m], far_x, t, z > m)
+    own_copy.wait()
+
+    half = SIDE // 2
+
+    def piece(side, column, k):
+        return all_pairs.at[side, 3 * column + k // 2, pl.ds((k % 2) * half, half)]
+
+    def diagonal(k):
+        arrived(piece(y, 1 - x, k), r_x1.at[k])
+        send(piece(y, 1 - x, k), piece(y, 1 - x, k), s_d1.at[k], r_d1.at[k], dp, far_y)
+
+    def from_right(d, m):
+        arrived(all_pairs.at[y, 3 * dp + 6 * d + m], r_l.at[d - 1, m], z + d < 4)
+        if d < 3:
+            ref = all_pairs.at[y, 3 * dp + 6 * d + m]
+            send(ref, ref, s_l.at[d, m], r_l.at[d, m], dp - 2, t, (z + d < 4) & (z > 0))
+
+    def right_along_x(d, m):
+        ref = all_pairs.at[y, 3 * dp + 6 * d + m]
+        send(ref, ref, s_x2.at[z + d, m], r_x2.at[z + d, m], far_x, t, z + d < 4)
+
+    for k in range(6):
+        arrived(piece(y, x, k), r_z1.at[k], z > 0)
+        send(piece(y, x, k), piece(y, x, k), s_z1.at[k], r_z1.at[k], dp + 2, t, z < 3)
+        send(piece(y, x, k), piece(y, x, k), s_x1.at[k], r_x1.at[k], far_x, t)
+        send(piece(y, x, k), piece(y, x, k), s_y1.at[k], r_y1.at[k], dp, far_y)
+        if k >= 1:
+            diagonal(k - 1)
+        if k % 2 == 1:
+            from_right(1, k // 2)
+    diagonal(5)
+
+    for m in range(3):
+        send(pack.at[m], all_pairs.at[y, 3 * dp + m], s_x2.at[z, m], r_x2.at[z, m], far_x, t, (z > 0) & (z <= m))
+    for m in range(3):
+        send(pack.at[m], all_pairs.at[y, 3 * dp + m], s_r.at[0, m], r_r.at[0, m], dp + 2, t, (z > 0) & (z < 3))
+    for m in range(3):
+        right_along_x(1, m)
+    for d in (2, 3):
+        for m in range(3):
+            from_right(d, m)
+            right_along_x(d, m)
+    for d in (1, 2):
+        for m in range(3):
+            ref = all_pairs.at[y, 3 * dp - 6 * d + m]
+            arrived(ref, r_r.at[d - 1, m], z - d > 0)
+            if d == 1:
+                send(ref, ref, s_r.at[1, m], r_r.at[1, m], dp + 2, t, (z - d > 0) & (z < 3))
+            send(ref, ref, s_x2.at[z - d, m], r_x2.at[z - d, m], far_x, t, z - d > 0)
+    for m in range(2):
+        ref = all_pairs.at[y, 6 + m]
+        arrived(ref, r_x2.at[1, m], x == 1)
+        send(ref, ref, s_y2.at[m], r_y2.at[m], dp, far_y)
+
+    for k in range(6):
+        arrived(piece(1 - y, x, k), r_y1.at[k])
+        arrived(piece(1 - y, 1 - x, k), r_d1.at[k])
+    for w in range(1, 4):
+        for m in range(3):
+            ref = all_pairs.at[y, 6 * w + 3 * (1 - x) + m]
+            if w == 1 and m < 2:
+                arrived(ref, r_x2.at[w, m], x == 0)
+            else:
+                arrived(ref, r_x2.at[w, m])
+    for m in range(2):
+        arrived(all_pairs.at[1 - y, 6 + m], r_y2.at[m])
+    for peer in peers:
+        arrived(vec_land.at[peer], r_v.at[peer])
+    vec_land[dp] = vec_pack[...]
+    vec_out[...] = jnp.concatenate([vec_land[d][:, : D // 8] for d in range(8)], axis=1)
+    for cond, copy in started:
+        if cond is None:
+            copy.wait_send()
+        else:
+            pl.when(cond)(copy.wait_send)
+
+
+def gather(block_weights, vector_params):
+    dma = pltpu.SemaphoreType.DMA
+    sizes = [(6,)] * 8 + [(3, 3)] * 2 + [(2, 3)] * 2 + [(4, 3)] * 2 + [(2,)] * 2 + [(7,), (8,)]
+    return pl.pallas_call(
+        gather_kernel,
+        in_specs=[pl.BlockSpec(memory_space=pltpu.VMEM)] * 2,
+        out_specs=[pl.BlockSpec(memory_space=pl.ANY), pl.BlockSpec(memory_space=pltpu.VMEM)],
+        out_shape=[
+            jax.ShapeDtypeStruct((2, 24, SIDE, PAIR), bf16),
+            jax.ShapeDtypeStruct((16, D), f32),
+        ],
+        scratch_shapes=[
+            pltpu.VMEM((3, SIDE, PAIR), bf16),
+            pltpu.VMEM((16, 128), f32),
+            pltpu.VMEM((8, 16, 128), f32),
+        ]
+        + [dma(size) for size in sizes]
+        + [dma],
+        compiler_params=params(collective_id=0, has_side_effects=True),
+        name="gather",
+    )(block_weights, vector_params)
 
 
 def project_kernel(tok, pas, vec, wq, norm, q, k, v, cat):
@@ -106,7 +266,12 @@
     return pl.pallas_call(
         project_kernel,
         grid=(seq // ROWS,),
-        in_specs=[row(D), pl.BlockSpec((1, ROWS), lambda i: (0, i)), full((16, D)), full(wq.shape)],
+        in_specs=[
+            row(D),
+            pl.BlockSpec((1, ROWS), lambda i: (0, i)),
+            full((16, D)),
+            full((2, 6, SIDE, PAIR)),
+        ],
         out_specs=[row(D), row(PAIR), row(PAIR), row(PAIR), full((3, D, PAIR))],
         out_shape=[
             jax.ShapeDtypeStruct((seq, D), bf16),
@@ -294,7 +459,7 @@
                 pl.BlockSpec((8, ROWS), lambda i, s, t: (0, i)),
                 half,
                 half,
-                full(wo.shape),
+                pl.BlockSpec((2, 2, SIDE, PAIR), lambda i, s, t: (0, 3, 0, 0)),
             ],
             out_specs=[row, full((seq, PAIR)), full((seq, PAIR)), full((2, SIDE, PAIR))],
             scratch_shapes=[
@@ -311,8 +476,8 @@
 
 
 def mlp_kernel(
-    place, tok, pas, vec, mine, other, cot, wo_mine, wo_other, w12,
-    out_send, out_keep, gn_send, gn_keep, second_keep, grads,
+    place, tok, pas, vec, mine, other, cot, wo_mine, wo_other, w1, w2,
+    out_send, out_keep, gn_send, gn_keep, second_keep, g_send, g_keep,
     wom, woo, up, down, gup, gdown,
 ):
     i = pl.program_id(0)
@@ -328,8 +493,8 @@
         for r in range(4):
             for m in range(2):
                 rows, cols = slice(r * SIDE, (r + 1) * SIDE), slice(m * PAIR, (m + 1) * PAIR)
-                up[rows, cols] = w12[2 * r + m]
-                down[rows, cols] = w12[8 + 2 * r + m]
+                up[rows, cols] = w1[0, 2 * r + m]
+                down[rows, cols] = w2[0, 2 * r + m]
         gup[...] = jnp.zeros_like(gup)
         gdown[...] = jnp.zeros_like(gdown)
 
@@ -367,11 +532,30 @@
         for r in range(4):
             for m in range(2):
                 rows, cols = slice(r * SIDE, (r + 1) * SIDE), slice(m * PAIR, (m + 1) * PAIR)
-                grads[2 * r + m] = gup[rows, cols].astype(bf16)
-                grads[8 + 2 * r + m] = gdown[rows, cols].astype(bf16)
-
-
-def mlp(place, tokens, passes, vec, mine, other, cotangent, wo_mine, wo_other, w12):
+                for at, total in ((8, gup), (16, gdown)):
+                    pair = at + 2 * r + m
+                    slot, column = (pair // 6 - 1) * 3 + pair % 3, pair // 3 % 2
+                    value = total[rows, cols].astype(bf16)
+
+                    @pl.when(place[2] == column)
+                    def _():
+                        g_keep[slot] = value
+
+                    @pl.when(place[2] != column)
+                    def _():
+                        g_send[slot] = value
+        for slot in range(2):
+
+            @pl.when(place[2] == 0)
+            def _():
+                g_keep[slot] = jnp.zeros((SIDE, PAIR), bf16)
+
+            @pl.when(place[2] != 0)
+            def _():
+                g_send[slot] = jnp.zeros((SIDE, PAIR), bf16)
+
+
+def mlp(place, tokens, passes, vec, mine, other, cotangent, pairs, wo_other):
     seq = tokens.shape[0]
     count = seq // ROWS
     where = lambda i, s: lax.rem(i + (1 - s[0]) * (count // 2), count)
@@ -391,11 +575,12 @@
                 row(PAIR),
                 row(PAIR),
                 row(D),
-                full(wo_mine.shape),
+                pl.BlockSpec((2, 2, SIDE, PAIR), lambda i, s: (0, 3, 0, 0)),
                 full(wo_other.shape),
-                full(w12.shape),
+                pl.BlockSpec((1, 8, SIDE, PAIR), lambda i, s: (s[1], 1, 0, 0)),
+                pl.BlockSpec((1, 8, SIDE, PAIR), lambda i, s: (s[1], 2, 0, 0)),
             ],
-            out_specs=[send, keep, send, keep, keep, full((16, SIDE, PAIR))],
+            out_specs=[send, keep, send, keep, keep, full((9, SIDE, PAIR)), full((9, SIDE, PAIR))],
             scratch_shapes=[
                 pltpu.VMEM((PAIR, D), bf16),
                 pltpu.VMEM((PAIR, D), bf16),
@@ -411,11 +596,12 @@
             half(bf16),
             half(f32),
             half(f32),
-            jax.ShapeDtypeStruct((16, SIDE, PAIR), bf16),
+            jax.ShapeDtypeStruct((9, SIDE, PAIR), bf16),
+            jax.ShapeDtypeStruct((9, SIDE, PAIR), bf16),
         ],
         compiler_params=params(),
         name="feed_forward",
-    )(place, tokens, passes, vec, mine, other, cotangent, wo_mine, wo_other, w12)
+    )(place, tokens, passes, vec, mine, other, cotangent, pairs, wo_other, pairs, pairs)
 
 
 def second_back_kernel(place, one, two, second, cot, vec, out, low, sums):
@@ -455,7 +641,7 @@
     )(place, one, two, second, cotangent, vec)
 
 
-def project_back_kernel(place, norm, dq, dk, dv, cat, send, keep, grads, acc):
+def project_back_kernel(place, norm, dq, dk, dv, cat, send, keep, g_send, g_keep, acc):
     i = pl.program_id(0)
     count = pl.num_programs(0)
 
@@ -481,9 +667,18 @@
         for x in range(3):
             for m in range(2):
                 at = 2 * m * SIDE
-                grads[2 * x + m] = jnp.concatenate(
+                value = jnp.concatenate(
                     [acc[x, at : at + SIDE], acc[x, at + SIDE : at + 2 * SIDE]], axis=1
                 ).astype(bf16)
+                slot, column = (2 * x + m) % 3, (2 * x + m) // 3
+
+                @pl.when(place[2] == column)
+                def _():
+                    g_keep[slot] = value
+
+                @pl.when(place[2] != column)
+                def _():
+                    g_send[slot] = value
 
 
 def project_back(place, norm, dq, dk, dv, cat):
@@ -500,10 +695,10 @@
             num_scalar_prefetch=1,
             grid=(count,),
             in_specs=[row(D), row(PAIR), row(PAIR), row(PAIR), full(cat.shape)],
-            out_specs=[send, keep, full((6, SIDE, PAIR))],
+            out_specs=[send, keep, full((3, SIDE, PAIR)), full((3, SIDE, PAIR))],
             scratch_shapes=[pltpu.VMEM((3, D, SIDE), f32)],
         ),
-        out_shape=[half, half, jax.ShapeDtypeStruct((6, SIDE, PAIR), bf16)],
+        out_shape=[half, half] + [jax.ShapeDtypeStruct((3, SIDE, PAIR), bf16)] * 2,
         compiler_params=params(),
         name="project_back",
     )(place, norm, dq, dk, dv, cat)
@@ -581,6 +776,28 @@
     return lax.ppermute(value, "tensor", [(t, t ^ bit) for t in range(NT)])
 
 
+def hop_x(value):
+    return lax.ppermute(value, "dp", [(d, d ^ 1) for d in range(8)])
+
+
+def hop_z(value, turn, ends):
+    pairs = [(d, (d + 2 * turn) % 8) for d in range(8) if (d // 2 + turn) % 4 in ends]
+    return lax.ppermute(value, "dp", pairs)
+
+
+def owners_sum(keep, send, z, ends):
+    both = (keep.astype(f32) + hop_x(send).astype(f32)).astype(bf16)
+
+    def term(turn):
+        at = jnp.clip((z + turn) % 4 - ends[0], 0, len(ends) - 1)
+        return lax.dynamic_index_in_dim(both, at, 0, keepdims=False)
+
+    total = term(0).astype(f32)
+    for turn in (1, 2, 3):
+        total = total + hop_z(term(turn), turn, ends).astype(f32)
+    return total
+
+
 def on_device(
     tokens,
     pass_ids,
@@ -594,41 +811,43 @@
     block_left_root,
     block_right_root,
 ):
-    t = lax.axis_index("tensor")
+    t, dp = lax.axis_index("tensor"), lax.axis_index("dp")
     core, side = t % 2, t // 2
-    place = jnp.stack([core, side]).astype(jnp.int32)
+    n_dp = lax.axis_size("dp")
+    small = n_dp == 8
+    z, column = (dp // 2, dp % 2) if small else (0, 0)
+    place = jnp.stack([core, side, jnp.asarray(column, jnp.int32)]).astype(jnp.int32)
     lens = doc_lengths[0]
     seq = tokens.shape[0]
     passes = pass_ids.reshape(1, seq)
     total_blocks = (D // SIDE) * (4 + 2 * (FF // D))
-    n_dp = lax.axis_size("dp")
-
-    every = lax.all_gather(block_weights.astype(bf16), "dp", axis=1, tiled=True)[0]
-    slots = every.shape[0]
-    pairs = to_pairs(every[:total_blocks])
-    vec = lax.all_gather(vector_params, "dp", axis=1, tiled=True)
-    vec = jnp.pad(vec, ((0, 16 - vec.shape[0]), (0, 0)))
-    shared = pairs[:8]
-    shared_far = swap(shared, 2)
-    both = jnp.where(side == 0, jnp.stack([shared, shared_far]), jnp.stack([shared_far, shared]))
-    wq, wo_mine = both[:, :6], both[:, 6:]
-    wo_other = swap(wo_mine, 1)
-    w12 = pairs[8:]
-
-    norm, q, k, v, cat = project(tokens, passes, vec, wq)
+    slots = block_weights.shape[1] * n_dp
+
+    if small:
+        pairs, vec = gather(block_weights, vector_params)
+    else:
+        every = lax.all_gather(block_weights.astype(bf16), "dp", axis=1, tiled=True)[0]
+        near = to_pairs(every[:total_blocks])
+        far = swap(near, 2)
+        pairs = jnp.where(side == 0, jnp.stack([near, far]), jnp.stack([far, near]))
+        vec = lax.all_gather(vector_params, "dp", axis=1, tiled=True)
+        vec = jnp.pad(vec, ((0, 16 - vec.shape[0]), (0, 0)))
+    wo_other = swap(pairs[:, 6:8], 1)
+
+    norm, q, k, v, cat = project(tokens, passes, vec, pairs)
     mine, lse = attend(lens, q, k, v)
     other = swap(mine, 1)
-    out_send, out_keep, gn_send, gn_keep, second, grads_12 = mlp(
-        place, tokens, passes, vec, mine, other, cotangent, wo_mine, wo_other, w12
+    out_send, out_keep, gn_send, gn_keep, second, w12_send, w12_keep = mlp(
+        place, tokens, passes, vec, mine, other, cotangent, pairs, wo_other
     )
     gn_chip = (gn_keep + swap(gn_send, 1).astype(f32)).astype(bf16)
     gn_far = swap(gn_chip, 2)
     grad_second, grad_attn, sums_two = second_back(place, gn_chip, gn_far, second, cotangent, vec)
     grad_attn_other = swap(grad_attn, 1)
     dq, dk, dv, grads_o = attend_back(
-        lens, place, q, k, v, mine, lse, grad_attn, grad_attn_other, wo_mine
+        lens, place, q, k, v, mine, lse, grad_attn, grad_attn_other, pairs
     )
-    g1_send, g1_keep, grads_qkv = project_back(place, norm, dq, dk, dv, cat)
+    g1_send, g1_keep, qkv_send, qkv_keep = project_back(place, norm, dq, dk, dv, cat)
     low_half, sums_one = first_back(
         place, tokens, passes, vec, g1_keep, swap(g1_send, 1), grad_second
     )
@@ -644,11 +863,33 @@
     output, input_grad = join(out_half), join(low_half)
     vector_part = jnp.concatenate([sums_one[: PASSES + 2], sums_two[:2]], axis=0)
     vector_part = vector_part + swap(vector_part, 1)
-    grad_blocks = from_pairs(jnp.concatenate([grads_qkv, grads_o, grads_12], axis=0)).astype(f32)
-    spare = jnp.zeros((slots - total_blocks, SIDE, SIDE), f32)
-    grad_blocks = jnp.concatenate([grad_blocks, spare], axis=0)[None]
-    owned = lax.psum_scatter(grad_blocks, "dp", scatter_dimension=1, tiled=True)
-    vector_grad = lax.psum_scatter(vector_part, "dp", scatter_dimension=1, tiled=True)
+    if small:
+        by_z = lambda value: value.reshape(-1, 3, SIDE, PAIR)
+        owned = owners_sum(by_z(w12_keep), by_z(w12_send), z, (1, 2, 3))
+        late = owners_sum(by_z(qkv_keep), by_z(qkv_send), z, (0,))
+        nothing = jnp.zeros_like(grads_o)
+        o_keep = jnp.where(column == 0, grads_o, nothing)
+        o_send = jnp.where(column == 0, nothing, grads_o)
+        o_sum = owners_sum(o_keep[None], o_send[None], z, (1,))
+        o_sum = jnp.concatenate([o_sum, jnp.zeros((1, SIDE, PAIR), f32)], axis=0)
+        owned = jnp.where(z == 0, late, owned + jnp.where(dp == 2, o_sum, 0.0))
+        owned = from_pairs(owned)[None]
+        vector_part = vector_part + hop_x(vector_part)
+        vector_sum = vector_part
+        for turn in (1, 2, 3):
+            vector_sum = vector_sum + hop_z(vector_part, turn, (0, 1, 2, 3))
+        wide = vector_params.shape[1]
+        vector_grad = lax.dynamic_slice_in_dim(vector_sum, dp * wide, wide, 1)
+    else:
+        up_down = jnp.stack([w12_keep.reshape(3, 3, SIDE, PAIR), w12_send.reshape(3, 3, SIDE, PAIR)], axis=1)
+        up_down = up_down.reshape(18, SIDE, PAIR)[2:]
+        grad_blocks = from_pairs(
+            jnp.concatenate([qkv_keep, qkv_send, grads_o, up_down], axis=0)
+        ).astype(f32)
+        spare = jnp.zeros((slots - total_blocks, SIDE, SIDE), f32)
+        grad_blocks = jnp.concatenate([grad_blocks, spare], axis=0)[None]
+        owned = lax.psum_scatter(grad_blocks, "dp", scatter_dimension=1, tiled=True)
+        vector_grad = lax.psum_scatter(vector_part, "dp", scatter_dimension=1, tiled=True)
     left_new, right_new, step, weight_new = precondition(
         owned, block_weights, block_left, block_right, block_left_root, block_right_root
     )

time: 627 us -> 389 us (0.62); the launches traced: 621 us -> 389 us
  waiting for transfers between devices: 327 us -> 104 us
  Pallas kernels: 158 us -> 209 us
  local copies, waits for them, and re-layouts: 52 us -> 7.69 us
  starting transfers between devices: 5.01 us -> 43.3 us
  blocking collectives: 30.7 us -> 0 us
  between operations: 14.4 us -> 1.2 us
  other arithmetic: 22.7 us -> 14.3 us
    reduce_scatter x1 -> x0, waiting for transfers between devices: 156 us -> none  [on_device(): owned = lax.psum_scatter(grad_blocks, 'dp', scatter_dimension=1, tiled=True)]
    all_gather x1 -> x0, waiting for transfers between devices: 83.8 us -> none  [on_device(): lax.all_gather(block_weights.astype(bf16), 'dp', axis=1, tiled=True)[0]]
    pallas_call x0 -> x1, Pallas kernels: none -> 52.5 us  [gather(): pl.pallas_call(gather_kernel, in_specs=[pl.BlockSpec(memory_space=pltpu.V...]
    ppermute x0 -> x16, waiting for transfers between devices: none -> 39.8 us  [the longest x12 39.7 us: hop_z(): return lax.ppermute(value, 'dp', pairs)]
    ppermute x0 -> x16, starting transfers between devices: none -> 39.2 us  [the longest x12 35.5 us: hop_z(): return lax.ppermute(value, 'dp', pairs)]
    all_gather x1 -> x0, blocking collectives: 30.7 us -> none  [on_device(): vec = lax.all_gather(vector_params, 'dp', axis=1, tiled=True)]
    ppermute x12 -> x11, waiting for transfers between devices: 87.7 us -> 63.8 us  [swap(): return lax.ppermute(value, 'tensor', [(t, t ^ bit) for t in range(NT)])]
    slice x6 -> x2, local copies, waits for them, and re-layouts: 18.9 us -> 1.35 us  [the longest x1 1.13 us: on_device(): wo_other = swap(pairs[:, 6:8], 1)]
  transfers between devices with their start and end apart: 15 -> 27, of which waited for: 9 -> 8; matrix products, arithmetic and copies ran while one was open for 7% -> 6% of each run, Pallas kernels for 0% -> 16%
where the time goes in v2:
time: 389 us
  Pallas kernels  209 us (54%)
  waiting for transfers between devices  104 us (27%)
  starting transfers between devices  43.3 us (11%)
  other arithmetic  14.3 us (4%)
  matrix products  9.94 us (3%)
  local copies, waits for them, and re-layouts  7.69 us (2%)
    ppermute x11, waiting for transfers between devices, swap(): return lax.ppermute(value, 'tensor', [(t, t ^ bit) for t in range(NT)])  63.8 us
    pallas_call x1, Pallas kernels, gather(): pl.pallas_call(gather_kernel, in_specs=[pl.BlockSpec(memory_space=pltpu.V...  52.5 us
    pallas_call x1, Pallas kernels, attend_back(): pl.pallas_call(attend_back_kernel, grid_spec=pltpu.PrefetchScalarGridSpec...  39.9 us
    ppermute x12, waiting for transfers between devices, hop_z(): return lax.ppermute(value, 'dp', pairs)  39.7 us
    pallas_call x1, Pallas kernels, mlp(): pl.pallas_call(mlp_kernel, grid_spec=pltpu.PrefetchScalarGridSpec(num_sca...  38 us
    ppermute x12, starting transfers between devices, hop_z(): return lax.ppermute(value, 'dp', pairs)  35.5 us
    pallas_call x1, Pallas kernels, attend(): pl.pallas_call(attend_kernel, grid_spec=pltpu.PrefetchScalarGridSpec(num_...  30.8 us
    pallas_call x1, Pallas kernels, project(): pl.pallas_call(project_kernel, grid=(seq // ROWS,), in_specs=[row(D), pl....  16.1 us
  transfers between devices with their start and end apart: 27, of which 8 were waited for; matrix products, arithmetic and copies ran while one was open for 6% of the time, Pallas kernels for 16%

profile of v2, /device:TPU:0, one launch (start us, length us, event | category | flops | bytes accessed | tf_op | source)
XLA Modules:
  0.0 389.2 jit_solution(4899448531288448143)
XLA Ops:
  0.7 52.5 %gather.1 = (bf16[2,24,192,384]{3,2,1,0:T(8,128)(2,1)}, f32[16,768]{1,0:T(8,128)}) custom-call(f32[1,6,192,192]{3,2,1,0:T(8,128)} %own.1, f32[9,96]{1,0:T(8,128)} %vec_own.1), custom_call_target="tpu_custom_call" | custom-call | tf_op jit(solution)/shard_map/gather/pallas_call | solution.py:225
  53.2 16.1 %project.1 = (bf16[2048,768]{1,0:T(8,128)(2,1)}, bf16[2048,384]{1,0:T(8,128)(2,1)}, bf16[2048,384]{1,0:T(8,128)(2,1)}, bf16[2048,384]{1,0:T(8,128)(2,1)}, bf16[3,768,384]{2,1,0:T(8,128)(2,1)}) custom-call(bf16[2048,768]{1,0:T(8,128)(2,1)} %tok.5, s32[1,2048]{1,0:T(1,128)} %bitcast.65, f32[16,768]{1,0:T(8,128)} %get-tuple-element.38.vec, ...), custom_call_target="tpu_custom_call" | custom-call | tf_op jit(solution)/shard_map/project/pallas_call | solution.py:266
  69.3 30.8 %attend.1 = (bf16[2048,384]{1,0:T(8,128)(2,1)}, f32[8,2048]{1,0:T(8,128)}) custom-call(s32[8]{0:T(128)} %bitcast.68, bf16[2048,384]{1,0:T(8,128)(2,1)} %get-tuple-element.40.q, bf16[2048,384]{1,0:T(8,128)(2,1)} %get-tuple-element.41.k, bf16[2048,384]{1,0:T(8,128)(2,1)} %get-tuple-element.42.v), custom_call_target="tpu_custom_call" | custom-call | tf_op jit(solution)/shard_map/attend/pallas_call | solution.py:349
  100.1 1.1 slice.15
  101.3 0.6 collective-permute-start.1
  101.8 0.6 pad_add_fusion.place
  102.4 2.1 collective-permute-done.1.wo_other
  104.5 1.1 copy-done.4
  105.7 38.0 %feed_forward.1 = (bf16[1024,768]{1,0:T(8,128)(2,1)}, bf16[1024,768]{1,0:T(8,128)(2,1)}, bf16[1024,768]{1,0:T(8,128)(2,1)}, f32[1024,768]{1,0:T(8,128)}, f32[102...) custom-call(s32[3]{0:T(128)} %pad_add_fusion.place, bf16[2048,768]{1,0:T(8,128)(2,1)} %tok.5, ...), custom_call_target="tpu_custom_call" | custom-call | tf_op jit(solution)/shard_map/feed_forward/pallas_call | solution.py:566
  143.6 0.2 collective-permute-start.5
  143.8 0.4 collective-permute-start.2
  144.2 3.1 collective-permute-done.5
  147.3 2.4 add_convert_fusion.one
  149.8 1.6 collective-permute-start.6
  151.4 0.5 add_convert_fusion.2
  151.8 0.6 collective-permute-start.3
  152.4 34.6 %collective-permute-done.6.two = bf16[1024,768]{1,0:T(8,128)(2,1)S(1)} collective-permute-done((bf16[1024,768]{1,0:T(8,128)(2,1)S(1)}, bf16[1024,768]{1,0:T(8,128)(2,1)S(1)}, u32[]{:S(2)}, u32[]{:S(2)}) %collective-permute-start.6) | collective-permute-done | bytes 1572896 | tf_op jit(solution)/shard_map/ppermute | solution.py:776
  187.1 1.2 copy-done.5
  188.2 7.7 %second_back.1 = (f32[1024,768]{1,0:T(8,128)}, bf16[1024,768]{1,0:T(8,128)(2,1)}, f32[8,768]{1,0:T(8,128)}) custom-call(s32[3]{0:T(128)} %pad_add_fusion.place, bf16[1024,768]{1,0:T(8,128)(2,1)} %copy-done.2, bf16[1024,768]{1,0:T(8,128)(2,1)} %copy-done.5, f32[1024,768]{1,0:T(8,128)} %get-tuple-element.44.second, bf16[2048,768]{1,0:T(8,128)(2,1)} %cot.3, ...), custom_call_target="tpu_custom_call" | custom-call | tf_op jit(solution)/shard_map/second_back/pallas_call | solution.py:626
  196.1 0.1 collective-permute-start.14
  196.1 23.9 %collective-permute-done.3 = bf16[1024,768]{1,0:T(8,128)(2,1)} collective-permute-done((bf16[1024,768]{1,0:T(8,128)(2,1)S(1)}, bf16[1024,768]{1,0:T(8,128)(2,1)}, u32[]{:S(2)}, u32[]{:S(2)}) %collective-permute-start.3) | collective-permute-done | bytes 1572896 | tf_op jit(solution)/shard_map/ppermute | solution.py:776
  220.1 1.9 add_convert_fusion.1
  222.2 39.9 %attend_back.1 = (bf16[2048,384]{1,0:T(8,128)(2,1)}, bf16[2048,384]{1,0:T(8,128)(2,1)}, bf16[2048,384]{1,0:T(8,128)(2,1)}, bf16[2,192,384]{2,1,0:T(8,128)(2,1)}) custom-call(s32[8]{0:T(128)} %bitcast.69, s32[3]{0:T(128)} %pad_add_fusion.place, bf16[2048,384]{1,0:T(8,128)(2,1)} %get-tuple-element.40.q, bf16[2048,384]{1,0:T(8,128)(2,1)} %get-tuple-element.41.k, ...), custom_call_target="tpu_custom_call" | custom-call | tf_op jit(solution)/shard_map/attend_back/pallas_call | solution.py:449
  262.2 14.6 %project_back.1 = (bf16[1024,768]{1,0:T(8,128)(2,1)}, bf16[1024,768]{1,0:T(8,128)(2,1)}, bf16[3,192,384]{2,1,0:T(8,128)(2,1)}, bf16[3,192,384]{2,1,0:T(8,128)(2,1)}) custom-call(s32[3]{0:T(128)} %pad_add_fusion.place, bf16[2048,768]{1,0:T(8,128)(2,1)} %get-tuple-element.47.norm, bf16[2048,384]{1,0:T(8,128)(2,1)} %get-tuple-element.52.dq, ...), custom_call_target="tpu_custom_call" | custom-call | tf_op jit(solution)/shard_map/project_back/pallas_call | solution.py:692
  276.8 2.1 collective-permute-start.10
  278.9 1.7 fusion
  280.6 0.1 dynamic-slice_bitcast_fusion.2
  280.7 3.5 collective-permute-start.15
  284.2 8.4 %collective-permute-start.17 = (bf16[3,192,384]{2,1,0:T(8,128)(2,1)S(1)}, bf16[3,192,384]{2,1,0:T(8,128)(2,1)S(1)}, u32[]{:S(2)}, u32[]{:S(2)}) collective-permute-start(bf16[3,192,384]{2,1,0:T(8,128)(2,1)S(1)} %get-tuple-element.75), channel_id=1, source_target_pairs={{0,24},{4,28},{16,8},{20,12},{24,16},{28,20},{1,25},{5,29},{17,9},... | collective-permute-start | bytes 1327112 | tf_op jit(solution)/shard_map/ppermute | solution.py:785
  292.7 0.7 slice.19
  293.4 0.1 fusion.16
  293.5 0.8 collective-permute-start.21
  294.4 0.7 collective-permute-start.20
  295.1 1.3 collective-permute-start.19
  296.4 1.6 broadcast_select_fusion.3
  298.0 0.1 fusion.15
  298.1 14.8 %collective-permute-start.16 = (bf16[3,192,384]{2,1,0:T(8,128)(2,1)S(1)}, bf16[3,192,384]{2,1,0:T(8,128)(2,1)S(1)}, u32[]{:S(2)}, u32[]{:S(2)}) collective-permute-start(bf16[3,192,384]{2,1,0:T(8,128)(2,1)S(1)} %get-tuple-element.76), channel_id=1, source_target_pairs={{0,16},{4,20},{8,24},{12,28},{24,8},{28,12},{1,17},{5,21},{9,25},{... | collective-permute-start | bytes 1327112 | tf_op jit(solution)/shard_map/ppermute | solution.py:785
  313.1 1.3 collective-permute-start.13
  314.4 1.3 collective-permute-start.12
  315.7 1.3 collective-permute-start.11
  317.0 1.9 pad_maximum_fusion
  318.9 0.1 convert_add_fusion.4
  319.0 2.8 collective-permute-done.16
  321.8 34.2 %collective-permute-done.13 = bf16[3,192,384]{2,1,0:T(8,128)(2,1)S(1)} collective-permute-done((bf16[3,192,384]{2,1,0:T(8,128)(2,1)S(1)}, bf16[3,192,384]{2,1,0:T(8,128)(2,1)S(1)}, u32[]{:S(2)}, u32[]{:S(2)}) %collective-permute-start.13) | collective-permute-done | bytes 442400 | tf_op jit(solution)/shard_map/ppermute | solution.py:785
  355.9 0.5 fusion.12
  356.4 0.2 fusion.20
  356.7 0.1 pad_maximum_fusion.2
  356.8 1.2 copy-done.10
  357.9 1.4 fusion.7
  359.3 1.1 copy-done.8
  360.5 9.6 %first_back.1 = (bf16[1024,768]{1,0:T(8,128)(2,1)}, f32[16,768]{1,0:T(8,128)}) custom-call(s32[3]{0:T(128)} %pad_add_fusion.place, bf16[2048,768]{1,0:T(8,128)(2,1)} %tok.5, s32[1,2048]{1,0:T(1,128)} %bitcast.67, f32[16,768]{1,0:T(8,128)} %get-tuple-element.38.vec, bf16[1024,768]{1,0:T(8,128)(2,1)} %get-tuple-element.56.one, bf16[1024,768]{1,0:T(8,128)(2,1)} %copy-done.8, ...), custom_call_target="tpu_custom_call" | custom-call | tf_op jit(solution)/shard_map/first_back/pallas_call | solution.py:728
  370.0 0.7 slice.18
  370.8 0.6 collective-permute-start.22
  371.4 2.8 bitcast_subtract_fusion
  374.2 1.5 collective-permute-start.23
  375.6 3.5 fusion.4
  379.2 1.0 collective-permute-start.25
  380.2 1.0 collective-permute-start.24
  381.2 2.4 fusion.2
  383.6 0.1 collective-permute-done.26
  383.7 2.7 collective-permute-done.25
  386.4 0.7 divide_subtract_fusion
  387.1 0.2 broadcast_select_fusion.1
  387.3 1.9 pad_maximum_fusion.1
  (62 shorter events, 0.6 us)
Async XLA Ops:
  0.6 370.7 %copy-start = (f32[1,6,192,192]{3,2,1,0:T(8,128)S(1)}, f32[1,6,192,192]{3,2,1,0:T(8,128)}, u32[]{:S(2)}) copy-start(f32[1,6,192,192]{3,2,1,0:T(8,128)} %param.21) | copy-start | bytes 2654212
  100.1 4.4 %collective-permute-start = (bf16[2048,384]{1,0:T(8,128)(2,1)}, bf16[2048,384]{1,0:T(8,128)(2,1)S(1)}, u32[]{:S(2)}, u32[]{:S(2)}) collective-permute-start(bf16[2048,384]{1,0:T(8,128)(2,1)} %get-tuple-element.43.mine.mixed), channel_id=1, source_target_pairs={{0,1},{1,0},{2,3},{3,2},{4,5},{5,4},{6,7},{7,6},{8,9},{9,8},{10,11... | collective-permute-start | bytes 4718600 | tf_op jit(solution)/shard_map/ppermute | solution.py:776
  101.3 3.3 collective-permute-start.1
  104.5 1.1 copy-start.4
  143.6 3.7 collective-permute-start.5
  143.8 7.5 %collective-permute-start.2 = (bf16[1024,768]{1,0:T(8,128)(2,1)}, bf16[1024,768]{1,0:T(8,128)(2,1)S(1)}, u32[]{:S(2)}, u32[]{:S(2)}) collective-permute-start(bf16[1024,768]{1,0:T(8,128)(2,1)} %get-tuple-element.46), channel_id=1, source_target_pairs={{0,1},{1,0},{2,3},{3,2},{4,5},{5,4},{6,7},{7,6},{8,9},{9,8},{10,11... | collective-permute-start | bytes 4718600 | tf_op jit(solution)/shard_map/ppermute | solution.py:776
  147.3 4.0 %copy-start.7 = (bf16[1024,768]{1,0:T(8,128)(2,1)S(1)}, bf16[1024,768]{1,0:T(8,128)(2,1)}, u32[]{:S(2)}) copy-start(bf16[1024,768]{1,0:T(8,128)(2,1)} %get-tuple-element.45) | copy-start | bytes 4718596
  149.7 2.1 copy-start.2
  149.8 37.3 %collective-permute-start.6 = (bf16[1024,768]{1,0:T(8,128)(2,1)S(1)}, bf16[1024,768]{1,0:T(8,128)(2,1)S(1)}, u32[]{:S(2)}, u32[]{:S(2)}) collective-permute-start(bf16[1024,768]{1,0:T(8,128)(2,1)S(1)} %add_convert_fusion.one), channel_id=1, source_target_pairs={{0,2},{1,3},{2,0},{3,1},{4,6},{5,7},{6,4},{7,5},{8,10},{9,11},{10,... | collective-permute-start | bytes 4718600 | tf_op jit(solution)/shard_map/ppermute | solution.py:776
  151.8 68.2 %collective-permute-start.3 = (bf16[1024,768]{1,0:T(8,128)(2,1)S(1)}, bf16[1024,768]{1,0:T(8,128)(2,1)}, u32[]{:S(2)}, u32[]{:S(2)}) collective-permute-start(bf16[1024,768]{1,0:T(8,128)(2,1)S(1)} %add_convert_fusion.2), channel_id=1, source_target_pairs={{0,2},{1,3},{2,0},{3,1},{4,6},{5,7},{6,4},{7,5},{8,10},{9,11},{10,... | collective-permute-start | bytes 4718600 | tf_op jit(solution)/shard_map/ppermute | solution.py:776
  187.1 1.2 copy-start.5
  188.2 31.8 %copy-start.1 = (f32[1024,768]{1,0:T(8,128)S(1)}, f32[1024,768]{1,0:T(8,128)}, u32[]{:S(2)}) copy-start(f32[1024,768]{1,0:T(8,128)} %get-tuple-element.44.second) | copy-start | bytes 9437188
  196.0 26.2 %collective-permute-start.7 = (bf16[1024,768]{1,0:T(8,128)(2,1)}, bf16[1024,768]{1,0:T(8,128)(2,1)}, u32[]{:S(2)}, u32[]{:S(2)}) collective-permute-start(bf16[1024,768]{1,0:T(8,128)(2,1)} %get-tuple-element.51.mine), channel_id=1, source_target_pairs={{0,1},{1,0},{2,3},{3,2},{4,5},{5,4},{6,7},{7,6},{8,9},{9,8},{10,11... | collective-permute-start | bytes 4718600 | tf_op jit(solution)/shard_map/ppermute | solution.py:776
  196.1 82.8 %collective-permute-start.14 = (bf16[3,3,192,384]{3,2,1,0:T(8,128)(2,1)}, bf16[3,3,192,384]{3,2,1,0:T(8,128)(2,1)}, u32[]{:S(2)}, u32[]{:S(2)}) collective-permute-start(bf16[3,3,192,384]{3,2,1,0:T(8,128)(2,1)} %bitcast.70), channel_id=1, source_target_pairs={{0,4},{4,0},{8,12},{12,8},{16,20},{20,16},{24,28},{28,24},{1,5},{5... | collective-permute-start | bytes 3981320 | tf_op jit(solution)/shard_map/ppermute | solution.py:780
  222.0 72.4 %collective-permute-start.4 = (bf16[1024,768]{1,0:T(8,128)(2,1)S(1)}, bf16[1024,768]{1,0:T(8,128)(2,1)}, u32[]{:S(2)}, u32[]{:S(2)}) collective-permute-start(bf16[1024,768]{1,0:T(8,128)(2,1)S(1)} %add_convert_fusion.1), channel_id=1, source_target_pairs={{0,1},{1,0},{2,3},{3,2},{4,5},{5,4},{6,7},{7,6},{8,9},{9,8},{10,11... | collective-permute-start | bytes 4718600 | tf_op jit(solution)/shard_map/ppermute | solution.py:776
  262.1 31.3 %collective-permute-start.18 = (bf16[1,2,192,384]{3,2,1,0:T(8,128)(2,1)S(1)}, bf16[1,2,192,384]{3,2,1,0:T(8,128)(2,1)S(1)}, u32[]{:S(2)}, u32[]{:S(2)}) collective-permute-start(bf16[1,2,192,384]{3,2,1,0:T(8,128)(2,1)S(1)} %select_bitcast_fusion), channel_id=1, source_target_pairs={{0,4},{4,0},{8,12},{12,8},{16,20},{20,16},{24,28},{28,24},{1,5},{5... | collective-permute-start | bytes 884744 | tf_op jit(solution)/shard_map/ppermute | solution.py:780
  262.2 16.7 %copy-start.9 = (bf16[9,192,384]{2,1,0:T(8,128)(2,1)S(1)}, bf16[9,192,384]{2,1,0:T(8,128)(2,1)}, u32[]{:S(2)}) copy-start(bf16[9,192,384]{2,1,0:T(8,128)(2,1)} %get-tuple-element.62) | copy-start | bytes 3981316
  276.8 18.3 %collective-permute-start.10 = (bf16[1,3,192,384]{3,2,1,0:T(8,128)(2,1)}, bf16[1,3,192,384]{3,2,1,0:T(8,128)(2,1)S(1)}, u32[]{:S(2)}, u32[]{:S(2)}) collective-permute-start(bf16[1,3,192,384]{3,2,1,0:T(8,128)(2,1)} %bitcast.71), channel_id=1, source_target_pairs={{0,4},{4,0},{8,12},{12,8},{16,20},{20,16},{24,28},{28,24},{1,5},{5... | collective-permute-start | bytes 1327112 | tf_op jit(solution)/shard_map/ppermute | solution.py:780
  280.6 12.9 %copy-start.11 = (bf16[2,192,384]{2,1,0:T(8,128)(2,1)S(1)}, bf16[2,192,384]{2,1,0:T(8,128)(2,1)}, u32[]{:S(2)}) copy-start(bf16[2,192,384]{2,1,0:T(8,128)(2,1)} %get-tuple-element.64) | copy-start | bytes 884740
  280.7 17.4 %collective-permute-start.15 = (bf16[3,192,384]{2,1,0:T(8,128)(2,1)S(1)}, bf16[3,192,384]{2,1,0:T(8,128)(2,1)S(1)}, u32[]{:S(2)}, u32[]{:S(2)}) collective-permute-start(bf16[3,192,384]{2,1,0:T(8,128)(2,1)S(1)} %get-tuple-element.74), channel_id=1, source_target_pairs={{0,8},{4,12},{8,16},{12,20},{16,24},{20,28},{1,9},{5,13},{9,17},{1... | collective-permute-start | bytes 1327112 | tf_op jit(solution)/shard_map/ppermute | solution.py:785
  284.2 28.7 %collective-permute-start.17 = (bf16[3,192,384]{2,1,0:T(8,128)(2,1)S(1)}, bf16[3,192,384]{2,1,0:T(8,128)(2,1)S(1)}, u32[]{:S(2)}, u32[]{:S(2)}) collective-permute-start(bf16[3,192,384]{2,1,0:T(8,128)(2,1)S(1)} %get-tuple-element.75), channel_id=1, source_target_pairs={{0,24},{4,28},{16,8},{20,12},{24,16},{28,20},{1,25},{5,29},{17,9},... | collective-permute-start | bytes 1327112 | tf_op jit(solution)/shard_map/ppermute | solution.py:785
  293.5 4.5 %copy-start.14 = (bf16[3,192,384]{2,1,0:T(8,128)(2,1)S(1)}, bf16[3,192,384]{2,1,0:T(8,128)(2,1)}, u32[]{:S(2)}) copy-start(bf16[3,192,384]{2,1,0:T(8,128)(2,1)} %get-tuple-element.60) | copy-start | bytes 1327108
  293.5 19.4 %copy-start.17 = (bf16[1024,768]{1,0:T(8,128)(2,1)S(1)}, bf16[1024,768]{1,0:T(8,128)(2,1)}, u32[]{:S(2)}) copy-start(bf16[1024,768]{1,0:T(8,128)(2,1)} %get-tuple-element.57) | copy-start | bytes 4718596
  293.5 19.5 %collective-permute-start.21 = (bf16[2,192,384]{2,1,0:T(8,128)(2,1)S(1)}, bf16[2,192,384]{2,1,0:T(8,128)(2,1)S(1)}, u32[]{:S(2)}, u32[]{:S(2)}) collective-permute-start(bf16[2,192,384]{2,1,0:T(8,128)(2,1)S(1)} %fusion.16), channel_id=1, source_target_pairs={{16,8},{20,12},{17,9},{21,13},{18,10},{22,14},{19,11},{23,15}} | collective-permute-start | bytes 884744 | tf_op jit(solution)/shard_map/ppermute | solution.py:785
  294.4 20.0 %collective-permute-start.20 = (bf16[2,192,384]{2,1,0:T(8,128)(2,1)S(1)}, bf16[2,192,384]{2,1,0:T(8,128)(2,1)S(1)}, u32[]{:S(2)}, u32[]{:S(2)}) collective-permute-start(bf16[2,192,384]{2,1,0:T(8,128)(2,1)S(1)} %fusion.16), channel_id=1, source_target_pairs={{24,8},{28,12},{25,9},{29,13},{26,10},{30,14},{27,11},{31,15}} | collective-permute-start | bytes 884744 | tf_op jit(solution)/shard_map/ppermute | solution.py:785
  295.1 20.6 %collective-permute-start.19 = (bf16[2,192,384]{2,1,0:T(8,128)(2,1)S(1)}, bf16[2,192,384]{2,1,0:T(8,128)(2,1)S(1)}, u32[]{:S(2)}, u32[]{:S(2)}) collective-permute-start(bf16[2,192,384]{2,1,0:T(8,128)(2,1)S(1)} %fusion.16), channel_id=1, source_target_pairs={{0,8},{4,12},{1,9},{5,13},{2,10},{6,14},{3,11},{7,15}} | collective-permute-start | bytes 884744 | tf_op jit(solution)/shard_map/ppermute | solution.py:785
  298.1 23.6 %collective-permute-start.16 = (bf16[3,192,384]{2,1,0:T(8,128)(2,1)S(1)}, bf16[3,192,384]{2,1,0:T(8,128)(2,1)S(1)}, u32[]{:S(2)}, u32[]{:S(2)}) collective-permute-start(bf16[3,192,384]{2,1,0:T(8,128)(2,1)S(1)} %get-tuple-element.76), channel_id=1, source_target_pairs={{0,16},{4,20},{8,24},{12,28},{24,8},{28,12},{1,17},{5,21},{9,25},{... | collective-permute-start | bytes 1327112 | tf_op jit(solution)/shard_map/ppermute | solution.py:785
  313.0 46.3 %collective-permute-start.8 = (bf16[1024,768]{1,0:T(8,128)(2,1)S(1)}, bf16[1024,768]{1,0:T(8,128)(2,1)S(1)}, u32[]{:S(2)}, u32[]{:S(2)}) collective-permute-start(bf16[1024,768]{1,0:T(8,128)(2,1)S(1)} %copy-done.17), channel_id=1, source_target_pairs={{0,1},{1,0},{2,3},{3,2},{4,5},{5,4},{6,7},{7,6},{8,9},{9,8},{10,11... | collective-permute-start | bytes 4718600 | tf_op jit(solution)/shard_map/ppermute | solution.py:776
  313.1 42.9 %collective-permute-start.13 = (bf16[3,192,384]{2,1,0:T(8,128)(2,1)S(1)}, bf16[3,192,384]{2,1,0:T(8,128)(2,1)S(1)}, u32[]{:S(2)}, u32[]{:S(2)}) collective-permute-start(bf16[3,192,384]{2,1,0:T(8,128)(2,1)S(1)} %fusion.15), channel_id=1, source_target_pairs={{8,0},{12,4},{9,1},{13,5},{10,2},{14,6},{11,3},{15,7}} | collective-permute-start | bytes 1327112 | tf_op jit(solution)/shard_map/ppermute | solution.py:785
  314.4 41.6 %collective-permute-start.12 = (bf16[3,192,384]{2,1,0:T(8,128)(2,1)S(1)}, bf16[3,192,384]{2,1,0:T(8,128)(2,1)S(1)}, u32[]{:S(2)}, u32[]{:S(2)}) collective-permute-start(bf16[3,192,384]{2,1,0:T(8,128)(2,1)S(1)} %fusion.15), channel_id=1, source_target_pairs={{16,0},{20,4},{17,1},{21,5},{18,2},{22,6},{19,3},{23,7}} | collective-permute-start | bytes 1327112 | tf_op jit(solution)/shard_map/ppermute | solution.py:785
  315.7 40.3 %collective-permute-start.11 = (bf16[3,192,384]{2,1,0:T(8,128)(2,1)S(1)}, bf16[3,192,384]{2,1,0:T(8,128)(2,1)S(1)}, u32[]{:S(2)}, u32[]{:S(2)}) collective-permute-start(bf16[3,192,384]{2,1,0:T(8,128)(2,1)S(1)} %fusion.15), channel_id=1, source_target_pairs={{24,0},{28,4},{25,1},{29,5},{26,2},{30,6},{27,3},{31,7}} | collective-permute-start | bytes 1327112 | tf_op jit(solution)/shard_map/ppermute | solution.py:785
  356.7 1.3 copy-start.10
  359.3 1.1 copy-start.8
  360.5 10.9 %copy-start.3 = (f32[1,6,192,192]{3,2,1,0:T(8,128)S(1)}, f32[1,6,192,192]{3,2,1,0:T(8,128)}, u32[]{:S(2)}) copy-start(f32[1,6,192,192]{3,2,1,0:T(8,128)} %own.1) | copy-start | bytes 2654212
  370.8 16.3 %collective-permute-start.9 = (bf16[1024,768]{1,0:T(8,128)(2,1)}, bf16[1024,768]{1,0:T(8,128)(2,1)S(1)}, u32[]{:S(2)}, u32[]{:S(2)}) collective-permute-start(bf16[1024,768]{1,0:T(8,128)(2,1)} %get-tuple-element.59), channel_id=1, source_target_pairs={{0,1},{1,0},{2,3},{3,2},{4,5},{5,4},{6,7},{7,6},{8,9},{9,8},{10,11... | collective-permute-start | bytes 4718600 | tf_op jit(solution)/shard_map/ppermute | solution.py:776
  370.8 4.8 %copy-start.12 = (f32[1,6,192,192]{3,2,1,0:T(8,128)S(1)}, f32[1,6,192,192]{3,2,1,0:T(8,128)}, u32[]{:S(2)}) copy-start(f32[1,6,192,192]{3,2,1,0:T(8,128)} %param.19) | copy-start | bytes 2654212
  370.8 3.3 collective-permute-start.22
  374.2 7.1 %copy-start.13 = (f32[1,6,192,192]{3,2,1,0:T(8,128)S(1)}, f32[1,6,192,192]{3,2,1,0:T(8,128)}, u32[]{:S(2)}) copy-start(f32[1,6,192,192]{3,2,1,0:T(8,128)} %param.18) | copy-start | bytes 2654212
  374.2 4.9 %collective-permute-start.23 = (f32[9,768]{1,0:T(8,128)S(1)}, f32[9,768]{1,0:T(8,128)S(1)}, u32[]{:S(2)}, u32[]{:S(2)}) collective-permute-start(f32[9,768]{1,0:T(8,128)S(1)} %fusion.18), channel_id=1, source_target_pairs={{0,4},{4,0},{8,12},{12,8},{16,20},{20,16},{24,28},{28,24},{1,5},{5... | collective-permute-start | bytes 82952 | tf_op jit(solution)/shard_map/ppermute | solution.py:780
  379.1 7.3 %copy-start.15 = (f32[9,96]{1,0:T(8,128)S(1)}, f32[9,96]{1,0:T(8,128)}, u32[]{:S(2)}) copy-start(f32[9,96]{1,0:T(8,128)} %vec_own.1) | copy-start | bytes 10372
  379.1 7.2 %copy-start.16 = (f32[9,96]{1,0:T(8,128)S(1)}, f32[9,96]{1,0:T(8,128)}, u32[]{:S(2)}) copy-start(f32[9,96]{1,0:T(8,128)} %param.17) | copy-start | bytes 10372
  379.1 7.9 %copy-start.6 = (bf16[1024,768]{1,0:T(8,128)(2,1)S(1)}, bf16[1024,768]{1,0:T(8,128)(2,1)}, u32[]{:S(2)}) copy-start(bf16[1024,768]{1,0:T(8,128)(2,1)} %get-tuple-element.59) | copy-start | bytes 4718596
  379.2 4.5 %collective-permute-start.26 = (f32[9,768]{1,0:T(8,128)S(1)}, f32[9,768]{1,0:T(8,128)S(1)}, u32[]{:S(2)}, u32[]{:S(2)}) collective-permute-start(f32[9,768]{1,0:T(8,128)S(1)} %add.180), channel_id=1, source_target_pairs={{0,24},{4,28},{8,0},{12,4},{16,8},{20,12},{24,16},{28,20},{1,25},{... | collective-permute-start | bytes 82952 | tf_op jit(solution)/shard_map/ppermute | solution.py:785
  379.2 7.1 %collective-permute-start.25 = (f32[9,768]{1,0:T(8,128)S(1)}, f32[9,768]{1,0:T(8,128)S(1)}, u32[]{:S(2)}, u32[]{:S(2)}) collective-permute-start(f32[9,768]{1,0:T(8,128)S(1)} %add.180), channel_id=1, source_target_pairs={{0,16},{4,20},{8,24},{12,28},{16,0},{20,4},{24,8},{28,12},{1,17},{... | collective-permute-start | bytes 82952 | tf_op jit(solution)/shard_map/ppermute | solution.py:785
  380.2 6.2 %collective-permute-start.24 = (f32[9,768]{1,0:T(8,128)S(1)}, f32[9,768]{1,0:T(8,128)S(1)}, u32[]{:S(2)}, u32[]{:S(2)}) collective-permute-start(f32[9,768]{1,0:T(8,128)S(1)} %add.180), channel_id=1, source_target_pairs={{0,8},{4,12},{8,16},{12,20},{16,24},{20,28},{24,0},{28,4},{1,9},{5... | collective-permute-start | bytes 82952 | tf_op jit(solution)/shard_map/ppermute | solution.py:785

commit v3 on v2

--- a/solution.py
+++ b/solution.py
@@ -77,6 +77,10 @@
 
 def params(**kw):
     return pltpu.CompilerParams(vmem_limit_bytes=VMEM_LIMIT, **kw)
+
+
+def cost(micros):
+    return pl.CostEstimate(flops=int(micros * 1.1e9), bytes_accessed=int(micros * 1e6), transcendentals=0)
 
 
 def full(shape):
@@ -281,6 +285,7 @@
             jax.ShapeDtypeStruct((3, D, PAIR), bf16),
         ],
         compiler_params=params(),
+        cost_estimate=cost(16),
         name="project",
     )(tokens, passes, vec, wq)
 
@@ -364,12 +369,13 @@
             jax.ShapeDtypeStruct((8, seq), f32),
         ],
         compiler_params=params(),
+        cost_estimate=cost(30),
         name="attend",
     )(lens, q, k, v)
 
 
 def attend_back_kernel(
-    lens, place, q, k, v, mixed, lse, mine, other, wo, dq, dk, dv, gwo, dk_acc, dv_acc, dq_acc, gwo_acc
+    lens, q, k, v, mixed, lse, grad_mixed, dq, dk, dv, dk_acc, dv_acc, dq_acc
 ):
     i = pl.program_id(0)
     count = pl.num_programs(0)
@@ -379,15 +385,6 @@
     def _():
         dk_acc[...] = jnp.zeros_like(dk_acc)
         dv_acc[...] = jnp.zeros_like(dv_acc)
-        gwo_acc[...] = jnp.zeros_like(gwo_acc)
-
-    half = (i >= count // 2).astype(jnp.int32)
-    grad = jnp.where(half == place[0], mine[...], other[...])
-    weight = jnp.concatenate(
-        [jnp.concatenate([wo[h, 0], wo[h, 1]], axis=1) for h in range(2)], axis=0
-    )
-    grad_mixed = nt(grad, weight).astype(bf16)
-    gwo_acc[...] += tn(mixed[...], grad)
 
     rows, starts, first = doc_state(lens, base)
     heads = lax.broadcasted_iota(jnp.int32, (8, 128), 0)
@@ -435,56 +432,72 @@
     def _():
         dk[...] = dk_acc[...].astype(bf16)
         dv[...] = dv_acc[...].astype(bf16)
-        at = pl.multiple_of(place[1] * SIDE, SIDE)
-        for m in range(2):
-            gwo[m] = gwo_acc[pl.ds(at, SIDE), m * PAIR : (m + 1) * PAIR].astype(bf16)
-
-
-def attend_back(lens, place, q, k, v, mixed, lse, mine, other, wo):
+
+
+def attend_back(lens, q, k, v, mixed, lse, grad_mixed):
     seq = q.shape[0]
     count = seq // ROWS
-    row = pl.BlockSpec((ROWS, PAIR), lambda i, s, t: (i, 0))
-    half = pl.BlockSpec((ROWS, D), lambda i, s, t: (lax.rem(i, count // 2), 0))
+    row = pl.BlockSpec((ROWS, PAIR), lambda i, s: (i, 0))
     wide = jax.ShapeDtypeStruct((seq, PAIR), bf16)
     return pl.pallas_call(
         attend_back_kernel,
         grid_spec=pltpu.PrefetchScalarGridSpec(
-            num_scalar_prefetch=2,
+            num_scalar_prefetch=1,
             grid=(count,),
             in_specs=[
                 row,
                 full((seq, PAIR)),
                 full((seq, PAIR)),
                 row,
-                pl.BlockSpec((8, ROWS), lambda i, s, t: (0, i)),
-                half,
-                half,
-                pl.BlockSpec((2, 2, SIDE, PAIR), lambda i, s, t: (0, 3, 0, 0)),
+                pl.BlockSpec((8, ROWS), lambda i, s: (0, i)),
+                row,
             ],
-            out_specs=[row, full((seq, PAIR)), full((seq, PAIR)), full((2, SIDE, PAIR))],
+            out_specs=[row, full((seq, PAIR)), full((seq, PAIR))],
             scratch_shapes=[
                 pltpu.VMEM((seq, PAIR), f32),
                 pltpu.VMEM((seq, PAIR), f32),
                 pltpu.VMEM((3, 128, 2 * ROWS), f32),
-                pltpu.VMEM((PAIR, D), f32),
             ],
         ),
-        out_shape=[wide, wide, wide, jax.ShapeDtypeStruct((2, SIDE, PAIR), bf16)],
+        out_shape=[wide, wide, wide],
         compiler_params=params(),
+        cost_estimate=cost(40),
         name="attend_back",
-    )(lens, place, q, k, v, mixed, lse, mine, other, wo)
-
-
-def mlp_kernel(
-    place, tok, pas, vec, mine, other, cot, wo_mine, wo_other, w1, w2,
-    out_send, out_keep, gn_send, gn_keep, second_keep, g_send, g_keep,
-    wom, woo, up, down, gup, gdown,
+    )(lens, q, k, v, mixed, lse, grad_mixed)
+
+
+def feed_kernel(
+    small, tok, pas, vec, mine, other, cot, wo_mine, wo_other, w1, w2,
+    out_send, out_keep, second_keep, grad_second, grad_mixed, sums, g_send, g_keep, o_send, o_keep,
+    wom, woo, up, down, gup, gdown, go, core_out, core_in, far_out, far_in, ga_out, ga_in, seconds,
+    s_core, r_core, s_far, r_far, s_ga, r_ga,
 ):
-    i = pl.program_id(0)
-    count = pl.num_programs(0)
-
-    @pl.when(i == 0)
-    def _():
+    step = pl.program_id(0)
+    half = core_out.shape[0]
+    t = lax.axis_index("tensor")
+    core, side = t % 2, t // 2
+    near, far = side * 2 + (1 - core), (1 - side) * 2 + core
+    column = lax.axis_index("dp") % 2 if small else 0
+
+    def copy(src, dst, s_sem, r_sem, j, to):
+        return pltpu.make_async_remote_copy(
+            src_ref=src.at[j],
+            dst_ref=dst.at[j],
+            send_sem=s_sem.at[j],
+            recv_sem=r_sem.at[j],
+            device_id={"tensor": to},
+            device_id_type=MESH,
+        )
+
+    core_copy = lambda j: copy(core_out, core_in, s_core, r_core, j, near)
+    far_copy = lambda j: copy(far_out, far_in, s_far, r_far, j, far)
+    ga_copy = lambda j: copy(ga_out, ga_in, s_ga, r_ga, j, near)
+    barrier = pltpu.get_barrier_semaphore()
+
+    @pl.when(step == 0)
+    def _():
+        for to in (near, far):
+            pl.semaphore_signal(barrier, inc=1, device_id={"tensor": to}, device_id_type=MESH)
         for h in range(2):
             for m in range(2):
                 rows, cols = slice(h * SIDE, (h + 1) * SIDE), slice(m * PAIR, (m + 1) * PAIR)
@@ -497,172 +510,223 @@
                 down[rows, cols] = w2[0, 2 * r + m]
         gup[...] = jnp.zeros_like(gup)
         gdown[...] = jnp.zeros_like(gdown)
-
-    first = embedded(tok[...], pas[...], vec[...])
-    second = first + (nn(mine[...], wom[...]) + nn(other[...], woo[...]))
-    hat, _ = hat_of(second)
-    low = (hat * vec[PASSES + 2 : PASSES + 3] + vec[PASSES + 3 : PASSES + 4]).astype(bf16)
-    upper = nn(low, up[...])
-    square = upper * upper
-    bent = jnp.tanh(gelu_coef * upper * (1.0 + 0.044715 * square))
-    act = (0.5 * upper * (1.0 + bent)).astype(bf16)
-    slope = 0.5 * (1.0 + bent) + (0.5 * gelu_coef) * upper * (1.0 - bent * bent) * (
-        1.0 + (3 * 0.044715) * square
-    )
-    out_part = nn(act, down[...])
-    grad_act = nt(cot[...], down[...])
-    gdown[...] += tn(act, cot[...])
-    grad_upper = (grad_act * slope).astype(bf16)
-    gn_part = nt(grad_upper, up[...])
-    gup[...] += tn(low, grad_upper)
-
-    @pl.when(i < count // 2)
-    def _():
-        out_send[...] = out_part.astype(bf16)
-        gn_send[...] = gn_part.astype(bf16)
-
-    @pl.when(i >= count // 2)
-    def _():
-        out_keep[...] = out_part.astype(bf16)
-        gn_keep[...] = gn_part
-        second_keep[...] = second
-
-    @pl.when(i == count - 1)
+        go[...] = jnp.zeros_like(go)
+        sums[...] = jnp.zeros_like(sums)
+        pl.semaphore_wait(barrier, 2)
+
+    @pl.when(step < 2 * half)
+    def _():
+        j = step // 2
+        owner = jnp.where(step % 2 == 0, 1 - core, core)
+        here = pl.ds(pl.multiple_of((owner * half + j) * ROWS, ROWS), ROWS)
+        first = embedded(tok[...], pas[...], vec[...])
+        second = first + (nn(mine[here, :], wom[...]) + nn(other[...], woo[...]))
+        hat, _ = hat_of(second)
+        low = (hat * vec[PASSES + 2 : PASSES + 3] + vec[PASSES + 3 : PASSES + 4]).astype(bf16)
+        upper = nn(low, up[...])
+        square = upper * upper
+        bent = jnp.tanh(gelu_coef * upper * (1.0 + 0.044715 * square))
+        act = (0.5 * upper * (1.0 + bent)).astype(bf16)
+        slope = 0.5 * (1.0 + bent) + (0.5 * gelu_coef) * upper * (1.0 - bent * bent) * (
+            1.0 + (3 * 0.044715) * square
+        )
+        grad_act = nt(cot[...], down[...])
+        grad_upper = (grad_act * slope).astype(bf16)
+        part = nt(grad_upper, up[...])
+
+        @pl.when(step % 2 == 0)
+        def _():
+            core_out[j] = part.astype(bf16)
+            core_copy(j).start()
+
+        @pl.when(step % 2 == 1)
+        def _():
+            core_copy(j).wait_recv()
+            far_out[j] = (part + core_in[j].astype(f32)).astype(bf16)
+            far_copy(j).start()
+            second_keep[...] = second
+            seconds[j] = second
+
+        gup[...] += tn(low, grad_upper)
+        gdown[...] += tn(act, cot[...])
+        out_part = nn(act, down[...]).astype(bf16)
+
+        @pl.when(step % 2 == 0)
+        def _():
+            out_send[...] = out_part
+
+        @pl.when(step % 2 == 1)
+        def _():
+            out_keep[...] = out_part
+
+    @pl.when(step == 2 * half - 1)
     def _():
         for r in range(4):
             for m in range(2):
                 rows, cols = slice(r * SIDE, (r + 1) * SIDE), slice(m * PAIR, (m + 1) * PAIR)
                 for at, total in ((8, gup), (16, gdown)):
                     pair = at + 2 * r + m
-                    slot, column = (pair // 6 - 1) * 3 + pair % 3, pair // 3 % 2
+                    slot, place = (pair // 6 - 1) * 3 + pair % 3, pair // 3 % 2
                     value = total[rows, cols].astype(bf16)
 
-                    @pl.when(place[2] == column)
+                    @pl.when(column == place)
                     def _():
                         g_keep[slot] = value
 
-                    @pl.when(place[2] != column)
+                    @pl.when(column != place)
                     def _():
                         g_send[slot] = value
         for slot in range(2):
 
-            @pl.when(place[2] == 0)
+            @pl.when(column == 0)
             def _():
                 g_keep[slot] = jnp.zeros((SIDE, PAIR), bf16)
 
-            @pl.when(place[2] != 0)
+            @pl.when(column != 0)
             def _():
                 g_send[slot] = jnp.zeros((SIDE, PAIR), bf16)
 
-
-def mlp(place, tokens, passes, vec, mine, other, cotangent, pairs, wo_other):
+    def through_out(grad, block):
+        here = pl.ds(pl.multiple_of(block * ROWS, ROWS), ROWS)
+        grad_mixed[here, :] = nt(grad, wom[...]).astype(bf16)
+        go[...] += tn(mine[here, :], grad)
+
+    @pl.when((step >= 2 * half) & (step < 3 * half))
+    def _():
+        j = step - 2 * half
+        hat, root = hat_of(seconds[j])
+        far_copy(j).wait_recv()
+        grad = far_out[j].astype(f32) + far_in[j].astype(f32)
+        result = cot[...].astype(f32) + norm_back(hat, root, grad, vec[PASSES + 2 : PASSES + 3])
+        low = result.astype(bf16)
+        ga_out[j] = low
+        ga_copy(j).start()
+        grad_second[...] = result
+        sums[0:1] += jnp.sum(grad * hat, axis=0, keepdims=True)
+        sums[1:2] += jnp.sum(grad, axis=0, keepdims=True)
+        through_out(low, core * half + j)
+
+    @pl.when(step > 2 * half)
+    def _():
+        j = step - 2 * half - 1
+        ga_copy(j).wait_recv()
+        through_out(ga_in[j], (1 - core) * half + j)
+
+    @pl.when(step == 3 * half)
+    def _():
+        at = pl.multiple_of(side * SIDE, SIDE)
+        for m in range(2):
+            value = go[pl.ds(at, SIDE), m * PAIR : (m + 1) * PAIR].astype(bf16)
+            none = jnp.zeros_like(value)
+            o_keep[m] = jnp.where(column == 0, value, none)
+            o_send[m] = jnp.where(column == 0, none, value)
+        for j in range(half):
+            core_copy(j).wait_send()
+            far_copy(j).wait_send()
+            ga_copy(j).wait_send()
+
+
+def feed(small, tokens, passes, vec, mine, other, cotangent, pairs, wo_other):
     seq = tokens.shape[0]
-    count = seq // ROWS
-    where = lambda i, s: lax.rem(i + (1 - s[0]) * (count // 2), count)
-    row = lambda n: pl.BlockSpec((ROWS, n), lambda i, s: (where(i, s), 0))
-    send = pl.BlockSpec((ROWS, D), lambda i, s: (jnp.minimum(i, count // 2 - 1), 0))
-    keep = pl.BlockSpec((ROWS, D), lambda i, s: (jnp.maximum(i - count // 2, 0), 0))
-    half = lambda kind: jax.ShapeDtypeStruct((seq // 2, D), kind)
+    half = seq // ROWS // 2
+
+    def block(i):
+        core = lax.axis_index("tensor") % 2
+        work = jnp.minimum(i, 2 * half - 1)
+        owner = jnp.where(work % 2 == 0, 1 - core, core)
+        return owner * half + work // 2
+
+    def cot_block(i):
+        core = lax.axis_index("tensor") % 2
+        return jnp.where(i < 2 * half, block(i), core * half + jnp.minimum(i - 2 * half, half - 1))
+
+    side = lambda: lax.axis_index("tensor") // 2
+    row = lambda n: pl.BlockSpec((ROWS, n), lambda i: (block(i), 0))
+    keep = pl.BlockSpec((ROWS, D), lambda i: (jnp.minimum(i // 2, half - 1), 0))
+    last = pl.BlockSpec((ROWS, D), lambda i: (jnp.clip(i - 2 * half, 0, half - 1), 0))
+    rows = lambda kind: jax.ShapeDtypeStruct((seq // 2, D), kind)
+    gr = lambda n: jax.ShapeDtypeStruct((n, SIDE, PAIR), bf16)
+    buffer = pltpu.VMEM((half, ROWS, D), bf16)
+    dma = pltpu.SemaphoreType.DMA((half,))
     return pl.pallas_call(
-        mlp_kernel,
-        grid_spec=pltpu.PrefetchScalarGridSpec(
-            num_scalar_prefetch=1,
-            grid=(count,),
-            in_specs=[
-                row(D),
-                pl.BlockSpec((1, ROWS), lambda i, s: (0, where(i, s))),
-                full((16, D)),
-                row(PAIR),
-                row(PAIR),
-                row(D),
-                pl.BlockSpec((2, 2, SIDE, PAIR), lambda i, s: (0, 3, 0, 0)),
-                full(wo_other.shape),
-                pl.BlockSpec((1, 8, SIDE, PAIR), lambda i, s: (s[1], 1, 0, 0)),
-                pl.BlockSpec((1, 8, SIDE, PAIR), lambda i, s: (s[1], 2, 0, 0)),
-            ],
-            out_specs=[send, keep, send, keep, keep, full((9, SIDE, PAIR)), full((9, SIDE, PAIR))],
-            scratch_shapes=[
-                pltpu.VMEM((PAIR, D), bf16),
-                pltpu.VMEM((PAIR, D), bf16),
-                pltpu.VMEM((D, D), bf16),
-                pltpu.VMEM((D, D), bf16),
-                pltpu.VMEM((D, D), f32),
-                pltpu.VMEM((D, D), f32),
-            ],
-        ),
+        functools.partial(feed_kernel, small),
+        grid=(3 * half + 1,),
+        in_specs=[
+            row(D),
+            pl.BlockSpec((1, ROWS), lambda i: (0, block(i))),
+            full((16, D)),
+            full((seq, PAIR)),
+            row(PAIR),
+            pl.BlockSpec((ROWS, D), lambda i: (cot_block(i), 0)),
+            pl.BlockSpec((2, 2, SIDE, PAIR), lambda i: (0, 3, 0, 0)),
+            full(wo_other.shape),
+            pl.BlockSpec((1, 8, SIDE, PAIR), lambda i: (side(), 1, 0, 0)),
+            pl.BlockSpec((1, 8, SIDE, PAIR), lambda i: (side(), 2, 0, 0)),
+        ],
+        out_specs=[
+            keep,
+            keep,
+            keep,
+            last,
+            full((seq, PAIR)),
+            full((8, D)),
+            full((9, SIDE, PAIR)),
+            full((9, SIDE, PAIR)),
+            full((2, SIDE, PAIR)),
+            full((2, SIDE, PAIR)),
+        ],
+        scratch_shapes=[
+            pltpu.VMEM((PAIR, D), bf16),
+            pltpu.VMEM((PAIR, D), bf16),
+            pltpu.VMEM((D, D), bf16),
+            pltpu.VMEM((D, D), bf16),
+            pltpu.VMEM((D, D), f32),
+            pltpu.VMEM((D, D), f32),
+            pltpu.VMEM((PAIR, D), f32),
+            buffer,
+            buffer,
+            buffer,
+            buffer,
+            buffer,
+            buffer,
+            pltpu.VMEM((half, ROWS, D), f32),
+            dma,
+            dma,
+            dma,
+            dma,
+            dma,
+            dma,
+        ],
         out_shape=[
-            half(bf16),
-            half(bf16),
-            half(bf16),
-            half(f32),
-            half(f32),
-            jax.ShapeDtypeStruct((9, SIDE, PAIR), bf16),
-            jax.ShapeDtypeStruct((9, SIDE, PAIR), bf16),
+            rows(bf16),
+            rows(bf16),
+            rows(f32),
+            rows(f32),
+            jax.ShapeDtypeStruct((seq, PAIR), bf16),
+            jax.ShapeDtypeStruct((8, D), f32),
+            gr(9),
+            gr(9),
+            gr(2),
+            gr(2),
         ],
-        compiler_params=params(),
+        compiler_params=params(collective_id=1, has_side_effects=True),
+        cost_estimate=cost(50),
         name="feed_forward",
-    )(place, tokens, passes, vec, mine, other, cotangent, pairs, wo_other, pairs, pairs)
-
-
-def second_back_kernel(place, one, two, second, cot, vec, out, low, sums):
-    @pl.when(pl.program_id(0) == 0)
-    def _():
-        sums[...] = jnp.zeros_like(sums)
-
-    grad = one[...].astype(f32) + two[...].astype(f32)
-    hat, root = hat_of(second[...])
-    result = cot[...].astype(f32) + norm_back(hat, root, grad, vec[PASSES + 2 : PASSES + 3])
-    out[...] = result
-    low[...] = result.astype(bf16)
-    sums[0:1] += jnp.sum(grad * hat, axis=0, keepdims=True)
-    sums[1:2] += jnp.sum(grad, axis=0, keepdims=True)
-
-
-def second_back(place, one, two, second, cotangent, vec):
-    rows = one.shape[0]
-    count = rows // ROWS
-    row = pl.BlockSpec((ROWS, D), lambda i, s: (i, 0))
-    mine = pl.BlockSpec((ROWS, D), lambda i, s: (i + s[0] * count, 0))
-    return pl.pallas_call(
-        second_back_kernel,
-        grid_spec=pltpu.PrefetchScalarGridSpec(
-            num_scalar_prefetch=1,
-            grid=(count,),
-            in_specs=[row, row, row, mine, full((16, D))],
-            out_specs=[row, row, full((8, D))],
-        ),
-        out_shape=[
-            jax.ShapeDtypeStruct((rows, D), f32),
-            jax.ShapeDtypeStruct((rows, D), bf16),
-            jax.ShapeDtypeStruct((8, D), f32),
-        ],
-        compiler_params=params(),
-        name="second_back",
-    )(place, one, two, second, cotangent, vec)
-
-
-def project_back_kernel(place, norm, dq, dk, dv, cat, send, keep, g_send, g_keep, acc):
+    )(tokens, passes, vec, mine, other, cotangent, pairs, wo_other, pairs, pairs)
+
+
+def qkv_grads_kernel(place, norm, dq, dk, dv, g_send, g_keep, acc):
     i = pl.program_id(0)
-    count = pl.num_programs(0)
 
     @pl.when(i == 0)
     def _():
         acc[...] = jnp.zeros_like(acc)
 
-    total = nt(dq[...], cat[0]) + nt(dk[...], cat[1]) + nt(dv[...], cat[2])
     for x, grad in enumerate((dq, dk, dv)):
         mine = jnp.where(place[1] == 0, grad[:, :SIDE].astype(f32), grad[:, SIDE:].astype(f32))
         acc[x] += tn(norm[...], mine.astype(bf16))
 
-    @pl.when(i < count // 2)
-    def _():
-        send[...] = total.astype(bf16)
-
-    @pl.when(i >= count // 2)
-    def _():
-        keep[...] = total.astype(bf16)
-
-    @pl.when(i == count - 1)
+    @pl.when(i == pl.num_programs(0) - 1)
     def _():
         for x in range(3):
             for m in range(2):
@@ -681,8 +745,41 @@
                     g_send[slot] = value
 
 
-def project_back(place, norm, dq, dk, dv, cat):
+def qkv_grads(place, norm, dq, dk, dv):
     seq = norm.shape[0]
+    row = lambda n: pl.BlockSpec((ROWS, n), lambda i, s: (i, 0))
+    return pl.pallas_call(
+        qkv_grads_kernel,
+        grid_spec=pltpu.PrefetchScalarGridSpec(
+            num_scalar_prefetch=1,
+            grid=(seq // ROWS,),
+            in_specs=[row(D), row(PAIR), row(PAIR), row(PAIR)],
+            out_specs=[full((3, SIDE, PAIR)), full((3, SIDE, PAIR))],
+            scratch_shapes=[pltpu.VMEM((3, D, SIDE), f32)],
+        ),
+        out_shape=[jax.ShapeDtypeStruct((3, SIDE, PAIR), bf16)] * 2,
+        compiler_params=params(),
+        cost_estimate=cost(8),
+        name="qkv_grads",
+    )(place, norm, dq, dk, dv)
+
+
+def project_back_kernel(place, dq, dk, dv, cat, send, keep):
+    i = pl.program_id(0)
+    count = pl.num_programs(0)
+    total = (nt(dq[...], cat[0]) + nt(dk[...], cat[1]) + nt(dv[...], cat[2])).astype(bf16)
+
+    @pl.when(i < count // 2)
+    def _():
+        send[...] = total
+
+    @pl.when(i >= count // 2)
+    def _():
+        keep[...] = total
+
+
+def project_back(place, dq, dk, dv, cat):
+    seq = dq.shape[0]
     count = seq // ROWS
     where = lambda i, s: lax.rem(i + (1 - s[0]) * (count // 2), count)
     row = lambda n: pl.BlockSpec((ROWS, n), lambda i, s: (where(i, s), 0))
@@ -694,14 +791,14 @@
         grid_spec=pltpu.PrefetchScalarGridSpec(
             num_scalar_prefetch=1,
             grid=(count,),
-            in_specs=[row(D), row(PAIR), row(PAIR), row(PAIR), full(cat.shape)],
-            out_specs=[send, keep, full((3, SIDE, PAIR)), full((3, SIDE, PAIR))],
-            scratch_shapes=[pltpu.VMEM((3, D, SIDE), f32)],
+            in_specs=[row(PAIR), row(PAIR), row(PAIR), full(cat.shape)],
+            out_specs=[send, keep],
         ),
-        out_shape=[half, half] + [jax.ShapeDtypeStruct((3, SIDE, PAIR), bf16)] * 2,
+        out_shape=[half, half],
         compiler_params=params(),
+        cost_estimate=cost(8),
         name="project_back",
-    )(place, norm, dq, dk, dv, cat)
+    )(place, dq, dk, dv, cat)
 
 
 def first_back_kernel(place, tok, pas, vec, one, two, grad_second, low, sums):
@@ -745,6 +842,7 @@
             jax.ShapeDtypeStruct((16, D), f32),
         ],
         compiler_params=params(),
+        cost_estimate=cost(9),
         name="first_back",
     )(place, tokens, passes, vec, one, two, grad_second)
 
@@ -785,17 +883,28 @@
     return lax.ppermute(value, "dp", pairs)
 
 
-def owners_sum(keep, send, z, ends):
-    both = (keep.astype(f32) + hop_x(send).astype(f32)).astype(bf16)
-
-    def term(turn):
+def terms_by_turn(keep, near, z, ends):
+    both = (keep.astype(f32) + near.astype(f32)).astype(bf16)
+    terms = []
+    for turn in range(4):
         at = jnp.clip((z + turn) % 4 - ends[0], 0, len(ends) - 1)
-        return lax.dynamic_index_in_dim(both, at, 0, keepdims=False)
-
-    total = term(0).astype(f32)
-    for turn in (1, 2, 3):
-        total = total + hop_z(term(turn), turn, ends).astype(f32)
+        terms.append(lax.dynamic_index_in_dim(both, at, 0, keepdims=False))
+    return terms
+
+
+def hops_z(terms, ends):
+    return [hop_z(terms[turn], turn, ends) for turn in (1, 2, 3)]
+
+
+def total_of(terms, far):
+    total = terms[0].astype(f32)
+    for value in far:
+        total = total + value.astype(f32)
     return total
+
+
+def tie(*values):
+    return lax.optimization_barrier(values)
 
 
 def on_device(
@@ -837,22 +946,47 @@
     norm, q, k, v, cat = project(tokens, passes, vec, pairs)
     mine, lse = attend(lens, q, k, v)
     other = swap(mine, 1)
-    out_send, out_keep, gn_send, gn_keep, second, w12_send, w12_keep = mlp(
-        place, tokens, passes, vec, mine, other, cotangent, pairs, wo_other
-    )
-    gn_chip = (gn_keep + swap(gn_send, 1).astype(f32)).astype(bf16)
-    gn_far = swap(gn_chip, 2)
-    grad_second, grad_attn, sums_two = second_back(place, gn_chip, gn_far, second, cotangent, vec)
-    grad_attn_other = swap(grad_attn, 1)
-    dq, dk, dv, grads_o = attend_back(
-        lens, place, q, k, v, mine, lse, grad_attn, grad_attn_other, pairs
-    )
-    g1_send, g1_keep, qkv_send, qkv_keep = project_back(place, norm, dq, dk, dv, cat)
-    low_half, sums_one = first_back(
-        place, tokens, passes, vec, g1_keep, swap(g1_send, 1), grad_second
-    )
+    (
+        out_send,
+        out_keep,
+        second,
+        grad_second,
+        grad_mixed,
+        sums_two,
+        w12_send,
+        w12_keep,
+        o_send,
+        o_keep,
+    ) = feed(small, tokens, passes, vec, mine, other, cotangent, pairs, wo_other)
     out_chip = (out_keep.astype(f32) + swap(out_send, 1).astype(f32)).astype(bf16)
-    out_half = (second + (out_chip.astype(f32) + swap(out_chip, 2).astype(f32))).astype(bf16)
+    out_far = swap(out_chip, 2)
+    if small:
+        by_z = lambda value: value.reshape(-1, 3, SIDE, PAIR)
+        w12_near = hop_x(by_z(w12_send))
+        o_near = hop_x(o_send)
+    out_chip, grad_mixed = tie(out_chip, grad_mixed)
+    dq, dk, dv = attend_back(lens, q, k, v, mine, lse, grad_mixed)
+    out_far, dq = tie(out_far, dq)
+    if small:
+        w12_near, o_near, dq = tie(w12_near, o_near, dq)
+        w12_terms = terms_by_turn(by_z(w12_keep), w12_near, z, (1, 2, 3))
+        o_terms = terms_by_turn(o_keep[None], o_near[None], z, (1,))
+        w12_terms, o_terms, dq = tie(w12_terms, o_terms, dq)
+        w12_far = hops_z(w12_terms, (1, 2, 3))
+        o_far = hops_z(o_terms, (1,))
+    qkv_send, qkv_keep = qkv_grads(place, norm, dq, dk, dv)
+    if small:
+        qkv_near = hop_x(by_z(qkv_send))
+        qkv_keep, dq = tie(qkv_keep, dq)
+    g1_send, g1_keep = project_back(place, dq, dk, dv, cat)
+    g1_near = swap(g1_send, 1)
+    if small:
+        qkv_near, g1_keep = tie(qkv_near, g1_keep)
+        qkv_terms = terms_by_turn(by_z(qkv_keep), qkv_near, z, (0,))
+        qkv_terms, g1_keep = tie(qkv_terms, g1_keep)
+        qkv_far = hops_z(qkv_terms, (0,))
+    low_half, sums_one = first_back(place, tokens, passes, vec, g1_keep, g1_near, grad_second)
+    out_half = (second + (out_chip.astype(f32) + out_far.astype(f32))).astype(bf16)
 
     def join(half):
         far = swap(half, 1)
@@ -864,13 +998,10 @@
     vector_part = jnp.concatenate([sums_one[: PASSES + 2], sums_two[:2]], axis=0)
     vector_part = vector_part + swap(vector_part, 1)
     if small:
-        by_z = lambda value: value.reshape(-1, 3, SIDE, PAIR)
-        owned = owners_sum(by_z(w12_keep), by_z(w12_send), z, (1, 2, 3))
-        late = owners_sum(by_z(qkv_keep), by_z(qkv_send), z, (0,))
-        nothing = jnp.zeros_like(grads_o)
-        o_keep = jnp.where(column == 0, grads_o, nothing)
-        o_send = jnp.where(column == 0, nothing, grads_o)
-        o_sum = owners_sum(o_keep[None], o_send[None], z, (1,))
+        o_far, w12_far, qkv_far, low_half = tie(o_far, w12_far, qkv_far, low_half)
+        owned = total_of(w12_terms, w12_far)
+        late = total_of(qkv_terms, qkv_far)
+        o_sum = total_of(o_terms, o_far)
         o_sum = jnp.concatenate([o_sum, jnp.zeros((1, SIDE, PAIR), f32)], axis=0)
         owned = jnp.where(z == 0, late, owned + jnp.where(dp == 2, o_sum, 0.0))
         owned = from_pairs(owned)[None]
@@ -881,10 +1012,12 @@
         wide = vector_params.shape[1]
         vector_grad = lax.dynamic_slice_in_dim(vector_sum, dp * wide, wide, 1)
     else:
-        up_down = jnp.stack([w12_keep.reshape(3, 3, SIDE, PAIR), w12_send.reshape(3, 3, SIDE, PAIR)], axis=1)
+        up_down = jnp.stack(
+            [w12_keep.reshape(3, 3, SIDE, PAIR), w12_send.reshape(3, 3, SIDE, PAIR)], axis=1
+        )
         up_down = up_down.reshape(18, SIDE, PAIR)[2:]
         grad_blocks = from_pairs(
-            jnp.concatenate([qkv_keep, qkv_send, grads_o, up_down], axis=0)
+            jnp.concatenate([qkv_keep, qkv_send, o_keep, up_down], axis=0)
         ).astype(f32)
         spare = jnp.zeros((slots - total_blocks, SIDE, SIDE), f32)
         grad_blocks = jnp.concatenate([grad_blocks, spare], axis=0)[None]

time: 389 us -> 327 us (0.84)
  waiting for transfers between devices: 104 us -> 30.4 us
  starting transfers between devices: 43.3 us -> 47.8 us
    ppermute x11 -> x8, waiting for transfers between devices: 63.8 us -> 6.4 us  [swap(): return lax.ppermute(value, 'tensor', [(t, t ^ bit) for t in range(NT)])]
    pallas_call x2, Pallas kernels: 45.7 us -> 63.9 us  [the longest x1 53.2 us: feed(): pl.pallas_call(functools.partial(feed_kernel, small), grid=(3 * half + 1,...]
    ppermute x12, waiting for transfers between devices: 39.7 us -> 24 us  [hop_z(): return lax.ppermute(value, 'dp', pairs)]
    pallas_call x1, Pallas kernels: 39.9 us -> 31.3 us  [attend_back(): pl.pallas_call(attend_back_kernel, grid_spec=pltpu.PrefetchScalarGridSpec...]
    ppermute x4, starting transfers between devices: 3.68 us -> 9.68 us  [hop_x(): return lax.ppermute(value, 'dp', [(d, d ^ 1) for d in range(8)])]
    pallas_call x1, Pallas kernels: 30.8 us -> 26 us  [attend(): pl.pallas_call(attend_kernel, grid_spec=pltpu.PrefetchScalarGridSpec(num_...]
  transfers between devices with their start and end apart: 27 -> 24, of which waited for: 8 -> 7; matrix products, arithmetic and copies ran while one was open for 6% -> 8% of each run, Pallas kernels for 16% -> 13%
where the time goes in v3:
time: 327 us; the launch traced here: 326 us
  Pallas kernels  211 us (65%)
  starting transfers between devices  47.8 us (15%)
  waiting for transfers between devices  30.4 us (9%)
  other arithmetic  15.4 us (5%)
  local copies, waits for them, and re-layouts  10.1 us (3%)
  matrix products  9.93 us (3%)
    pallas_call x1, Pallas kernels, feed(): pl.pallas_call(functools.partial(feed_kernel, small), grid=(3 * half + 1,...  53.2 us
    pallas_call x1, Pallas kernels, gather(): pl.pallas_call(gather_kernel, in_specs=[pl.BlockSpec(memory_space=pltpu.V...  52.5 us
    ppermute x12, starting transfers between devices, hop_z(): return lax.ppermute(value, 'dp', pairs)  35.4 us
    pallas_call x1, Pallas kernels, attend_back(): pl.pallas_call(attend_back_kernel, grid_spec=pltpu.PrefetchScalarGridSpec...  31.3 us
    pallas_call x1, Pallas kernels, attend(): pl.pallas_call(attend_kernel, grid_spec=pltpu.PrefetchScalarGridSpec(num_...  26 us
    ppermute x12, waiting for transfers between devices, hop_z(): return lax.ppermute(value, 'dp', pairs)  24 us
    pallas_call x1, Pallas kernels, project(): pl.pallas_call(project_kernel, grid=(seq // ROWS,), in_specs=[row(D), pl....  16.1 us
    pallas_call x1, Pallas kernels, project_back(): pl.pallas_call(project_back_kernel, grid_spec=pltpu.PrefetchScalarGridSpe...  11.4 us
  transfers between devices with their start and end apart: 24, of which 7 were waited for; matrix products, arithmetic and copies ran while one was open for 8% of the time, Pallas kernels for 13%

profile of v3, /device:TPU:0, one launch (start us, length us, event | category | flops | bytes accessed | tf_op | source)
XLA Modules:
  0.0 325.5 jit_solution(3763988849358015279)
XLA Ops:
  0.7 52.5 %gather.1 = (bf16[2,24,192,384]{3,2,1,0:T(8,128)(2,1)}, f32[16,768]{1,0:T(8,128)}) custom-call(f32[1,6,192,192]{3,2,1,0:T(8,128)} %own.1, f32[9,96]{1,0:T(8,128)} %vec_own.1), custom_call_target="tpu_custom_call" | custom-call | tf_op jit(solution)/shard_map/gather/pallas_call | solution.py:229
  53.2 16.1 %project.1 = (bf16[2048,768]{1,0:T(8,128)(2,1)}, bf16[2048,384]{1,0:T(8,128)(2,1)}, bf16[2048,384]{1,0:T(8,128)(2,1)}, bf16[2048,384]{1,0:T(8,128)(2,1)}, bf16[3,768,384]{2,1,0:T(8,128)(2,1)}) custom-call(bf16[2048,768]{1,0:T(8,128)(2,1)} %tok.5, s32[1,2048]{1,0:T(1,128)} %bitcast.58, f32[16,768]{1,0:T(8,128)} %get-tuple-element.71.vec, ...), custom_call_target="tpu_custom_call" | custom-call | flops 17600000000 | bytes 16000000 | tf_op jit(solution)/shard_map/project/pallas_call | solution.py:270
  69.3 26.0 %attend.1 = (bf16[2048,384]{1,0:T(8,128)(2,1)}, f32[8,2048]{1,0:T(8,128)}) custom-call(s32[8]{0:T(128)} %bitcast.61, bf16[2048,384]{1,0:T(8,128)(2,1)} %get-tuple-element.73.q, bf16[2048,384]{1,0:T(8,128)(2,1)} %get-tuple-element.74.k, bf16[2048,384]{1,0:T(8,128)(2,1)} %get-tuple-element.75.v), custom_call_target="tpu_custom_call" | custom-call | flops 32999999488 | bytes 30000000 | tf_op jit(solution)/shard_map/attend/pallas_call | solution.py:354
  95.3 1.1 slice.15
  96.4 0.6 collective-permute-start.1
  97.0 2.5 collective-permute-done.1.wo_other
  99.6 0.8 copy-done.21
  100.4 1.2 copy-done.20
  101.6 53.2 %feed_forward.1 = (bf16[1024,768]{1,0:T(8,128)(2,1)}, bf16[1024,768]{1,0:T(8,128)(2,1)}, f32[1024,768]{1,0:T(8,128)}, f32[1024,768]{1,0:T(8,128)}, bf16[2048,384...) custom-call(bf16[2048,768]{1,0:T(8,128)(2,1)} %tok.5, ...), custom_call_target="tpu_custom_call" | custom-call | flops 54999998464 | bytes 50000000 | tf_op jit(solution)/shard_map/feed_forward/pallas_call | solution.py:651
  154.8 0.4 collective-permute-start.2
  155.2 0.7 pad_add_fusion.place
  155.8 5.5 %collective-permute-start.5 = (bf16[3,3,192,384]{3,2,1,0:T(8,128)(2,1)}, bf16[3,3,192,384]{3,2,1,0:T(8,128)(2,1)S(1)}, u32[]{:S(2)}, u32[]{:S(2)}) collective-permute-start(bf16[3,3,192,384]{3,2,1,0:T(8,128)(2,1)} %bitcast.57), channel_id=1, source_target_pairs={{0,4},{4,0},{8,12},{12,8},{16,20},{20,16},{24,28},{28,24},{1,5},{5... | collective-permute-start | bytes 3981320 | tf_op jit(solution)/shard_map/ppermute | solution.py:878
  161.4 1.2 copy-done.2
  162.6 2.3 add_convert_fusion.1
  164.8 1.1 collective-permute-start.3
  166.0 31.3 %attend_back.1 = (bf16[2048,384]{1,0:T(8,128)(2,1)}, bf16[2048,384]{1,0:T(8,128)(2,1)}, bf16[2048,384]{1,0:T(8,128)(2,1)}) custom-call(s32[8]{0:T(128)} %bitcast.62, bf16[2048,384]{1,0:T(8,128)(2,1)} %get-tuple-element.73.q, bf16[2048,384]{1,0:T(8,128)(2,1)} %get-tuple-element.74.k, bf16[2048,384]{1,0:T(8,128)(2,1)} %get-tuple-element.75.v, ...), custom_call_target="tpu_custom_call" | custom-call | flops 44000002048 | bytes 40000000 | tf_op jit(solution)/shard_map/attend_back/pallas_call | solution.py:442
  197.3 3.8 %collective-permute-done.3 = bf16[1024,768]{1,0:T(8,128)(2,1)S(1)} collective-permute-done((bf16[1024,768]{1,0:T(8,128)(2,1)S(1)}, bf16[1024,768]{1,0:T(8,128)(2,1)S(1)}, u32[]{:S(2)}, u32[]{:S(2)}) %collective-permute-start.3) | collective-permute-done | bytes 1572896 | tf_op jit(solution)/shard_map/ppermute | solution.py:874
  201.1 0.1 add_convert_fusion.2
  201.2 0.3 fusion
  201.6 0.7 copy-done.4
  202.2 1.1 dynamic-slice_bitcast_fusion
  203.3 10.7 %qkv_grads.1 = (bf16[3,192,384]{2,1,0:T(8,128)(2,1)}, bf16[3,192,384]{2,1,0:T(8,128)(2,1)}) custom-call(s32[3]{0:T(128)} %pad_add_fusion.place, bf16[2048,768]{1,0:T(8,128)(2,1)} %get-tuple-element.86.norm, bf16[2048,384]{1,0:T(8,128)(2,1)} %get-tuple-element.101.dq, bf16[2048,384]{1,0:T(8,128)(2,1)} %get-tuple-element.96.dk, ...), custom_call_target="tpu_custom_call" | custom-call | flops 8800000000 | bytes 8000000 | tf_op jit(solution)/shard_map/qkv_grads/pallas_call | solution.py:751
  214.0 11.4 %project_back.1 = (bf16[1024,768]{1,0:T(8,128)(2,1)}, bf16[1024,768]{1,0:T(8,128)(2,1)}) custom-call(s32[3]{0:T(128)} %pad_add_fusion.place, bf16[2048,384]{1,0:T(8,128)(2,1)} %get-tuple-element.101.dq, bf16[2048,384]{1,0:T(8,128)(2,1)} %get-tuple-element.96.dk, bf16[2048,384]{1,0:T(8,128)(2,1)} %get-tuple-element.97.dv, ...), custom_call_target="tpu_custom_call" | custom-call | flops 8800000000 | bytes 8000000 | tf_op jit(solution)/shard_map/project_back/pallas_call | solution.py:789
  225.4 3.5 %collective-permute-start.7 = (bf16[1,3,192,384]{3,2,1,0:T(8,128)(2,1)}, bf16[1,3,192,384]{3,2,1,0:T(8,128)(2,1)}, u32[]{:S(2)}, u32[]{:S(2)}) collective-permute-start(bf16[1,3,192,384]{3,2,1,0:T(8,128)(2,1)} %bitcast.12), channel_id=1, source_target_pairs={{0,4},{4,0},{8,12},{12,8},{16,20},{20,16},{24,28},{28,24},{1,5},{5... | collective-permute-start | bytes 1327112 | tf_op jit(solution)/shard_map/ppermute | solution.py:878
  228.9 4.6 %collective-permute-start.10 = (bf16[2,192,384]{2,1,0:T(8,128)(2,1)S(1)}, bf16[2,192,384]{2,1,0:T(8,128)(2,1)}, u32[]{:S(2)}, u32[]{:S(2)}) collective-permute-start(bf16[2,192,384]{2,1,0:T(8,128)(2,1)S(1)} %add_convert_fusion.2), channel_id=1, source_target_pairs={{0,8},{4,12},{1,9},{5,13},{2,10},{6,14},{3,11},{7,15}} | collective-permute-start | bytes 884744 | tf_op jit(solution)/shard_map/ppermute | solution.py:883
  233.5 0.7 slice.19
  234.2 1.3 collective-permute-start.13
  235.6 8.3 %collective-permute-start.14 = (bf16[3,192,384]{2,1,0:T(8,128)(2,1)}, bf16[3,192,384]{2,1,0:T(8,128)(2,1)S(1)}, u32[]{:S(2)}, u32[]{:S(2)}) collective-permute-start(bf16[3,192,384]{2,1,0:T(8,128)(2,1)} %get-tuple-element.115), channel_id=1, source_target_pairs={{0,16},{4,20},{8,24},{12,28},{24,8},{28,12},{1,17},{5,21},{9,25},{... | collective-permute-start | bytes 1327112 | tf_op jit(solution)/shard_map/ppermute | solution.py:883
  243.9 0.7 collective-permute-start.11
  244.6 1.4 collective-permute-start.12
  246.0 2.9 add_convert_fusion
  248.9 1.1 fusion.10
  250.0 11.4 %collective-permute-start.15 = (bf16[3,192,384]{2,1,0:T(8,128)(2,1)S(1)}, bf16[3,192,384]{2,1,0:T(8,128)(2,1)S(1)}, u32[]{:S(2)}, u32[]{:S(2)}) collective-permute-start(bf16[3,192,384]{2,1,0:T(8,128)(2,1)S(1)} %copy-done.9), channel_id=1, source_target_pairs={{0,24},{4,28},{16,8},{20,12},{24,16},{28,20},{1,25},{5,29},{17,9},... | collective-permute-start | bytes 1327112 | tf_op jit(solution)/shard_map/ppermute | solution.py:883
  261.5 0.1 collective-permute-start.4
  261.6 1.3 collective-permute-start.16
  262.9 1.3 collective-permute-start.17
  264.2 1.3 collective-permute-start.18
  265.5 9.6 %first_back.1 = (bf16[1024,768]{1,0:T(8,128)(2,1)}, f32[16,768]{1,0:T(8,128)}) custom-call(s32[3]{0:T(128)} %pad_add_fusion.place, bf16[2048,768]{1,0:T(8,128)(2,1)} %tok.5, s32[1,2048]{1,0:T(1,128)} %bitcast.60, f32[16,768]{1,0:T(8,128)} %get-tuple-element.71.vec, bf16[1024,768]{1,0:T(8,128)(2,1)} %get-tuple-element.106.one, ...), custom_call_target="tpu_custom_call" | custom-call | flops 9900000256 | bytes 9000000 | tf_op jit(solution)/shard_map/first_back/pallas_call | solution.py:825
  275.2 0.8 slice.18
  276.0 0.5 collective-permute-start.19
  276.5 3.8 %collective-permute-done.16 = bf16[3,192,384]{2,1,0:T(8,128)(2,1)S(1)} collective-permute-done((bf16[3,192,384]{2,1,0:T(8,128)(2,1)S(1)}, bf16[3,192,384]{2,1,0:T(8,128)(2,1)S(1)}, u32[]{:S(2)}, u32[]{:S(2)}) %collective-permute-start.16) | collective-permute-done | bytes 442400 | tf_op jit(solution)/shard_map/ppermute | solution.py:883
  280.3 14.5 %collective-permute-done.17 = bf16[3,192,384]{2,1,0:T(8,128)(2,1)} collective-permute-done((bf16[3,192,384]{2,1,0:T(8,128)(2,1)S(1)}, bf16[3,192,384]{2,1,0:T(8,128)(2,1)}, u32[]{:S(2)}, u32[]{:S(2)}) %collective-permute-start.17) | collective-permute-done | bytes 442400 | tf_op jit(solution)/shard_map/ppermute | solution.py:883
  294.9 4.8 %collective-permute-done.18 = bf16[3,192,384]{2,1,0:T(8,128)(2,1)} collective-permute-done((bf16[3,192,384]{2,1,0:T(8,128)(2,1)S(1)}, bf16[3,192,384]{2,1,0:T(8,128)(2,1)}, u32[]{:S(2)}, u32[]{:S(2)}) %collective-permute-start.18) | collective-permute-done | bytes 442400 | tf_op jit(solution)/shard_map/ppermute | solution.py:883
  299.7 1.2 convert_add_fusion.2
  300.9 1.6 add_select_fusion
  302.5 0.2 fusion.14
  302.8 0.1 pad_maximum_fusion.2
  302.9 1.2 copy-done.6
  304.0 1.3 fusion.7
  305.4 0.2 broadcast_select_fusion.3
  305.6 1.0 copy-done.1
  306.7 2.8 bitcast_subtract_fusion
  309.4 2.4 fusion.2
  311.8 0.7 collective-permute-start.20
  312.5 3.5 %fusion.4 = f32[1,6,192,192]{3,2,1,0:T(8,128)} fusion(f32[1,6,192,192]{3,2,1,0:T(8,128)S(1)} %copy-done.8, f32[6,192,192]{2,1,0:T(8,128)S(1)} %bitcast.54), kind=kOutput, calls=%fused_computation.15 | convolution fusion | flops 510050304 | bytes 2654208 | tf_op jit(solution)/shard_map/...ji,...jk->...ik/dot_general | solution.py:855
  316.0 0.1 collective-permute-start.21
  316.0 0.1 collective-permute-start.22
  316.1 3.7 %collective-permute-start.23 = (f32[9,768]{1,0:T(8,128)S(1)}, f32[9,768]{1,0:T(8,128)S(1)}, u32[]{:S(2)}, u32[]{:S(2)}) collective-permute-start(f32[9,768]{1,0:T(8,128)S(1)} %add.177), channel_id=1, source_target_pairs={{0,24},{4,28},{8,0},{12,4},{16,8},{20,12},{24,16},{28,20},{1,25},{... | collective-permute-start | bytes 82952 | tf_op jit(solution)/shard_map/ppermute | solution.py:883
  319.8 1.9 pad_maximum_fusion
  321.7 0.3 collective-permute-done.21
  322.0 0.5 collective-permute-done.22
  322.5 0.7 divide_subtract_fusion
  323.2 0.4 broadcast_select_fusion.1
  323.7 1.9 pad_maximum_fusion.1
  (62 shorter events, 0.2 us)
Async XLA Ops:
  0.6 305.0 %copy-start = (f32[1,6,192,192]{3,2,1,0:T(8,128)S(1)}, f32[1,6,192,192]{3,2,1,0:T(8,128)}, u32[]{:S(2)}) copy-start(f32[1,6,192,192]{3,2,1,0:T(8,128)} %param.21) | copy-start | bytes 2654212
  95.3 4.3 %collective-permute-start = (bf16[2048,384]{1,0:T(8,128)(2,1)}, bf16[2048,384]{1,0:T(8,128)(2,1)S(1)}, u32[]{:S(2)}, u32[]{:S(2)}) collective-permute-start(bf16[2048,384]{1,0:T(8,128)(2,1)} %get-tuple-element.76.mine.mixed), channel_id=1, source_target_pairs={{0,1},{1,0},{2,3},{3,2},{4,5},{5,4},{6,7},{7,6},{8,9},{9,8},{10,11... | collective-permute-start | bytes 4718600 | tf_op jit(solution)/shard_map/ppermute | solution.py:874
  96.4 3.1 collective-permute-start.1
  99.6 0.8 copy-start.21
  100.4 1.2 copy-start.20
  154.8 6.6 %collective-permute-start.2 = (bf16[1024,768]{1,0:T(8,128)(2,1)}, bf16[1024,768]{1,0:T(8,128)(2,1)S(1)}, u32[]{:S(2)}, u32[]{:S(2)}) collective-permute-start(bf16[1024,768]{1,0:T(8,128)(2,1)} %get-tuple-element.79), channel_id=1, source_target_pairs={{0,1},{1,0},{2,3},{3,2},{4,5},{5,4},{6,7},{7,6},{8,9},{9,8},{10,11... | collective-permute-start | bytes 4718600 | tf_op jit(solution)/shard_map/ppermute | solution.py:874
  155.8 45.3 %collective-permute-start.5 = (bf16[3,3,192,384]{3,2,1,0:T(8,128)(2,1)}, bf16[3,3,192,384]{3,2,1,0:T(8,128)(2,1)S(1)}, u32[]{:S(2)}, u32[]{:S(2)}) collective-permute-start(bf16[3,3,192,384]{3,2,1,0:T(8,128)(2,1)} %bitcast.57), channel_id=1, source_target_pairs={{0,4},{4,0},{8,12},{12,8},{16,20},{20,16},{24,28},{28,24},{1,5},{5... | collective-permute-start | bytes 3981320 | tf_op jit(solution)/shard_map/ppermute | solution.py:878
  161.4 39.7 %collective-permute-start.6 = (bf16[2,192,384]{2,1,0:T(8,128)(2,1)}, bf16[2,192,384]{2,1,0:T(8,128)(2,1)S(1)}, u32[]{:S(2)}, u32[]{:S(2)}) collective-permute-start(bf16[2,192,384]{2,1,0:T(8,128)(2,1)} %get-tuple-element.89), channel_id=1, source_target_pairs={{0,4},{4,0},{8,12},{12,8},{16,20},{20,16},{24,28},{28,24},{1,5},{5... | collective-permute-start | bytes 884744 | tf_op jit(solution)/shard_map/ppermute | solution.py:878
  161.4 1.2 copy-start.2
  164.8 36.3 %collective-permute-start.3 = (bf16[1024,768]{1,0:T(8,128)(2,1)S(1)}, bf16[1024,768]{1,0:T(8,128)(2,1)S(1)}, u32[]{:S(2)}, u32[]{:S(2)}) collective-permute-start(bf16[1024,768]{1,0:T(8,128)(2,1)S(1)} %add_convert_fusion.1), channel_id=1, source_target_pairs={{0,2},{1,3},{2,0},{3,1},{4,6},{5,7},{6,4},{7,5},{8,10},{9,11},{10,... | collective-permute-start | bytes 4718600 | tf_op jit(solution)/shard_map/ppermute | solution.py:874
  166.0 35.2 %copy-start.15 = (bf16[2,192,384]{2,1,0:T(8,128)(2,1)S(1)}, bf16[2,192,384]{2,1,0:T(8,128)(2,1)}, u32[]{:S(2)}) copy-start(bf16[2,192,384]{2,1,0:T(8,128)(2,1)} %get-tuple-element.92) | copy-start | bytes 884740
  166.0 35.2 %copy-start.5 = (bf16[9,192,384]{2,1,0:T(8,128)(2,1)S(1)}, bf16[9,192,384]{2,1,0:T(8,128)(2,1)}, u32[]{:S(2)}) copy-start(bf16[9,192,384]{2,1,0:T(8,128)(2,1)} %get-tuple-element.87) | copy-start | bytes 3981316
  201.1 1.1 copy-start.4
  225.4 38.8 %collective-permute-start.8 = (bf16[1024,768]{1,0:T(8,128)(2,1)}, bf16[1024,768]{1,0:T(8,128)(2,1)}, u32[]{:S(2)}, u32[]{:S(2)}) collective-permute-start(bf16[1024,768]{1,0:T(8,128)(2,1)} %get-tuple-element.107), channel_id=1, source_target_pairs={{0,1},{1,0},{2,3},{3,2},{4,5},{5,4},{6,7},{7,6},{8,9},{9,8},{10,11... | collective-permute-start | bytes 4718600 | tf_op jit(solution)/shard_map/ppermute | solution.py:874
  225.4 19.1 %collective-permute-start.7 = (bf16[1,3,192,384]{3,2,1,0:T(8,128)(2,1)}, bf16[1,3,192,384]{3,2,1,0:T(8,128)(2,1)}, u32[]{:S(2)}, u32[]{:S(2)}) collective-permute-start(bf16[1,3,192,384]{3,2,1,0:T(8,128)(2,1)} %bitcast.12), channel_id=1, source_target_pairs={{0,4},{4,0},{8,12},{12,8},{16,20},{20,16},{24,28},{28,24},{1,5},{5... | collective-permute-start | bytes 1327112 | tf_op jit(solution)/shard_map/ppermute | solution.py:878
  228.9 15.0 %collective-permute-start.10 = (bf16[2,192,384]{2,1,0:T(8,128)(2,1)S(1)}, bf16[2,192,384]{2,1,0:T(8,128)(2,1)}, u32[]{:S(2)}, u32[]{:S(2)}) collective-permute-start(bf16[2,192,384]{2,1,0:T(8,128)(2,1)S(1)} %add_convert_fusion.2), channel_id=1, source_target_pairs={{0,8},{4,12},{1,9},{5,13},{2,10},{6,14},{3,11},{7,15}} | collective-permute-start | bytes 884744 | tf_op jit(solution)/shard_map/ppermute | solution.py:883
  234.2 27.3 %collective-permute-start.13 = (bf16[3,192,384]{2,1,0:T(8,128)(2,1)}, bf16[3,192,384]{2,1,0:T(8,128)(2,1)S(1)}, u32[]{:S(2)}, u32[]{:S(2)}) collective-permute-start(bf16[3,192,384]{2,1,0:T(8,128)(2,1)} %get-tuple-element.114), channel_id=1, source_target_pairs={{0,8},{4,12},{8,16},{12,20},{16,24},{20,28},{1,9},{5,13},{9,17},{1... | collective-permute-start | bytes 1327112 | tf_op jit(solution)/shard_map/ppermute | solution.py:883
  235.6 27.3 %collective-permute-start.14 = (bf16[3,192,384]{2,1,0:T(8,128)(2,1)}, bf16[3,192,384]{2,1,0:T(8,128)(2,1)S(1)}, u32[]{:S(2)}, u32[]{:S(2)}) collective-permute-start(bf16[3,192,384]{2,1,0:T(8,128)(2,1)} %get-tuple-element.115), channel_id=1, source_target_pairs={{0,16},{4,20},{8,24},{12,28},{24,8},{28,12},{1,17},{5,21},{9,25},{... | collective-permute-start | bytes 1327112 | tf_op jit(solution)/shard_map/ppermute | solution.py:883
  243.9 6.1 %collective-permute-start.11 = (bf16[2,192,384]{2,1,0:T(8,128)(2,1)S(1)}, bf16[2,192,384]{2,1,0:T(8,128)(2,1)S(1)}, u32[]{:S(2)}, u32[]{:S(2)}) collective-permute-start(bf16[2,192,384]{2,1,0:T(8,128)(2,1)S(1)} %add_convert_fusion.2), channel_id=1, source_target_pairs={{24,8},{28,12},{25,9},{29,13},{26,10},{30,14},{27,11},{31,15}} | collective-permute-start | bytes 884744 | tf_op jit(solution)/shard_map/ppermute | solution.py:883
  244.6 16.9 %collective-permute-start.12 = (bf16[2,192,384]{2,1,0:T(8,128)(2,1)S(1)}, bf16[2,192,384]{2,1,0:T(8,128)(2,1)}, u32[]{:S(2)}, u32[]{:S(2)}) collective-permute-start(bf16[2,192,384]{2,1,0:T(8,128)(2,1)S(1)} %add_convert_fusion.2), channel_id=1, source_target_pairs={{16,8},{20,12},{17,9},{21,13},{18,10},{22,14},{19,11},{23,15}} | collective-permute-start | bytes 884744 | tf_op jit(solution)/shard_map/ppermute | solution.py:883
  246.0 2.9 copy-start.10
  246.0 4.1 %copy-start.9 = (bf16[3,192,384]{2,1,0:T(8,128)(2,1)S(1)}, bf16[3,192,384]{2,1,0:T(8,128)(2,1)}, u32[]{:S(2)}) copy-start(bf16[3,192,384]{2,1,0:T(8,128)(2,1)} %get-tuple-element.116) | copy-start | bytes 1327108
  250.0 11.4 %copy-start.16 = (bf16[2,192,384]{2,1,0:T(8,128)(2,1)}, bf16[2,192,384]{2,1,0:T(8,128)(2,1)S(1)}, u32[]{:S(2)}) copy-start(bf16[2,192,384]{2,1,0:T(8,128)(2,1)S(1)} %collective-permute-done.11) | copy-start | bytes 884740
  250.0 25.9 %collective-permute-start.15 = (bf16[3,192,384]{2,1,0:T(8,128)(2,1)S(1)}, bf16[3,192,384]{2,1,0:T(8,128)(2,1)S(1)}, u32[]{:S(2)}, u32[]{:S(2)}) collective-permute-start(bf16[3,192,384]{2,1,0:T(8,128)(2,1)S(1)} %copy-done.9), channel_id=1, source_target_pairs={{0,24},{4,28},{16,8},{20,12},{24,16},{28,20},{1,25},{5,29},{17,9},... | collective-permute-start | bytes 1327112 | tf_op jit(solution)/shard_map/ppermute | solution.py:883
  261.5 43.9 %collective-permute-start.4 = (bf16[1024,768]{1,0:T(8,128)(2,1)S(1)}, bf16[1024,768]{1,0:T(8,128)(2,1)S(1)}, u32[]{:S(2)}, u32[]{:S(2)}) collective-permute-start(bf16[1024,768]{1,0:T(8,128)(2,1)S(1)} %add_convert_fusion), channel_id=1, source_target_pairs={{0,1},{1,0},{2,3},{3,2},{4,5},{5,4},{6,7},{7,6},{8,9},{9,8},{10,11... | collective-permute-start | bytes 4718600 | tf_op jit(solution)/shard_map/ppermute | solution.py:874
  261.6 13.6 %copy-start.11 = (bf16[3,192,384]{2,1,0:T(8,128)(2,1)}, bf16[3,192,384]{2,1,0:T(8,128)(2,1)S(1)}, u32[]{:S(2)}) copy-start(bf16[3,192,384]{2,1,0:T(8,128)(2,1)S(1)} %collective-permute-done.13) | copy-start | bytes 1327108
  261.6 18.8 %collective-permute-start.16 = (bf16[3,192,384]{2,1,0:T(8,128)(2,1)S(1)}, bf16[3,192,384]{2,1,0:T(8,128)(2,1)S(1)}, u32[]{:S(2)}, u32[]{:S(2)}) collective-permute-start(bf16[3,192,384]{2,1,0:T(8,128)(2,1)S(1)} %fusion.10), channel_id=1, source_target_pairs={{24,0},{28,4},{25,1},{29,5},{26,2},{30,6},{27,3},{31,7}} | collective-permute-start | bytes 1327112 | tf_op jit(solution)/shard_map/ppermute | solution.py:883
  262.9 1.3 copy-start.13
  262.9 32.0 %collective-permute-start.17 = (bf16[3,192,384]{2,1,0:T(8,128)(2,1)S(1)}, bf16[3,192,384]{2,1,0:T(8,128)(2,1)}, u32[]{:S(2)}, u32[]{:S(2)}) collective-permute-start(bf16[3,192,384]{2,1,0:T(8,128)(2,1)S(1)} %fusion.10), channel_id=1, source_target_pairs={{16,0},{20,4},{17,1},{21,5},{18,2},{22,6},{19,3},{23,7}} | collective-permute-start | bytes 1327112 | tf_op jit(solution)/shard_map/ppermute | solution.py:883
  264.2 35.5 %collective-permute-start.18 = (bf16[3,192,384]{2,1,0:T(8,128)(2,1)S(1)}, bf16[3,192,384]{2,1,0:T(8,128)(2,1)}, u32[]{:S(2)}, u32[]{:S(2)}) collective-permute-start(bf16[3,192,384]{2,1,0:T(8,128)(2,1)S(1)} %fusion.10), channel_id=1, source_target_pairs={{8,0},{12,4},{9,1},{13,5},{10,2},{14,6},{11,3},{15,7}} | collective-permute-start | bytes 1327112 | tf_op jit(solution)/shard_map/ppermute | solution.py:883
  265.5 34.2 %copy-start.17 = (bf16[2,192,384]{2,1,0:T(8,128)(2,1)S(1)}, bf16[2,192,384]{2,1,0:T(8,128)(2,1)}, u32[]{:S(2)}) copy-start(bf16[2,192,384]{2,1,0:T(8,128)(2,1)} %copy-done.16) | copy-start | bytes 884740
  275.1 25.7 %copy-start.14 = (bf16[3,192,384]{2,1,0:T(8,128)(2,1)S(1)}, bf16[3,192,384]{2,1,0:T(8,128)(2,1)}, u32[]{:S(2)}) copy-start(bf16[3,192,384]{2,1,0:T(8,128)(2,1)} %copy-done.13) | copy-start | bytes 1327108
  275.1 25.7 %copy-start.12 = (bf16[3,192,384]{2,1,0:T(8,128)(2,1)S(1)}, bf16[3,192,384]{2,1,0:T(8,128)(2,1)}, u32[]{:S(2)}) copy-start(bf16[3,192,384]{2,1,0:T(8,128)(2,1)} %copy-done.11) | copy-start | bytes 1327108
  276.0 35.8 %collective-permute-start.19 = (f32[9,768]{1,0:T(8,128)S(1)}, f32[9,768]{1,0:T(8,128)S(1)}, u32[]{:S(2)}, u32[]{:S(2)}) collective-permute-start(f32[9,768]{1,0:T(8,128)S(1)} %pad_maximum_fusion.3), channel_id=1, source_target_pairs={{0,1},{1,0},{2,3},{3,2},{4,5},{5,4},{6,7},{7,6},{8,9},{9,8},{10,11... | collective-permute-start | bytes 82952 | tf_op jit(solution)/shard_map/ppermute | solution.py:874
  280.3 42.9 %collective-permute-start.9 = (bf16[1024,768]{1,0:T(8,128)(2,1)}, bf16[1024,768]{1,0:T(8,128)(2,1)S(1)}, u32[]{:S(2)}, u32[]{:S(2)}) collective-permute-start(bf16[1024,768]{1,0:T(8,128)(2,1)} %get-tuple-element.109), channel_id=1, source_target_pairs={{0,1},{1,0},{2,3},{3,2},{4,5},{5,4},{6,7},{7,6},{8,9},{9,8},{10,11... | collective-permute-start | bytes 4718600 | tf_op jit(solution)/shard_map/ppermute | solution.py:874
  302.8 1.3 copy-start.6
  305.4 1.3 copy-start.1
  306.7 2.8 copy-start.7
  309.4 3.0 copy-start.8
  311.8 4.2 %collective-permute-start.20 = (f32[9,768]{1,0:T(8,128)S(1)}, f32[9,768]{1,0:T(8,128)S(1)}, u32[]{:S(2)}, u32[]{:S(2)}) collective-permute-start(f32[9,768]{1,0:T(8,128)S(1)} %fusion.12), channel_id=1, source_target_pairs={{0,4},{4,0},{8,12},{12,8},{16,20},{20,16},{24,28},{28,24},{1,5},{5... | collective-permute-start | bytes 82952 | tf_op jit(solution)/shard_map/ppermute | solution.py:878
  316.0 6.0 %collective-permute-start.21 = (f32[9,768]{1,0:T(8,128)S(1)}, f32[9,768]{1,0:T(8,128)S(1)}, u32[]{:S(2)}, u32[]{:S(2)}) collective-permute-start(f32[9,768]{1,0:T(8,128)S(1)} %add.177), channel_id=1, source_target_pairs={{0,8},{4,12},{8,16},{12,20},{16,24},{20,28},{24,0},{28,4},{1,9},{5... | collective-permute-start | bytes 82952 | tf_op jit(solution)/shard_map/ppermute | solution.py:883
  316.0 6.5 %collective-permute-start.22 = (f32[9,768]{1,0:T(8,128)S(1)}, f32[9,768]{1,0:T(8,128)S(1)}, u32[]{:S(2)}, u32[]{:S(2)}) collective-permute-start(f32[9,768]{1,0:T(8,128)S(1)} %add.177), channel_id=1, source_target_pairs={{0,16},{4,20},{8,24},{12,28},{16,0},{20,4},{24,8},{28,12},{1,17},{... | collective-permute-start | bytes 82952 | tf_op jit(solution)/shard_map/ppermute | solution.py:883
  316.1 6.4 %collective-permute-start.23 = (f32[9,768]{1,0:T(8,128)S(1)}, f32[9,768]{1,0:T(8,128)S(1)}, u32[]{:S(2)}, u32[]{:S(2)}) collective-permute-start(f32[9,768]{1,0:T(8,128)S(1)} %add.177), channel_id=1, source_target_pairs={{0,24},{4,28},{8,0},{12,4},{16,8},{20,12},{24,16},{28,20},{1,25},{... | collective-permute-start | bytes 82952 | tf_op jit(solution)/shard_map/ppermute | solution.py:883
  319.8 2.7 copy-start.18
  319.8 2.7 copy-start.19
  319.8 3.4 %copy-start.3 = (bf16[1024,768]{1,0:T(8,128)(2,1)S(1)}, bf16[1024,768]{1,0:T(8,128)(2,1)}, u32[]{:S(2)}) copy-start(bf16[1024,768]{1,0:T(8,128)(2,1)} %get-tuple-element.109) | copy-start | bytes 4718596

commit v4 on v3

--- a/solution.py
+++ b/solution.py
@@ -468,16 +468,20 @@
 
 def feed_kernel(
     small, tok, pas, vec, mine, other, cot, wo_mine, wo_other, w1, w2,
-    out_send, out_keep, second_keep, grad_second, grad_mixed, sums, g_send, g_keep, o_send, o_keep,
-    wom, woo, up, down, gup, gdown, go, core_out, core_in, far_out, far_in, ga_out, ga_in, seconds,
-    s_core, r_core, s_far, r_far, s_ga, r_ga,
+    out_chip, second_keep, grad_second, grad_mixed, sums, o_send, o_keep, *rest,
 ):
+    results, rest = (rest[:4], rest[4:]) if small else (rest[:2], rest[2:])
+    (
+        wom, woo, up, down, gup, gdown, go, core_out, core_in, far_out, far_in, ga_out, ga_in, oc_out, oc_in, seconds,
+        g_send, g_keep, g_in, s_core, r_core, s_far, r_far, s_ga, r_ga, s_oc, r_oc, s_x, r_x,
+    ) = rest
     step = pl.program_id(0)
     half = core_out.shape[0]
-    t = lax.axis_index("tensor")
+    t, dp = lax.axis_index("tensor"), lax.axis_index("dp")
     core, side = t % 2, t // 2
     near, far = side * 2 + (1 - core), (1 - side) * 2 + core
-    column = lax.axis_index("dp") % 2 if small else 0
+    z, column = (dp // 2, dp % 2) if small else (0, 0)
+    far_x = z * 2 + 1 - column
 
     def copy(src, dst, s_sem, r_sem, j, to):
         return pltpu.make_async_remote_copy(
@@ -492,12 +496,26 @@
     core_copy = lambda j: copy(core_out, core_in, s_core, r_core, j, near)
     far_copy = lambda j: copy(far_out, far_in, s_far, r_far, j, far)
     ga_copy = lambda j: copy(ga_out, ga_in, s_ga, r_ga, j, near)
+    oc_copy = lambda j: copy(oc_out, oc_in, s_oc, r_oc, j, near)
+
+    def x_copy(slot):
+        return pltpu.make_async_remote_copy(
+            src_ref=g_send.at[slot],
+            dst_ref=g_in.at[slot],
+            send_sem=s_x.at[slot],
+            recv_sem=r_x.at[slot],
+            device_id={"dp": far_x},
+            device_id_type=MESH,
+        )
+
     barrier = pltpu.get_barrier_semaphore()
 
     @pl.when(step == 0)
     def _():
         for to in (near, far):
             pl.semaphore_signal(barrier, inc=1, device_id={"tensor": to}, device_id_type=MESH)
+        if small:
+            pl.semaphore_signal(barrier, inc=1, device_id={"dp": far_x}, device_id_type=MESH)
         for h in range(2):
             for m in range(2):
                 rows, cols = slice(h * SIDE, (h + 1) * SIDE), slice(m * PAIR, (m + 1) * PAIR)
@@ -512,7 +530,7 @@
         gdown[...] = jnp.zeros_like(gdown)
         go[...] = jnp.zeros_like(go)
         sums[...] = jnp.zeros_like(sums)
-        pl.semaphore_wait(barrier, 2)
+        pl.semaphore_wait(barrier, 3 if small else 2)
 
     @pl.when(step < 2 * half)
     def _():
@@ -549,15 +567,17 @@
 
         gup[...] += tn(low, grad_upper)
         gdown[...] += tn(act, cot[...])
-        out_part = nn(act, down[...]).astype(bf16)
+        out_part = nn(act, down[...])
 
         @pl.when(step % 2 == 0)
         def _():
-            out_send[...] = out_part
+            oc_out[j] = out_part.astype(bf16)
+            oc_copy(j).start()
 
         @pl.when(step % 2 == 1)
         def _():
-            out_keep[...] = out_part
+            oc_copy(j).wait_recv()
+            out_chip[...] = (out_part + oc_in[j].astype(f32)).astype(bf16)
 
     @pl.when(step == 2 * half - 1)
     def _():
@@ -576,15 +596,14 @@
                     @pl.when(column != place)
                     def _():
                         g_send[slot] = value
+        if small:
+            for slot in range(9):
+                pl.when((column == 0) | (slot > 1))(x_copy(slot).start)
         for slot in range(2):
 
             @pl.when(column == 0)
             def _():
                 g_keep[slot] = jnp.zeros((SIDE, PAIR), bf16)
-
-            @pl.when(column != 0)
-            def _():
-                g_send[slot] = jnp.zeros((SIDE, PAIR), bf16)
 
     def through_out(grad, block):
         here = pl.ds(pl.multiple_of(block * ROWS, ROWS), ROWS)
@@ -622,8 +641,27 @@
             o_send[m] = jnp.where(column == 0, none, value)
         for j in range(half):
             core_copy(j).wait_send()
+            oc_copy(j).wait_send()
             far_copy(j).wait_send()
             ga_copy(j).wait_send()
+        if small:
+            for slot in range(9):
+                pl.when((column == 1) | (slot > 1))(x_copy(slot).wait_recv)
+                pl.when((column == 0) | (slot > 1))(x_copy(slot).wait_send)
+            for slot in range(9):
+                if slot > 1:
+                    value = (g_keep[slot].astype(f32) + g_in[slot].astype(f32)).astype(bf16)
+                else:
+                    other_term = jnp.where(column == 1, g_in[slot], jnp.zeros((SIDE, PAIR), bf16))
+                    value = (g_keep[slot].astype(f32) + other_term.astype(f32)).astype(bf16)
+                for turn in range(4):
+
+                    @pl.when(z + turn == slot // 3 + 1 + 4 * (z + turn >= 4).astype(jnp.int32))
+                    def _():
+                        results[turn][slot % 3] = value
+        else:
+            results[0][...] = g_send[...]
+            results[1][...] = g_keep[...]
 
 
 def feed(small, tokens, passes, vec, mine, other, cotangent, pairs, wo_other):
@@ -646,6 +684,7 @@
     last = pl.BlockSpec((ROWS, D), lambda i: (jnp.clip(i - 2 * half, 0, half - 1), 0))
     rows = lambda kind: jax.ShapeDtypeStruct((seq // 2, D), kind)
     gr = lambda n: jax.ShapeDtypeStruct((n, SIDE, PAIR), bf16)
+    ends = [(3, SIDE, PAIR)] * 4 if small else [(9, SIDE, PAIR)] * 2
     buffer = pltpu.VMEM((half, ROWS, D), bf16)
     dma = pltpu.SemaphoreType.DMA((half,))
     return pl.pallas_call(
@@ -666,15 +705,13 @@
         out_specs=[
             keep,
             keep,
-            keep,
             last,
             full((seq, PAIR)),
             full((8, D)),
-            full((9, SIDE, PAIR)),
-            full((9, SIDE, PAIR)),
             full((2, SIDE, PAIR)),
             full((2, SIDE, PAIR)),
-        ],
+        ]
+        + [full(shape) for shape in ends],
         scratch_shapes=[
             pltpu.VMEM((PAIR, D), bf16),
             pltpu.VMEM((PAIR, D), bf16),
@@ -683,39 +720,29 @@
             pltpu.VMEM((D, D), f32),
             pltpu.VMEM((D, D), f32),
             pltpu.VMEM((PAIR, D), f32),
-            buffer,
-            buffer,
-            buffer,
-            buffer,
-            buffer,
-            buffer,
-            pltpu.VMEM((half, ROWS, D), f32),
-            dma,
-            dma,
-            dma,
-            dma,
-            dma,
-            dma,
-        ],
+        ]
+        + [buffer] * 8
+        + [pltpu.VMEM((half, ROWS, D), f32)]
+        + [pltpu.VMEM((9, SIDE, PAIR), bf16)] * 3
+        + [dma] * 8
+        + [pltpu.SemaphoreType.DMA((9,))] * 2,
         out_shape=[
-            rows(bf16),
             rows(bf16),
             rows(f32),
             rows(f32),
             jax.ShapeDtypeStruct((seq, PAIR), bf16),
             jax.ShapeDtypeStruct((8, D), f32),
-            gr(9),
-            gr(9),
             gr(2),
             gr(2),
-        ],
+        ]
+        + [jax.ShapeDtypeStruct(shape, bf16) for shape in ends],
         compiler_params=params(collective_id=1, has_side_effects=True),
         cost_estimate=cost(50),
         name="feed_forward",
     )(tokens, passes, vec, mine, other, cotangent, pairs, wo_other, pairs, pairs)
 
 
-def qkv_grads_kernel(place, norm, dq, dk, dv, g_send, g_keep, acc):
+def qkv_grads_kernel(place, norm, dq, dk, dv, o_send, o_keep, g_send, g_keep, acc):
     i = pl.program_id(0)
 
     @pl.when(i == 0)
@@ -728,6 +755,9 @@
 
     @pl.when(i == pl.num_programs(0) - 1)
     def _():
+        for m in range(2):
+            g_send[3 + m] = o_send[m]
+            g_keep[3 + m] = o_keep[m]
         for x in range(3):
             for m in range(2):
                 at = 2 * m * SIDE
@@ -745,7 +775,7 @@
                     g_send[slot] = value
 
 
-def qkv_grads(place, norm, dq, dk, dv):
+def qkv_grads(place, norm, dq, dk, dv, o_send, o_keep):
     seq = norm.shape[0]
     row = lambda n: pl.BlockSpec((ROWS, n), lambda i, s: (i, 0))
     return pl.pallas_call(
@@ -753,98 +783,256 @@
         grid_spec=pltpu.PrefetchScalarGridSpec(
             num_scalar_prefetch=1,
             grid=(seq // ROWS,),
-            in_specs=[row(D), row(PAIR), row(PAIR), row(PAIR)],
-            out_specs=[full((3, SIDE, PAIR)), full((3, SIDE, PAIR))],
+            in_specs=[row(D), row(PAIR), row(PAIR), row(PAIR)] + [full((2, SIDE, PAIR))] * 2,
+            out_specs=[full((5, SIDE, PAIR)), full((5, SIDE, PAIR))],
             scratch_shapes=[pltpu.VMEM((3, D, SIDE), f32)],
         ),
-        out_shape=[jax.ShapeDtypeStruct((3, SIDE, PAIR), bf16)] * 2,
+        out_shape=[jax.ShapeDtypeStruct((5, SIDE, PAIR), bf16)] * 2,
         compiler_params=params(),
         cost_estimate=cost(8),
         name="qkv_grads",
-    )(place, norm, dq, dk, dv)
-
-
-def project_back_kernel(place, dq, dk, dv, cat, send, keep):
+    )(place, norm, dq, dk, dv, o_send, o_keep)
+
+
+CHUNK = SIDE // 2
+CHUNKS = 10
+
+
+def last_kernel(small, dq, dk, dv, cat, tok, pas, vec, grad_second, sums_two, g_send, g_keep, low, *rest):
+    if small:
+        late, vec_sum = rest[:2]
+        rest = rest[2:]
+        (
+            core_out, core_in, sums, core_sums, x_in, z_in, z_out, up_in, v_out, v_in,
+            s_core, r_core, s_sum, r_sum, s_x, r_x, s_z, r_z, s_up, r_up, s_v, r_v,
+        ) = rest
+    else:
+        vec_sum, core_out, core_in, sums, core_sums, s_core, r_core, s_sum, r_sum = rest
     i = pl.program_id(0)
-    count = pl.num_programs(0)
-    total = (nt(dq[...], cat[0]) + nt(dk[...], cat[1]) + nt(dv[...], cat[2])).astype(bf16)
-
-    @pl.when(i < count // 2)
-    def _():
-        send[...] = total
-
-    @pl.when(i >= count // 2)
-    def _():
-        keep[...] = total
-
-
-def project_back(place, dq, dk, dv, cat):
+    half = core_out.shape[0]
+    t, dp = lax.axis_index("tensor"), lax.axis_index("dp")
+    core, side = t % 2, t // 2
+    near = side * 2 + (1 - core)
+    z, column = (dp // 2, dp % 2) if small else (0, 0)
+    far_x = z * 2 + 1 - column
+    peers = [lax.rem(dp + k, 8) for k in range(1, 8)]
+
+    def copy(src, dst, s_sem, r_sem, to):
+        return pltpu.make_async_remote_copy(
+            src_ref=src, dst_ref=dst, send_sem=s_sem, recv_sem=r_sem, device_id=to, device_id_type=MESH
+        )
+
+    core_copy = lambda j: copy(core_out.at[j], core_in.at[j], s_core.at[j], r_core.at[j], {"tensor": near})
+    sum_copy = lambda: copy(sums, core_sums, s_sum, r_sum, {"tensor": near})
+
+    def part_of(ref, k):
+        return ref.at[k // 2, pl.ds((k % 2) * CHUNK, CHUNK)]
+
+    x_copy = lambda k: copy(part_of(g_send, k), x_in.at[k], s_x.at[k], r_x.at[k], {"dp": far_x})
+    z_copy = lambda k: copy(z_out.at[k], z_in.at[k], s_z.at[k], r_z.at[k], {"dp": dp - 2})
+    up_copy = lambda k: copy(z_out.at[k], up_in.at[k - 6], s_up.at[k - 6], r_up.at[k - 6], {"dp": dp + 2})
+    v_copy = lambda n: copy(v_out.at[peers[n]], v_in.at[dp], s_v.at[n], r_v.at[dp], {"dp": peers[n]})
+    barrier = pltpu.get_barrier_semaphore()
+
+    @pl.when(i == 0)
+    def _():
+        pl.semaphore_signal(barrier, inc=1, device_id={"tensor": near}, device_id_type=MESH)
+        if small:
+            for peer in peers:
+                pl.semaphore_signal(barrier, inc=1, device_id={"dp": peer}, device_id_type=MESH)
+            late[...] = jnp.zeros_like(late)
+        sums[...] = jnp.zeros_like(sums)
+        sums[PASSES + 2 : PASSES + 4] = sums_two[0:2]
+        pl.semaphore_wait(barrier, 8 if small else 1)
+        if small:
+            for k in range(CHUNKS):
+                if k < 6:
+                    x_copy(k).start()
+                else:
+                    pl.when(column == 1)(x_copy(k).start)
+
+    @pl.when(i < 2 * half)
+    def _():
+        part = nt(dq[...], cat[0]) + nt(dk[...], cat[1]) + nt(dv[...], cat[2])
+
+        @pl.when(i < half)
+        def _():
+            core_out[i] = part.astype(bf16)
+            core_copy(i).start()
+
+        @pl.when(i >= half)
+        def _():
+            j = i - half
+            hat, root = hat_of(embedded(tok[...], pas[...], vec[...]))
+            core_copy(j).wait_recv()
+            grad = part + core_in[j].astype(f32)
+            result = grad_second[...] + norm_back(hat, root, grad, vec[PASSES : PASSES + 1])
+            low[...] = result.astype(bf16)
+            chosen = one_hot(pas[...])
+            high, mid, tail = split_three(result)
+            sums[...] += nn(chosen, high) + nn(chosen, mid) + nn(chosen, tail)
+            sums[PASSES : PASSES + 1] += jnp.sum(grad * hat, axis=0, keepdims=True)
+            sums[PASSES + 1 : PASSES + 2] += jnp.sum(grad, axis=0, keepdims=True)
+
+    @pl.when(i == 2 * half - 1)
+    def _():
+        sum_copy().start()
+
+    if small:
+
+        def term_of(k):
+            x_copy(k).wait_recv()
+            keep = g_keep[k // 2, pl.ds(pl.multiple_of((k % 2) * CHUNK, 16), CHUNK), :]
+            return keep.astype(f32) + x_in[k].astype(f32)
+
+        def keep_late(k, pair, total):
+            late[pair, pl.ds(pl.multiple_of((k % 2) * CHUNK, 16), CHUNK), :] = total
+
+        k = i - 2 - 2 * (3 - z)
+
+        @pl.when((k >= 0) & (k < 6))
+        def _():
+            total = term_of(k)
+
+            @pl.when(z == 3)
+            def _():
+                z_out[k] = total.astype(bf16)
+                z_copy(k).start()
+
+            @pl.when((z == 1) | (z == 2))
+            def _():
+                z_copy(k).wait_recv()
+                z_out[k] = (total + z_in[k].astype(f32)).astype(bf16)
+                z_copy(k).start()
+
+            @pl.when(z == 0)
+            def _():
+                z_copy(k).wait_recv()
+                keep_late(k, k // 2, total + z_in[k].astype(f32))
+
+        @pl.when((k >= 6) & (k < CHUNKS) & (column == 0) & (z > 0))
+        def _():
+            total = term_of(k)
+
+            @pl.when(z == 3)
+            def _():
+                z_out[k] = total.astype(bf16)
+                z_copy(k).start()
+
+            @pl.when(z == 2)
+            def _():
+                z_copy(k).wait_recv()
+                z_out[k] = (total + z_in[k].astype(f32)).astype(bf16)
+                z_copy(k).start()
+
+            @pl.when(z == 1)
+            def _():
+                z_copy(k).wait_recv()
+                up_copy(k).wait_recv()
+                keep_late(k, k // 2 - 3, total + z_in[k].astype(f32) + up_in[k - 6].astype(f32))
+
+        @pl.when((i >= 8) & (i < 12) & (column == 0) & (z == 0))
+        def _():
+            z_out[i - 2] = term_of(i - 2).astype(bf16)
+            up_copy(i - 2).start()
+
+    @pl.when(i == 2 * half + 1)
+    def _():
+        sum_copy().wait_recv()
+        total = sums[...] + core_sums[...]
+        if small:
+            wide = D // 8
+            for d in range(8):
+                v_out[d, :, 0:wide] = total[:, d * wide : (d + 1) * wide]
+                v_out[d, :, wide:] = jnp.zeros((16, 128 - wide), f32)
+            for n in range(7):
+                v_copy(n).start()
+        else:
+            vec_sum[...] = total
+
+    @pl.when(i == pl.num_programs(0) - 1)
+    def _():
+        for j in range(half):
+            core_copy(j).wait_send()
+        sum_copy().wait_send()
+        if small:
+            for peer in peers:
+                copy(v_out.at[0], v_in.at[peer], s_v.at[0], r_v.at[peer], {"dp": far_x}).wait_recv()
+            v_in[dp] = v_out[dp]
+            total = v_in[0]
+            for d in range(1, 8):
+                total = total + v_in[d]
+            vec_sum[...] = total
+            for n in range(7):
+                v_copy(n).wait_send()
+            for k in range(CHUNKS):
+                if k < 6:
+                    x_copy(k).wait_send()
+                    pl.when(z > 0)(z_copy(k).wait_send)
+                else:
+                    pl.when(column == 1)(x_copy(k).wait_send)
+                    pl.when((column == 0) & (z > 1))(z_copy(k).wait_send)
+                    pl.when((column == 0) & (z == 0))(up_copy(k).wait_send)
+
+
+def last(small, dq, dk, dv, cat, tokens, passes, vec, grad_second, sums_two, g_send, g_keep):
     seq = dq.shape[0]
-    count = seq // ROWS
-    where = lambda i, s: lax.rem(i + (1 - s[0]) * (count // 2), count)
-    row = lambda n: pl.BlockSpec((ROWS, n), lambda i, s: (where(i, s), 0))
-    send = pl.BlockSpec((ROWS, D), lambda i, s: (jnp.minimum(i, count // 2 - 1), 0))
-    keep = pl.BlockSpec((ROWS, D), lambda i, s: (jnp.maximum(i - count // 2, 0), 0))
-    half = jax.ShapeDtypeStruct((seq // 2, D), bf16)
+    half = seq // ROWS // 2
+    core = lambda: lax.axis_index("tensor") % 2
+
+    def block(i):
+        work = jnp.minimum(i, 2 * half - 1)
+        return lax.rem(work + (1 - core()) * half, 2 * half)
+
+    own = lambda i: jnp.clip(i - half, 0, half - 1)
+    row = pl.BlockSpec((ROWS, PAIR), lambda i: (block(i), 0))
+    mine = pl.BlockSpec((ROWS, D), lambda i: (own(i), 0))
+    dma = pltpu.SemaphoreType.DMA
+    out_specs = [mine]
+    out_shape = [jax.ShapeDtypeStruct((seq // 2, D), bf16)]
+    scratch = [
+        pltpu.VMEM((half, ROWS, D), bf16),
+        pltpu.VMEM((half, ROWS, D), bf16),
+        pltpu.VMEM((16, D), f32),
+        pltpu.VMEM((16, D), f32),
+    ]
+    sems = [dma((half,)), dma((half,)), dma, dma]
+    if small:
+        out_specs += [full((3, SIDE, PAIR)), full((16, 128))]
+        out_shape += [
+            jax.ShapeDtypeStruct((3, SIDE, PAIR), f32),
+            jax.ShapeDtypeStruct((16, 128), f32),
+        ]
+        scratch += [pltpu.VMEM((CHUNKS, CHUNK, PAIR), bf16)] * 3
+        scratch += [pltpu.VMEM((4, CHUNK, PAIR), bf16)]
+        scratch += [pltpu.VMEM((8, 16, 128), f32)] * 2
+        sems += [dma((CHUNKS,))] * 4 + [dma((4,))] * 2 + [dma((7,)), dma((8,))]
+    else:
+        out_specs += [full((16, D))]
+        out_shape += [jax.ShapeDtypeStruct((16, D), f32)]
     return pl.pallas_call(
-        project_back_kernel,
-        grid_spec=pltpu.PrefetchScalarGridSpec(
-            num_scalar_prefetch=1,
-            grid=(count,),
-            in_specs=[row(PAIR), row(PAIR), row(PAIR), full(cat.shape)],
-            out_specs=[send, keep],
-        ),
-        out_shape=[half, half],
-        compiler_params=params(),
-        cost_estimate=cost(8),
-        name="project_back",
-    )(place, dq, dk, dv, cat)
-
-
-def first_back_kernel(place, tok, pas, vec, one, two, grad_second, low, sums):
-    @pl.when(pl.program_id(0) == 0)
-    def _():
-        sums[...] = jnp.zeros_like(sums)
-
-    grad = one[...].astype(f32) + two[...].astype(f32)
-    hat, root = hat_of(embedded(tok[...], pas[...], vec[...]))
-    result = grad_second[...] + norm_back(hat, root, grad, vec[PASSES : PASSES + 1])
-    low[...] = result.astype(bf16)
-    chosen = one_hot(pas[...])
-    high, mid, rest = split_three(result)
-    sums[...] += nn(chosen, high) + nn(chosen, mid) + nn(chosen, rest)
-    sums[PASSES : PASSES + 1] += jnp.sum(grad * hat, axis=0, keepdims=True)
-    sums[PASSES + 1 : PASSES + 2] += jnp.sum(grad, axis=0, keepdims=True)
-
-
-def first_back(place, tokens, passes, vec, one, two, grad_second):
-    rows = one.shape[0]
-    count = rows // ROWS
-    row = pl.BlockSpec((ROWS, D), lambda i, s: (i, 0))
-    mine = pl.BlockSpec((ROWS, D), lambda i, s: (i + s[0] * count, 0))
-    return pl.pallas_call(
-        first_back_kernel,
-        grid_spec=pltpu.PrefetchScalarGridSpec(
-            num_scalar_prefetch=1,
-            grid=(count,),
-            in_specs=[
-                mine,
-                pl.BlockSpec((1, ROWS), lambda i, s: (0, i + s[0] * count)),
-                full((16, D)),
-                row,
-                row,
-                row,
-            ],
-            out_specs=[row, full((16, D))],
-        ),
-        out_shape=[
-            jax.ShapeDtypeStruct((rows, D), bf16),
-            jax.ShapeDtypeStruct((16, D), f32),
+        functools.partial(last_kernel, small),
+        grid=(2 * half + 8 if small else 2 * half + 2,),
+        in_specs=[
+            row,
+            row,
+            row,
+            full(cat.shape),
+            pl.BlockSpec((ROWS, D), lambda i: (core() * half + own(i), 0)),
+            pl.BlockSpec((1, ROWS), lambda i: (0, core() * half + own(i))),
+            full((16, D)),
+            mine,
+            full((8, D)),
+            full(g_send.shape),
+            full(g_keep.shape),
         ],
-        compiler_params=params(),
-        cost_estimate=cost(9),
-        name="first_back",
-    )(place, tokens, passes, vec, one, two, grad_second)
+        out_specs=out_specs,
+        out_shape=out_shape,
+        scratch_shapes=scratch + sems,
+        compiler_params=params(collective_id=2, has_side_effects=True),
+        cost_estimate=cost(30),
+        name="last",
+    )(dq, dk, dv, cat, tokens, passes, vec, grad_second, sums_two, g_send, g_keep)
 
 
 def precondition(grad, weight, left, right, left_root, right_root):
@@ -874,33 +1062,9 @@
     return lax.ppermute(value, "tensor", [(t, t ^ bit) for t in range(NT)])
 
 
-def hop_x(value):
-    return lax.ppermute(value, "dp", [(d, d ^ 1) for d in range(8)])
-
-
 def hop_z(value, turn, ends):
     pairs = [(d, (d + 2 * turn) % 8) for d in range(8) if (d // 2 + turn) % 4 in ends]
     return lax.ppermute(value, "dp", pairs)
-
-
-def terms_by_turn(keep, near, z, ends):
-    both = (keep.astype(f32) + near.astype(f32)).astype(bf16)
-    terms = []
-    for turn in range(4):
-        at = jnp.clip((z + turn) % 4 - ends[0], 0, len(ends) - 1)
-        terms.append(lax.dynamic_index_in_dim(both, at, 0, keepdims=False))
-    return terms
-
-
-def hops_z(terms, ends):
-    return [hop_z(terms[turn], turn, ends) for turn in (1, 2, 3)]
-
-
-def total_of(terms, far):
-    total = terms[0].astype(f32)
-    for value in far:
-        total = total + value.astype(f32)
-    return total
 
 
 def tie(*values):
@@ -946,46 +1110,19 @@
     norm, q, k, v, cat = project(tokens, passes, vec, pairs)
     mine, lse = attend(lens, q, k, v)
     other = swap(mine, 1)
-    (
-        out_send,
-        out_keep,
-        second,
-        grad_second,
-        grad_mixed,
-        sums_two,
-        w12_send,
-        w12_keep,
-        o_send,
-        o_keep,
-    ) = feed(small, tokens, passes, vec, mine, other, cotangent, pairs, wo_other)
-    out_chip = (out_keep.astype(f32) + swap(out_send, 1).astype(f32)).astype(bf16)
+    out_chip, second, grad_second, grad_mixed, sums_two, o_send, o_keep, *ends = feed(
+        small, tokens, passes, vec, mine, other, cotangent, pairs, wo_other
+    )
     out_far = swap(out_chip, 2)
     if small:
-        by_z = lambda value: value.reshape(-1, 3, SIDE, PAIR)
-        w12_near = hop_x(by_z(w12_send))
-        o_near = hop_x(o_send)
-    out_chip, grad_mixed = tie(out_chip, grad_mixed)
+        far = [hop_z(ends[turn], turn, (1, 2, 3)) for turn in (1, 2, 3)]
     dq, dk, dv = attend_back(lens, q, k, v, mine, lse, grad_mixed)
-    out_far, dq = tie(out_far, dq)
+    g_send, g_keep = qkv_grads(place, norm, dq, dk, dv, o_send, o_keep)
     if small:
-        w12_near, o_near, dq = tie(w12_near, o_near, dq)
-        w12_terms = terms_by_turn(by_z(w12_keep), w12_near, z, (1, 2, 3))
-        o_terms = terms_by_turn(o_keep[None], o_near[None], z, (1,))
-        w12_terms, o_terms, dq = tie(w12_terms, o_terms, dq)
-        w12_far = hops_z(w12_terms, (1, 2, 3))
-        o_far = hops_z(o_terms, (1,))
-    qkv_send, qkv_keep = qkv_grads(place, norm, dq, dk, dv)
-    if small:
-        qkv_near = hop_x(by_z(qkv_send))
-        qkv_keep, dq = tie(qkv_keep, dq)
-    g1_send, g1_keep = project_back(place, dq, dk, dv, cat)
-    g1_near = swap(g1_send, 1)
-    if small:
-        qkv_near, g1_keep = tie(qkv_near, g1_keep)
-        qkv_terms = terms_by_turn(by_z(qkv_keep), qkv_near, z, (0,))
-        qkv_terms, g1_keep = tie(qkv_terms, g1_keep)
-        qkv_far = hops_z(qkv_terms, (0,))
-    low_half, sums_one = first_back(place, tokens, passes, vec, g1_keep, g1_near, grad_second)
+        *far, out_far, g_send = tie(*far, out_far, g_send)
+    low_half, *sums = last(
+        small, dq, dk, dv, cat, tokens, passes, vec, grad_second, sums_two, g_send, g_keep
+    )
     out_half = (second + (out_chip.astype(f32) + out_far.astype(f32))).astype(bf16)
 
     def join(half):
@@ -995,29 +1132,22 @@
         return jnp.concatenate([low, high], axis=0)
 
     output, input_grad = join(out_half), join(low_half)
-    vector_part = jnp.concatenate([sums_one[: PASSES + 2], sums_two[:2]], axis=0)
-    vector_part = vector_part + swap(vector_part, 1)
     if small:
-        o_far, w12_far, qkv_far, low_half = tie(o_far, w12_far, qkv_far, low_half)
-        owned = total_of(w12_terms, w12_far)
-        late = total_of(qkv_terms, qkv_far)
-        o_sum = total_of(o_terms, o_far)
-        o_sum = jnp.concatenate([o_sum, jnp.zeros((1, SIDE, PAIR), f32)], axis=0)
-        owned = jnp.where(z == 0, late, owned + jnp.where(dp == 2, o_sum, 0.0))
-        owned = from_pairs(owned)[None]
-        vector_part = vector_part + hop_x(vector_part)
-        vector_sum = vector_part
-        for turn in (1, 2, 3):
-            vector_sum = vector_sum + hop_z(vector_part, turn, (0, 1, 2, 3))
-        wide = vector_params.shape[1]
-        vector_grad = lax.dynamic_slice_in_dim(vector_sum, dp * wide, wide, 1)
+        late, vector_sum = sums
+        early = ends[0].astype(f32)
+        for value in far:
+            early = early + value.astype(f32)
+        owned = from_pairs(late + jnp.where(z == 0, 0.0, early))[None]
+        vector_grad = vector_sum[: PASSES + 4, : vector_params.shape[1]]
     else:
+        vector_part = sums[0][: PASSES + 4]
+        w12_send, w12_keep = ends
         up_down = jnp.stack(
             [w12_keep.reshape(3, 3, SIDE, PAIR), w12_send.reshape(3, 3, SIDE, PAIR)], axis=1
         )
         up_down = up_down.reshape(18, SIDE, PAIR)[2:]
         grad_blocks = from_pairs(
-            jnp.concatenate([qkv_keep, qkv_send, o_keep, up_down], axis=0)
+            jnp.concatenate([g_keep[:3], g_send[:3], o_keep, up_down], axis=0)
         ).astype(f32)
         spare = jnp.zeros((slots - total_blocks, SIDE, SIDE), f32)
         grad_blocks = jnp.concatenate([grad_blocks, spare], axis=0)[None]

time: 327 us -> 294 us (0.90)
  Pallas kernels: 211 us -> 254 us
  starting transfers between devices: 47.8 us -> 15.8 us
  waiting for transfers between devices: 30.4 us -> 2.11 us
  other arithmetic: 15.4 us -> 6.17 us
  local copies, waits for them, and re-layouts: 10.1 us -> 4.52 us
    ppermute x12 -> x3, waiting for transfers between devices: 24 us -> 0.01 us  [hop_z(): return lax.ppermute(value, 'dp', pairs)]
    ppermute x12 -> x3, starting transfers between devices: 35.4 us -> 14.1 us  [hop_z(): return lax.ppermute(value, 'dp', pairs)]
    pallas_call x1, Pallas kernels: 53.2 us -> 71.8 us  [feed(): pl.pallas_call(functools.partial(feed_kernel, small), grid=(3 * half + 1,...]
    pallas_call x2 -> x1, Pallas kernels: 21 us -> 35.5 us  [last(): pl.pallas_call(functools.partial(last_kernel, small), grid=(2 * half + 8...]
    ppermute x4 -> x0, starting transfers between devices: 9.68 us -> none  [hop_x(): return lax.ppermute(value, 'dp', [(d, d ^ 1) for d in range(8)])]
    pallas_call x1, Pallas kernels: 26 us -> 30.8 us  [attend(): pl.pallas_call(attend_kernel, grid_spec=pltpu.PrefetchScalarGridSpec(num_...]
    pallas_call x1, Pallas kernels: 31.3 us -> 35.7 us  [attend_back(): pl.pallas_call(attend_back_kernel, grid_spec=pltpu.PrefetchScalarGridSpec...]
    ppermute x8 -> x5, waiting for transfers between devices: 6.4 us -> 2.11 us  [swap(): return lax.ppermute(value, 'tensor', [(t, t ^ bit) for t in range(NT)])]
  transfers between devices with their start and end apart: 24 -> 8, of which waited for: 7 -> 1; matrix products, arithmetic and copies ran while one was open for 8% -> 5% of each run, Pallas kernels for 13% -> 16%
where the time goes in v4:
time: 294 us; the launch traced here: 293 us
  Pallas kernels  254 us (86%)
  starting transfers between devices  15.8 us (5%)
  matrix products  9.93 us (3%)
  other arithmetic  6.17 us (2%)
  local copies, waits for them, and re-layouts  4.52 us (2%)
    pallas_call x1, Pallas kernels, feed(): pl.pallas_call(functools.partial(feed_kernel, small), grid=(3 * half + 1,...  71.8 us
    pallas_call x1, Pallas kernels, gather(): pl.pallas_call(gather_kernel, in_specs=[pl.BlockSpec(memory_space=pltpu.V...  52.5 us
    pallas_call x1, Pallas kernels, attend_back(): pl.pallas_call(attend_back_kernel, grid_spec=pltpu.PrefetchScalarGridSpec...  35.7 us
    pallas_call x1, Pallas kernels, last(): pl.pallas_call(functools.partial(last_kernel, small), grid=(2 * half + 8...  35.5 us
    pallas_call x1, Pallas kernels, attend(): pl.pallas_call(attend_kernel, grid_spec=pltpu.PrefetchScalarGridSpec(num_...  30.8 us
    pallas_call x1, Pallas kernels, project(): pl.pallas_call(project_kernel, grid=(seq // ROWS,), in_specs=[row(D), pl....  16.1 us
    ppermute x3, starting transfers between devices, hop_z(): return lax.ppermute(value, 'dp', pairs)  14.1 us
    pallas_call x1, Pallas kernels, qkv_grads(): pl.pallas_call(qkv_grads_kernel, grid_spec=pltpu.PrefetchScalarGridSpec(n...  11.1 us
  transfers between devices with their start and end apart: 8, of which 1 were waited for; matrix products, arithmetic and copies ran while one was open for 5% of the time, Pallas kernels for 16%

profile of v4, /device:TPU:0, one launch (start us, length us, event | category | flops | bytes accessed | tf_op | source)
XLA Modules:
  0.0 293.1 jit_solution(16845163731888937387)
XLA Ops:
  0.6 0.0 copy-start
  0.7 52.5 %gather.1 = (bf16[2,24,192,384]{3,2,1,0:T(8,128)(2,1)}, f32[16,768]{1,0:T(8,128)}) custom-call(f32[1,6,192,192]{3,2,1,0:T(8,128)} %own.1, f32[9,96]{1,0:T(8,128)} %vec_own.1), custom_call_target="tpu_custom_call" | custom-call | tf_op jit(solution)/shard_map/gather/pallas_call | solution.py:229
  53.2 16.1 %project.1 = (bf16[2048,768]{1,0:T(8,128)(2,1)}, bf16[2048,384]{1,0:T(8,128)(2,1)}, bf16[2048,384]{1,0:T(8,128)(2,1)}, bf16[2048,384]{1,0:T(8,128)(2,1)}, bf16[3,768,384]{2,1,0:T(8,128)(2,1)}) custom-call(bf16[2048,768]{1,0:T(8,128)(2,1)} %tok.5, s32[1,2048]{1,0:T(1,128)} %bitcast.39, f32[16,768]{1,0:T(8,128)} %get-tuple-element.42.vec, ...), custom_call_target="tpu_custom_call" | custom-call | flops 17600000000 | bytes 16000000 | tf_op jit(solution)/shard_map/project/pallas_call | solution.py:270
  69.3 30.8 %attend.1 = (bf16[2048,384]{1,0:T(8,128)(2,1)}, f32[8,2048]{1,0:T(8,128)}) custom-call(s32[8]{0:T(128)} %bitcast.42, bf16[2048,384]{1,0:T(8,128)(2,1)} %get-tuple-element.44.q, bf16[2048,384]{1,0:T(8,128)(2,1)} %get-tuple-element.45.k, bf16[2048,384]{1,0:T(8,128)(2,1)} %get-tuple-element.46.v), custom_call_target="tpu_custom_call" | custom-call | flops 32999999488 | bytes 30000000 | tf_op jit(solution)/shard_map/attend/pallas_call | solution.py:354
  100.1 0.0 collective-permute-start
  100.2 1.1 slice.12
  101.3 0.6 collective-permute-start.1
  101.9 0.6 pad_add_fusion.place
  102.4 2.1 collective-permute-done.1.wo_other
  104.5 0.0 collective-permute-done.other
  104.5 1.1 copy-done.17
  105.7 71.8 %feed_forward.1 = (bf16[1024,768]{1,0:T(8,128)(2,1)}, f32[1024,768]{1,0:T(8,128)}, f32[1024,768]{1,0:T(8,128)}, bf16[2048,384]{1,0:T(8,128)(2,1)}, f32[8,768]{1,...) custom-call(bf16[2048,768]{1,0:T(8,128)(2,1)} %tok.5, ...), custom_call_target="tpu_custom_call" | custom-call | flops 54999998464 | bytes 50000000 | tf_op jit(solution)/shard_map/feed_forward/pallas_call | solution.py:690
  177.5 3.0 %collective-permute-start.2 = (bf16[3,192,384]{2,1,0:T(8,128)(2,1)}, bf16[3,192,384]{2,1,0:T(8,128)(2,1)S(1)}, u32[]{:S(2)}, u32[]{:S(2)}) collective-permute-start(bf16[3,192,384]{2,1,0:T(8,128)(2,1)} %get-tuple-element.50), channel_id=1, source_target_pairs={{0,8},{4,12},{8,16},{12,20},{16,24},{20,28},{1,9},{5,13},{9,17},{1... | collective-permute-start | bytes 1327112 | tf_op jit(solution)/shard_map/ppermute | solution.py:1067
  180.6 9.6 %collective-permute-start.3 = (bf16[3,192,384]{2,1,0:T(8,128)(2,1)}, bf16[3,192,384]{2,1,0:T(8,128)(2,1)S(1)}, u32[]{:S(2)}, u32[]{:S(2)}) collective-permute-start(bf16[3,192,384]{2,1,0:T(8,128)(2,1)} %get-tuple-element.51), channel_id=1, source_target_pairs={{0,16},{4,20},{8,24},{12,28},{24,8},{28,12},{1,17},{5,21},{9,25},{... | collective-permute-start | bytes 1327112 | tf_op jit(solution)/shard_map/ppermute | solution.py:1067
  190.2 1.4 collective-permute-start.4
  191.6 0.6 collective-permute-start.5
  192.2 35.7 %attend_back.1 = (bf16[2048,384]{1,0:T(8,128)(2,1)}, bf16[2048,384]{1,0:T(8,128)(2,1)}, bf16[2048,384]{1,0:T(8,128)(2,1)}) custom-call(s32[8]{0:T(128)} %bitcast.43, bf16[2048,384]{1,0:T(8,128)(2,1)} %get-tuple-element.44.q, bf16[2048,384]{1,0:T(8,128)(2,1)} %get-tuple-element.45.k, bf16[2048,384]{1,0:T(8,128)(2,1)} %get-tuple-element.46.v, ...), custom_call_target="tpu_custom_call" | custom-call | flops 44000002048 | bytes 40000000 | tf_op jit(solution)/shard_map/attend_back/pallas_call | solution.py:442
  227.9 11.1 %qkv_grads.1 = (bf16[5,192,384]{2,1,0:T(8,128)(2,1)}, bf16[5,192,384]{2,1,0:T(8,128)(2,1)}) custom-call(s32[3]{0:T(128)} %pad_add_fusion.place, bf16[2048,768]{1,0:T(8,128)(2,1)} %get-tuple-element.53.norm, bf16[2048,384]{1,0:T(8,128)(2,1)} %get-tuple-element.56.dq, bf16[2048,384]{1,0:T(8,128)(2,1)} %get-tuple-element.57.dk, ...), custom_call_target="tpu_custom_call" | custom-call | flops 8800000000 | bytes 8000000 | tf_op jit(solution)/shard_map/qkv_grads/pallas_call | solution.py:781
  239.0 0.0 collective-permute-done.2
  239.0 0.0 collective-permute-done.3
  239.0 0.0 copy-start.10
  239.0 0.0 collective-permute-done.4
  239.0 0.0 copy-start.12
  239.0 0.0 collective-permute-done.5
  239.0 0.7 copy-done.10
  239.7 0.1 copy-done.12
  239.9 35.5 %last.1 = (bf16[1024,768]{1,0:T(8,128)(2,1)}, f32[3,192,384]{2,1,0:T(8,128)}, f32[16,128]{1,0:T(8,128)}) custom-call(bf16[2048,384]{1,0:T(8,128)(2,1)} %get-tuple-element.56.dq, bf16[2048,384]{1,0:T(8,128)(2,1)} %get-tuple-element.57.dk, bf16[2048,384]{1,0:T(8,128)(2,1)} %get-tuple-element.58.dv, bf16[3,768,384]{2,1,0:T(8,128)(2,1)} %get-tuple-element.63.cat, ...), custom_call_target="tpu_custom_call" | custom-call | flops 32999999488 | bytes 30000000 | tf_op jit(solution)/shard_map/last/pallas_call | solution.py:1013
  275.4 0.1 collective-permute-start.7
  275.5 0.0 copy-done.2
  275.5 0.0 copy-done.4
  275.5 0.0 copy-start.8
  275.5 0.0 copy-start.9
  275.6 0.0 copy-start.11
  275.6 0.0 copy-start.13
  275.6 0.5 add_convert_fusion
  276.1 0.5 collective-permute-start.6
  276.6 0.1 copy-done.8
  276.7 0.1 copy-done.9
  276.8 0.1 copy-done.11
  276.9 0.1 copy-done.13
  277.1 0.3 select_add_fusion
  277.3 0.2 fusion.10
  277.6 0.0 copy-start.14
  277.6 0.0 copy-start.15
  277.6 0.0 copy-start.16
  277.6 0.0 copy-start.5
  277.6 0.1 pad_maximum_fusion.2
  277.7 0.6 copy-done.14
  278.3 0.0 copy-done.15
  278.3 0.0 copy-done.16
  278.3 0.6 divide_subtract_fusion
  278.9 1.3 fusion.6
  280.3 0.0 copy-done.6
  280.3 0.0 copy-start.7
  280.3 2.3 fusion.1
  282.7 3.5 %fusion.3 = f32[1,6,192,192]{3,2,1,0:T(8,128)} fusion(f32[1,6,192,192]{3,2,1,0:T(8,128)S(1)} %copy-done.7, f32[6,192,192]{2,1,0:T(8,128)S(1)} %bitcast.37), kind=kOutput, calls=%fused_computation.12 | convolution fusion | flops 510050304 | bytes 2654208 | tf_op jit(solution)/shard_map/...ji,...jk->...ik/dot_general | solution.py:1043
  286.1 0.0 copy-done
  286.1 2.8 bitcast_subtract_fusion
  288.9 0.0 collective-permute-done.7
  288.9 0.0 collective-permute-done.6
  288.9 0.0 copy-done.3
  288.9 0.4 broadcast_select_fusion.1
  289.3 1.9 pad_maximum_fusion
  291.2 1.9 pad_maximum_fusion.1
  (9 shorter events, 0.0 us)
Async XLA Ops:
  0.6 285.5 %copy-start = (f32[1,6,192,192]{3,2,1,0:T(8,128)S(1)}, f32[1,6,192,192]{3,2,1,0:T(8,128)}, u32[]{:S(2)}) copy-start(f32[1,6,192,192]{3,2,1,0:T(8,128)} %param.21) | copy-start | bytes 2654212
  100.1 4.4 %collective-permute-start = (bf16[2048,384]{1,0:T(8,128)(2,1)}, bf16[2048,384]{1,0:T(8,128)(2,1)S(1)}, u32[]{:S(2)}, u32[]{:S(2)}) collective-permute-start(bf16[2048,384]{1,0:T(8,128)(2,1)} %get-tuple-element.47.mine.mixed), channel_id=1, source_target_pairs={{0,1},{1,0},{2,3},{3,2},{4,5},{5,4},{6,7},{7,6},{8,9},{9,8},{10,11... | collective-permute-start | bytes 4718600 | tf_op jit(solution)/shard_map/ppermute | solution.py:1062
  101.3 3.3 %collective-permute-start.1 = (bf16[2,2,192,384]{3,2,1,0:T(8,128)(2,1)S(1)}, bf16[2,2,192,384]{3,2,1,0:T(8,128)(2,1)}, u32[]{:S(2)}, u32[]{:S(2)}) collective-permute-start(bf16[2,2,192,384]{3,2,1,0:T(8,128)(2,1)S(1)} %slice.12), channel_id=1, source_target_pairs={{0,1},{1,0},{2,3},{3,2},{4,5},{5,4},{6,7},{7,6},{8,9},{9,8},{10,11... | collective-permute-start | bytes 1769480 | tf_op jit(solution)/shard_map/ppermute | solution.py:1062
  104.5 1.1 copy-start.17
  177.5 61.5 %collective-permute-start.2 = (bf16[3,192,384]{2,1,0:T(8,128)(2,1)}, bf16[3,192,384]{2,1,0:T(8,128)(2,1)S(1)}, u32[]{:S(2)}, u32[]{:S(2)}) collective-permute-start(bf16[3,192,384]{2,1,0:T(8,128)(2,1)} %get-tuple-element.50), channel_id=1, source_target_pairs={{0,8},{4,12},{8,16},{12,20},{16,24},{20,28},{1,9},{5,13},{9,17},{1... | collective-permute-start | bytes 1327112 | tf_op jit(solution)/shard_map/ppermute | solution.py:1067
  180.6 58.4 %collective-permute-start.3 = (bf16[3,192,384]{2,1,0:T(8,128)(2,1)}, bf16[3,192,384]{2,1,0:T(8,128)(2,1)S(1)}, u32[]{:S(2)}, u32[]{:S(2)}) collective-permute-start(bf16[3,192,384]{2,1,0:T(8,128)(2,1)} %get-tuple-element.51), channel_id=1, source_target_pairs={{0,16},{4,20},{8,24},{12,28},{24,8},{28,12},{1,17},{5,21},{9,25},{... | collective-permute-start | bytes 1327112 | tf_op jit(solution)/shard_map/ppermute | solution.py:1067
  190.2 48.8 %collective-permute-start.4 = (bf16[3,192,384]{2,1,0:T(8,128)(2,1)}, bf16[3,192,384]{2,1,0:T(8,128)(2,1)S(1)}, u32[]{:S(2)}, u32[]{:S(2)}) collective-permute-start(bf16[3,192,384]{2,1,0:T(8,128)(2,1)} %get-tuple-element.52), channel_id=1, source_target_pairs={{0,24},{4,28},{16,8},{20,12},{24,16},{28,20},{1,25},{5,29},{17,9},... | collective-permute-start | bytes 1327112 | tf_op jit(solution)/shard_map/ppermute | solution.py:1067
  191.6 47.4 %collective-permute-start.5 = (bf16[1024,768]{1,0:T(8,128)(2,1)}, bf16[1024,768]{1,0:T(8,128)(2,1)S(1)}, u32[]{:S(2)}, u32[]{:S(2)}) collective-permute-start(bf16[1024,768]{1,0:T(8,128)(2,1)} %get-tuple-element.49), channel_id=1, source_target_pairs={{0,2},{1,3},{2,0},{3,1},{4,6},{5,7},{6,4},{7,5},{8,10},{9,11},{10,... | collective-permute-start | bytes 4718600 | tf_op jit(solution)/shard_map/ppermute | solution.py:1062
  239.0 0.8 copy-start.10
  239.0 0.9 copy-start.12
  239.9 35.6 %copy-start.2 = (f32[1024,768]{1,0:T(8,128)S(1)}, f32[1024,768]{1,0:T(8,128)}, u32[]{:S(2)}) copy-start(f32[1024,768]{1,0:T(8,128)} %get-tuple-element.48) | copy-start | bytes 9437188
  239.9 35.6 %copy-start.4 = (bf16[1024,768]{1,0:T(8,128)(2,1)S(1)}, bf16[1024,768]{1,0:T(8,128)(2,1)}, u32[]{:S(2)}) copy-start(bf16[1024,768]{1,0:T(8,128)(2,1)} %get-tuple-element.49) | copy-start | bytes 4718596
  275.4 13.5 %collective-permute-start.7 = (bf16[1024,768]{1,0:T(8,128)(2,1)}, bf16[1024,768]{1,0:T(8,128)(2,1)S(1)}, u32[]{:S(2)}, u32[]{:S(2)}) collective-permute-start(bf16[1024,768]{1,0:T(8,128)(2,1)} %get-tuple-element.68), channel_id=1, source_target_pairs={{0,1},{1,0},{2,3},{3,2},{4,5},{5,4},{6,7},{7,6},{8,9},{9,8},{10,11... | collective-permute-start | bytes 4718600 | tf_op jit(solution)/shard_map/ppermute | solution.py:1062
  275.5 1.2 copy-start.8
  275.5 1.3 copy-start.9
  275.6 1.4 copy-start.11
  275.6 1.5 copy-start.13
  276.1 12.8 %collective-permute-start.6 = (bf16[1024,768]{1,0:T(8,128)(2,1)S(1)}, bf16[1024,768]{1,0:T(8,128)(2,1)S(1)}, u32[]{:S(2)}, u32[]{:S(2)}) collective-permute-start(bf16[1024,768]{1,0:T(8,128)(2,1)S(1)} %add_convert_fusion), channel_id=1, source_target_pairs={{0,1},{1,0},{2,3},{3,2},{4,5},{5,4},{6,7},{7,6},{8,9},{9,8},{10,11... | collective-permute-start | bytes 4718600 | tf_op jit(solution)/shard_map/ppermute | solution.py:1062
  277.6 0.7 copy-start.14
  277.6 0.7 copy-start.15
  277.6 0.7 copy-start.16
  277.6 1.3 copy-start.5
  278.9 1.3 copy-start.6
  280.3 2.4 copy-start.7
  282.6 3.5 %copy-start.1 = (f32[1,6,192,192]{3,2,1,0:T(8,128)S(1)}, f32[1,6,192,192]{3,2,1,0:T(8,128)}, u32[]{:S(2)}) copy-start(f32[1,6,192,192]{3,2,1,0:T(8,128)} %own.1) | copy-start | bytes 2654212
  286.1 2.8 copy-start.3

commit v5 on v4

--- a/solution.py
+++ b/solution.py
@@ -14,6 +14,7 @@
 SIDE = 192
 PAIR = 2 * SIDE
 ROWS = 256
+WIDE = 512
 DOCS = 8
 NT = 4
 
@@ -55,9 +56,8 @@
 
 
 def embedded(tokens, pass_row, vec):
-    chosen = one_hot(pass_row)
-    high, mid, low = split_three(vec)
-    return tokens.astype(f32) + (tn(chosen, high) + tn(chosen, mid) + tn(chosen, low))
+    chosen = jnp.concatenate([one_hot(pass_row)] * 3, axis=0)
+    return tokens.astype(f32) + tn(chosen, jnp.concatenate(split_three(vec), axis=0))
 
 
 def hat_of(hidden):
@@ -265,14 +265,14 @@
 
 def project(tokens, passes, vec, wq):
     seq = tokens.shape[0]
-    row = lambda n: pl.BlockSpec((ROWS, n), lambda i: (i, 0))
+    row = lambda n: pl.BlockSpec((WIDE, n), lambda i: (i, 0))
     wide = jax.ShapeDtypeStruct((seq, PAIR), bf16)
     return pl.pallas_call(
         project_kernel,
-        grid=(seq // ROWS,),
+        grid=(seq // WIDE,),
         in_specs=[
             row(D),
-            pl.BlockSpec((1, ROWS), lambda i: (0, i)),
+            pl.BlockSpec((1, WIDE), lambda i: (0, i)),
             full((16, D)),
             full((2, 6, SIDE, PAIR)),
         ],
@@ -313,37 +313,38 @@
     return jnp.concatenate([both[:HD, :ROWS], both[HD:, ROWS:]], axis=0).T
 
 
-def attend_kernel(lens, q, k, v, out, lse, top, total, acc):
+def attend_kernel(lens, q, k, v, out, lse, acc):
     i = pl.program_id(0)
     base = i * ROWS
     rows, starts, first = doc_state(lens, base)
     pairs = [two_heads(q[:, p * 128 : (p + 1) * 128] * bf16(0.125)) for p in range(3)]
     for p in range(3):
-        top[p] = jnp.full((1, 2 * ROWS), masked_score, f32)
-        total[p] = jnp.zeros((1, 2 * ROWS), f32)
         acc[p] = jnp.zeros((128, 2 * ROWS), f32)
 
     def step(j, carry):
         at = pl.multiple_of(j * ROWS, ROWS)
         keys = at + lax.broadcasted_iota(jnp.int32, (ROWS, 2 * ROWS), 0)
         seen = (keys >= starts) & (keys <= rows)
+        here = pl.ds(at, ROWS)
+        head = lambda p: slice(p * 128, (p + 1) * 128)
+        scores = [jnp.where(seen, nt(k[here, head(p)], pairs[p]), masked_score) for p in range(3)]
+        state = []
         for p in range(3):
-            cols = slice(p * 128, (p + 1) * 128)
-            scores = jnp.where(seen, nt(k[pl.ds(at, ROWS), cols], pairs[p]), masked_score)
-            before = top[p]
-            now = jnp.maximum(before, jnp.max(scores, axis=0, keepdims=True))
-            probs = jnp.exp(scores - now)
+            before, total = carry[2 * p], carry[2 * p + 1]
+            now = jnp.maximum(before, jnp.max(scores[p], axis=0, keepdims=True))
+            probs = jnp.exp(scores[p] - now)
             fade = jnp.exp(before - now)
-            top[p] = now
-            total[p] = total[p] * fade + jnp.sum(probs, axis=0, keepdims=True)
-            acc[p] = acc[p] * fade + tn(v[pl.ds(at, ROWS), cols], probs.astype(bf16))
-        return carry
-
-    lax.fori_loop(first // ROWS, i + 1, step, 0)
+            state += [now, total * fade + jnp.sum(probs, axis=0, keepdims=True)]
+            acc[p] = acc[p] * fade + tn(v[here, head(p)], probs.astype(bf16))
+        return tuple(state)
+
+    zero = jnp.zeros((1, 2 * ROWS), f32)
+    state = lax.fori_loop(first // ROWS, i + 1, step, (zero + masked_score, zero) * 3)
     lines = []
     for p in range(3):
-        out[:, p * 128 : (p + 1) * 128] = one_above(acc[p] / total[p]).astype(bf16)
-        line = top[p] + jnp.log(total[p])
+        top, total = state[2 * p], state[2 * p + 1]
+        out[:, p * 128 : (p + 1) * 128] = one_above(acc[p] / total).astype(bf16)
+        line = top + jnp.log(total)
         lines += [line[:, :ROWS], line[:, ROWS:]]
     lse[...] = jnp.concatenate(lines + lines[:2], axis=0)
 
@@ -359,8 +360,6 @@
             in_specs=[row, full((seq, PAIR)), full((seq, PAIR))],
             out_specs=[row, pl.BlockSpec((8, ROWS), lambda i, s: (0, i))],
             scratch_shapes=[
-                pltpu.VMEM((3, 1, 2 * ROWS), f32),
-                pltpu.VMEM((3, 1, 2 * ROWS), f32),
                 pltpu.VMEM((3, 128, 2 * ROWS), f32),
             ],
         ),
@@ -389,20 +388,15 @@
     rows, starts, first = doc_state(lens, base)
     heads = lax.broadcasted_iota(jnp.int32, (8, 128), 0)
     lanes = lax.broadcasted_iota(jnp.int32, (8, 128), 1)
-    pick = (lanes // HD == heads).astype(f32)
+    pick = (lanes // HD == heads).astype(f32).astype(bf16)
     queries, grads, inner, lines = [], [], [], []
     for p in range(3):
         cols = slice(p * 128, (p + 1) * 128)
         queries.append(two_heads(q[:, cols] * bf16(0.125)))
         grads.append(two_heads(grad_mixed[:, cols]))
         product = grad_mixed[:, cols].astype(f32) * mixed[:, cols].astype(f32)
-        sums = lax.dot_general(
-            pick,
-            product,
-            (((1,), (1,)), ((), ())),
-            precision=lax.Precision.HIGHEST,
-            preferred_element_type=f32,
-        )
+        high, low, _ = split_three(product)
+        sums = nt(pick, high) + nt(pick, low)
         inner.append(jnp.concatenate([sums[0:1], sums[1:2]], axis=1))
         lines.append(jnp.concatenate([lse[2 * p : 2 * p + 1], lse[2 * p + 1 : 2 * p + 2]], axis=1))
         dq_acc[p] = jnp.zeros((128, 2 * ROWS), f32)
@@ -468,7 +462,7 @@
 
 def feed_kernel(
     small, tok, pas, vec, mine, other, cot, wo_mine, wo_other, w1, w2,
-    out_chip, second_keep, grad_second, grad_mixed, sums, o_send, o_keep, *rest,
+    out_chip, second_keep, grad_second, grad_mixed, sums, mid_send, mid_keep, *rest,
 ):
     results, rest = (rest[:4], rest[4:]) if small else (rest[:2], rest[2:])
     (
@@ -588,22 +582,18 @@
                     pair = at + 2 * r + m
                     slot, place = (pair // 6 - 1) * 3 + pair % 3, pair // 3 % 2
                     value = total[rows, cols].astype(bf16)
+                    kept, sent, n = (mid_keep, mid_send, slot) if slot < 3 else (g_keep, g_send, slot - 3)
 
                     @pl.when(column == place)
                     def _():
-                        g_keep[slot] = value
+                        kept[n] = value
 
                     @pl.when(column != place)
                     def _():
-                        g_send[slot] = value
+                        sent[n] = value
         if small:
-            for slot in range(9):
-                pl.when((column == 0) | (slot > 1))(x_copy(slot).start)
-        for slot in range(2):
-
-            @pl.when(column == 0)
-            def _():
-                g_keep[slot] = jnp.zeros((SIDE, PAIR), bf16)
+            for n in range(6):
+                x_copy(n).start()
 
     def through_out(grad, block):
         here = pl.ds(pl.multiple_of(block * ROWS, ROWS), ROWS)
@@ -636,29 +626,30 @@
         at = pl.multiple_of(side * SIDE, SIDE)
         for m in range(2):
             value = go[pl.ds(at, SIDE), m * PAIR : (m + 1) * PAIR].astype(bf16)
-            none = jnp.zeros_like(value)
-            o_keep[m] = jnp.where(column == 0, value, none)
-            o_send[m] = jnp.where(column == 0, none, value)
+
+            @pl.when(column == 0)
+            def _():
+                mid_keep[m] = value
+
+            @pl.when(column != 0)
+            def _():
+                mid_send[m] = value
+
         for j in range(half):
             core_copy(j).wait_send()
             oc_copy(j).wait_send()
             far_copy(j).wait_send()
             ga_copy(j).wait_send()
         if small:
-            for slot in range(9):
-                pl.when((column == 1) | (slot > 1))(x_copy(slot).wait_recv)
-                pl.when((column == 0) | (slot > 1))(x_copy(slot).wait_send)
-            for slot in range(9):
-                if slot > 1:
-                    value = (g_keep[slot].astype(f32) + g_in[slot].astype(f32)).astype(bf16)
-                else:
-                    other_term = jnp.where(column == 1, g_in[slot], jnp.zeros((SIDE, PAIR), bf16))
-                    value = (g_keep[slot].astype(f32) + other_term.astype(f32)).astype(bf16)
+            for n in range(6):
+                x_copy(n).wait_send()
+                x_copy(n).wait_recv()
+                value = (g_keep[n].astype(f32) + g_in[n].astype(f32)).astype(bf16)
                 for turn in range(4):
 
-                    @pl.when(z + turn == slot // 3 + 1 + 4 * (z + turn >= 4).astype(jnp.int32))
+                    @pl.when(lax.rem(z + turn, 4) == n // 3 + 2)
                     def _():
-                        results[turn][slot % 3] = value
+                        results[turn][n % 3] = value
         else:
             results[0][...] = g_send[...]
             results[1][...] = g_keep[...]
@@ -684,7 +675,7 @@
     last = pl.BlockSpec((ROWS, D), lambda i: (jnp.clip(i - 2 * half, 0, half - 1), 0))
     rows = lambda kind: jax.ShapeDtypeStruct((seq // 2, D), kind)
     gr = lambda n: jax.ShapeDtypeStruct((n, SIDE, PAIR), bf16)
-    ends = [(3, SIDE, PAIR)] * 4 if small else [(9, SIDE, PAIR)] * 2
+    ends = [(3, SIDE, PAIR)] * 4 if small else [(6, SIDE, PAIR)] * 2
     buffer = pltpu.VMEM((half, ROWS, D), bf16)
     dma = pltpu.SemaphoreType.DMA((half,))
     return pl.pallas_call(
@@ -708,8 +699,8 @@
             last,
             full((seq, PAIR)),
             full((8, D)),
-            full((2, SIDE, PAIR)),
-            full((2, SIDE, PAIR)),
+            full((3, SIDE, PAIR)),
+            full((3, SIDE, PAIR)),
         ]
         + [full(shape) for shape in ends],
         scratch_shapes=[
@@ -723,17 +714,17 @@
         ]
         + [buffer] * 8
         + [pltpu.VMEM((half, ROWS, D), f32)]
-        + [pltpu.VMEM((9, SIDE, PAIR), bf16)] * 3
+        + [pltpu.VMEM((6, SIDE, PAIR), bf16)] * 3
         + [dma] * 8
-        + [pltpu.SemaphoreType.DMA((9,))] * 2,
+        + [pltpu.SemaphoreType.DMA((6,))] * 2,
         out_shape=[
             rows(bf16),
             rows(f32),
             rows(f32),
             jax.ShapeDtypeStruct((seq, PAIR), bf16),
             jax.ShapeDtypeStruct((8, D), f32),
-            gr(2),
-            gr(2),
+            gr(3),
+            gr(3),
         ]
         + [jax.ShapeDtypeStruct(shape, bf16) for shape in ends],
         compiler_params=params(collective_id=1, has_side_effects=True),
@@ -742,28 +733,24 @@
     )(tokens, passes, vec, mine, other, cotangent, pairs, wo_other, pairs, pairs)
 
 
-def qkv_grads_kernel(place, norm, dq, dk, dv, o_send, o_keep, g_send, g_keep, acc):
+def qkv_grads_kernel(place, norm, dq, dk, dv, mid_send, mid_keep, g_send, g_keep, acc):
     i = pl.program_id(0)
 
     @pl.when(i == 0)
     def _():
         acc[...] = jnp.zeros_like(acc)
 
-    for x, grad in enumerate((dq, dk, dv)):
-        mine = jnp.where(place[1] == 0, grad[:, :SIDE].astype(f32), grad[:, SIDE:].astype(f32))
-        acc[x] += tn(norm[...], mine.astype(bf16))
+    mine = [jnp.where(place[1] == 0, grad[:, :SIDE], grad[:, SIDE:]) for grad in (dq, dk, dv)]
+    acc[...] += tn(jnp.concatenate(mine, axis=1), norm[...])
 
     @pl.when(i == pl.num_programs(0) - 1)
     def _():
-        for m in range(2):
-            g_send[3 + m] = o_send[m]
-            g_keep[3 + m] = o_keep[m]
+        for m in range(3):
+            g_send[3 + m] = mid_send[m]
+            g_keep[3 + m] = mid_keep[m]
         for x in range(3):
             for m in range(2):
-                at = 2 * m * SIDE
-                value = jnp.concatenate(
-                    [acc[x, at : at + SIDE], acc[x, at + SIDE : at + 2 * SIDE]], axis=1
-                ).astype(bf16)
+                value = acc[x * SIDE : (x + 1) * SIDE, m * PAIR : (m + 1) * PAIR].astype(bf16)
                 slot, column = (2 * x + m) % 3, (2 * x + m) // 3
 
                 @pl.when(place[2] == column)
@@ -775,27 +762,27 @@
                     g_send[slot] = value
 
 
-def qkv_grads(place, norm, dq, dk, dv, o_send, o_keep):
+def qkv_grads(place, norm, dq, dk, dv, mid_send, mid_keep):
     seq = norm.shape[0]
-    row = lambda n: pl.BlockSpec((ROWS, n), lambda i, s: (i, 0))
+    row = lambda n: pl.BlockSpec((WIDE, n), lambda i, s: (i, 0))
     return pl.pallas_call(
         qkv_grads_kernel,
         grid_spec=pltpu.PrefetchScalarGridSpec(
             num_scalar_prefetch=1,
-            grid=(seq // ROWS,),
-            in_specs=[row(D), row(PAIR), row(PAIR), row(PAIR)] + [full((2, SIDE, PAIR))] * 2,
-            out_specs=[full((5, SIDE, PAIR)), full((5, SIDE, PAIR))],
-            scratch_shapes=[pltpu.VMEM((3, D, SIDE), f32)],
+            grid=(seq // WIDE,),
+            in_specs=[row(D), row(PAIR), row(PAIR), row(PAIR)] + [full((3, SIDE, PAIR))] * 2,
+            out_specs=[full((6, SIDE, PAIR)), full((6, SIDE, PAIR))],
+            scratch_shapes=[pltpu.VMEM((3 * SIDE, D), f32)],
         ),
-        out_shape=[jax.ShapeDtypeStruct((5, SIDE, PAIR), bf16)] * 2,
+        out_shape=[jax.ShapeDtypeStruct((6, SIDE, PAIR), bf16)] * 2,
         compiler_params=params(),
         cost_estimate=cost(8),
         name="qkv_grads",
-    )(place, norm, dq, dk, dv, o_send, o_keep)
+    )(place, norm, dq, dk, dv, mid_send, mid_keep)
 
 
 CHUNK = SIDE // 2
-CHUNKS = 10
+CHUNKS = 12
 
 
 def last_kernel(small, dq, dk, dv, cat, tok, pas, vec, grad_second, sums_two, g_send, g_keep, low, *rest):
@@ -846,10 +833,7 @@
         pl.semaphore_wait(barrier, 8 if small else 1)
         if small:
             for k in range(CHUNKS):
-                if k < 6:
-                    x_copy(k).start()
-                else:
-                    pl.when(column == 1)(x_copy(k).start)
+                x_copy(k).start()
 
     @pl.when(i < 2 * half)
     def _():
@@ -869,8 +853,8 @@
             result = grad_second[...] + norm_back(hat, root, grad, vec[PASSES : PASSES + 1])
             low[...] = result.astype(bf16)
             chosen = one_hot(pas[...])
-            high, mid, tail = split_three(result)
-            sums[...] += nn(chosen, high) + nn(chosen, mid) + nn(chosen, tail)
+            high, mid, _ = split_three(result)
+            sums[...] += nn(chosen, high) + nn(chosen, mid)
             sums[PASSES : PASSES + 1] += jnp.sum(grad * hat, axis=0, keepdims=True)
             sums[PASSES + 1 : PASSES + 2] += jnp.sum(grad, axis=0, keepdims=True)
 
@@ -888,53 +872,37 @@
         def keep_late(k, pair, total):
             late[pair, pl.ds(pl.multiple_of((k % 2) * CHUNK, 16), CHUNK), :] = total
 
-        k = i - 2 - 2 * (3 - z)
-
-        @pl.when((k >= 0) & (k < 6))
+        k = i - 1 - (3 - z)
+
+        @pl.when((k >= 0) & (k < CHUNKS) & ((z > 0) | (k < 6)))
         def _():
             total = term_of(k)
 
-            @pl.when(z == 3)
-            def _():
-                z_out[k] = total.astype(bf16)
-                z_copy(k).start()
-
-            @pl.when((z == 1) | (z == 2))
+            @pl.when(z < 3)
             def _():
                 z_copy(k).wait_recv()
-                z_out[k] = (total + z_in[k].astype(f32)).astype(bf16)
+
+            below = jnp.where(z < 3, z_in[k].astype(f32), 0.0)
+            passed = total + below
+
+            @pl.when((z > 1) | ((z == 1) & (k < 6)))
+            def _():
+                z_out[k] = passed.astype(bf16)
                 z_copy(k).start()
 
             @pl.when(z == 0)
             def _():
-                z_copy(k).wait_recv()
-                keep_late(k, k // 2, total + z_in[k].astype(f32))
-
-        @pl.when((k >= 6) & (k < CHUNKS) & (column == 0) & (z > 0))
+                keep_late(k, k // 2, passed)
+
+            @pl.when((z == 1) & (k >= 6))
+            def _():
+                up_copy(k).wait_recv()
+                keep_late(k, k // 2 - 3, passed + up_in[k - 6].astype(f32))
+
+        @pl.when((i >= 7) & (i < 13) & (z == 0))
         def _():
-            total = term_of(k)
-
-            @pl.when(z == 3)
-            def _():
-                z_out[k] = total.astype(bf16)
-                z_copy(k).start()
-
-            @pl.when(z == 2)
-            def _():
-                z_copy(k).wait_recv()
-                z_out[k] = (total + z_in[k].astype(f32)).astype(bf16)
-                z_copy(k).start()
-
-            @pl.when(z == 1)
-            def _():
-                z_copy(k).wait_recv()
-                up_copy(k).wait_recv()
-                keep_late(k, k // 2 - 3, total + z_in[k].astype(f32) + up_in[k - 6].astype(f32))
-
-        @pl.when((i >= 8) & (i < 12) & (column == 0) & (z == 0))
-        def _():
-            z_out[i - 2] = term_of(i - 2).astype(bf16)
-            up_copy(i - 2).start()
+            z_out[i - 1] = term_of(i - 1).astype(bf16)
+            up_copy(i - 1).start()
 
     @pl.when(i == 2 * half + 1)
     def _():
@@ -966,13 +934,12 @@
             for n in range(7):
                 v_copy(n).wait_send()
             for k in range(CHUNKS):
+                x_copy(k).wait_send()
                 if k < 6:
-                    x_copy(k).wait_send()
                     pl.when(z > 0)(z_copy(k).wait_send)
                 else:
-                    pl.when(column == 1)(x_copy(k).wait_send)
-                    pl.when((column == 0) & (z > 1))(z_copy(k).wait_send)
-                    pl.when((column == 0) & (z == 0))(up_copy(k).wait_send)
+                    pl.when(z > 1)(z_copy(k).wait_send)
+                    pl.when(z == 0)(up_copy(k).wait_send)
 
 
 def last(small, dq, dk, dv, cat, tokens, passes, vec, grad_second, sums_two, g_send, g_keep):
@@ -1004,15 +971,15 @@
             jax.ShapeDtypeStruct((16, 128), f32),
         ]
         scratch += [pltpu.VMEM((CHUNKS, CHUNK, PAIR), bf16)] * 3
-        scratch += [pltpu.VMEM((4, CHUNK, PAIR), bf16)]
+        scratch += [pltpu.VMEM((6, CHUNK, PAIR), bf16)]
         scratch += [pltpu.VMEM((8, 16, 128), f32)] * 2
-        sems += [dma((CHUNKS,))] * 4 + [dma((4,))] * 2 + [dma((7,)), dma((8,))]
+        sems += [dma((CHUNKS,))] * 4 + [dma((6,))] * 2 + [dma((7,)), dma((8,))]
     else:
         out_specs += [full((16, D))]
         out_shape += [jax.ShapeDtypeStruct((16, D), f32)]
     return pl.pallas_call(
         functools.partial(last_kernel, small),
-        grid=(2 * half + 8 if small else 2 * half + 2,),
+        grid=(2 * half + 7 if small else 2 * half + 2,),
         in_specs=[
             row,
             row,
@@ -1048,6 +1015,48 @@
     return (left_new, right_new, step, weight - rate_matrix * step)
 
 
+def two_part(value):
+    high = value.astype(bf16)
+    return high, (value - high.astype(f32)).astype(bf16)
+
+
+def dot_three(dot, a, b):
+    return dot(a[0], b[0]) + (dot(a[0], b[1]) + dot(a[1], b[0]))
+
+
+def renew_kernel(place, late, own, one, two, three, weight, left, right, left_root, right_root, left_new, right_new, step, new):
+    early = own[0].astype(f32) + one[0].astype(f32) + two[0].astype(f32) + three[0].astype(f32)
+    z = place[3]
+    both = late[0] + jnp.where(z > 1, early, 0.0)
+    for n in range(2):
+        grad = both[:, n * SIDE : (n + 1) * SIDE]
+        grad = two_part(jnp.where(z == 0, grad.T, grad))
+        left_new[0, n] = decay * left[0, n] + (1.0 - decay) * dot_three(nt, grad, grad)
+        right_new[0, n] = decay * right[0, n] + (1.0 - decay) * dot_three(tn, grad, grad)
+        half = dot_three(nn, two_part(left_root[0, n]), grad)
+        value = dot_three(nn, two_part(half), two_part(right_root[0, n]))
+        step[0, n] = value
+        new[0, n] = weight[0, n] - rate_matrix * value
+
+
+def renew(place, late, own, far, weight, left, right, left_root, right_root):
+    pair = pl.BlockSpec((1, SIDE, PAIR), lambda i, s: (i, 0, 0))
+    slot = pl.BlockSpec((1, 2, SIDE, SIDE), lambda i, s: (0, i, 0, 0))
+    return pl.pallas_call(
+        renew_kernel,
+        grid_spec=pltpu.PrefetchScalarGridSpec(
+            num_scalar_prefetch=1,
+            grid=(3,),
+            in_specs=[pair] * 5 + [slot] * 5,
+            out_specs=[slot] * 4,
+        ),
+        out_shape=[jax.ShapeDtypeStruct(weight.shape, f32)] * 4,
+        compiler_params=params(),
+        cost_estimate=cost(5),
+        name="renew",
+    )(place, late, own, *far, weight, left, right, left_root, right_root)
+
+
 def to_pairs(blocks):
     n = blocks.shape[0] // 2
     return blocks.reshape(n, 2, SIDE, SIDE).transpose(0, 2, 1, 3).reshape(n, SIDE, PAIR)
@@ -1089,7 +1098,7 @@
     n_dp = lax.axis_size("dp")
     small = n_dp == 8
     z, column = (dp // 2, dp % 2) if small else (0, 0)
-    place = jnp.stack([core, side, jnp.asarray(column, jnp.int32)]).astype(jnp.int32)
+    place = jnp.stack([core, side, jnp.asarray(column), jnp.asarray(z)]).astype(jnp.int32)
     lens = doc_lengths[0]
     seq = tokens.shape[0]
     passes = pass_ids.reshape(1, seq)
@@ -1110,14 +1119,14 @@
     norm, q, k, v, cat = project(tokens, passes, vec, pairs)
     mine, lse = attend(lens, q, k, v)
     other = swap(mine, 1)
-    out_chip, second, grad_second, grad_mixed, sums_two, o_send, o_keep, *ends = feed(
+    out_chip, second, grad_second, grad_mixed, sums_two, mid_send, mid_keep, *ends = feed(
         small, tokens, passes, vec, mine, other, cotangent, pairs, wo_other
     )
     out_far = swap(out_chip, 2)
     if small:
-        far = [hop_z(ends[turn], turn, (1, 2, 3)) for turn in (1, 2, 3)]
+        far = [hop_z(ends[turn], turn, (2, 3)) for turn in (1, 2, 3)]
     dq, dk, dv = attend_back(lens, q, k, v, mine, lse, grad_mixed)
-    g_send, g_keep = qkv_grads(place, norm, dq, dk, dv, o_send, o_keep)
+    g_send, g_keep = qkv_grads(place, norm, dq, dk, dv, mid_send, mid_keep)
     if small:
         *far, out_far, g_send = tie(*far, out_far, g_send)
     low_half, *sums = last(
@@ -1134,28 +1143,29 @@
     output, input_grad = join(out_half), join(low_half)
     if small:
         late, vector_sum = sums
-        early = ends[0].astype(f32)
-        for value in far:
-            early = early + value.astype(f32)
-        owned = from_pairs(late + jnp.where(z == 0, 0.0, early))[None]
+        left_new, right_new, step, weight_new = renew(
+            place, late, ends[0], far, block_weights, block_left, block_right, block_left_root, block_right_root
+        )
         vector_grad = vector_sum[: PASSES + 4, : vector_params.shape[1]]
     else:
         vector_part = sums[0][: PASSES + 4]
-        w12_send, w12_keep = ends
-        up_down = jnp.stack(
-            [w12_keep.reshape(3, 3, SIDE, PAIR), w12_send.reshape(3, 3, SIDE, PAIR)], axis=1
+        send, keep = ends
+        rest = jnp.stack(
+            [
+                jnp.concatenate([mid_keep, keep]).reshape(3, 3, SIDE, PAIR),
+                jnp.concatenate([mid_send, send]).reshape(3, 3, SIDE, PAIR),
+            ],
+            axis=1,
         )
-        up_down = up_down.reshape(18, SIDE, PAIR)[2:]
-        grad_blocks = from_pairs(
-            jnp.concatenate([g_keep[:3], g_send[:3], o_keep, up_down], axis=0)
-        ).astype(f32)
-        spare = jnp.zeros((slots - total_blocks, SIDE, SIDE), f32)
-        grad_blocks = jnp.concatenate([grad_blocks, spare], axis=0)[None]
+        grad_qkv = from_pairs(jnp.concatenate([g_keep[:3], g_send[:3]], axis=0)).swapaxes(1, 2)
+        grad_rest = from_pairs(rest.reshape(18, SIDE, PAIR))
+        spare = jnp.zeros((slots - total_blocks, SIDE, SIDE), bf16)
+        grad_blocks = jnp.concatenate([grad_qkv, grad_rest, spare], axis=0)[None].astype(f32)
         owned = lax.psum_scatter(grad_blocks, "dp", scatter_dimension=1, tiled=True)
         vector_grad = lax.psum_scatter(vector_part, "dp", scatter_dimension=1, tiled=True)
-    left_new, right_new, step, weight_new = precondition(
-        owned, block_weights, block_left, block_right, block_left_root, block_right_root
-    )
+        left_new, right_new, step, weight_new = precondition(
+            owned, block_weights, block_left, block_right, block_left_root, block_right_root
+        )
     moment_new = decay * vector_moment + (1.0 - decay) * vector_grad * vector_grad
     vector_new = vector_params - rate_vector * vector_grad / (jnp.sqrt(moment_new) + moment_eps)
     return (

time: 294 us -> 270 us (0.918)
  Pallas kernels: 254 us -> 235 us
  matrix products: 9.93 us -> 0 us
  starting transfers between devices: 15.8 us -> 19.5 us
    pallas_call x1, Pallas kernels: 71.8 us -> 60.6 us  [feed(): pl.pallas_call(functools.partial(feed_kernel, small), grid=(3 * half + 1,...]
    dot_general x4 -> x0, matrix products: 9.93 us -> none  [the longest x1 3.49 us: precondition(): jnp.einsum('...ji,...jk->...ik', grad, grad, precision=high)]
    pallas_call x1, Pallas kernels: 30.8 us -> 21.2 us  [attend(): pl.pallas_call(attend_kernel, grid_spec=pltpu.PrefetchScalarGridSpec(num_...]
    pallas_call x2 -> x3, Pallas kernels: 51.7 us -> 60.9 us  [the longest x1 41.2 us: last(): pl.pallas_call(functools.partial(last_kernel, small), grid=(2 * half + 7...]
    pallas_call x1, Pallas kernels: 35.7 us -> 30.8 us  [attend_back(): pl.pallas_call(attend_back_kernel, grid_spec=pltpu.PrefetchScalarGridSpec...]
    ppermute x3, starting transfers between devices: 14.1 us -> 17.2 us  [hop_z(): return lax.ppermute(value, 'dp', pairs)]
  transfers between devices with their start and end apart: 8 -> 8, of which waited for: 1 -> 1; matrix products, arithmetic and copies ran while one was open for 5% -> 2% of each run, Pallas kernels for 16% -> 18%
where the time goes in v5:
time: 270 us
  Pallas kernels  235 us (87%)
  starting transfers between devices  19.5 us (7%)
  other arithmetic  8.66 us (3%)
  local copies, waits for them, and re-layouts  4.63 us (2%)
    pallas_call x1, Pallas kernels, feed(): pl.pallas_call(functools.partial(feed_kernel, small), grid=(3 * half + 1,...  60.6 us
    pallas_call x1, Pallas kernels, gather(): pl.pallas_call(gather_kernel, in_specs=[pl.BlockSpec(memory_space=pltpu.V...  52.4 us
    pallas_call x1, Pallas kernels, last(): pl.pallas_call(functools.partial(last_kernel, small), grid=(2 * half + 7...  41.2 us
    pallas_call x1, Pallas kernels, attend_back(): pl.pallas_call(attend_back_kernel, grid_spec=pltpu.PrefetchScalarGridSpec...  30.8 us
    pallas_call x1, Pallas kernels, attend(): pl.pallas_call(attend_kernel, grid_spec=pltpu.PrefetchScalarGridSpec(num_...  21.2 us
    ppermute x3, starting transfers between devices, hop_z(): return lax.ppermute(value, 'dp', pairs)  17.2 us
    pallas_call x1, Pallas kernels, project(): pl.pallas_call(project_kernel, grid=(seq // WIDE,), in_specs=[row(D), pl....  11.4 us
    pallas_call x1, Pallas kernels, qkv_grads(): pl.pallas_call(qkv_grads_kernel, grid_spec=pltpu.PrefetchScalarGridSpec(n...  8.68 us
  transfers between devices with their start and end apart: 8, of which 1 were waited for; matrix products, arithmetic and copies ran while one was open for 2% of the time, Pallas kernels for 18%

profile of v5, /device:TPU:0, one launch (start us, length us, event | category | flops | bytes accessed | tf_op | source)
XLA Modules:
  0.0 270.2 jit_solution(10165509749883953859)
XLA Ops:
  0.6 52.4 %gather.1 = (bf16[2,24,192,384]{3,2,1,0:T(8,128)(2,1)}, f32[16,768]{1,0:T(8,128)}) custom-call(f32[1,6,192,192]{3,2,1,0:T(8,128)} %weight.1, f32[9,96]{1,0:T(8,128)} %vec_own.1), custom_call_target="tpu_custom_call" | custom-call | tf_op jit(solution)/shard_map/gather/pallas_call | solution.py:229
  53.1 11.4 %project.1 = (bf16[2048,768]{1,0:T(8,128)(2,1)}, bf16[2048,384]{1,0:T(8,128)(2,1)}, bf16[2048,384]{1,0:T(8,128)(2,1)}, bf16[2048,384]{1,0:T(8,128)(2,1)}, bf16[3,768,384]{2,1,0:T(8,128)(2,1)}) custom-call(bf16[2048,768]{1,0:T(8,128)(2,1)} %tok.5, s32[1,2048]{1,0:T(1,128)} %bitcast.6, f32[16,768]{1,0:T(8,128)} %get-tuple-element.46.vec, ...), custom_call_target="tpu_custom_call" | custom-call | flops 17600000000 | bytes 16000000 | tf_op jit(solution)/shard_map/project/pallas_call | solution.py:270
  64.4 21.2 %attend.1 = (bf16[2048,384]{1,0:T(8,128)(2,1)}, f32[8,2048]{1,0:T(8,128)}) custom-call(s32[8]{0:T(128)} %bitcast.9, bf16[2048,384]{1,0:T(8,128)(2,1)} %get-tuple-element.48.q, bf16[2048,384]{1,0:T(8,128)(2,1)} %get-tuple-element.49.k, bf16[2048,384]{1,0:T(8,128)(2,1)} %get-tuple-element.50.v), custom_call_target="tpu_custom_call" | custom-call | flops 32999999488 | bytes 30000000 | tf_op jit(solution)/shard_map/attend/pallas_call | solution.py:355
  85.6 0.0 collective-permute-start
  85.6 1.1 slice.6
  86.7 0.6 collective-permute-start.1
  87.3 0.6 pad_add_fusion.place
  87.9 2.0 collective-permute-done.1.wo_other
  89.8 0.0 copy-start.8
  89.9 0.0 collective-permute-done.other
  89.9 0.8 copy-done.8
  90.7 0.0 copy-start.7
  90.7 1.1 copy-done.7
  91.8 60.6 %feed_forward.1 = (bf16[1024,768]{1,0:T(8,128)(2,1)}, f32[1024,768]{1,0:T(8,128)}, f32[1024,768]{1,0:T(8,128)}, bf16[2048,384]{1,0:T(8,128)(2,1)}, f32[8,768]{1,...) custom-call(bf16[2048,768]{1,0:T(8,128)(2,1)} %tok.5, ...), custom_call_target="tpu_custom_call" | custom-call | flops 54999998464 | bytes 50000000 | tf_op jit(solution)/shard_map/feed_forward/pallas_call | solution.py:681
  152.5 0.7 collective-permute-start.2
  153.1 15.0 %collective-permute-start.3 = (bf16[3,192,384]{2,1,0:T(8,128)(2,1)}, bf16[3,192,384]{2,1,0:T(8,128)(2,1)S(1)}, u32[]{:S(2)}, u32[]{:S(2)}) collective-permute-start(bf16[3,192,384]{2,1,0:T(8,128)(2,1)} %get-tuple-element.55), channel_id=1, source_target_pairs={{0,16},{4,20},{8,24},{12,28},{1,17},{5,21},{9,25},{13,29},{2,18},{... | collective-permute-start | bytes 1327112 | tf_op jit(solution)/shard_map/ppermute | solution.py:1076
  168.2 1.5 collective-permute-start.4
  169.7 1.1 collective-permute-start.5
  170.8 30.8 %attend_back.1 = (bf16[2048,384]{1,0:T(8,128)(2,1)}, bf16[2048,384]{1,0:T(8,128)(2,1)}, bf16[2048,384]{1,0:T(8,128)(2,1)}) custom-call(s32[8]{0:T(128)} %bitcast.10, bf16[2048,384]{1,0:T(8,128)(2,1)} %get-tuple-element.48.q, bf16[2048,384]{1,0:T(8,128)(2,1)} %get-tuple-element.49.k, bf16[2048,384]{1,0:T(8,128)(2,1)} %get-tuple-element.50.v, ...), custom_call_target="tpu_custom_call" | custom-call | flops 44000002048 | bytes 40000000 | tf_op jit(solution)/shard_map/attend_back/pallas_call | solution.py:436
  201.6 8.7 %qkv_grads.1 = (bf16[6,192,384]{2,1,0:T(8,128)(2,1)}, bf16[6,192,384]{2,1,0:T(8,128)(2,1)}) custom-call(s32[4]{0:T(128)} %pad_add_fusion.place, bf16[2048,768]{1,0:T(8,128)(2,1)} %get-tuple-element.57.norm, bf16[2048,384]{1,0:T(8,128)(2,1)} %get-tuple-element.60.dq, bf16[2048,384]{1,0:T(8,128)(2,1)} %get-tuple-element.61.dk, ...), custom_call_target="tpu_custom_call" | custom-call | flops 8800000000 | bytes 8000000 | tf_op jit(solution)/shard_map/qkv_grads/pallas_call | solution.py:768
  210.3 0.0 collective-permute-done.2.one
  210.3 0.0 copy-start.9
  210.3 0.0 collective-permute-done.3.two
  210.3 0.0 copy-start.10
  210.3 0.0 collective-permute-done.4.three
  210.3 0.0 copy-start.11
  210.3 0.0 collective-permute-done.5
  210.3 0.0 copy-start.3
  210.4 0.7 copy-done.9
  211.1 0.1 copy-done.10
  211.2 0.1 copy-done.11
  211.4 0.5 copy-done.3
  211.9 0.0 copy-start
  211.9 0.0 copy-start.2
  211.9 41.2 %last.1 = (bf16[1024,768]{1,0:T(8,128)(2,1)}, f32[3,192,384]{2,1,0:T(8,128)}, f32[16,128]{1,0:T(8,128)}) custom-call(bf16[2048,384]{1,0:T(8,128)(2,1)} %get-tuple-element.60.dq, bf16[2048,384]{1,0:T(8,128)(2,1)} %get-tuple-element.61.dk, bf16[2048,384]{1,0:T(8,128)(2,1)} %get-tuple-element.62.dv, bf16[3,768,384]{2,1,0:T(8,128)(2,1)} %get-tuple-element.67.cat, ...), custom_call_target="tpu_custom_call" | custom-call | flops 32999999488 | bytes 30000000 | tf_op jit(solution)/shard_map/last/pallas_call | solution.py:980
  253.0 0.1 collective-permute-start.7
  253.1 0.0 copy-done
  253.1 0.0 copy-done.2
  253.1 0.0 copy-start.4
  253.1 0.0 copy-start.5
  253.2 0.0 copy-start.6
  253.2 1.9 add_convert_fusion
  255.1 0.5 collective-permute-start.6
  255.6 0.0 copy-done.4
  255.6 0.0 copy-done.5
  255.6 0.0 copy-done.6
  255.6 0.6 divide_subtract_fusion
  256.2 0.0 copy-start.1
  256.3 8.4 %renew.1 = (f32[1,6,192,192]{3,2,1,0:T(8,128)}, f32[1,6,192,192]{3,2,1,0:T(8,128)}, f32[1,6,192,192]{3,2,1,0:T(8,128)}, f32[1,6,192,192]{3,2,1,0:T(8,128)}) custom-call(s32[4]{0:T(128)} %pad_add_fusion.place, f32[3,192,384]{2,1,0:T(8,128)} %get-tuple-element.73.late, bf16[3,192,384]{2,1,0:T(8,128)(2,1)} %get-tuple-element.74.own, ...), custom_call_target="tpu_custom_call" | custom-call | flops 5500000256 | bytes 5000000 | tf_op jit(solution)/shard_map/renew/pallas_call | solution.py:1045
  264.7 0.0 collective-permute-done.7
  264.7 0.0 collective-permute-done.6
  264.7 0.0 copy-done.1
  264.7 1.8 broadcast_select_fusion.1
  266.5 1.9 pad_maximum_fusion
  268.4 1.9 pad_maximum_fusion.1
Async XLA Ops:
  85.6 4.3 %collective-permute-start = (bf16[2048,384]{1,0:T(8,128)(2,1)}, bf16[2048,384]{1,0:T(8,128)(2,1)S(1)}, u32[]{:S(2)}, u32[]{:S(2)}) collective-permute-start(bf16[2048,384]{1,0:T(8,128)(2,1)} %get-tuple-element.51.mine.mixed), channel_id=1, source_target_pairs={{0,1},{1,0},{2,3},{3,2},{4,5},{5,4},{6,7},{7,6},{8,9},{9,8},{10,11... | collective-permute-start | bytes 4718600 | tf_op jit(solution)/shard_map/ppermute | solution.py:1071
  86.7 3.1 %collective-permute-start.1 = (bf16[2,2,192,384]{3,2,1,0:T(8,128)(2,1)S(1)}, bf16[2,2,192,384]{3,2,1,0:T(8,128)(2,1)S(1)}, u32[]{:S(2)}, u32[]{:S(2)}) collective-permute-start(bf16[2,2,192,384]{3,2,1,0:T(8,128)(2,1)S(1)} %slice.6), channel_id=1, source_target_pairs={{0,1},{1,0},{2,3},{3,2},{4,5},{5,4},{6,7},{7,6},{8,9},{9,8},{10,11... | collective-permute-start | bytes 1769480 | tf_op jit(solution)/shard_map/ppermute | solution.py:1071
  89.8 0.8 copy-start.8
  90.7 1.1 copy-start.7
  152.5 57.8 %collective-permute-start.2 = (bf16[3,192,384]{2,1,0:T(8,128)(2,1)}, bf16[3,192,384]{2,1,0:T(8,128)(2,1)S(1)}, u32[]{:S(2)}, u32[]{:S(2)}) collective-permute-start(bf16[3,192,384]{2,1,0:T(8,128)(2,1)} %get-tuple-element.54), channel_id=1, source_target_pairs={{8,16},{12,20},{16,24},{20,28},{9,17},{13,21},{17,25},{21,29},{10,... | collective-permute-start | bytes 1327112 | tf_op jit(solution)/shard_map/ppermute | solution.py:1076
  153.1 57.1 %collective-permute-start.3 = (bf16[3,192,384]{2,1,0:T(8,128)(2,1)}, bf16[3,192,384]{2,1,0:T(8,128)(2,1)S(1)}, u32[]{:S(2)}, u32[]{:S(2)}) collective-permute-start(bf16[3,192,384]{2,1,0:T(8,128)(2,1)} %get-tuple-element.55), channel_id=1, source_target_pairs={{0,16},{4,20},{8,24},{12,28},{1,17},{5,21},{9,25},{13,29},{2,18},{... | collective-permute-start | bytes 1327112 | tf_op jit(solution)/shard_map/ppermute | solution.py:1076
  168.2 42.2 %collective-permute-start.4 = (bf16[3,192,384]{2,1,0:T(8,128)(2,1)}, bf16[3,192,384]{2,1,0:T(8,128)(2,1)S(1)}, u32[]{:S(2)}, u32[]{:S(2)}) collective-permute-start(bf16[3,192,384]{2,1,0:T(8,128)(2,1)} %get-tuple-element.56), channel_id=1, source_target_pairs={{0,24},{4,28},{24,16},{28,20},{1,25},{5,29},{25,17},{29,21},{2,26}... | collective-permute-start | bytes 1327112 | tf_op jit(solution)/shard_map/ppermute | solution.py:1076
  169.7 40.7 %collective-permute-start.5 = (bf16[1024,768]{1,0:T(8,128)(2,1)}, bf16[1024,768]{1,0:T(8,128)(2,1)S(1)}, u32[]{:S(2)}, u32[]{:S(2)}) collective-permute-start(bf16[1024,768]{1,0:T(8,128)(2,1)} %get-tuple-element.53), channel_id=1, source_target_pairs={{0,2},{1,3},{2,0},{3,1},{4,6},{5,7},{6,4},{7,5},{8,10},{9,11},{10,... | collective-permute-start | bytes 4718600 | tf_op jit(solution)/shard_map/ppermute | solution.py:1071
  210.3 0.8 copy-start.9
  210.3 0.9 copy-start.10
  210.3 1.0 copy-start.11
  210.3 1.5 copy-start.3
  211.9 41.3 %copy-start = (f32[1024,768]{1,0:T(8,128)S(1)}, f32[1024,768]{1,0:T(8,128)}, u32[]{:S(2)}) copy-start(f32[1024,768]{1,0:T(8,128)} %get-tuple-element.52) | copy-start | bytes 9437188
  211.9 41.3 %copy-start.2 = (bf16[1024,768]{1,0:T(8,128)(2,1)S(1)}, bf16[1024,768]{1,0:T(8,128)(2,1)}, u32[]{:S(2)}) copy-start(bf16[1024,768]{1,0:T(8,128)(2,1)} %get-tuple-element.53) | copy-start | bytes 4718596
  253.0 11.6 %collective-permute-start.7 = (bf16[1024,768]{1,0:T(8,128)(2,1)}, bf16[1024,768]{1,0:T(8,128)(2,1)S(1)}, u32[]{:S(2)}, u32[]{:S(2)}) collective-permute-start(bf16[1024,768]{1,0:T(8,128)(2,1)} %get-tuple-element.72), channel_id=1, source_target_pairs={{0,1},{1,0},{2,3},{3,2},{4,5},{5,4},{6,7},{7,6},{8,9},{9,8},{10,11... | collective-permute-start | bytes 4718600 | tf_op jit(solution)/shard_map/ppermute | solution.py:1071
  253.1 2.5 copy-start.4
  253.1 2.5 copy-start.5
  253.2 2.5 copy-start.6
  255.1 9.6 %collective-permute-start.6 = (bf16[1024,768]{1,0:T(8,128)(2,1)S(1)}, bf16[1024,768]{1,0:T(8,128)(2,1)}, u32[]{:S(2)}, u32[]{:S(2)}) collective-permute-start(bf16[1024,768]{1,0:T(8,128)(2,1)S(1)} %add_convert_fusion), channel_id=1, source_target_pairs={{0,1},{1,0},{2,3},{3,2},{4,5},{5,4},{6,7},{7,6},{8,9},{9,8},{10,11... | collective-permute-start | bytes 4718600 | tf_op jit(solution)/shard_map/ppermute | solution.py:1071
  256.2 8.4 %copy-start.1 = (bf16[1024,768]{1,0:T(8,128)(2,1)S(1)}, bf16[1024,768]{1,0:T(8,128)(2,1)}, u32[]{:S(2)}) copy-start(bf16[1024,768]{1,0:T(8,128)(2,1)} %get-tuple-element.72) | copy-start | bytes 4718596

commit v6 on v5

--- a/solution.py
+++ b/solution.py
@@ -87,35 +87,46 @@
     return pl.BlockSpec(shape, lambda *_: (0,) * len(shape))
 
 
-def gather_kernel(own, vec_own, all_pairs, vec_out, pack, vec_pack, vec_land, *sems):
-    (s_z1, r_z1, s_x1, r_x1, s_y1, r_y1, s_d1, r_d1, s_l, r_l, s_r, r_r, s_x2, r_x2, s_y2, r_y2, s_v, r_v, loc) = sems
+def gather_kernel(
+    own, vec_own, tokens, passes,
+    all_pairs, wo_other, vec_out, norm, q, k_out, v, cat,
+    pack, vec_pack, vec_land, wq, tok, norm_s, qkv_s, cat_s, *sems,
+):
+    (
+        s_z1, r_z1, s_x1, r_x1, s_y1, r_y1, s_d1, r_d1, s_l, r_l, s_r, r_r, s_x2, r_x2, s_y2, r_y2, s_v, r_v, s_c, r_c,
+        s_out, s_cat, s_tok, loc,
+    ) = sems
     dp, t = lax.axis_index("dp"), lax.axis_index("tensor")
     z, x = dp // 2, dp % 2
     y, core = t // 2, t % 2
-    far_x, far_y = z * 2 + (1 - x), (1 - y) * 2 + core
+    far_x, far_y, near = z * 2 + (1 - x), (1 - y) * 2 + core, y * 2 + (1 - core)
 
     barrier = pltpu.get_barrier_semaphore()
-    peers = [lax.rem(dp + k, 8) for k in range(1, 8)]
+    peers = [lax.rem(dp + n, 8) for n in range(1, 8)]
     for peer in peers:
-        pl.semaphore_signal(barrier, inc=1, device_id={"dp": peer, "tensor": t}, device_id_type=MESH)
-    pl.semaphore_signal(barrier, inc=1, device_id={"dp": dp, "tensor": far_y}, device_id_type=MESH)
-
+        pl.semaphore_signal(barrier, inc=1, device_id={"dp": peer}, device_id_type=MESH)
+    for to in (far_y, near):
+        pl.semaphore_signal(barrier, inc=1, device_id={"tensor": to}, device_id_type=MESH)
+
+    tok_copy = pltpu.make_async_copy(tokens, tok, s_tok)
+    tok_copy.start()
     for m in range(3):
-        pack[m] = jnp.concatenate([own[0, 2 * m], own[0, 2 * m + 1]], axis=1).astype(bf16)
+        pair = jnp.concatenate([own[0, 2 * m], own[0, 2 * m + 1]], axis=1).astype(bf16)
+        pack[m] = pair
+
+        @pl.when(z == 0)
+        def _():
+            wq[y, 3 * x + m] = pair
+
     vec_pack[...] = jnp.zeros_like(vec_pack)
     vec_pack[0 : PASSES + 4, 0 : D // 8] = vec_own[...]
-    pl.semaphore_wait(barrier, 8)
+    pl.semaphore_wait(barrier, 9)
 
     started = []
 
-    def send(src, dst, s_sem, r_sem, dp_to, t_to, cond=None):
+    def send(src, dst, s_sem, r_sem, to, cond=None):
         copy = pltpu.make_async_remote_copy(
-            src_ref=src,
-            dst_ref=dst,
-            send_sem=s_sem,
-            recv_sem=r_sem,
-            device_id={"dp": dp_to, "tensor": t_to},
-            device_id_type=MESH,
+            src_ref=src, dst_ref=dst, send_sem=s_sem, recv_sem=r_sem, device_id=to, device_id_type=MESH
         )
         started.append((cond, copy))
         if cond is None:
@@ -125,84 +136,123 @@
 
     def arrived(dst, r_sem, cond=None):
         copy = pltpu.make_async_remote_copy(
-            src_ref=dst,
-            dst_ref=dst,
-            send_sem=loc,
-            recv_sem=r_sem,
-            device_id={"dp": far_x, "tensor": t},
-            device_id_type=MESH,
+            src_ref=dst, dst_ref=dst, send_sem=loc, recv_sem=r_sem, device_id={"dp": far_x}, device_id_type=MESH
         )
         if cond is None:
             copy.wait_recv()
         else:
             pl.when(cond)(copy.wait_recv)
 
+    to_x, to_y, to_left, to_right = {"dp": far_x}, {"tensor": far_y}, {"dp": dp - 2}, {"dp": dp + 2}
+    half = SIDE // 2
+
+    def piece(side, column, k):
+        return wq.at[side, 3 * column + k // 2, pl.ds((k % 2) * half, half)]
+
+    def at_z(d, m):
+        return all_pairs.at[y, 3 * dp + 6 * d + m]
+
     own_copy = pltpu.make_async_copy(pack, all_pairs.at[y, pl.ds(3 * dp, 3)], loc)
-    own_copy.start()
+    pl.when(z > 0)(own_copy.start)
 
     for m in range(3):
-        send(pack.at[m], all_pairs.at[y, 3 * dp + m], s_l.at[0, m], r_l.at[0, m], dp - 2, t, z > 0)
-    for k, peer in enumerate(peers):
-        send(vec_pack, vec_land.at[dp], s_v.at[k], r_v.at[dp], peer, t)
+        send(pack.at[m], at_z(0, m), s_l.at[0, m], r_l.at[0, m], to_left, z > 0)
+    for n, peer in enumerate(peers):
+        send(vec_pack, vec_land.at[dp], s_v.at[n], r_v.at[dp], {"dp": peer})
     for m in range(3):
-        send(pack.at[m], all_pairs.at[y, 3 * dp + m], s_x2.at[z, m], r_x2.at[z, m], far_x, t, z > m)
-    own_copy.wait()
-
-    half = SIDE // 2
-
-    def piece(side, column, k):
-        return all_pairs.at[side, 3 * column + k // 2, pl.ds((k % 2) * half, half)]
+        send(pack.at[m], at_z(0, m), s_x2.at[z, m], r_x2.at[z, m], to_x, z > m)
 
     def diagonal(k):
         arrived(piece(y, 1 - x, k), r_x1.at[k])
-        send(piece(y, 1 - x, k), piece(y, 1 - x, k), s_d1.at[k], r_d1.at[k], dp, far_y)
+        send(piece(y, 1 - x, k), piece(y, 1 - x, k), s_d1.at[k], r_d1.at[k], to_y)
 
     def from_right(d, m):
-        arrived(all_pairs.at[y, 3 * dp + 6 * d + m], r_l.at[d - 1, m], z + d < 4)
+        arrived(at_z(d, m), r_l.at[d - 1, m], z + d < 4)
         if d < 3:
-            ref = all_pairs.at[y, 3 * dp + 6 * d + m]
-            send(ref, ref, s_l.at[d, m], r_l.at[d, m], dp - 2, t, (z + d < 4) & (z > 0))
-
-    def right_along_x(d, m):
-        ref = all_pairs.at[y, 3 * dp + 6 * d + m]
-        send(ref, ref, s_x2.at[z + d, m], r_x2.at[z + d, m], far_x, t, z + d < 4)
+            send(at_z(d, m), at_z(d, m), s_l.at[d, m], r_l.at[d, m], to_left, (z + d < 4) & (z > 0))
+
+    def from_left(d, m):
+        arrived(at_z(-d, m), r_r.at[d - 1, m], z - d > 0)
+        if d == 1:
+            send(at_z(-d, m), at_z(-d, m), s_r.at[1, m], r_r.at[1, m], to_right, (z - d > 0) & (z < 3))
+
+    def along_x(d, m, cond):
+        send(at_z(d, m), at_z(d, m), s_x2.at[z + d, m], r_x2.at[z + d, m], to_x, cond)
 
     for k in range(6):
         arrived(piece(y, x, k), r_z1.at[k], z > 0)
-        send(piece(y, x, k), piece(y, x, k), s_z1.at[k], r_z1.at[k], dp + 2, t, z < 3)
-        send(piece(y, x, k), piece(y, x, k), s_x1.at[k], r_x1.at[k], far_x, t)
-        send(piece(y, x, k), piece(y, x, k), s_y1.at[k], r_y1.at[k], dp, far_y)
+        send(piece(y, x, k), piece(y, x, k), s_z1.at[k], r_z1.at[k], to_right, z < 3)
+        send(piece(y, x, k), piece(y, x, k), s_x1.at[k], r_x1.at[k], to_x)
+        send(piece(y, x, k), piece(y, x, k), s_y1.at[k], r_y1.at[k], to_y)
+        if k == 5:
+            for m in range(3):
+                send(pack.at[m], at_z(0, m), s_r.at[0, m], r_r.at[0, m], to_right, (z > 0) & (z < 3))
+                send(pack.at[m], at_z(0, m), s_x2.at[z, m], r_x2.at[z, m], to_x, (z > 0) & (z <= m))
         if k >= 1:
             diagonal(k - 1)
         if k % 2 == 1:
             from_right(1, k // 2)
     diagonal(5)
-
+    pl.when(z > 0)(own_copy.wait)
     for m in range(3):
-        send(pack.at[m], all_pairs.at[y, 3 * dp + m], s_x2.at[z, m], r_x2.at[z, m], far_x, t, (z > 0) & (z <= m))
+        along_x(1, m, z + 1 < 4)
     for m in range(3):
-        send(pack.at[m], all_pairs.at[y, 3 * dp + m], s_r.at[0, m], r_r.at[0, m], dp + 2, t, (z > 0) & (z < 3))
-    for m in range(3):
-        right_along_x(1, m)
-    for d in (2, 3):
-        for m in range(3):
-            from_right(d, m)
-            right_along_x(d, m)
-    for d in (1, 2):
-        for m in range(3):
-            ref = all_pairs.at[y, 3 * dp - 6 * d + m]
-            arrived(ref, r_r.at[d - 1, m], z - d > 0)
-            if d == 1:
-                send(ref, ref, s_r.at[1, m], r_r.at[1, m], dp + 2, t, (z - d > 0) & (z < 3))
-            send(ref, ref, s_x2.at[z - d, m], r_x2.at[z - d, m], far_x, t, z - d > 0)
-    for m in range(2):
-        ref = all_pairs.at[y, 6 + m]
-        arrived(ref, r_x2.at[1, m], x == 1)
-        send(ref, ref, s_y2.at[m], r_y2.at[m], dp, far_y)
-
+        from_right(2, m)
     for k in range(6):
         arrived(piece(1 - y, x, k), r_y1.at[k])
         arrived(piece(1 - y, 1 - x, k), r_d1.at[k])
+    for peer in peers:
+        arrived(vec_land.at[peer], r_v.at[peer])
+    vec_land[dp] = vec_pack[...]
+    vec = jnp.concatenate([vec_land[d][:, : D // 8] for d in range(8)], axis=1)
+    vec_out[...] = vec
+    for n in range(3):
+        for i in range(4):
+            at = (i % 2) * SIDE
+            parts = [wq[h, 2 * n + i // 2][:, at : at + SIDE] for h in range(2)]
+            cat_s[n, i * SIDE : (i + 1) * SIDE, :] = jnp.concatenate(parts, axis=1)
+    writes = [pltpu.make_async_copy(cat_s, cat, s_cat)]
+    writes[0].start()
+    tok_copy.wait()
+
+    def rows_of(b):
+        rows = slice(b * WIDE, (b + 1) * WIDE)
+        hat, _ = hat_of(embedded(tok[rows, :], passes[:, rows], vec))
+        low = (hat * vec[PASSES : PASSES + 1] + vec[PASSES + 1 : PASSES + 2]).astype(bf16)
+        norm_s[rows, :] = low
+        writes.append(pltpu.make_async_copy(norm_s.at[rows, :], norm.at[rows, :], s_out.at[b, 3]))
+        writes[-1].start()
+        for n, out in enumerate((q, k_out, v)):
+            qkv_s[n, rows, :] = nn(low, cat_s[n]).astype(bf16)
+            writes.append(pltpu.make_async_copy(qkv_s.at[n, rows, :], out.at[rows, :], s_out.at[b, n]))
+            writes[-1].start()
+
+    count = tok.shape[0] // WIDE
+    for b in range(count):
+        rows_of(b)
+        if b == 0:
+            for m in range(3):
+                from_left(1, m)
+                along_x(-1, m, z - 1 > 0)
+                along_x(2, m, z + 2 < 4)
+        if b == 1:
+            for m in range(3):
+                from_right(3, m)
+                along_x(3, m, z + 3 < 4)
+        if b == 2:
+            for m in range(3):
+                from_left(2, m)
+                along_x(-2, m, z - 2 > 0)
+        if b == 3:
+            for m in range(2):
+                ref = all_pairs.at[y, 6 + m]
+                arrived(ref, r_x2.at[1, m], x == 1)
+                send(ref, ref, s_y2.at[m], r_y2.at[m], to_y)
+                send(ref, wo_other.at[y, m], s_c.at[0, m], r_c.at[y, m], {"tensor": near})
+    for m in range(2):
+        ref = all_pairs.at[1 - y, 6 + m]
+        arrived(ref, r_y2.at[m])
+        send(ref, wo_other.at[1 - y, m], s_c.at[1, m], r_c.at[1 - y, m], {"tensor": near})
     for w in range(1, 4):
         for m in range(3):
             ref = all_pairs.at[y, 6 * w + 3 * (1 - x) + m]
@@ -210,12 +260,11 @@
                 arrived(ref, r_x2.at[w, m], x == 0)
             else:
                 arrived(ref, r_x2.at[w, m])
-    for m in range(2):
-        arrived(all_pairs.at[1 - y, 6 + m], r_y2.at[m])
-    for peer in peers:
-        arrived(vec_land.at[peer], r_v.at[peer])
-    vec_land[dp] = vec_pack[...]
-    vec_out[...] = jnp.concatenate([vec_land[d][:, : D // 8] for d in range(8)], axis=1)
+    for h in range(2):
+        for m in range(2):
+            arrived(wo_other.at[h, m], r_c.at[h, m])
+    for copy in writes:
+        copy.wait()
     for cond, copy in started:
         if cond is None:
             copy.wait_send()
@@ -223,27 +272,43 @@
             pl.when(cond)(copy.wait_send)
 
 
-def gather(block_weights, vector_params):
+def gather(block_weights, vector_params, tokens, passes):
+    seq = tokens.shape[0]
     dma = pltpu.SemaphoreType.DMA
-    sizes = [(6,)] * 8 + [(3, 3)] * 2 + [(2, 3)] * 2 + [(4, 3)] * 2 + [(2,)] * 2 + [(7,), (8,)]
+    sizes = [(6,)] * 8 + [(3, 3)] * 2 + [(2, 3)] * 2 + [(4, 3)] * 2 + [(2,)] * 2 + [(7,), (8,)] + [(2, 2)] * 2
+    sizes += [(seq // WIDE, 4)]
+    vmem, far = pl.BlockSpec(memory_space=pltpu.VMEM), pl.BlockSpec(memory_space=pl.ANY)
+    wide = jax.ShapeDtypeStruct((seq, PAIR), bf16)
     return pl.pallas_call(
         gather_kernel,
-        in_specs=[pl.BlockSpec(memory_space=pltpu.VMEM)] * 2,
-        out_specs=[pl.BlockSpec(memory_space=pl.ANY), pl.BlockSpec(memory_space=pltpu.VMEM)],
+        in_specs=[vmem, vmem, far, vmem],
+        out_specs=[far, far, vmem, far, far, far, far, far],
         out_shape=[
             jax.ShapeDtypeStruct((2, 24, SIDE, PAIR), bf16),
+            jax.ShapeDtypeStruct((2, 2, SIDE, PAIR), bf16),
             jax.ShapeDtypeStruct((16, D), f32),
+            jax.ShapeDtypeStruct((seq, D), bf16),
+            wide,
+            wide,
+            wide,
+            jax.ShapeDtypeStruct((3, D, PAIR), bf16),
         ],
         scratch_shapes=[
             pltpu.VMEM((3, SIDE, PAIR), bf16),
             pltpu.VMEM((16, 128), f32),
             pltpu.VMEM((8, 16, 128), f32),
+            pltpu.VMEM((2, 6, SIDE, PAIR), bf16),
+            pltpu.VMEM((seq, D), bf16),
+            pltpu.VMEM((seq, D), bf16),
+            pltpu.VMEM((3, seq, PAIR), bf16),
+            pltpu.VMEM((3, D, PAIR), bf16),
         ]
         + [dma(size) for size in sizes]
-        + [dma],
+        + [dma] * 3,
         compiler_params=params(collective_id=0, has_side_effects=True),
+        cost_estimate=cost(60),
         name="gather",
-    )(block_weights, vector_params)
+    )(block_weights, vector_params, tokens, passes)
 
 
 def project_kernel(tok, pas, vec, wq, norm, q, k, v, cat):
@@ -461,13 +526,13 @@
 
 
 def feed_kernel(
-    small, tok, pas, vec, mine, other, cot, wo_mine, wo_other, w1, w2,
+    small, tok, pas, vec, mine, cot, wo_mine, wo_other, w1, w2,
     out_chip, second_keep, grad_second, grad_mixed, sums, mid_send, mid_keep, *rest,
 ):
     results, rest = (rest[:4], rest[4:]) if small else (rest[:2], rest[2:])
     (
-        wom, woo, up, down, gup, gdown, go, core_out, core_in, far_out, far_in, ga_out, ga_in, oc_out, oc_in, seconds,
-        g_send, g_keep, g_in, s_core, r_core, s_far, r_far, s_ga, r_ga, s_oc, r_oc, s_x, r_x,
+        wo, other, up, down, gup, gdown, go, core_out, core_in, far_out, far_in, ga_out, ga_in, oc_out, oc_in,
+        g_send, g_keep, g_in, s_core, r_core, s_far, r_far, s_ga, r_ga, s_oc, r_oc, s_x, r_x, s_m, r_m,
     ) = rest
     step = pl.program_id(0)
     half = core_out.shape[0]
@@ -502,6 +567,17 @@
             device_id_type=MESH,
         )
 
+    def mixed_copy(block):
+        rows = pl.ds(pl.multiple_of(block * ROWS, ROWS), ROWS)
+        return pltpu.make_async_remote_copy(
+            src_ref=mine.at[rows],
+            dst_ref=other.at[rows],
+            send_sem=s_m.at[block],
+            recv_sem=r_m.at[block],
+            device_id={"tensor": near},
+            device_id_type=MESH,
+        )
+
     barrier = pltpu.get_barrier_semaphore()
 
     @pl.when(step == 0)
@@ -513,18 +589,21 @@
         for h in range(2):
             for m in range(2):
                 rows, cols = slice(h * SIDE, (h + 1) * SIDE), slice(m * PAIR, (m + 1) * PAIR)
-                wom[rows, cols] = wo_mine[h, m]
-                woo[rows, cols] = wo_other[h, m]
+                wo[rows, cols] = wo_mine[h, m]
+                wo[PAIR + h * SIDE : PAIR + (h + 1) * SIDE, cols] = wo_other[h, m]
         for r in range(4):
             for m in range(2):
                 rows, cols = slice(r * SIDE, (r + 1) * SIDE), slice(m * PAIR, (m + 1) * PAIR)
                 up[rows, cols] = w1[0, 2 * r + m]
                 down[rows, cols] = w2[0, 2 * r + m]
+        pl.semaphore_wait(barrier, 3 if small else 2)
+        for j in range(half):
+            mixed_copy(core * half + j).start()
+            mixed_copy((1 - core) * half + j).start()
         gup[...] = jnp.zeros_like(gup)
         gdown[...] = jnp.zeros_like(gdown)
         go[...] = jnp.zeros_like(go)
         sums[...] = jnp.zeros_like(sums)
-        pl.semaphore_wait(barrier, 3 if small else 2)
 
     @pl.when(step < 2 * half)
     def _():
@@ -532,7 +611,8 @@
         owner = jnp.where(step % 2 == 0, 1 - core, core)
         here = pl.ds(pl.multiple_of((owner * half + j) * ROWS, ROWS), ROWS)
         first = embedded(tok[...], pas[...], vec[...])
-        second = first + (nn(mine[here, :], wom[...]) + nn(other[...], woo[...]))
+        mixed_copy(owner * half + j).wait_recv()
+        second = first + nn(jnp.concatenate([mine[here, :], other[here, :]], axis=1), wo[...])
         hat, _ = hat_of(second)
         low = (hat * vec[PASSES + 2 : PASSES + 3] + vec[PASSES + 3 : PASSES + 4]).astype(bf16)
         upper = nn(low, up[...])
@@ -556,8 +636,7 @@
             core_copy(j).wait_recv()
             far_out[j] = (part + core_in[j].astype(f32)).astype(bf16)
             far_copy(j).start()
-            second_keep[...] = second
-            seconds[j] = second
+            second_keep[pl.ds(pl.multiple_of(j * ROWS, ROWS), ROWS), :] = second
 
         gup[...] += tn(low, grad_upper)
         gdown[...] += tn(act, cot[...])
@@ -597,13 +676,13 @@
 
     def through_out(grad, block):
         here = pl.ds(pl.multiple_of(block * ROWS, ROWS), ROWS)
-        grad_mixed[here, :] = nt(grad, wom[...]).astype(bf16)
+        grad_mixed[here, :] = nt(grad, wo[:PAIR, :]).astype(bf16)
         go[...] += tn(mine[here, :], grad)
 
     @pl.when((step >= 2 * half) & (step < 3 * half))
     def _():
         j = step - 2 * half
-        hat, root = hat_of(seconds[j])
+        hat, root = hat_of(second_keep[pl.ds(pl.multiple_of(j * ROWS, ROWS), ROWS), :])
         far_copy(j).wait_recv()
         grad = far_out[j].astype(f32) + far_in[j].astype(f32)
         result = cot[...].astype(f32) + norm_back(hat, root, grad, vec[PASSES + 2 : PASSES + 3])
@@ -638,6 +717,8 @@
         for j in range(half):
             core_copy(j).wait_send()
             oc_copy(j).wait_send()
+            mixed_copy(j).wait_send()
+            mixed_copy(half + j).wait_send()
             far_copy(j).wait_send()
             ga_copy(j).wait_send()
         if small:
@@ -655,7 +736,7 @@
             results[1][...] = g_keep[...]
 
 
-def feed(small, tokens, passes, vec, mine, other, cotangent, pairs, wo_other):
+def feed(small, tokens, passes, vec, mine, cotangent, pairs, wo_other):
     seq = tokens.shape[0]
     half = seq // ROWS // 2
 
@@ -686,7 +767,6 @@
             pl.BlockSpec((1, ROWS), lambda i: (0, block(i))),
             full((16, D)),
             full((seq, PAIR)),
-            row(PAIR),
             pl.BlockSpec((ROWS, D), lambda i: (cot_block(i), 0)),
             pl.BlockSpec((2, 2, SIDE, PAIR), lambda i: (0, 3, 0, 0)),
             full(wo_other.shape),
@@ -695,7 +775,7 @@
         ],
         out_specs=[
             keep,
-            keep,
+            full((seq // 2, D)),
             last,
             full((seq, PAIR)),
             full((8, D)),
@@ -704,8 +784,8 @@
         ]
         + [full(shape) for shape in ends],
         scratch_shapes=[
-            pltpu.VMEM((PAIR, D), bf16),
-            pltpu.VMEM((PAIR, D), bf16),
+            pltpu.VMEM((D, D), bf16),
+            pltpu.VMEM((seq, PAIR), bf16),
             pltpu.VMEM((D, D), bf16),
             pltpu.VMEM((D, D), bf16),
             pltpu.VMEM((D, D), f32),
@@ -713,10 +793,10 @@
             pltpu.VMEM((PAIR, D), f32),
         ]
         + [buffer] * 8
-        + [pltpu.VMEM((half, ROWS, D), f32)]
         + [pltpu.VMEM((6, SIDE, PAIR), bf16)] * 3
         + [dma] * 8
-        + [pltpu.SemaphoreType.DMA((6,))] * 2,
+        + [pltpu.SemaphoreType.DMA((6,))] * 2
+        + [pltpu.SemaphoreType.DMA((2 * half,))] * 2,
         out_shape=[
             rows(bf16),
             rows(f32),
@@ -730,7 +810,7 @@
         compiler_params=params(collective_id=1, has_side_effects=True),
         cost_estimate=cost(50),
         name="feed_forward",
-    )(tokens, passes, vec, mine, other, cotangent, pairs, wo_other, pairs, pairs)
+    )(tokens, passes, vec, mine, cotangent, pairs, wo_other, pairs, pairs)
 
 
 def qkv_grads_kernel(place, norm, dq, dk, dv, mid_send, mid_keep, g_send, g_keep, acc):
@@ -832,7 +912,7 @@
         sums[PASSES + 2 : PASSES + 4] = sums_two[0:2]
         pl.semaphore_wait(barrier, 8 if small else 1)
         if small:
-            for k in range(CHUNKS):
+            for k in range(6):
                 x_copy(k).start()
 
     @pl.when(i < 2 * half)
@@ -865,9 +945,17 @@
     if small:
 
         def term_of(k):
-            x_copy(k).wait_recv()
-            keep = g_keep[k // 2, pl.ds(pl.multiple_of((k % 2) * CHUNK, 16), CHUNK), :]
-            return keep.astype(f32) + x_in[k].astype(f32)
+            rows = pl.ds(pl.multiple_of((k % 2) * CHUNK, 16), CHUNK)
+
+            @pl.when(k < 6)
+            def _():
+                x_copy(k).wait_recv()
+
+            @pl.when(k >= 6)
+            def _():
+                x_in[k] = g_send[k // 2, rows, :]
+
+            return g_keep[k // 2, rows, :].astype(f32) + x_in[k].astype(f32)
 
         def keep_late(k, pair, total):
             late[pair, pl.ds(pl.multiple_of((k % 2) * CHUNK, 16), CHUNK), :] = total
@@ -934,8 +1022,8 @@
             for n in range(7):
                 v_copy(n).wait_send()
             for k in range(CHUNKS):
-                x_copy(k).wait_send()
                 if k < 6:
+                    x_copy(k).wait_send()
                     pl.when(z > 0)(z_copy(k).wait_send)
                 else:
                     pl.when(z > 1)(z_copy(k).wait_send)
@@ -973,7 +1061,7 @@
         scratch += [pltpu.VMEM((CHUNKS, CHUNK, PAIR), bf16)] * 3
         scratch += [pltpu.VMEM((6, CHUNK, PAIR), bf16)]
         scratch += [pltpu.VMEM((8, 16, 128), f32)] * 2
-        sems += [dma((CHUNKS,))] * 4 + [dma((6,))] * 2 + [dma((7,)), dma((8,))]
+        sems += [dma((6,))] * 2 + [dma((CHUNKS,))] * 2 + [dma((6,))] * 2 + [dma((7,)), dma((8,))]
     else:
         out_specs += [full((16, D))]
         out_shape += [jax.ShapeDtypeStruct((16, D), f32)]
@@ -1071,6 +1159,10 @@
     return lax.ppermute(value, "tensor", [(t, t ^ bit) for t in range(NT)])
 
 
+def hop_x(value):
+    return lax.ppermute(value, "dp", [(d, d ^ 1) for d in range(8)])
+
+
 def hop_z(value, turn, ends):
     pairs = [(d, (d + 2 * turn) % 8) for d in range(8) if (d // 2 + turn) % 4 in ends]
     return lax.ppermute(value, "dp", pairs)
@@ -1106,7 +1198,7 @@
     slots = block_weights.shape[1] * n_dp
 
     if small:
-        pairs, vec = gather(block_weights, vector_params)
+        pairs, wo_other, vec, norm, q, k, v, cat = gather(block_weights, vector_params, tokens, passes)
     else:
         every = lax.all_gather(block_weights.astype(bf16), "dp", axis=1, tiled=True)[0]
         near = to_pairs(every[:total_blocks])
@@ -1114,17 +1206,16 @@
         pairs = jnp.where(side == 0, jnp.stack([near, far]), jnp.stack([far, near]))
         vec = lax.all_gather(vector_params, "dp", axis=1, tiled=True)
         vec = jnp.pad(vec, ((0, 16 - vec.shape[0]), (0, 0)))
-    wo_other = swap(pairs[:, 6:8], 1)
-
-    norm, q, k, v, cat = project(tokens, passes, vec, pairs)
+        wo_other = swap(pairs[:, 6:8], 1)
+        norm, q, k, v, cat = project(tokens, passes, vec, pairs)
     mine, lse = attend(lens, q, k, v)
-    other = swap(mine, 1)
     out_chip, second, grad_second, grad_mixed, sums_two, mid_send, mid_keep, *ends = feed(
-        small, tokens, passes, vec, mine, other, cotangent, pairs, wo_other
+        small, tokens, passes, vec, mine, cotangent, pairs, wo_other
     )
     out_far = swap(out_chip, 2)
     if small:
         far = [hop_z(ends[turn], turn, (2, 3)) for turn in (1, 2, 3)]
+        mid_send = hop_x(mid_send)
     dq, dk, dv = attend_back(lens, q, k, v, mine, lse, grad_mixed)
     g_send, g_keep = qkv_grads(place, norm, dq, dk, dv, mid_send, mid_keep)
     if small:

time: 270 us -> 263 us (0.974)
  local copies, waits for them, and re-layouts: 4.63 us -> 0.81 us
  Pallas kernels: 235 us -> 232 us
    pallas_call x2 -> x1, Pallas kernels: 63.8 us -> 52.3 us  [gather(): pl.pallas_call(gather_kernel, in_specs=[vmem, vmem, far, vmem], out_specs...]
    pallas_call x1, Pallas kernels: 30.8 us -> 35.6 us  [attend_back(): pl.pallas_call(attend_back_kernel, grid_spec=pltpu.PrefetchScalarGridSpec...]
    pallas_call x1, Pallas kernels: 21.2 us -> 24.8 us  [attend(): pl.pallas_call(attend_kernel, grid_spec=pltpu.PrefetchScalarGridSpec(num_...]
  transfers between devices with their start and end apart: 8 -> 7, of which waited for: 1 -> 0; matrix products, arithmetic and copies ran while one was open for 2% -> 1% of each run, Pallas kernels for 18% -> 20%
where the time goes in v6:
time: 263 us; the launch traced here: 264 us
  Pallas kernels  232 us (88%)
  starting transfers between devices  21.3 us (8%)
  other arithmetic  8.74 us (3%)
    pallas_call x1, Pallas kernels, feed(): pl.pallas_call(functools.partial(feed_kernel, small), grid=(3 * half + 1,...  63.2 us
    pallas_call x1, Pallas kernels, gather(): pl.pallas_call(gather_kernel, in_specs=[vmem, vmem, far, vmem], out_specs...  52.3 us
    pallas_call x1, Pallas kernels, last(): pl.pallas_call(functools.partial(last_kernel, small), grid=(2 * half + 7...  38.8 us
    pallas_call x1, Pallas kernels, attend_back(): pl.pallas_call(attend_back_kernel, grid_spec=pltpu.PrefetchScalarGridSpec...  35.6 us
    pallas_call x1, Pallas kernels, attend(): pl.pallas_call(attend_kernel, grid_spec=pltpu.PrefetchScalarGridSpec(num_...  24.8 us
    ppermute x3, starting transfers between devices, hop_z(): return lax.ppermute(value, 'dp', pairs)  18.6 us
    pallas_call x1, Pallas kernels, qkv_grads(): pl.pallas_call(qkv_grads_kernel, grid_spec=pltpu.PrefetchScalarGridSpec(n...  8.68 us
    pallas_call x1, Pallas kernels, renew(): pl.pallas_call(renew_kernel, grid_spec=pltpu.PrefetchScalarGridSpec(num_s...  8.4 us
  transfers between devices with their start and end apart: 7, of which 0 were waited for; matrix products, arithmetic and copies ran while one was open for 1% of the time, Pallas kernels for 20%

profile of v6, /device:TPU:0, one launch (start us, length us, event | category | flops | bytes accessed | tf_op | source)
XLA Modules:
  0.0 263.6 jit_solution(8427165271838512366)
XLA Ops:
  0.6 52.3 %gather.1 = (bf16[2,24,192,384]{3,2,1,0:T(8,128)(2,1)}, bf16[2,2,192,384]{3,2,1,0:T(8,128)(2,1)}, f32[16,768]{1,0:T(8,128)}, bf16[2048,768]{1,0:T(8,128)(2,1)}, ...) custom-call(f32[1,6,192,192]{3,2,1,0:T(8,128)} %weight.1, ...), custom_call_target="tpu_custom_call" | custom-call | flops 65999998976 | bytes 60000000 | tf_op jit(solution)/shard_map/gather/pallas_call | solution.py:282
  52.9 24.8 %attend.1 = (bf16[2048,384]{1,0:T(8,128)(2,1)}, f32[8,2048]{1,0:T(8,128)}) custom-call(s32[8]{0:T(128)} %bitcast.9, bf16[2048,384]{1,0:T(8,128)(2,1)} %get-tuple-element.48.q, bf16[2048,384]{1,0:T(8,128)(2,1)} %get-tuple-element.49.k, bf16[2048,384]{1,0:T(8,128)(2,1)} %get-tuple-element.50.v), custom_call_target="tpu_custom_call" | custom-call | flops 32999999488 | bytes 30000000 | tf_op jit(solution)/shard_map/attend/pallas_call | solution.py:420
  77.8 63.2 %feed_forward.1 = (bf16[1024,768]{1,0:T(8,128)(2,1)}, f32[1024,768]{1,0:T(8,128)}, f32[1024,768]{1,0:T(8,128)}, bf16[2048,384]{1,0:T(8,128)(2,1)}, f32[8,768]{1,...) custom-call(bf16[2048,768]{1,0:T(8,128)(2,1)} %tok.3, ...), custom_call_target="tpu_custom_call" | custom-call | flops 54999998464 | bytes 50000000 | tf_op jit(solution)/shard_map/feed_forward/pallas_call | solution.py:762
  141.0 0.7 collective-permute-start
  141.7 16.6 %collective-permute-start.1 = (bf16[3,192,384]{2,1,0:T(8,128)(2,1)}, bf16[3,192,384]{2,1,0:T(8,128)(2,1)S(1)}, u32[]{:S(2)}, u32[]{:S(2)}) collective-permute-start(bf16[3,192,384]{2,1,0:T(8,128)(2,1)} %get-tuple-element.57), channel_id=1, source_target_pairs={{0,16},{4,20},{8,24},{12,28},{1,17},{5,21},{9,25},{13,29},{2,18},{... | collective-permute-start | bytes 1327112 | tf_op jit(solution)/shard_map/ppermute | solution.py:1168
  158.2 1.3 collective-permute-start.2
  159.6 1.0 collective-permute-start.3
  160.6 1.1 collective-permute-start.4
  161.7 35.6 %attend_back.1 = (bf16[2048,384]{1,0:T(8,128)(2,1)}, bf16[2048,384]{1,0:T(8,128)(2,1)}, bf16[2048,384]{1,0:T(8,128)(2,1)}) custom-call(s32[8]{0:T(128)} %bitcast.10, bf16[2048,384]{1,0:T(8,128)(2,1)} %get-tuple-element.48.q, bf16[2048,384]{1,0:T(8,128)(2,1)} %get-tuple-element.49.k, bf16[2048,384]{1,0:T(8,128)(2,1)} %get-tuple-element.50.v, ...), custom_call_target="tpu_custom_call" | custom-call | flops 44000002048 | bytes 40000000 | tf_op jit(solution)/shard_map/attend_back/pallas_call | solution.py:501
  197.3 0.7 pad_add_fusion.place
  198.0 0.0 collective-permute-done.4.mid_send
  198.0 0.0 copy-start.10
  198.0 0.8 copy-done.10
  198.8 8.7 %qkv_grads.1 = (bf16[6,192,384]{2,1,0:T(8,128)(2,1)}, bf16[6,192,384]{2,1,0:T(8,128)(2,1)}) custom-call(s32[4]{0:T(128)} %pad_add_fusion.place, bf16[2048,768]{1,0:T(8,128)(2,1)} %get-tuple-element.59.norm, bf16[2048,384]{1,0:T(8,128)(2,1)} %get-tuple-element.62.dq, bf16[2048,384]{1,0:T(8,128)(2,1)} %get-tuple-element.63.dk, ...), custom_call_target="tpu_custom_call" | custom-call | flops 8800000000 | bytes 8000000 | tf_op jit(solution)/shard_map/qkv_grads/pallas_call | solution.py:848
  207.5 0.0 collective-permute-done.one
  207.5 0.0 copy-start.7
  207.5 0.0 collective-permute-done.1.two
  207.5 0.0 copy-start.8
  207.5 0.0 collective-permute-done.2.three
  207.5 0.0 copy-start.9
  207.5 0.0 collective-permute-done.3
  207.5 0.0 copy-start.3
  207.5 0.0 copy-start
  207.5 0.0 copy-start.2
  207.5 38.8 %last.1 = (bf16[1024,768]{1,0:T(8,128)(2,1)}, f32[3,192,384]{2,1,0:T(8,128)}, f32[16,128]{1,0:T(8,128)}) custom-call(bf16[2048,384]{1,0:T(8,128)(2,1)} %get-tuple-element.62.dq, bf16[2048,384]{1,0:T(8,128)(2,1)} %get-tuple-element.63.dk, bf16[2048,384]{1,0:T(8,128)(2,1)} %get-tuple-element.64.dv, bf16[3,768,384]{2,1,0:T(8,128)(2,1)} %get-tuple-element.69.cat, ...), custom_call_target="tpu_custom_call" | custom-call | flops 32999999488 | bytes 30000000 | tf_op jit(solution)/shard_map/last/pallas_call | solution.py:1068
  246.4 0.0 copy-done.7
  246.4 0.0 copy-done.8
  246.4 0.0 copy-done.9
  246.4 0.0 copy-done.3
  246.4 0.1 collective-permute-start.6
  246.5 0.0 copy-done
  246.5 0.0 copy-done.2
  246.5 0.0 copy-start.4
  246.5 0.0 copy-start.5
  246.5 0.0 copy-start.6
  246.5 1.9 add_convert_fusion
  248.4 0.5 collective-permute-start.5
  249.0 0.0 copy-done.4
  249.0 0.0 copy-done.5
  249.0 0.0 copy-done.6
  249.0 0.6 divide_subtract_fusion
  249.6 0.0 copy-start.1
  249.6 8.4 %renew.1 = (f32[1,6,192,192]{3,2,1,0:T(8,128)}, f32[1,6,192,192]{3,2,1,0:T(8,128)}, f32[1,6,192,192]{3,2,1,0:T(8,128)}, f32[1,6,192,192]{3,2,1,0:T(8,128)}) custom-call(s32[4]{0:T(128)} %pad_add_fusion.place, f32[3,192,384]{2,1,0:T(8,128)} %get-tuple-element.75.late, bf16[3,192,384]{2,1,0:T(8,128)(2,1)} %get-tuple-element.76.own, ...), custom_call_target="tpu_custom_call" | custom-call | flops 5500000256 | bytes 5000000 | tf_op jit(solution)/shard_map/renew/pallas_call | solution.py:1133
  258.0 0.0 collective-permute-done.6
  258.0 0.0 collective-permute-done.5
  258.0 0.0 copy-done.1
  258.0 1.8 broadcast_select_fusion.1
  259.9 1.9 pad_maximum_fusion
  261.7 1.9 pad_maximum_fusion.1
Async XLA Ops:
  141.0 66.5 %collective-permute-start = (bf16[3,192,384]{2,1,0:T(8,128)(2,1)}, bf16[3,192,384]{2,1,0:T(8,128)(2,1)S(1)}, u32[]{:S(2)}, u32[]{:S(2)}) collective-permute-start(bf16[3,192,384]{2,1,0:T(8,128)(2,1)} %get-tuple-element.56), channel_id=1, source_target_pairs={{8,16},{12,20},{16,24},{20,28},{9,17},{13,21},{17,25},{21,29},{10,... | collective-permute-start | bytes 1327112 | tf_op jit(solution)/shard_map/ppermute | solution.py:1168
  141.7 65.8 %collective-permute-start.1 = (bf16[3,192,384]{2,1,0:T(8,128)(2,1)}, bf16[3,192,384]{2,1,0:T(8,128)(2,1)S(1)}, u32[]{:S(2)}, u32[]{:S(2)}) collective-permute-start(bf16[3,192,384]{2,1,0:T(8,128)(2,1)} %get-tuple-element.57), channel_id=1, source_target_pairs={{0,16},{4,20},{8,24},{12,28},{1,17},{5,21},{9,25},{13,29},{2,18},{... | collective-permute-start | bytes 1327112 | tf_op jit(solution)/shard_map/ppermute | solution.py:1168
  158.2 49.2 %collective-permute-start.2 = (bf16[3,192,384]{2,1,0:T(8,128)(2,1)}, bf16[3,192,384]{2,1,0:T(8,128)(2,1)S(1)}, u32[]{:S(2)}, u32[]{:S(2)}) collective-permute-start(bf16[3,192,384]{2,1,0:T(8,128)(2,1)} %get-tuple-element.58), channel_id=1, source_target_pairs={{0,24},{4,28},{24,16},{28,20},{1,25},{5,29},{25,17},{29,21},{2,26}... | collective-permute-start | bytes 1327112 | tf_op jit(solution)/shard_map/ppermute | solution.py:1168
  159.6 47.9 %collective-permute-start.3 = (bf16[1024,768]{1,0:T(8,128)(2,1)}, bf16[1024,768]{1,0:T(8,128)(2,1)S(1)}, u32[]{:S(2)}, u32[]{:S(2)}) collective-permute-start(bf16[1024,768]{1,0:T(8,128)(2,1)} %get-tuple-element.55), channel_id=1, source_target_pairs={{0,2},{1,3},{2,0},{3,1},{4,6},{5,7},{6,4},{7,5},{8,10},{9,11},{10,... | collective-permute-start | bytes 4718600 | tf_op jit(solution)/shard_map/ppermute | solution.py:1159
  160.6 37.5 %collective-permute-start.4 = (bf16[3,192,384]{2,1,0:T(8,128)(2,1)}, bf16[3,192,384]{2,1,0:T(8,128)(2,1)S(1)}, u32[]{:S(2)}, u32[]{:S(2)}) collective-permute-start(bf16[3,192,384]{2,1,0:T(8,128)(2,1)} %get-tuple-element.65), channel_id=1, source_target_pairs={{0,4},{4,0},{8,12},{12,8},{16,20},{20,16},{24,28},{28,24},{1,5},{5... | collective-permute-start | bytes 1327112 | tf_op jit(solution)/shard_map/ppermute | solution.py:1163
  198.0 0.8 copy-start.10
  207.5 38.9 %copy-start.7 = (bf16[3,192,384]{2,1,0:T(8,128)(2,1)}, bf16[3,192,384]{2,1,0:T(8,128)(2,1)S(1)}, u32[]{:S(2)}) copy-start(bf16[3,192,384]{2,1,0:T(8,128)(2,1)S(1)} %collective-permute-done.one) | copy-start | bytes 1327108
  207.5 38.9 %copy-start.8 = (bf16[3,192,384]{2,1,0:T(8,128)(2,1)}, bf16[3,192,384]{2,1,0:T(8,128)(2,1)S(1)}, u32[]{:S(2)}) copy-start(bf16[3,192,384]{2,1,0:T(8,128)(2,1)S(1)} %collective-permute-done.1.two) | copy-start | bytes 1327108
  207.5 38.9 %copy-start.9 = (bf16[3,192,384]{2,1,0:T(8,128)(2,1)}, bf16[3,192,384]{2,1,0:T(8,128)(2,1)S(1)}, u32[]{:S(2)}) copy-start(bf16[3,192,384]{2,1,0:T(8,128)(2,1)S(1)} %collective-permute-done.2.three) | copy-start | bytes 1327108
  207.5 38.9 %copy-start.3 = (bf16[1024,768]{1,0:T(8,128)(2,1)}, bf16[1024,768]{1,0:T(8,128)(2,1)S(1)}, u32[]{:S(2)}) copy-start(bf16[1024,768]{1,0:T(8,128)(2,1)S(1)} %collective-permute-done.3) | copy-start | bytes 4718596
  207.5 38.9 %copy-start = (f32[1024,768]{1,0:T(8,128)S(1)}, f32[1024,768]{1,0:T(8,128)}, u32[]{:S(2)}) copy-start(f32[1024,768]{1,0:T(8,128)} %get-tuple-element.54) | copy-start | bytes 9437188
  207.5 38.9 %copy-start.2 = (bf16[1024,768]{1,0:T(8,128)(2,1)S(1)}, bf16[1024,768]{1,0:T(8,128)(2,1)}, u32[]{:S(2)}) copy-start(bf16[1024,768]{1,0:T(8,128)(2,1)} %get-tuple-element.55) | copy-start | bytes 4718596
  246.4 11.6 %collective-permute-start.6 = (bf16[1024,768]{1,0:T(8,128)(2,1)}, bf16[1024,768]{1,0:T(8,128)(2,1)S(1)}, u32[]{:S(2)}, u32[]{:S(2)}) collective-permute-start(bf16[1024,768]{1,0:T(8,128)(2,1)} %get-tuple-element.74), channel_id=1, source_target_pairs={{0,1},{1,0},{2,3},{3,2},{4,5},{5,4},{6,7},{7,6},{8,9},{9,8},{10,11... | collective-permute-start | bytes 4718600 | tf_op jit(solution)/shard_map/ppermute | solution.py:1159
  246.5 2.5 copy-start.4
  246.5 2.5 copy-start.5
  246.5 2.5 copy-start.6
  248.4 9.6 %collective-permute-start.5 = (bf16[1024,768]{1,0:T(8,128)(2,1)S(1)}, bf16[1024,768]{1,0:T(8,128)(2,1)}, u32[]{:S(2)}, u32[]{:S(2)}) collective-permute-start(bf16[1024,768]{1,0:T(8,128)(2,1)S(1)} %add_convert_fusion), channel_id=1, source_target_pairs={{0,1},{1,0},{2,3},{3,2},{4,5},{5,4},{6,7},{7,6},{8,9},{9,8},{10,11... | collective-permute-start | bytes 4718600 | tf_op jit(solution)/shard_map/ppermute | solution.py:1159
  249.6 8.4 %copy-start.1 = (bf16[1024,768]{1,0:T(8,128)(2,1)S(1)}, bf16[1024,768]{1,0:T(8,128)(2,1)}, u32[]{:S(2)}) copy-start(bf16[1024,768]{1,0:T(8,128)(2,1)} %get-tuple-element.74) | copy-start | bytes 4718596

commit v7 on v6

--- a/solution.py
+++ b/solution.py
@@ -197,7 +197,10 @@
     for m in range(3):
         along_x(1, m, z + 1 < 4)
     for m in range(3):
+        from_left(1, m)
+        along_x(-1, m, z - 1 > 0)
         from_right(2, m)
+        along_x(2, m, z + 2 < 4)
     for k in range(6):
         arrived(piece(1 - y, x, k), r_y1.at[k])
         arrived(piece(1 - y, 1 - x, k), r_d1.at[k])
@@ -232,18 +235,13 @@
         rows_of(b)
         if b == 0:
             for m in range(3):
-                from_left(1, m)
-                along_x(-1, m, z - 1 > 0)
-                along_x(2, m, z + 2 < 4)
-        if b == 1:
-            for m in range(3):
                 from_right(3, m)
                 along_x(3, m, z + 3 < 4)
-        if b == 2:
+        if b == 1:
             for m in range(3):
                 from_left(2, m)
                 along_x(-2, m, z - 2 > 0)
-        if b == 3:
+        if b == 2:
             for m in range(2):
                 ref = all_pairs.at[y, 6 + m]
                 arrived(ref, r_x2.at[1, m], x == 1)
@@ -865,16 +863,20 @@
 CHUNKS = 12
 
 
-def last_kernel(small, dq, dk, dv, cat, tok, pas, vec, grad_second, sums_two, g_send, g_keep, low, *rest):
+def last_kernel(
+    small, dq, dk, dv, cat, tok, pas, vec, grad_second, sums_two, second, chip, far, g_send, g_keep, output, input_grad, *rest
+):
     if small:
         late, vec_sum = rest[:2]
         rest = rest[2:]
         (
             core_out, core_in, sums, core_sums, x_in, z_in, z_out, up_in, v_out, v_in,
-            s_core, r_core, s_sum, r_sum, s_x, r_x, s_z, r_z, s_up, r_up, s_v, r_v,
+            s_core, r_core, s_sum, r_sum, s_x, r_x, s_z, r_z, s_up, r_up, s_v, r_v, ready, s_own, s_res, r_res,
         ) = rest
     else:
-        vec_sum, core_out, core_in, sums, core_sums, s_core, r_core, s_sum, r_sum = rest
+        (
+            vec_sum, core_out, core_in, sums, core_sums, s_core, r_core, s_sum, r_sum, ready, s_own, s_res, r_res,
+        ) = rest
     i = pl.program_id(0)
     half = core_out.shape[0]
     t, dp = lax.axis_index("tensor"), lax.axis_index("dp")
@@ -891,6 +893,15 @@
 
     core_copy = lambda j: copy(core_out.at[j], core_in.at[j], s_core.at[j], r_core.at[j], {"tensor": near})
     sum_copy = lambda: copy(sums, core_sums, s_sum, r_sum, {"tensor": near})
+
+    def rows_at(n, j, owner):
+        rows = pl.ds(pl.multiple_of((owner * half + j) * ROWS, ROWS), ROWS)
+        return (output, input_grad)[n].at[rows]
+
+    own_result = lambda n, j: pltpu.make_async_copy(ready.at[n, j], rows_at(n, j, core), s_own.at[n, j])
+    near_result = lambda n, j, owner: copy(
+        ready.at[n, j], rows_at(n, j, owner), s_res.at[n, j], r_res.at[n, j], {"tensor": near}
+    )
 
     def part_of(ref, k):
         return ref.at[k // 2, pl.ds((k % 2) * CHUNK, CHUNK)]
@@ -931,7 +942,11 @@
             core_copy(j).wait_recv()
             grad = part + core_in[j].astype(f32)
             result = grad_second[...] + norm_back(hat, root, grad, vec[PASSES : PASSES + 1])
-            low[...] = result.astype(bf16)
+            ready[0, j] = (second[...] + (chip[...].astype(f32) + far[...].astype(f32))).astype(bf16)
+            ready[1, j] = result.astype(bf16)
+            for n in range(2):
+                own_result(n, j).start()
+                near_result(n, j, core).start()
             chosen = one_hot(pas[...])
             high, mid, _ = split_three(result)
             sums[...] += nn(chosen, high) + nn(chosen, mid)
@@ -960,10 +975,7 @@
         def keep_late(k, pair, total):
             late[pair, pl.ds(pl.multiple_of((k % 2) * CHUNK, 16), CHUNK), :] = total
 
-        k = i - 1 - (3 - z)
-
-        @pl.when((k >= 0) & (k < CHUNKS) & ((z > 0) | (k < 6)))
-        def _():
+        def pass_on(k):
             total = term_of(k)
 
             @pl.when(z < 3)
@@ -987,10 +999,18 @@
                 up_copy(k).wait_recv()
                 keep_late(k, k // 2 - 3, passed + up_in[k - 6].astype(f32))
 
-        @pl.when((i >= 7) & (i < 13) & (z == 0))
+        for n in range(2):
+            at = 2 * (i - 1 - (3 - z)) + n
+            k = jnp.where(at < 4, at + 6, jnp.where(at < 10, at - 4, at))
+
+            @pl.when((at >= 0) & (at < CHUNKS) & ((z > 0) | (k < 6)))
+            def _(k=k):
+                pass_on(k)
+
+        @pl.when((i >= 1) & (i < 7) & (z == 0))
         def _():
-            z_out[i - 1] = term_of(i - 1).astype(bf16)
-            up_copy(i - 1).start()
+            z_out[i + 5] = term_of(i + 5).astype(bf16)
+            up_copy(i + 5).start()
 
     @pl.when(i == 2 * half + 1)
     def _():
@@ -1010,6 +1030,10 @@
     def _():
         for j in range(half):
             core_copy(j).wait_send()
+            for n in range(2):
+                own_result(n, j).wait()
+                near_result(n, j, core).wait_send()
+                near_result(n, j, 1 - core).wait_recv()
         sum_copy().wait_send()
         if small:
             for peer in peers:
@@ -1030,7 +1054,9 @@
                     pl.when(z == 0)(up_copy(k).wait_send)
 
 
-def last(small, dq, dk, dv, cat, tokens, passes, vec, grad_second, sums_two, g_send, g_keep):
+def last(
+    small, dq, dk, dv, cat, tokens, passes, vec, grad_second, sums_two, second, chip, far, g_send, g_keep
+):
     seq = dq.shape[0]
     half = seq // ROWS // 2
     core = lambda: lax.axis_index("tensor") % 2
@@ -1043,8 +1069,8 @@
     row = pl.BlockSpec((ROWS, PAIR), lambda i: (block(i), 0))
     mine = pl.BlockSpec((ROWS, D), lambda i: (own(i), 0))
     dma = pltpu.SemaphoreType.DMA
-    out_specs = [mine]
-    out_shape = [jax.ShapeDtypeStruct((seq // 2, D), bf16)]
+    out_specs = [pl.BlockSpec(memory_space=pl.ANY)] * 2
+    out_shape = [jax.ShapeDtypeStruct((seq, D), bf16)] * 2
     scratch = [
         pltpu.VMEM((half, ROWS, D), bf16),
         pltpu.VMEM((half, ROWS, D), bf16),
@@ -1065,9 +1091,10 @@
     else:
         out_specs += [full((16, D))]
         out_shape += [jax.ShapeDtypeStruct((16, D), f32)]
+    scratch_more = [pltpu.VMEM((2, half, ROWS, D), bf16)] + [dma((2, half))] * 3
     return pl.pallas_call(
         functools.partial(last_kernel, small),
-        grid=(2 * half + 7 if small else 2 * half + 2,),
+        grid=(2 * half + 3 if small else 2 * half + 2,),
         in_specs=[
             row,
             row,
@@ -1078,16 +1105,19 @@
             full((16, D)),
             mine,
             full((8, D)),
+            mine,
+            mine,
+            mine,
             full(g_send.shape),
             full(g_keep.shape),
         ],
         out_specs=out_specs,
         out_shape=out_shape,
-        scratch_shapes=scratch + sems,
+        scratch_shapes=scratch + sems + scratch_more,
         compiler_params=params(collective_id=2, has_side_effects=True),
         cost_estimate=cost(30),
         name="last",
-    )(dq, dk, dv, cat, tokens, passes, vec, grad_second, sums_two, g_send, g_keep)
+    )(dq, dk, dv, cat, tokens, passes, vec, grad_second, sums_two, second, chip, far, g_send, g_keep)
 
 
 def precondition(grad, weight, left, right, left_root, right_root):
@@ -1220,18 +1250,9 @@
     g_send, g_keep = qkv_grads(place, norm, dq, dk, dv, mid_send, mid_keep)
     if small:
         *far, out_far, g_send = tie(*far, out_far, g_send)
-    low_half, *sums = last(
-        small, dq, dk, dv, cat, tokens, passes, vec, grad_second, sums_two, g_send, g_keep
+    output, input_grad, *sums = last(
+        small, dq, dk, dv, cat, tokens, passes, vec, grad_second, sums_two, second, out_chip, out_far, g_send, g_keep
     )
-    out_half = (second + (out_chip.astype(f32) + out_far.astype(f32))).astype(bf16)
-
-    def join(half):
-        far = swap(half, 1)
-        low = jnp.where(core == 0, half, far)
-        high = jnp.where(core == 0, far, half)
-        return jnp.concatenate([low, high], axis=0)
-
-    output, input_grad = join(out_half), join(low_half)
     if small:
         late, vector_sum = sums
         left_new, right_new, step, weight_new = renew(

time: 263 us -> 256 us (0.973)
  other arithmetic: 8.74 us -> 1.91 us
  local copies, waits for them, and re-layouts: 0.81 us -> 6.65 us
  starting transfers between devices: 21.3 us -> 15.8 us
    unnamed x22 -> x20, local copies, waits for them, and re-layouts: 0.81 us -> 6.65 us
    ppermute x3, starting transfers between devices: 18.6 us -> 13.7 us  [hop_z(): return lax.ppermute(value, 'dp', pairs)]
    concatenate x2 -> x0, other arithmetic: 3.73 us -> none  [join(): return jnp.concatenate([low, high], axis=0)]
  transfers between devices with their start and end apart: 7 -> 5, of which waited for: 0 -> 0; matrix products, arithmetic and copies ran while one was open for 1% -> 0% of each run, Pallas kernels for 20% -> 17%
where the time goes in v7:
time: 256 us; the launch traced here: 255 us
  Pallas kernels  230 us (90%)
  starting transfers between devices  15.8 us (6%)
  local copies, waits for them, and re-layouts  6.65 us (3%)
    pallas_call x1, Pallas kernels, feed(): pl.pallas_call(functools.partial(feed_kernel, small), grid=(3 * half + 1,...  62.5 us
    pallas_call x1, Pallas kernels, gather(): pl.pallas_call(gather_kernel, in_specs=[vmem, vmem, far, vmem], out_specs...  52.3 us
    pallas_call x1, Pallas kernels, last(): pl.pallas_call(functools.partial(last_kernel, small), grid=(2 * half + 3...  39.3 us
    pallas_call x1, Pallas kernels, attend_back(): pl.pallas_call(attend_back_kernel, grid_spec=pltpu.PrefetchScalarGridSpec...  34.5 us
    pallas_call x1, Pallas kernels, attend(): pl.pallas_call(attend_kernel, grid_spec=pltpu.PrefetchScalarGridSpec(num_...  24 us
    ppermute x3, starting transfers between devices, hop_z(): return lax.ppermute(value, 'dp', pairs)  13.7 us
    pallas_call x1, Pallas kernels, qkv_grads(): pl.pallas_call(qkv_grads_kernel, grid_spec=pltpu.PrefetchScalarGridSpec(n...  8.68 us
    pallas_call x1, Pallas kernels, renew(): pl.pallas_call(renew_kernel, grid_spec=pltpu.PrefetchScalarGridSpec(num_s...  8.52 us
  transfers between devices with their start and end apart: 5, of which 0 were waited for; matrix products, arithmetic and copies ran while one was open for 0% of the time, Pallas kernels for 17%

profile of v7, /device:TPU:0, one launch (start us, length us, event | category | flops | bytes accessed | tf_op | source)
XLA Modules:
  0.0 255.0 jit_solution(9963117284937391224)
XLA Ops:
  0.6 52.3 %gather.1 = (bf16[2,24,192,384]{3,2,1,0:T(8,128)(2,1)}, bf16[2,2,192,384]{3,2,1,0:T(8,128)(2,1)}, f32[16,768]{1,0:T(8,128)}, bf16[2048,768]{1,0:T(8,128)(2,1)}, ...) custom-call(f32[1,6,192,192]{3,2,1,0:T(8,128)} %weight.1, ...), custom_call_target="tpu_custom_call" | custom-call | flops 65999998976 | bytes 60000000 | tf_op jit(solution)/shard_map/gather/pallas_call | solution.py:280
  52.9 24.0 %attend.1 = (bf16[2048,384]{1,0:T(8,128)(2,1)}, f32[8,2048]{1,0:T(8,128)}) custom-call(s32[8]{0:T(128)} %bitcast.9, bf16[2048,384]{1,0:T(8,128)(2,1)} %get-tuple-element.48.q, bf16[2048,384]{1,0:T(8,128)(2,1)} %get-tuple-element.49.k, bf16[2048,384]{1,0:T(8,128)(2,1)} %get-tuple-element.50.v), custom_call_target="tpu_custom_call" | custom-call | flops 32999999488 | bytes 30000000 | tf_op jit(solution)/shard_map/attend/pallas_call | solution.py:418
  76.9 62.5 %feed_forward.1 = (bf16[1024,768]{1,0:T(8,128)(2,1)}, f32[1024,768]{1,0:T(8,128)}, f32[1024,768]{1,0:T(8,128)}, bf16[2048,384]{1,0:T(8,128)(2,1)}, f32[8,768]{1,...) custom-call(bf16[2048,768]{1,0:T(8,128)(2,1)} %tok.3, ...), custom_call_target="tpu_custom_call" | custom-call | flops 54999998464 | bytes 50000000 | tf_op jit(solution)/shard_map/feed_forward/pallas_call | solution.py:760
  139.4 0.7 collective-permute-start
  140.1 11.7 %collective-permute-start.1 = (bf16[3,192,384]{2,1,0:T(8,128)(2,1)}, bf16[3,192,384]{2,1,0:T(8,128)(2,1)S(1)}, u32[]{:S(2)}, u32[]{:S(2)}) collective-permute-start(bf16[3,192,384]{2,1,0:T(8,128)(2,1)} %get-tuple-element.66), channel_id=1, source_target_pairs={{0,16},{4,20},{8,24},{12,28},{1,17},{5,21},{9,25},{13,29},{2,18},{... | collective-permute-start | bytes 1327112 | tf_op jit(solution)/shard_map/ppermute | solution.py:1198
  151.8 1.3 collective-permute-start.2
  153.1 0.6 collective-permute-start.3
  153.7 1.5 collective-permute-start.4
  155.2 34.5 %attend_back.1 = (bf16[2048,384]{1,0:T(8,128)(2,1)}, bf16[2048,384]{1,0:T(8,128)(2,1)}, bf16[2048,384]{1,0:T(8,128)(2,1)}) custom-call(s32[8]{0:T(128)} %bitcast.10, bf16[2048,384]{1,0:T(8,128)(2,1)} %get-tuple-element.48.q, bf16[2048,384]{1,0:T(8,128)(2,1)} %get-tuple-element.49.k, bf16[2048,384]{1,0:T(8,128)(2,1)} %get-tuple-element.50.v, ...), custom_call_target="tpu_custom_call" | custom-call | flops 44000002048 | bytes 40000000 | tf_op jit(solution)/shard_map/attend_back/pallas_call | solution.py:499
  189.8 0.6 pad_add_fusion.place
  190.3 0.0 collective-permute-done.4.mid_send
  190.4 0.0 copy-start.8
  190.4 0.8 copy-done.8
  191.1 8.7 %qkv_grads.1 = (bf16[6,192,384]{2,1,0:T(8,128)(2,1)}, bf16[6,192,384]{2,1,0:T(8,128)(2,1)}) custom-call(s32[4]{0:T(128)} %pad_add_fusion.place, bf16[2048,768]{1,0:T(8,128)(2,1)} %get-tuple-element.68.norm, bf16[2048,384]{1,0:T(8,128)(2,1)} %get-tuple-element.57.dq, bf16[2048,384]{1,0:T(8,128)(2,1)} %get-tuple-element.58.dk, ...), custom_call_target="tpu_custom_call" | custom-call | flops 8800000000 | bytes 8000000 | tf_op jit(solution)/shard_map/qkv_grads/pallas_call | solution.py:846
  199.8 0.0 collective-permute-done.one
  199.8 0.0 copy-start.5
  199.8 0.0 collective-permute-done.1.two
  199.8 0.0 copy-start.6
  199.8 0.0 collective-permute-done.2.three
  199.8 0.0 copy-start.7
  199.8 0.0 collective-permute-done.3.far
  199.9 0.0 copy-start.4
  199.9 1.2 copy-done.4
  201.0 0.0 copy-start.2
  201.1 0.0 copy-start.3
  201.1 39.3 %last.1 = (bf16[2048,768]{1,0:T(8,128)(2,1)}, bf16[2048,768]{1,0:T(8,128)(2,1)}, f32[3,192,384]{2,1,0:T(8,128)}, f32[16,128]{1,0:T(8,128)}) custom-call(bf16[2048,384]{1,0:T(8,128)(2,1)} %get-tuple-element.57.dq, bf16[2048,384]{1,0:T(8,128)(2,1)} %get-tuple-element.58.dk, bf16[2048,384]{1,0:T(8,128)(2,1)} %get-tuple-element.59.dv, ...), custom_call_target="tpu_custom_call" | custom-call | flops 32999999488 | bytes 30000000 | tf_op jit(solution)/shard_map/last/pallas_call | solution.py:1095
  240.4 0.0 copy-done.5
  240.4 0.0 copy-done.6
  240.4 0.0 copy-done.7
  240.4 0.0 copy-done.2
  240.4 0.0 copy-done.3
  240.4 1.3 divide_subtract_fusion
  241.8 0.0 copy-start.1
  241.8 8.5 %renew.1 = (f32[1,6,192,192]{3,2,1,0:T(8,128)}, f32[1,6,192,192]{3,2,1,0:T(8,128)}, f32[1,6,192,192]{3,2,1,0:T(8,128)}, f32[1,6,192,192]{3,2,1,0:T(8,128)}) custom-call(s32[4]{0:T(128)} %pad_add_fusion.place, f32[3,192,384]{2,1,0:T(8,128)} %get-tuple-element.77.late, bf16[3,192,384]{2,1,0:T(8,128)(2,1)} %get-tuple-element.78.own, ...), custom_call_target="tpu_custom_call" | custom-call | flops 5500000256 | bytes 5000000 | tf_op jit(solution)/shard_map/renew/pallas_call | solution.py:1163
  250.3 0.0 copy-done.1
  250.3 0.0 copy-start
  250.3 1.7 copy.22
  252.0 1.3 copy-done
  253.3 1.7 copy.23
Async XLA Ops:
  139.4 60.4 %collective-permute-start = (bf16[3,192,384]{2,1,0:T(8,128)(2,1)}, bf16[3,192,384]{2,1,0:T(8,128)(2,1)S(1)}, u32[]{:S(2)}, u32[]{:S(2)}) collective-permute-start(bf16[3,192,384]{2,1,0:T(8,128)(2,1)} %get-tuple-element.65), channel_id=1, source_target_pairs={{8,16},{12,20},{16,24},{20,28},{9,17},{13,21},{17,25},{21,29},{10,... | collective-permute-start | bytes 1327112 | tf_op jit(solution)/shard_map/ppermute | solution.py:1198
  140.1 59.7 %collective-permute-start.1 = (bf16[3,192,384]{2,1,0:T(8,128)(2,1)}, bf16[3,192,384]{2,1,0:T(8,128)(2,1)S(1)}, u32[]{:S(2)}, u32[]{:S(2)}) collective-permute-start(bf16[3,192,384]{2,1,0:T(8,128)(2,1)} %get-tuple-element.66), channel_id=1, source_target_pairs={{0,16},{4,20},{8,24},{12,28},{1,17},{5,21},{9,25},{13,29},{2,18},{... | collective-permute-start | bytes 1327112 | tf_op jit(solution)/shard_map/ppermute | solution.py:1198
  151.8 48.1 %collective-permute-start.2 = (bf16[3,192,384]{2,1,0:T(8,128)(2,1)}, bf16[3,192,384]{2,1,0:T(8,128)(2,1)S(1)}, u32[]{:S(2)}, u32[]{:S(2)}) collective-permute-start(bf16[3,192,384]{2,1,0:T(8,128)(2,1)} %get-tuple-element.67), channel_id=1, source_target_pairs={{0,24},{4,28},{24,16},{28,20},{1,25},{5,29},{25,17},{29,21},{2,26}... | collective-permute-start | bytes 1327112 | tf_op jit(solution)/shard_map/ppermute | solution.py:1198
  153.1 46.7 %collective-permute-start.3 = (bf16[1024,768]{1,0:T(8,128)(2,1)}, bf16[1024,768]{1,0:T(8,128)(2,1)S(1)}, u32[]{:S(2)}, u32[]{:S(2)}) collective-permute-start(bf16[1024,768]{1,0:T(8,128)(2,1)} %get-tuple-element.64.chip), channel_id=1, source_target_pairs={{0,2},{1,3},{2,0},{3,1},{4,6},{5,7},{6,4},{7,5},{8,10},{9,11},{10,... | collective-permute-start | bytes 4718600 | tf_op jit(solution)/shard_map/ppermute | solution.py:1189
  153.7 36.7 %collective-permute-start.4 = (bf16[3,192,384]{2,1,0:T(8,128)(2,1)}, bf16[3,192,384]{2,1,0:T(8,128)(2,1)S(1)}, u32[]{:S(2)}, u32[]{:S(2)}) collective-permute-start(bf16[3,192,384]{2,1,0:T(8,128)(2,1)} %get-tuple-element.69), channel_id=1, source_target_pairs={{0,4},{4,0},{8,12},{12,8},{16,20},{20,16},{24,28},{28,24},{1,5},{5... | collective-permute-start | bytes 1327112 | tf_op jit(solution)/shard_map/ppermute | solution.py:1193
  190.4 0.8 copy-start.8
  199.8 40.6 %copy-start.5 = (bf16[3,192,384]{2,1,0:T(8,128)(2,1)}, bf16[3,192,384]{2,1,0:T(8,128)(2,1)S(1)}, u32[]{:S(2)}) copy-start(bf16[3,192,384]{2,1,0:T(8,128)(2,1)S(1)} %collective-permute-done.one) | copy-start | bytes 1327108
  199.8 40.6 %copy-start.6 = (bf16[3,192,384]{2,1,0:T(8,128)(2,1)}, bf16[3,192,384]{2,1,0:T(8,128)(2,1)S(1)}, u32[]{:S(2)}) copy-start(bf16[3,192,384]{2,1,0:T(8,128)(2,1)S(1)} %collective-permute-done.1.two) | copy-start | bytes 1327108
  199.8 40.6 %copy-start.7 = (bf16[3,192,384]{2,1,0:T(8,128)(2,1)}, bf16[3,192,384]{2,1,0:T(8,128)(2,1)S(1)}, u32[]{:S(2)}) copy-start(bf16[3,192,384]{2,1,0:T(8,128)(2,1)S(1)} %collective-permute-done.2.three) | copy-start | bytes 1327108
  199.9 1.2 copy-start.4
  201.0 39.4 %copy-start.2 = (f32[9,96]{1,0:T(8,128)S(1)}, f32[9,96]{1,0:T(8,128)}, u32[]{:S(2)}) copy-start(f32[9,96]{1,0:T(8,128)} %vec_own.1) | copy-start | bytes 10372
  201.1 39.4 %copy-start.3 = (f32[9,96]{1,0:T(8,128)S(1)}, f32[9,96]{1,0:T(8,128)}, u32[]{:S(2)}) copy-start(f32[9,96]{1,0:T(8,128)} %param.17) | copy-start | bytes 10372
  241.8 8.5 %copy-start.1 = (bf16[2048,768]{1,0:T(8,128)(2,1)S(1)}, bf16[2048,768]{1,0:T(8,128)(2,1)}, u32[]{:S(2)}) copy-start(bf16[2048,768]{1,0:T(8,128)(2,1)} %get-tuple-element.99) | copy-start | bytes 9437188
  250.3 3.0 %copy-start = (bf16[2048,768]{1,0:T(8,128)(2,1)S(1)}, bf16[2048,768]{1,0:T(8,128)(2,1)}, u32[]{:S(2)}) copy-start(bf16[2048,768]{1,0:T(8,128)(2,1)} %get-tuple-element.100) | copy-start | bytes 9437188

commit v8 on v7

--- a/solution.py
+++ b/solution.py
@@ -28,7 +28,6 @@
 f32 = jnp.float32
 bf16 = jnp.bfloat16
 MESH = pl.DeviceIdType.MESH
-VMEM_LIMIT = 56 * 1024 * 1024
 
 
 def nn(a, b):
@@ -75,8 +74,8 @@
     return root * (scaled - first - hat * second)
 
 
-def params(**kw):
-    return pltpu.CompilerParams(vmem_limit_bytes=VMEM_LIMIT, **kw)
+def params(mebibytes=56, **kw):
+    return pltpu.CompilerParams(vmem_limit_bytes=mebibytes * 1024 * 1024, **kw)
 
 
 def cost(micros):
@@ -861,6 +860,12 @@
 
 CHUNK = SIDE // 2
 CHUNKS = 12
+TAKEN = (
+    ((8, 4), (9, 12)),
+    ((5, 1), (6, 3), (7, 4), (8, 7), (9, 12)),
+    ((3, 1), (4, 3), (5, 4), (6, 5), (7, 6), (8, 9), (9, 12)),
+    ((1, 2), (2, 3), (3, 5), (4, 6), (5, 8), (6, 10), (7, 12)),
+)
 
 
 def last_kernel(
@@ -957,62 +962,7 @@
     def _():
         sum_copy().start()
 
-    if small:
-
-        def term_of(k):
-            rows = pl.ds(pl.multiple_of((k % 2) * CHUNK, 16), CHUNK)
-
-            @pl.when(k < 6)
-            def _():
-                x_copy(k).wait_recv()
-
-            @pl.when(k >= 6)
-            def _():
-                x_in[k] = g_send[k // 2, rows, :]
-
-            return g_keep[k // 2, rows, :].astype(f32) + x_in[k].astype(f32)
-
-        def keep_late(k, pair, total):
-            late[pair, pl.ds(pl.multiple_of((k % 2) * CHUNK, 16), CHUNK), :] = total
-
-        def pass_on(k):
-            total = term_of(k)
-
-            @pl.when(z < 3)
-            def _():
-                z_copy(k).wait_recv()
-
-            below = jnp.where(z < 3, z_in[k].astype(f32), 0.0)
-            passed = total + below
-
-            @pl.when((z > 1) | ((z == 1) & (k < 6)))
-            def _():
-                z_out[k] = passed.astype(bf16)
-                z_copy(k).start()
-
-            @pl.when(z == 0)
-            def _():
-                keep_late(k, k // 2, passed)
-
-            @pl.when((z == 1) & (k >= 6))
-            def _():
-                up_copy(k).wait_recv()
-                keep_late(k, k // 2 - 3, passed + up_in[k - 6].astype(f32))
-
-        for n in range(2):
-            at = 2 * (i - 1 - (3 - z)) + n
-            k = jnp.where(at < 4, at + 6, jnp.where(at < 10, at - 4, at))
-
-            @pl.when((at >= 0) & (at < CHUNKS) & ((z > 0) | (k < 6)))
-            def _(k=k):
-                pass_on(k)
-
-        @pl.when((i >= 1) & (i < 7) & (z == 0))
-        def _():
-            z_out[i + 5] = term_of(i + 5).astype(bf16)
-            up_copy(i + 5).start()
-
-    @pl.when(i == 2 * half + 1)
+    @pl.when(i == 2 * half)
     def _():
         sum_copy().wait_recv()
         total = sums[...] + core_sums[...]
@@ -1025,6 +975,70 @@
                 v_copy(n).start()
         else:
             vec_sum[...] = total
+
+    if small:
+
+        def term_of(k):
+            rows = pl.ds(pl.multiple_of((k % 2) * CHUNK, 16), CHUNK)
+
+            @pl.when(jnp.asarray(k) < 6)
+            def _():
+                x_copy(k).wait_recv()
+
+            @pl.when(jnp.asarray(k) >= 6)
+            def _():
+                x_in[k] = g_send[k // 2, rows, :]
+
+            return g_keep[k // 2, rows, :].astype(f32) + x_in[k].astype(f32)
+
+        def keep_late(k, pair, total):
+            late[pair, pl.ds(pl.multiple_of((k % 2) * CHUNK, 16), CHUNK), :] = total
+
+        def pass_on(k):
+            total = term_of(k)
+
+            @pl.when(z < 3)
+            def _():
+                z_copy(k).wait_recv()
+
+            below = jnp.where(z < 3, z_in[k].astype(f32), 0.0)
+            passed = total + below
+
+            @pl.when((z > 1) | ((z == 1) & (k < 6)))
+            def _():
+                z_out[k] = passed.astype(bf16)
+                z_copy(k).start()
+
+            @pl.when(z == 0)
+            def _():
+                keep_late(k, k // 2, passed)
+
+            @pl.when((z == 1) & (k >= 6))
+            def _():
+                up_copy(k).wait_recv()
+                keep_late(k, k // 2 - 3, passed + up_in[k - 6].astype(f32))
+
+        def at_position(p, carry):
+            k = jnp.where(p < 2, p + 6, jnp.where(p < 8, p - 2, p))
+
+            @pl.when((z > 0) | (k < 6))
+            def _():
+                pass_on(k)
+
+            return carry
+
+        begin, end = jnp.int32(0), jnp.int32(0)
+        for place, line in enumerate(TAKEN):
+            for at, upto in line:
+                begin = jnp.where((z == place) & (i > at), upto, begin)
+                end = jnp.where((z == place) & (i >= at), upto, end)
+        lax.fori_loop(begin, end, at_position, 0)
+
+        @pl.when((i == 1) & (z == 0))
+        def _():
+            for k in range(6, CHUNKS):
+                z_out[k] = term_of(k).astype(bf16)
+                up_copy(k).start()
 
     @pl.when(i == pl.num_programs(0) - 1)
     def _():
@@ -1094,7 +1108,7 @@
     scratch_more = [pltpu.VMEM((2, half, ROWS, D), bf16)] + [dma((2, half))] * 3
     return pl.pallas_call(
         functools.partial(last_kernel, small),
-        grid=(2 * half + 3 if small else 2 * half + 2,),
+        grid=(2 * half + 2,),
         in_specs=[
             row,
             row,
@@ -1142,7 +1156,21 @@
     return dot(a[0], b[0]) + (dot(a[0], b[1]) + dot(a[1], b[0]))
 
 
-def renew_kernel(place, late, own, one, two, three, weight, left, right, left_root, right_root, left_new, right_new, step, new):
+def renew_kernel(
+    place, late, own, one, two, three, weight, left, right, left_root, right_root, output, input_grad,
+    left_new, right_new, step, new, output_new, input_grad_new, sems,
+):
+    i = pl.program_id(0)
+    copies = [
+        pltpu.make_async_copy(output, output_new, sems.at[0]),
+        pltpu.make_async_copy(input_grad, input_grad_new, sems.at[1]),
+    ]
+
+    @pl.when(i == 0)
+    def _():
+        for copy in copies:
+            copy.start()
+
     early = own[0].astype(f32) + one[0].astype(f32) + two[0].astype(f32) + three[0].astype(f32)
     z = place[3]
     both = late[0] + jnp.where(z > 1, early, 0.0)
@@ -1156,8 +1184,13 @@
         step[0, n] = value
         new[0, n] = weight[0, n] - rate_matrix * value
 
-
-def renew(place, late, own, far, weight, left, right, left_root, right_root):
+    @pl.when(i == pl.num_programs(0) - 1)
+    def _():
+        for copy in copies:
+            copy.wait()
+
+
+def renew(place, late, own, far, weight, left, right, left_root, right_root, output, input_grad):
     pair = pl.BlockSpec((1, SIDE, PAIR), lambda i, s: (i, 0, 0))
     slot = pl.BlockSpec((1, 2, SIDE, SIDE), lambda i, s: (0, i, 0, 0))
     return pl.pallas_call(
@@ -1165,14 +1198,16 @@
         grid_spec=pltpu.PrefetchScalarGridSpec(
             num_scalar_prefetch=1,
             grid=(3,),
-            in_specs=[pair] * 5 + [slot] * 5,
-            out_specs=[slot] * 4,
+            in_specs=[pair] * 5 + [slot] * 5 + [pl.BlockSpec(memory_space=pltpu.HBM)] * 2,
+            out_specs=[slot] * 4 + [pl.BlockSpec(memory_space=pltpu.HBM)] * 2,
+            scratch_shapes=[pltpu.SemaphoreType.DMA((2,))],
         ),
-        out_shape=[jax.ShapeDtypeStruct(weight.shape, f32)] * 4,
-        compiler_params=params(),
+        out_shape=[jax.ShapeDtypeStruct(weight.shape, f32)] * 4
+        + [jax.ShapeDtypeStruct(value.shape, value.dtype) for value in (output, input_grad)],
+        compiler_params=params(56),
         cost_estimate=cost(5),
         name="renew",
-    )(place, late, own, *far, weight, left, right, left_root, right_root)
+    )(place, late, own, *far, weight, left, right, left_root, right_root, output, input_grad)
 
 
 def to_pairs(blocks):
@@ -1255,8 +1290,9 @@
     )
     if small:
         late, vector_sum = sums
-        left_new, right_new, step, weight_new = renew(
-            place, late, ends[0], far, block_weights, block_left, block_right, block_left_root, block_right_root
+        left_new, right_new, step, weight_new, output, input_grad = renew(
+            place, late, ends[0], far, block_weights, block_left, block_right, block_left_root, block_right_root,
+            output, input_grad,
         )
         vector_grad = vector_sum[: PASSES + 4, : vector_params.shape[1]]
     else:

time: 256 us -> 436 us (1.70)
  Pallas kernels: 230 us -> 415 us
  local copies, waits for them, and re-layouts: 6.65 us -> 1.97 us
    pallas_call x1, Pallas kernels: 8.52 us -> 195 us  [renew(): pl.pallas_call(renew_kernel, grid_spec=pltpu.PrefetchScalarGridSpec(num_s...]
    unnamed x20 -> x14, local copies, waits for them, and re-layouts: 6.65 us -> 1.97 us
  transfers between devices with their start and end apart: 5 -> 5, of which waited for: 0 -> 0; matrix products, arithmetic and copies ran while one was open for 0% -> 0% of each run, Pallas kernels for 17% -> 10%
where the time goes in v8:
time: 436 us
  Pallas kernels  415 us (95%)
  starting transfers between devices  15.6 us (4%)
    pallas_call x1, Pallas kernels, renew(): pl.pallas_call(renew_kernel, grid_spec=pltpu.PrefetchScalarGridSpec(num_s...  195 us
    pallas_call x1, Pallas kernels, feed(): pl.pallas_call(functools.partial(feed_kernel, small), grid=(3 * half + 1,...  62.5 us
    pallas_call x1, Pallas kernels, gather(): pl.pallas_call(gather_kernel, in_specs=[vmem, vmem, far, vmem], out_specs...  52.3 us
    pallas_call x1, Pallas kernels, last(): pl.pallas_call(functools.partial(last_kernel, small), grid=(2 * half + 2,...  35.9 us
    pallas_call x1, Pallas kernels, attend_back(): pl.pallas_call(attend_back_kernel, grid_spec=pltpu.PrefetchScalarGridSpec...  35.7 us
    pallas_call x1, Pallas kernels, attend(): pl.pallas_call(attend_kernel, grid_spec=pltpu.PrefetchScalarGridSpec(num_...  24.8 us
    ppermute x3, starting transfers between devices, hop_z(): return lax.ppermute(value, 'dp', pairs)  13.4 us
  transfers between devices with their start and end apart: 5, of which 0 were waited for; matrix products, arithmetic and copies ran while one was open for 0% of the time, Pallas kernels for 10%

profile of v8, /device:TPU:0, one launch (start us, length us, event | category | flops | bytes accessed | tf_op | source)
XLA Modules:
  0.0 435.7 jit_solution(2818629704915017509)
XLA Ops:
  0.6 52.3 %gather.1 = (bf16[2,24,192,384]{3,2,1,0:T(8,128)(2,1)}, bf16[2,2,192,384]{3,2,1,0:T(8,128)(2,1)}, f32[16,768]{1,0:T(8,128)}, bf16[2048,768]{1,0:T(8,128)(2,1)}, ...) custom-call(f32[1,6,192,192]{3,2,1,0:T(8,128)} %weight.1, ...), custom_call_target="tpu_custom_call" | custom-call | flops 65999998976 | bytes 60000000 | tf_op jit(solution)/shard_map/gather/pallas_call | solution.py:279
  52.9 24.8 %attend.1 = (bf16[2048,384]{1,0:T(8,128)(2,1)}, f32[8,2048]{1,0:T(8,128)}) custom-call(s32[8]{0:T(128)} %bitcast.9, bf16[2048,384]{1,0:T(8,128)(2,1)} %get-tuple-element.50.q, bf16[2048,384]{1,0:T(8,128)(2,1)} %get-tuple-element.51.k, bf16[2048,384]{1,0:T(8,128)(2,1)} %get-tuple-element.52.v), custom_call_target="tpu_custom_call" | custom-call | flops 32999999488 | bytes 30000000 | tf_op jit(solution)/shard_map/attend/pallas_call | solution.py:417
  77.8 62.5 %feed_forward.1 = (bf16[1024,768]{1,0:T(8,128)(2,1)}, f32[1024,768]{1,0:T(8,128)}, f32[1024,768]{1,0:T(8,128)}, bf16[2048,384]{1,0:T(8,128)(2,1)}, f32[8,768]{1,...) custom-call(bf16[2048,768]{1,0:T(8,128)(2,1)} %tok.3, ...), custom_call_target="tpu_custom_call" | custom-call | flops 54999998464 | bytes 50000000 | tf_op jit(solution)/shard_map/feed_forward/pallas_call | solution.py:759
  140.3 1.4 collective-permute-start.4
  141.8 0.7 collective-permute-start.3
  142.5 0.7 collective-permute-start
  143.2 11.4 %collective-permute-start.1 = (bf16[3,192,384]{2,1,0:T(8,128)(2,1)}, bf16[3,192,384]{2,1,0:T(8,128)(2,1)S(1)}, u32[]{:S(2)}, u32[]{:S(2)}) collective-permute-start(bf16[3,192,384]{2,1,0:T(8,128)(2,1)} %get-tuple-element.68), channel_id=1, source_target_pairs={{0,16},{4,20},{8,24},{12,28},{1,17},{5,21},{9,25},{13,29},{2,18},{... | collective-permute-start | bytes 1327112 | tf_op jit(solution)/shard_map/ppermute | solution.py:1233
  154.6 1.3 collective-permute-start.2
  155.9 35.7 %attend_back.1 = (bf16[2048,384]{1,0:T(8,128)(2,1)}, bf16[2048,384]{1,0:T(8,128)(2,1)}, bf16[2048,384]{1,0:T(8,128)(2,1)}) custom-call(s32[8]{0:T(128)} %bitcast.10, bf16[2048,384]{1,0:T(8,128)(2,1)} %get-tuple-element.50.q, bf16[2048,384]{1,0:T(8,128)(2,1)} %get-tuple-element.51.k, bf16[2048,384]{1,0:T(8,128)(2,1)} %get-tuple-element.52.v, ...), custom_call_target="tpu_custom_call" | custom-call | flops 44000002048 | bytes 40000000 | tf_op jit(solution)/shard_map/attend_back/pallas_call | solution.py:498
  191.6 0.6 pad_add_fusion.place
  192.2 0.0 collective-permute-done.4.mid_send
  192.2 0.0 copy-start.6
  192.2 0.8 copy-done.6
  193.0 8.7 %qkv_grads.1 = (bf16[6,192,384]{2,1,0:T(8,128)(2,1)}, bf16[6,192,384]{2,1,0:T(8,128)(2,1)}) custom-call(s32[4]{0:T(128)} %pad_add_fusion.place, bf16[2048,768]{1,0:T(8,128)(2,1)} %get-tuple-element.70.norm, bf16[2048,384]{1,0:T(8,128)(2,1)} %get-tuple-element.59.dq, bf16[2048,384]{1,0:T(8,128)(2,1)} %get-tuple-element.60.dk, ...), custom_call_target="tpu_custom_call" | custom-call | flops 8800000000 | bytes 8000000 | tf_op jit(solution)/shard_map/qkv_grads/pallas_call | solution.py:845
  201.7 0.0 collective-permute-done.one
  201.7 0.0 copy-start.3
  201.7 0.0 collective-permute-done.1.two
  201.7 0.0 copy-start.4
  201.7 0.0 collective-permute-done.2.three
  201.7 0.0 copy-start.5
  201.7 0.0 collective-permute-done.3.far
  201.7 0.0 copy-start.2
  201.7 1.2 copy-done.2
  202.9 0.0 copy-start
  202.9 0.0 copy-start.1
  202.9 35.9 %last.1 = (bf16[2048,768]{1,0:T(8,128)(2,1)}, bf16[2048,768]{1,0:T(8,128)(2,1)}, f32[3,192,384]{2,1,0:T(8,128)}, f32[16,128]{1,0:T(8,128)}) custom-call(bf16[2048,384]{1,0:T(8,128)(2,1)} %get-tuple-element.59.dq, bf16[2048,384]{1,0:T(8,128)(2,1)} %get-tuple-element.60.dk, bf16[2048,384]{1,0:T(8,128)(2,1)} %get-tuple-element.61.dv, ...), custom_call_target="tpu_custom_call" | custom-call | flops 32999999488 | bytes 30000000 | tf_op jit(solution)/shard_map/last/pallas_call | solution.py:1109
  238.8 0.0 copy-done.3
  238.8 0.0 copy-done.4
  238.8 0.0 copy-done.5
  238.8 0.0 copy-done
  238.8 0.0 copy-done.1
  238.9 1.3 divide_subtract_fusion
  240.2 195.3 %renew.1 = (f32[1,6,192,192]{3,2,1,0:T(8,128)}, f32[1,6,192,192]{3,2,1,0:T(8,128)}, f32[1,6,192,192]{3,2,1,0:T(8,128)}, f32[1,6,192,192]{3,2,1,0:T(8,128)}, bf16...) custom-call(s32[4]{0:T(128)} %pad_add_fusion.place, f32[3,192,384]{2,1,0:T(8,128)} %get-tuple-element.77.late, ...), custom_call_target="tpu_custom_call" | custom-call | flops 5500000256 | bytes 5000000 | tf_op jit(solution)/shard_map/renew/pallas_call | solution.py:1196
Async XLA Ops:
  140.3 51.9 %collective-permute-start.4 = (bf16[3,192,384]{2,1,0:T(8,128)(2,1)}, bf16[3,192,384]{2,1,0:T(8,128)(2,1)S(1)}, u32[]{:S(2)}, u32[]{:S(2)}) collective-permute-start(bf16[3,192,384]{2,1,0:T(8,128)(2,1)} %get-tuple-element.71), channel_id=1, source_target_pairs={{0,4},{4,0},{8,12},{12,8},{16,20},{20,16},{24,28},{28,24},{1,5},{5... | collective-permute-start | bytes 1327112 | tf_op jit(solution)/shard_map/ppermute | solution.py:1228
  141.8 60.0 %collective-permute-start.3 = (bf16[1024,768]{1,0:T(8,128)(2,1)}, bf16[1024,768]{1,0:T(8,128)(2,1)S(1)}, u32[]{:S(2)}, u32[]{:S(2)}) collective-permute-start(bf16[1024,768]{1,0:T(8,128)(2,1)} %get-tuple-element.66.chip), channel_id=1, source_target_pairs={{0,2},{1,3},{2,0},{3,1},{4,6},{5,7},{6,4},{7,5},{8,10},{9,11},{10,... | collective-permute-start | bytes 4718600 | tf_op jit(solution)/shard_map/ppermute | solution.py:1224
  142.5 59.2 %collective-permute-start = (bf16[3,192,384]{2,1,0:T(8,128)(2,1)}, bf16[3,192,384]{2,1,0:T(8,128)(2,1)S(1)}, u32[]{:S(2)}, u32[]{:S(2)}) collective-permute-start(bf16[3,192,384]{2,1,0:T(8,128)(2,1)} %get-tuple-element.67), channel_id=1, source_target_pairs={{8,16},{12,20},{16,24},{20,28},{9,17},{13,21},{17,25},{21,29},{10,... | collective-permute-start | bytes 1327112 | tf_op jit(solution)/shard_map/ppermute | solution.py:1233
  143.2 58.5 %collective-permute-start.1 = (bf16[3,192,384]{2,1,0:T(8,128)(2,1)}, bf16[3,192,384]{2,1,0:T(8,128)(2,1)S(1)}, u32[]{:S(2)}, u32[]{:S(2)}) collective-permute-start(bf16[3,192,384]{2,1,0:T(8,128)(2,1)} %get-tuple-element.68), channel_id=1, source_target_pairs={{0,16},{4,20},{8,24},{12,28},{1,17},{5,21},{9,25},{13,29},{2,18},{... | collective-permute-start | bytes 1327112 | tf_op jit(solution)/shard_map/ppermute | solution.py:1233
  154.6 47.1 %collective-permute-start.2 = (bf16[3,192,384]{2,1,0:T(8,128)(2,1)}, bf16[3,192,384]{2,1,0:T(8,128)(2,1)S(1)}, u32[]{:S(2)}, u32[]{:S(2)}) collective-permute-start(bf16[3,192,384]{2,1,0:T(8,128)(2,1)} %get-tuple-element.69), channel_id=1, source_target_pairs={{0,24},{4,28},{24,16},{28,20},{1,25},{5,29},{25,17},{29,21},{2,26}... | collective-permute-start | bytes 1327112 | tf_op jit(solution)/shard_map/ppermute | solution.py:1233
  192.2 0.8 copy-start.6
  201.7 37.1 %copy-start.3 = (bf16[3,192,384]{2,1,0:T(8,128)(2,1)}, bf16[3,192,384]{2,1,0:T(8,128)(2,1)S(1)}, u32[]{:S(2)}) copy-start(bf16[3,192,384]{2,1,0:T(8,128)(2,1)S(1)} %collective-permute-done.one) | copy-start | bytes 1327108
  201.7 37.1 %copy-start.4 = (bf16[3,192,384]{2,1,0:T(8,128)(2,1)}, bf16[3,192,384]{2,1,0:T(8,128)(2,1)S(1)}, u32[]{:S(2)}) copy-start(bf16[3,192,384]{2,1,0:T(8,128)(2,1)S(1)} %collective-permute-done.1.two) | copy-start | bytes 1327108
  201.7 37.1 %copy-start.5 = (bf16[3,192,384]{2,1,0:T(8,128)(2,1)}, bf16[3,192,384]{2,1,0:T(8,128)(2,1)S(1)}, u32[]{:S(2)}) copy-start(bf16[3,192,384]{2,1,0:T(8,128)(2,1)S(1)} %collective-permute-done.2.three) | copy-start | bytes 1327108
  201.7 1.2 copy-start.2
  202.9 35.9 %copy-start = (f32[9,96]{1,0:T(8,128)S(1)}, f32[9,96]{1,0:T(8,128)}, u32[]{:S(2)}) copy-start(f32[9,96]{1,0:T(8,128)} %vec_own.1) | copy-start | bytes 10372
  202.9 35.9 %copy-start.1 = (f32[9,96]{1,0:T(8,128)S(1)}, f32[9,96]{1,0:T(8,128)}, u32[]{:S(2)}) copy-start(f32[9,96]{1,0:T(8,128)} %param.17) | copy-start | bytes 10372

commit v9 on v8

--- a/solution.py
+++ b/solution.py
@@ -810,79 +810,36 @@
     )(tokens, passes, vec, mine, cotangent, pairs, wo_other, pairs, pairs)
 
 
-def qkv_grads_kernel(place, norm, dq, dk, dv, mid_send, mid_keep, g_send, g_keep, acc):
-    i = pl.program_id(0)
-
-    @pl.when(i == 0)
-    def _():
-        acc[...] = jnp.zeros_like(acc)
-
-    mine = [jnp.where(place[1] == 0, grad[:, :SIDE], grad[:, SIDE:]) for grad in (dq, dk, dv)]
-    acc[...] += tn(jnp.concatenate(mine, axis=1), norm[...])
-
-    @pl.when(i == pl.num_programs(0) - 1)
-    def _():
-        for m in range(3):
-            g_send[3 + m] = mid_send[m]
-            g_keep[3 + m] = mid_keep[m]
-        for x in range(3):
-            for m in range(2):
-                value = acc[x * SIDE : (x + 1) * SIDE, m * PAIR : (m + 1) * PAIR].astype(bf16)
-                slot, column = (2 * x + m) % 3, (2 * x + m) // 3
-
-                @pl.when(place[2] == column)
-                def _():
-                    g_keep[slot] = value
-
-                @pl.when(place[2] != column)
-                def _():
-                    g_send[slot] = value
-
-
-def qkv_grads(place, norm, dq, dk, dv, mid_send, mid_keep):
-    seq = norm.shape[0]
-    row = lambda n: pl.BlockSpec((WIDE, n), lambda i, s: (i, 0))
-    return pl.pallas_call(
-        qkv_grads_kernel,
-        grid_spec=pltpu.PrefetchScalarGridSpec(
-            num_scalar_prefetch=1,
-            grid=(seq // WIDE,),
-            in_specs=[row(D), row(PAIR), row(PAIR), row(PAIR)] + [full((3, SIDE, PAIR))] * 2,
-            out_specs=[full((6, SIDE, PAIR)), full((6, SIDE, PAIR))],
-            scratch_shapes=[pltpu.VMEM((3 * SIDE, D), f32)],
-        ),
-        out_shape=[jax.ShapeDtypeStruct((6, SIDE, PAIR), bf16)] * 2,
-        compiler_params=params(),
-        cost_estimate=cost(8),
-        name="qkv_grads",
-    )(place, norm, dq, dk, dv, mid_send, mid_keep)
-
-
 CHUNK = SIDE // 2
 CHUNKS = 12
 TAKEN = (
-    ((8, 4), (9, 12)),
-    ((5, 1), (6, 3), (7, 4), (8, 7), (9, 12)),
-    ((3, 1), (4, 3), (5, 4), (6, 5), (7, 6), (8, 9), (9, 12)),
-    ((1, 2), (2, 3), (3, 5), (4, 6), (5, 8), (6, 10), (7, 12)),
+    ((12, 12),),
+    ((4, 1), (5, 2), (6, 3), (7, 5), (8, 6), (10, 7), (11, 8), (12, 12)),
+    ((2, 1), (3, 2), (4, 4), (5, 5), (6, 6), (8, 7), (9, 8), (10, 9), (11, 11), (12, 12)),
+    ((0, 2), (1, 4), (2, 6), (6, 7), (7, 8), (8, 10), (9, 11), (10, 12)),
 )
+GRAD_STEPS = 4
 
 
 def last_kernel(
-    small, dq, dk, dv, cat, tok, pas, vec, grad_second, sums_two, second, chip, far, g_send, g_keep, output, input_grad, *rest
+    small, norm, dq_wide, dk_wide, dv_wide, dq, dk, dv, cat, tok, pas, vec, grad_second, sums_two, second, chip, far,
+    mid_near, mid_keep, output, input_grad, *rest,
 ):
     if small:
         late, vec_sum = rest[:2]
         rest = rest[2:]
         (
-            core_out, core_in, sums, core_sums, x_in, z_in, z_out, up_in, v_out, v_in,
-            s_core, r_core, s_sum, r_sum, s_x, r_x, s_z, r_z, s_up, r_up, s_v, r_v, ready, s_own, s_res, r_res,
+            core_out, core_in, sums, core_sums, x_in, z_in, z_out, up_in, v_out, v_in, total,
+            s_core, r_core, s_sum, r_sum, s_x, r_x, s_z, r_z, s_up, r_up, s_v, r_v, ready, acc, g_send, g_keep,
+            s_own, s_res, r_res,
         ) = rest
     else:
         (
-            vec_sum, core_out, core_in, sums, core_sums, s_core, r_core, s_sum, r_sum, ready, s_own, s_res, r_res,
+            vec_sum, send_out, keep_out, core_out, core_in, sums, core_sums, s_core, r_core, s_sum, r_sum, ready, acc,
+            g_send, g_keep, s_own, s_res, r_res,
         ) = rest
-    i = pl.program_id(0)
+    step = pl.program_id(0)
+    i = step - GRAD_STEPS
     half = core_out.shape[0]
     t, dp = lax.axis_index("tensor"), lax.axis_index("dp")
     core, side = t % 2, t // 2
@@ -917,7 +874,7 @@
     v_copy = lambda n: copy(v_out.at[peers[n]], v_in.at[dp], s_v.at[n], r_v.at[dp], {"dp": peers[n]})
     barrier = pltpu.get_barrier_semaphore()
 
-    @pl.when(i == 0)
+    @pl.when(step == 0)
     def _():
         pl.semaphore_signal(barrier, inc=1, device_id={"tensor": near}, device_id_type=MESH)
         if small:
@@ -926,12 +883,36 @@
             late[...] = jnp.zeros_like(late)
         sums[...] = jnp.zeros_like(sums)
         sums[PASSES + 2 : PASSES + 4] = sums_two[0:2]
+        acc[...] = jnp.zeros_like(acc)
         pl.semaphore_wait(barrier, 8 if small else 1)
+
+    @pl.when(step < GRAD_STEPS)
+    def _():
+        mine = [jnp.where(side == 0, grad[:, :SIDE], grad[:, SIDE:]) for grad in (dq_wide, dk_wide, dv_wide)]
+        acc[...] += tn(jnp.concatenate(mine, axis=1), norm[...])
+
+    @pl.when(step == GRAD_STEPS - 1)
+    def _():
+        for n in range(3):
+            for m in range(2):
+                value = acc[n * SIDE : (n + 1) * SIDE, m * PAIR : (m + 1) * PAIR].astype(bf16)
+                slot, place = (2 * n + m) % 3, (2 * n + m) // 3
+
+                @pl.when(column == place)
+                def _():
+                    g_keep[slot] = value
+
+                @pl.when(column != place)
+                def _():
+                    g_send[slot] = value
         if small:
             for k in range(6):
                 x_copy(k).start()
-
-    @pl.when(i < 2 * half)
+        else:
+            send_out[...] = g_send[...]
+            keep_out[...] = g_keep[...]
+
+    @pl.when((i >= 0) & (i < 2 * half))
     def _():
         part = nt(dq[...], cat[0]) + nt(dk[...], cat[1]) + nt(dv[...], cat[2])
 
@@ -984,25 +965,26 @@
             @pl.when(jnp.asarray(k) < 6)
             def _():
                 x_copy(k).wait_recv()
+                total[...] = g_keep[k // 2, rows, :].astype(f32) + x_in[k].astype(f32)
 
             @pl.when(jnp.asarray(k) >= 6)
             def _():
-                x_in[k] = g_send[k // 2, rows, :]
-
-            return g_keep[k // 2, rows, :].astype(f32) + x_in[k].astype(f32)
+                total[...] = mid_keep[k // 2 - 3, rows, :].astype(f32) + mid_near[k // 2 - 3, rows, :].astype(f32)
+
+            return total[...]
 
         def keep_late(k, pair, total):
             late[pair, pl.ds(pl.multiple_of((k % 2) * CHUNK, 16), CHUNK), :] = total
 
         def pass_on(k):
-            total = term_of(k)
+            term = term_of(k)
 
             @pl.when(z < 3)
             def _():
                 z_copy(k).wait_recv()
 
             below = jnp.where(z < 3, z_in[k].astype(f32), 0.0)
-            passed = total + below
+            passed = term + below
 
             @pl.when((z > 1) | ((z == 1) & (k < 6)))
             def _():
@@ -1019,7 +1001,7 @@
                 keep_late(k, k // 2 - 3, passed + up_in[k - 6].astype(f32))
 
         def at_position(p, carry):
-            k = jnp.where(p < 2, p + 6, jnp.where(p < 8, p - 2, p))
+            k = jnp.where(p < 6, p + 6, p - 6)
 
             @pl.when((z > 0) | (k < 6))
             def _():
@@ -1030,17 +1012,17 @@
         begin, end = jnp.int32(0), jnp.int32(0)
         for place, line in enumerate(TAKEN):
             for at, upto in line:
-                begin = jnp.where((z == place) & (i > at), upto, begin)
-                end = jnp.where((z == place) & (i >= at), upto, end)
+                begin = jnp.where((z == place) & (step > at), upto, begin)
+                end = jnp.where((z == place) & (step >= at), upto, end)
         lax.fori_loop(begin, end, at_position, 0)
 
-        @pl.when((i == 1) & (z == 0))
+        @pl.when((step == 0) & (z == 0))
         def _():
             for k in range(6, CHUNKS):
                 z_out[k] = term_of(k).astype(bf16)
                 up_copy(k).start()
 
-    @pl.when(i == pl.num_programs(0) - 1)
+    @pl.when(step == pl.num_programs(0) - 1)
     def _():
         for j in range(half):
             core_copy(j).wait_send()
@@ -1069,17 +1051,19 @@
 
 
 def last(
-    small, dq, dk, dv, cat, tokens, passes, vec, grad_second, sums_two, second, chip, far, g_send, g_keep
+    small, norm, dq, dk, dv, cat, tokens, passes, vec, grad_second, sums_two, second, chip, far, mid_near, mid_keep
 ):
     seq = dq.shape[0]
     half = seq // ROWS // 2
     core = lambda: lax.axis_index("tensor") % 2
 
     def block(i):
-        work = jnp.minimum(i, 2 * half - 1)
+        work = jnp.clip(i - GRAD_STEPS, 0, 2 * half - 1)
         return lax.rem(work + (1 - core()) * half, 2 * half)
 
-    own = lambda i: jnp.clip(i - half, 0, half - 1)
+    own = lambda i: jnp.clip(i - GRAD_STEPS - half, 0, half - 1)
+    tall = seq // GRAD_STEPS
+    wide = lambda n: pl.BlockSpec((tall, n), lambda i: (jnp.minimum(i, GRAD_STEPS - 1), 0))
     row = pl.BlockSpec((ROWS, PAIR), lambda i: (block(i), 0))
     mine = pl.BlockSpec((ROWS, D), lambda i: (own(i), 0))
     dma = pltpu.SemaphoreType.DMA
@@ -1100,16 +1084,21 @@
         ]
         scratch += [pltpu.VMEM((CHUNKS, CHUNK, PAIR), bf16)] * 3
         scratch += [pltpu.VMEM((6, CHUNK, PAIR), bf16)]
-        scratch += [pltpu.VMEM((8, 16, 128), f32)] * 2
+        scratch += [pltpu.VMEM((8, 16, 128), f32)] * 2 + [pltpu.VMEM((CHUNK, PAIR), f32)]
         sems += [dma((6,))] * 2 + [dma((CHUNKS,))] * 2 + [dma((6,))] * 2 + [dma((7,)), dma((8,))]
     else:
-        out_specs += [full((16, D))]
-        out_shape += [jax.ShapeDtypeStruct((16, D), f32)]
-    scratch_more = [pltpu.VMEM((2, half, ROWS, D), bf16)] + [dma((2, half))] * 3
+        out_specs += [full((16, D)), full((3, SIDE, PAIR)), full((3, SIDE, PAIR))]
+        out_shape += [jax.ShapeDtypeStruct((16, D), f32)] + [jax.ShapeDtypeStruct((3, SIDE, PAIR), bf16)] * 2
+    scratch_more = [pltpu.VMEM((2, half, ROWS, D), bf16), pltpu.VMEM((3 * SIDE, D), f32)]
+    scratch_more += [pltpu.VMEM((3, SIDE, PAIR), bf16)] * 2 + [dma((2, half))] * 3
     return pl.pallas_call(
         functools.partial(last_kernel, small),
-        grid=(2 * half + 2,),
+        grid=(GRAD_STEPS + 2 * half + 2,),
         in_specs=[
+            wide(D),
+            wide(PAIR),
+            wide(PAIR),
+            wide(PAIR),
             row,
             row,
             row,
@@ -1122,16 +1111,16 @@
             mine,
             mine,
             mine,
-            full(g_send.shape),
-            full(g_keep.shape),
+            full(mid_near.shape),
+            full(mid_keep.shape),
         ],
         out_specs=out_specs,
         out_shape=out_shape,
         scratch_shapes=scratch + sems + scratch_more,
         compiler_params=params(collective_id=2, has_side_effects=True),
-        cost_estimate=cost(30),
+        cost_estimate=cost(38),
         name="last",
-    )(dq, dk, dv, cat, tokens, passes, vec, grad_second, sums_two, second, chip, far, g_send, g_keep)
+    )(norm, dq, dk, dv, dq, dk, dv, cat, tokens, passes, vec, grad_second, sums_two, second, chip, far, mid_near, mid_keep)
 
 
 def precondition(grad, weight, left, right, left_root, right_root):
@@ -1157,57 +1146,43 @@
 
 
 def renew_kernel(
-    place, late, own, one, two, three, weight, left, right, left_root, right_root, output, input_grad,
-    left_new, right_new, step, new, output_new, input_grad_new, sems,
+    late, own, one, two, three, weight, left, right, left_root, right_root, output, input_grad,
+    left_new, right_new, step, new, output_new, input_grad_new,
 ):
-    i = pl.program_id(0)
-    copies = [
-        pltpu.make_async_copy(output, output_new, sems.at[0]),
-        pltpu.make_async_copy(input_grad, input_grad_new, sems.at[1]),
-    ]
-
-    @pl.when(i == 0)
-    def _():
-        for copy in copies:
-            copy.start()
-
-    early = own[0].astype(f32) + one[0].astype(f32) + two[0].astype(f32) + three[0].astype(f32)
-    z = place[3]
-    both = late[0] + jnp.where(z > 1, early, 0.0)
-    for n in range(2):
-        grad = both[:, n * SIDE : (n + 1) * SIDE]
-        grad = two_part(jnp.where(z == 0, grad.T, grad))
-        left_new[0, n] = decay * left[0, n] + (1.0 - decay) * dot_three(nt, grad, grad)
-        right_new[0, n] = decay * right[0, n] + (1.0 - decay) * dot_three(tn, grad, grad)
-        half = dot_three(nn, two_part(left_root[0, n]), grad)
-        value = dot_three(nn, two_part(half), two_part(right_root[0, n]))
-        step[0, n] = value
-        new[0, n] = weight[0, n] - rate_matrix * value
-
-    @pl.when(i == pl.num_programs(0) - 1)
-    def _():
-        for copy in copies:
-            copy.wait()
-
-
-def renew(place, late, own, far, weight, left, right, left_root, right_root, output, input_grad):
-    pair = pl.BlockSpec((1, SIDE, PAIR), lambda i, s: (i, 0, 0))
-    slot = pl.BlockSpec((1, 2, SIDE, SIDE), lambda i, s: (0, i, 0, 0))
+    output_new[...] = output[...]
+    input_grad_new[...] = input_grad[...]
+
+    @pl.when(pl.program_id(0) < 3)
+    def _():
+        early = own[0].astype(f32) + one[0].astype(f32) + two[0].astype(f32) + three[0].astype(f32)
+        z = lax.axis_index("dp") // 2
+        both = late[0] + jnp.where(z > 1, early, 0.0)
+        for n in range(2):
+            grad = both[:, n * SIDE : (n + 1) * SIDE]
+            grad = two_part(jnp.where(z == 0, grad.T, grad))
+            left_new[0, n] = decay * left[0, n] + (1.0 - decay) * dot_three(nt, grad, grad)
+            right_new[0, n] = decay * right[0, n] + (1.0 - decay) * dot_three(tn, grad, grad)
+            half = dot_three(nn, two_part(left_root[0, n]), grad)
+            value = dot_three(nn, two_part(half), two_part(right_root[0, n]))
+            step[0, n] = value
+            new[0, n] = weight[0, n] - rate_matrix * value
+
+
+def renew(late, own, far, weight, left, right, left_root, right_root, output, input_grad):
+    pair = pl.BlockSpec((1, SIDE, PAIR), lambda i: (jnp.minimum(i, 2), 0, 0))
+    slot = pl.BlockSpec((1, 2, SIDE, SIDE), lambda i: (0, jnp.minimum(i, 2), 0, 0))
+    rows = pl.BlockSpec((output.shape[0] // 4, D), lambda i: (i, 0))
     return pl.pallas_call(
         renew_kernel,
-        grid_spec=pltpu.PrefetchScalarGridSpec(
-            num_scalar_prefetch=1,
-            grid=(3,),
-            in_specs=[pair] * 5 + [slot] * 5 + [pl.BlockSpec(memory_space=pltpu.HBM)] * 2,
-            out_specs=[slot] * 4 + [pl.BlockSpec(memory_space=pltpu.HBM)] * 2,
-            scratch_shapes=[pltpu.SemaphoreType.DMA((2,))],
-        ),
+        grid=(4,),
+        in_specs=[pair] * 5 + [slot] * 5 + [rows] * 2,
+        out_specs=[slot] * 4 + [rows] * 2,
         out_shape=[jax.ShapeDtypeStruct(weight.shape, f32)] * 4
         + [jax.ShapeDtypeStruct(value.shape, value.dtype) for value in (output, input_grad)],
-        compiler_params=params(56),
-        cost_estimate=cost(5),
+        compiler_params=params(),
+        cost_estimate=cost(8),
         name="renew",
-    )(place, late, own, *far, weight, left, right, left_root, right_root, output, input_grad)
+    )(late, own, *far, weight, left, right, left_root, right_root, output, input_grad)
 
 
 def to_pairs(blocks):
@@ -1255,7 +1230,6 @@
     n_dp = lax.axis_size("dp")
     small = n_dp == 8
     z, column = (dp // 2, dp % 2) if small else (0, 0)
-    place = jnp.stack([core, side, jnp.asarray(column), jnp.asarray(z)]).astype(jnp.int32)
     lens = doc_lengths[0]
     seq = tokens.shape[0]
     passes = pass_ids.reshape(1, seq)
@@ -1282,21 +1256,21 @@
         far = [hop_z(ends[turn], turn, (2, 3)) for turn in (1, 2, 3)]
         mid_send = hop_x(mid_send)
     dq, dk, dv = attend_back(lens, q, k, v, mine, lse, grad_mixed)
-    g_send, g_keep = qkv_grads(place, norm, dq, dk, dv, mid_send, mid_keep)
     if small:
-        *far, out_far, g_send = tie(*far, out_far, g_send)
+        *far, out_far, mid_send, dq = tie(*far, out_far, mid_send, dq)
     output, input_grad, *sums = last(
-        small, dq, dk, dv, cat, tokens, passes, vec, grad_second, sums_two, second, out_chip, out_far, g_send, g_keep
+        small, norm, dq, dk, dv, cat, tokens, passes, vec, grad_second, sums_two, second, out_chip, out_far,
+        mid_send, mid_keep,
     )
     if small:
         late, vector_sum = sums
         left_new, right_new, step, weight_new, output, input_grad = renew(
-            place, late, ends[0], far, block_weights, block_left, block_right, block_left_root, block_right_root,
+            late, ends[0], far, block_weights, block_left, block_right, block_left_root, block_right_root,
             output, input_grad,
         )
         vector_grad = vector_sum[: PASSES + 4, : vector_params.shape[1]]
     else:
-        vector_part = sums[0][: PASSES + 4]
+        vector_part, g_send, g_keep = sums[0][: PASSES + 4], *sums[1:]
         send, keep = ends
         rest = jnp.stack(
             [
@@ -1305,7 +1279,7 @@
             ],
             axis=1,
         )
-        grad_qkv = from_pairs(jnp.concatenate([g_keep[:3], g_send[:3]], axis=0)).swapaxes(1, 2)
+        grad_qkv = from_pairs(jnp.concatenate([g_keep, g_send], axis=0)).swapaxes(1, 2)
         grad_rest = from_pairs(rest.reshape(18, SIDE, PAIR))
         spare = jnp.zeros((slots - total_blocks, SIDE, SIDE), bf16)
         grad_blocks = jnp.concatenate([grad_qkv, grad_rest, spare], axis=0)[None].astype(f32)

time: 436 us -> 249 us (0.57)
  Pallas kernels: 415 us -> 228 us
    pallas_call x3 -> x2, Pallas kernels: 240 us -> 54.7 us  [the longest x1 43.3 us: last(): pl.pallas_call(functools.partial(last_kernel, small), grid=(GRAD_STEPS +...]
  transfers between devices with their start and end apart: 5 -> 5, of which waited for: 0 -> 0; matrix products, arithmetic and copies ran while one was open for 0% -> 0% of each run, Pallas kernels for 10% -> 14%
where the time goes in v9:
time: 249 us; the launch traced here: 248 us
  Pallas kernels  228 us (92%)
  starting transfers between devices  16.6 us (7%)
    pallas_call x1, Pallas kernels, feed(): pl.pallas_call(functools.partial(feed_kernel, small), grid=(3 * half + 1,...  62.6 us
    pallas_call x1, Pallas kernels, gather(): pl.pallas_call(gather_kernel, in_specs=[vmem, vmem, far, vmem], out_specs...  52.3 us
    pallas_call x1, Pallas kernels, last(): pl.pallas_call(functools.partial(last_kernel, small), grid=(GRAD_STEPS +...  43.3 us
    pallas_call x1, Pallas kernels, attend_back(): pl.pallas_call(attend_back_kernel, grid_spec=pltpu.PrefetchScalarGridSpec...  34.5 us
    pallas_call x1, Pallas kernels, attend(): pl.pallas_call(attend_kernel, grid_spec=pltpu.PrefetchScalarGridSpec(num_...  24 us
    ppermute x3, starting transfers between devices, hop_z(): return lax.ppermute(value, 'dp', pairs)  14.6 us
    pallas_call x1, Pallas kernels, renew(): pl.pallas_call(renew_kernel, grid=(4,), in_specs=[pair] * 5 + [slot] * 5...  11.4 us
  transfers between devices with their start and end apart: 5, of which 0 were waited for; matrix products, arithmetic and copies ran while one was open for 0% of the time, Pallas kernels for 14%

profile of v9, /device:TPU:0, one launch (start us, length us, event | category | flops | bytes accessed | tf_op | source)
XLA Modules:
  0.0 248.4 jit_solution(15155635594424730881)
XLA Ops:
  0.6 52.3 %gather.1 = (bf16[2,24,192,384]{3,2,1,0:T(8,128)(2,1)}, bf16[2,2,192,384]{3,2,1,0:T(8,128)(2,1)}, f32[16,768]{1,0:T(8,128)}, bf16[2048,768]{1,0:T(8,128)(2,1)}, ...) custom-call(f32[1,6,192,192]{3,2,1,0:T(8,128)} %weight.1, ...), custom_call_target="tpu_custom_call" | custom-call | flops 65999998976 | bytes 60000000 | tf_op jit(solution)/shard_map/gather/pallas_call | solution.py:279
  52.9 24.0 %attend.1 = (bf16[2048,384]{1,0:T(8,128)(2,1)}, f32[8,2048]{1,0:T(8,128)}) custom-call(s32[8]{0:T(128)} %bitcast.5, bf16[2048,384]{1,0:T(8,128)(2,1)} %get-tuple-element.51.q, bf16[2048,384]{1,0:T(8,128)(2,1)} %get-tuple-element.52.k, bf16[2048,384]{1,0:T(8,128)(2,1)} %get-tuple-element.53.v), custom_call_target="tpu_custom_call" | custom-call | flops 32999999488 | bytes 30000000 | tf_op jit(solution)/shard_map/attend/pallas_call | solution.py:417
  76.9 62.6 %feed_forward.1 = (bf16[1024,768]{1,0:T(8,128)(2,1)}, f32[1024,768]{1,0:T(8,128)}, f32[1024,768]{1,0:T(8,128)}, bf16[2048,384]{1,0:T(8,128)(2,1)}, f32[8,768]{1,...) custom-call(bf16[2048,768]{1,0:T(8,128)(2,1)} %tok.3, ...), custom_call_target="tpu_custom_call" | custom-call | flops 54999998464 | bytes 50000000 | tf_op jit(solution)/shard_map/feed_forward/pallas_call | solution.py:759
  139.5 0.7 collective-permute-start
  140.2 12.5 %collective-permute-start.1 = (bf16[3,192,384]{2,1,0:T(8,128)(2,1)}, bf16[3,192,384]{2,1,0:T(8,128)(2,1)S(1)}, u32[]{:S(2)}, u32[]{:S(2)}) collective-permute-start(bf16[3,192,384]{2,1,0:T(8,128)(2,1)} %get-tuple-element.58), channel_id=1, source_target_pairs={{0,16},{4,20},{8,24},{12,28},{1,17},{5,21},{9,25},{13,29},{2,18},{... | collective-permute-start | bytes 1327112 | tf_op jit(solution)/shard_map/ppermute | solution.py:1208
  152.8 1.3 collective-permute-start.2
  154.1 0.7 collective-permute-start.4
  154.8 1.4 collective-permute-start.3
  156.2 34.5 %attend_back.1 = (bf16[2048,384]{1,0:T(8,128)(2,1)}, bf16[2048,384]{1,0:T(8,128)(2,1)}, bf16[2048,384]{1,0:T(8,128)(2,1)}) custom-call(s32[8]{0:T(128)} %bitcast.6, bf16[2048,384]{1,0:T(8,128)(2,1)} %get-tuple-element.51.q, bf16[2048,384]{1,0:T(8,128)(2,1)} %get-tuple-element.52.k, bf16[2048,384]{1,0:T(8,128)(2,1)} %get-tuple-element.53.v, ...), custom_call_target="tpu_custom_call" | custom-call | flops 44000002048 | bytes 40000000 | tf_op jit(solution)/shard_map/attend_back/pallas_call | solution.py:498
  190.8 0.0 collective-permute-done.one
  190.8 0.0 copy-start.3
  190.8 0.0 collective-permute-done.1.two
  190.8 0.0 copy-start.4
  190.8 0.0 collective-permute-done.2.three
  190.8 0.0 copy-start.5
  190.8 0.0 collective-permute-done.4.mid_near
  190.8 0.0 copy-start.6
  190.8 0.0 collective-permute-done.3.far
  190.9 0.0 copy-start.2
  190.9 0.8 copy-done.6
  191.7 0.5 copy-done.2
  192.2 0.0 copy-start
  192.2 0.0 copy-start.1
  192.2 43.3 %last.1 = (bf16[2048,768]{1,0:T(8,128)(2,1)}, bf16[2048,768]{1,0:T(8,128)(2,1)}, f32[3,192,384]{2,1,0:T(8,128)}, f32[16,128]{1,0:T(8,128)}) custom-call(bf16[2048,768]{1,0:T(8,128)(2,1)} %get-tuple-element.49.norm, bf16[2048,384]{1,0:T(8,128)(2,1)} %get-tuple-element.65.dq_wide.dq, bf16[2048,384]{1,0:T(8,128)(2,1)} %get-tuple-element.66.dk_wide.dk, ...), custom_call_target="tpu_custom_call" | custom-call | flops 41799999488 | bytes 38000000 | tf_op jit(solution)/shard_map/last/pallas_call | solution.py:1094
  235.5 0.0 copy-done.3
  235.5 0.0 copy-done.4
  235.5 0.0 copy-done.5
  235.5 0.0 copy-done
  235.5 0.0 copy-done.1
  235.5 1.3 divide_subtract_fusion
  236.8 11.4 %renew.1 = (f32[1,6,192,192]{3,2,1,0:T(8,128)}, f32[1,6,192,192]{3,2,1,0:T(8,128)}, f32[1,6,192,192]{3,2,1,0:T(8,128)}, f32[1,6,192,192]{3,2,1,0:T(8,128)}, bf16...) custom-call(f32[3,192,384]{2,1,0:T(8,128)} %get-tuple-element.75.late, bf16[3,192,384]{2,1,0:T(8,128)(2,1)} %get-tuple-element.76.own, ...), custom_call_target="tpu_custom_call" | custom-call | flops 8800000000 | bytes 8000000 | tf_op jit(solution)/shard_map/renew/pallas_call | solution.py:1175
Async XLA Ops:
  139.5 51.2 %collective-permute-start = (bf16[3,192,384]{2,1,0:T(8,128)(2,1)}, bf16[3,192,384]{2,1,0:T(8,128)(2,1)S(1)}, u32[]{:S(2)}, u32[]{:S(2)}) collective-permute-start(bf16[3,192,384]{2,1,0:T(8,128)(2,1)} %get-tuple-element.57), channel_id=1, source_target_pairs={{8,16},{12,20},{16,24},{20,28},{9,17},{13,21},{17,25},{21,29},{10,... | collective-permute-start | bytes 1327112 | tf_op jit(solution)/shard_map/ppermute | solution.py:1208
  140.2 50.5 %collective-permute-start.1 = (bf16[3,192,384]{2,1,0:T(8,128)(2,1)}, bf16[3,192,384]{2,1,0:T(8,128)(2,1)S(1)}, u32[]{:S(2)}, u32[]{:S(2)}) collective-permute-start(bf16[3,192,384]{2,1,0:T(8,128)(2,1)} %get-tuple-element.58), channel_id=1, source_target_pairs={{0,16},{4,20},{8,24},{12,28},{1,17},{5,21},{9,25},{13,29},{2,18},{... | collective-permute-start | bytes 1327112 | tf_op jit(solution)/shard_map/ppermute | solution.py:1208
  152.8 38.0 %collective-permute-start.2 = (bf16[3,192,384]{2,1,0:T(8,128)(2,1)}, bf16[3,192,384]{2,1,0:T(8,128)(2,1)S(1)}, u32[]{:S(2)}, u32[]{:S(2)}) collective-permute-start(bf16[3,192,384]{2,1,0:T(8,128)(2,1)} %get-tuple-element.59), channel_id=1, source_target_pairs={{0,24},{4,28},{24,16},{28,20},{1,25},{5,29},{25,17},{29,21},{2,26}... | collective-permute-start | bytes 1327112 | tf_op jit(solution)/shard_map/ppermute | solution.py:1208
  154.1 36.7 %collective-permute-start.4 = (bf16[3,192,384]{2,1,0:T(8,128)(2,1)}, bf16[3,192,384]{2,1,0:T(8,128)(2,1)S(1)}, u32[]{:S(2)}, u32[]{:S(2)}) collective-permute-start(bf16[3,192,384]{2,1,0:T(8,128)(2,1)} %get-tuple-element.61), channel_id=1, source_target_pairs={{0,4},{4,0},{8,12},{12,8},{16,20},{20,16},{24,28},{28,24},{1,5},{5... | collective-permute-start | bytes 1327112 | tf_op jit(solution)/shard_map/ppermute | solution.py:1203
  154.8 36.0 %collective-permute-start.3 = (bf16[1024,768]{1,0:T(8,128)(2,1)}, bf16[1024,768]{1,0:T(8,128)(2,1)S(1)}, u32[]{:S(2)}, u32[]{:S(2)}) collective-permute-start(bf16[1024,768]{1,0:T(8,128)(2,1)} %get-tuple-element.60.chip), channel_id=1, source_target_pairs={{0,2},{1,3},{2,0},{3,1},{4,6},{5,7},{6,4},{7,5},{8,10},{9,11},{10,... | collective-permute-start | bytes 4718600 | tf_op jit(solution)/shard_map/ppermute | solution.py:1199
  190.8 44.7 %copy-start.3 = (bf16[3,192,384]{2,1,0:T(8,128)(2,1)}, bf16[3,192,384]{2,1,0:T(8,128)(2,1)S(1)}, u32[]{:S(2)}) copy-start(bf16[3,192,384]{2,1,0:T(8,128)(2,1)S(1)} %collective-permute-done.one) | copy-start | bytes 1327108
  190.8 44.7 %copy-start.4 = (bf16[3,192,384]{2,1,0:T(8,128)(2,1)}, bf16[3,192,384]{2,1,0:T(8,128)(2,1)S(1)}, u32[]{:S(2)}) copy-start(bf16[3,192,384]{2,1,0:T(8,128)(2,1)S(1)} %collective-permute-done.1.two) | copy-start | bytes 1327108
  190.8 44.7 %copy-start.5 = (bf16[3,192,384]{2,1,0:T(8,128)(2,1)}, bf16[3,192,384]{2,1,0:T(8,128)(2,1)S(1)}, u32[]{:S(2)}) copy-start(bf16[3,192,384]{2,1,0:T(8,128)(2,1)S(1)} %collective-permute-done.2.three) | copy-start | bytes 1327108
  190.8 0.9 copy-start.6
  190.9 1.3 copy-start.2
  192.2 43.3 %copy-start = (f32[9,96]{1,0:T(8,128)S(1)}, f32[9,96]{1,0:T(8,128)}, u32[]{:S(2)}) copy-start(f32[9,96]{1,0:T(8,128)} %vec_own.1) | copy-start | bytes 10372
  192.2 43.3 %copy-start.1 = (f32[9,96]{1,0:T(8,128)S(1)}, f32[9,96]{1,0:T(8,128)}, u32[]{:S(2)}) copy-start(f32[9,96]{1,0:T(8,128)} %param.17) | copy-start | bytes 10372

commit v10 on v9

--- a/solution.py
+++ b/solution.py
@@ -158,6 +158,7 @@
         send(pack.at[m], at_z(0, m), s_l.at[0, m], r_l.at[0, m], to_left, z > 0)
     for n, peer in enumerate(peers):
         send(vec_pack, vec_land.at[dp], s_v.at[n], r_v.at[dp], {"dp": peer})
+    send(pack.at[0], at_z(0, 0), s_r.at[0, 0], r_r.at[0, 0], to_right, z == 2)
     for m in range(3):
         send(pack.at[m], at_z(0, m), s_x2.at[z, m], r_x2.at[z, m], to_x, z > m)
 
@@ -170,10 +171,11 @@
         if d < 3:
             send(at_z(d, m), at_z(d, m), s_l.at[d, m], r_l.at[d, m], to_left, (z + d < 4) & (z > 0))
 
-    def from_left(d, m):
-        arrived(at_z(-d, m), r_r.at[d - 1, m], z - d > 0)
+    def from_left(d, m, cond):
+        arrived(at_z(-d, m), r_r.at[d - 1, m], cond)
         if d == 1:
-            send(at_z(-d, m), at_z(-d, m), s_r.at[1, m], r_r.at[1, m], to_right, (z - d > 0) & (z < 3))
+            send(at_z(-d, m), at_z(-d, m), s_r.at[1, m], r_r.at[1, m], to_right, cond & (z < 3))
+        along_x(-d, m, cond)
 
     def along_x(d, m, cond):
         send(at_z(d, m), at_z(d, m), s_x2.at[z + d, m], r_x2.at[z + d, m], to_x, cond)
@@ -185,7 +187,7 @@
         send(piece(y, x, k), piece(y, x, k), s_y1.at[k], r_y1.at[k], to_y)
         if k == 5:
             for m in range(3):
-                send(pack.at[m], at_z(0, m), s_r.at[0, m], r_r.at[0, m], to_right, (z > 0) & (z < 3))
+                send(pack.at[m], at_z(0, m), s_r.at[0, m], r_r.at[0, m], to_right, (z == 1) | ((z == 2) & (m > 0)))
                 send(pack.at[m], at_z(0, m), s_x2.at[z, m], r_x2.at[z, m], to_x, (z > 0) & (z <= m))
         if k >= 1:
             diagonal(k - 1)
@@ -196,8 +198,7 @@
     for m in range(3):
         along_x(1, m, z + 1 < 4)
     for m in range(3):
-        from_left(1, m)
-        along_x(-1, m, z - 1 > 0)
+        from_left(1, m, z > 1)
         from_right(2, m)
         along_x(2, m, z + 2 < 4)
     for k in range(6):
@@ -238,8 +239,7 @@
                 along_x(3, m, z + 3 < 4)
         if b == 1:
             for m in range(3):
-                from_left(2, m)
-                along_x(-2, m, z - 2 > 0)
+                from_left(2, m, z == 3)
         if b == 2:
             for m in range(2):
                 ref = all_pairs.at[y, 6 + m]
@@ -813,16 +813,16 @@
 CHUNK = SIDE // 2
 CHUNKS = 12
 TAKEN = (
-    ((12, 12),),
-    ((4, 1), (5, 2), (6, 3), (7, 5), (8, 6), (10, 7), (11, 8), (12, 12)),
-    ((2, 1), (3, 2), (4, 4), (5, 5), (6, 6), (8, 7), (9, 8), (10, 9), (11, 11), (12, 12)),
-    ((0, 2), (1, 4), (2, 6), (6, 7), (7, 8), (8, 10), (9, 11), (10, 12)),
+    ((8, 3), (10, 4), (12, 12)),
+    ((5, 1), (7, 3), (8, 4), (9, 6), (10, 7), (11, 8), (12, 12)),
+    ((2, 2), (4, 3), (5, 4), (7, 6), (8, 8), (9, 9), (10, 11), (12, 12)),
+    ((0, 3), (2, 5), (4, 6), (5, 7), (6, 8), (7, 12)),
 )
-GRAD_STEPS = 4
+GRAD_STEPS = 3
 
 
 def last_kernel(
-    small, norm, dq_wide, dk_wide, dv_wide, dq, dk, dv, cat, tok, pas, vec, grad_second, sums_two, second, chip, far,
+    small, norm_all, dq_all, dk_all, dv_all, cat, tok, pas, vec, grad_second, sums_two, second, chip, far,
     mid_near, mid_keep, output, input_grad, *rest,
 ):
     if small:
@@ -830,13 +830,13 @@
         rest = rest[2:]
         (
             core_out, core_in, sums, core_sums, x_in, z_in, z_out, up_in, v_out, v_in, total,
-            s_core, r_core, s_sum, r_sum, s_x, r_x, s_z, r_z, s_up, r_up, s_v, r_v, ready, acc, g_send, g_keep,
-            s_own, s_res, r_res,
+            s_core, r_core, s_sum, r_sum, s_x, r_x, s_z, r_z, s_up, r_up, s_v, r_v, ready, norm, dq, dk, dv, g_send, g_keep,
+            s_own, s_res, r_res, s_in,
         ) = rest
     else:
         (
-            vec_sum, send_out, keep_out, core_out, core_in, sums, core_sums, s_core, r_core, s_sum, r_sum, ready, acc,
-            g_send, g_keep, s_own, s_res, r_res,
+            vec_sum, send_out, keep_out, core_out, core_in, sums, core_sums, s_core, r_core, s_sum, r_sum, ready,
+            norm, dq, dk, dv, g_send, g_keep, s_own, s_res, r_res, s_in,
         ) = rest
     step = pl.program_id(0)
     i = step - GRAD_STEPS
@@ -874,8 +874,15 @@
     v_copy = lambda n: copy(v_out.at[peers[n]], v_in.at[dp], s_v.at[n], r_v.at[dp], {"dp": peers[n]})
     barrier = pltpu.get_barrier_semaphore()
 
+    loads = [
+        pltpu.make_async_copy(src, dst, s_in.at[n])
+        for n, (src, dst) in enumerate(((norm_all, norm), (dq_all, dq), (dv_all, dv), (dk_all, dk)))
+    ]
+
     @pl.when(step == 0)
     def _():
+        for load in loads:
+            load.start()
         pl.semaphore_signal(barrier, inc=1, device_id={"tensor": near}, device_id_type=MESH)
         if small:
             for peer in peers:
@@ -883,38 +890,57 @@
             late[...] = jnp.zeros_like(late)
         sums[...] = jnp.zeros_like(sums)
         sums[PASSES + 2 : PASSES + 4] = sums_two[0:2]
-        acc[...] = jnp.zeros_like(acc)
         pl.semaphore_wait(barrier, 8 if small else 1)
 
-    @pl.when(step < GRAD_STEPS)
-    def _():
-        mine = [jnp.where(side == 0, grad[:, :SIDE], grad[:, SIDE:]) for grad in (dq_wide, dk_wide, dv_wide)]
-        acc[...] += tn(jnp.concatenate(mine, axis=1), norm[...])
-
-    @pl.when(step == GRAD_STEPS - 1)
-    def _():
-        for n in range(3):
+    def mine_of(grad):
+        return jnp.where(side == 0, grad[:, :SIDE], grad[:, SIDE:])
+
+    def pairs_of(grad):
+        value = tn(grad, norm[...]).astype(bf16)
+        return value[:, :PAIR], value[:, PAIR:]
+
+    second_two = jnp.where(jnp.asarray(column) == 0, 1, 0)
+
+    @pl.when(step == 0)
+    def _():
+        for load in loads[:3]:
+            load.wait()
+        both = pairs_of(jnp.where(jnp.asarray(column) == 0, mine_of(dv), mine_of(dq)))
+        for m in range(2):
+            g_send[second_two + m] = both[m]
+        if small:
+            for m in range(4):
+                x_copy(2 * second_two + m).start()
+
+    @pl.when(step == 1)
+    def _():
+        loads[3].wait()
+        both = pairs_of(mine_of(dk))
+        for place, (kept, sent) in enumerate(((0, 1), (1, 0))):
+
+            @pl.when(jnp.asarray(column) == place)
+            def _():
+                g_keep[2 - 2 * place] = both[kept]
+                g_send[2 * place] = both[sent]
+
+        if small:
             for m in range(2):
-                value = acc[n * SIDE : (n + 1) * SIDE, m * PAIR : (m + 1) * PAIR].astype(bf16)
-                slot, place = (2 * n + m) % 3, (2 * n + m) // 3
-
-                @pl.when(column == place)
-                def _():
-                    g_keep[slot] = value
-
-                @pl.when(column != place)
-                def _():
-                    g_send[slot] = value
-        if small:
-            for k in range(6):
-                x_copy(k).start()
-        else:
+                x_copy(4 * column + m).start()
+
+    @pl.when(step == 2)
+    def _():
+        both = pairs_of(jnp.where(jnp.asarray(column) == 0, mine_of(dq), mine_of(dv)))
+        for m in range(2):
+            g_keep[1 - second_two + m] = both[m]
+        if not small:
             send_out[...] = g_send[...]
             keep_out[...] = g_keep[...]
 
     @pl.when((i >= 0) & (i < 2 * half))
     def _():
-        part = nt(dq[...], cat[0]) + nt(dk[...], cat[1]) + nt(dv[...], cat[2])
+        block = lax.rem(i + (1 - core) * half, 2 * half)
+        rows = pl.ds(pl.multiple_of(block * ROWS, ROWS), ROWS)
+        part = nt(dq[rows, :], cat[0]) + nt(dk[rows, :], cat[1]) + nt(dv[rows, :], cat[2])
 
         @pl.when(i < half)
         def _():
@@ -943,6 +969,71 @@
     def _():
         sum_copy().start()
 
+    if small:
+
+        def term_of(k):
+            rows = pl.ds(pl.multiple_of((k % 2) * CHUNK, 16), CHUNK)
+
+            @pl.when(jnp.asarray(k) < 6)
+            def _():
+                x_copy(k).wait_recv()
+                total[...] = g_keep[k // 2, rows, :].astype(f32) + x_in[k].astype(f32)
+
+            @pl.when(jnp.asarray(k) >= 6)
+            def _():
+                total[...] = mid_keep[k // 2 - 3, rows, :].astype(f32) + mid_near[k // 2 - 3, rows, :].astype(f32)
+
+            return total[...]
+
+        def keep_late(k, pair, total):
+            late[pair, pl.ds(pl.multiple_of((k % 2) * CHUNK, 16), CHUNK), :] = total
+
+        def pass_on(k):
+            term = term_of(k)
+
+            @pl.when(z < 3)
+            def _():
+                z_copy(k).wait_recv()
+
+            below = jnp.where(z < 3, z_in[k].astype(f32), 0.0)
+            passed = term + below
+
+            @pl.when((z > 1) | ((z == 1) & (k < 6)))
+            def _():
+                z_out[k] = passed.astype(bf16)
+                z_copy(k).start()
+
+            @pl.when(z == 0)
+            def _():
+                keep_late(k, k // 2, passed)
+
+            @pl.when((z == 1) & (k >= 6))
+            def _():
+                up_copy(k).wait_recv()
+                keep_late(k, k // 2 - 3, passed + up_in[k - 6].astype(f32))
+
+        def at_position(p, carry):
+            k = jnp.where(p < 3, p + 6, jnp.where(p < 9, lax.rem(p + 3 + 2 * column, 6), p))
+
+            @pl.when((z > 0) | (k < 6))
+            def _():
+                pass_on(k)
+
+            return carry
+
+        begin, end = jnp.int32(0), jnp.int32(0)
+        for place, line in enumerate(TAKEN):
+            for at, upto in line:
+                begin = jnp.where((z == place) & (step > at), upto, begin)
+                end = jnp.where((z == place) & (step >= at), upto, end)
+        lax.fori_loop(begin, end, at_position, 0)
+
+        @pl.when((step == 0) & (z == 0))
+        def _():
+            for k in range(6, CHUNKS):
+                z_out[k] = term_of(k).astype(bf16)
+                up_copy(k).start()
+
     @pl.when(i == 2 * half)
     def _():
         sum_copy().wait_recv()
@@ -956,71 +1047,6 @@
                 v_copy(n).start()
         else:
             vec_sum[...] = total
-
-    if small:
-
-        def term_of(k):
-            rows = pl.ds(pl.multiple_of((k % 2) * CHUNK, 16), CHUNK)
-
-            @pl.when(jnp.asarray(k) < 6)
-            def _():
-                x_copy(k).wait_recv()
-                total[...] = g_keep[k // 2, rows, :].astype(f32) + x_in[k].astype(f32)
-
-            @pl.when(jnp.asarray(k) >= 6)
-            def _():
-                total[...] = mid_keep[k // 2 - 3, rows, :].astype(f32) + mid_near[k // 2 - 3, rows, :].astype(f32)
-
-            return total[...]
-
-        def keep_late(k, pair, total):
-            late[pair, pl.ds(pl.multiple_of((k % 2) * CHUNK, 16), CHUNK), :] = total
-
-        def pass_on(k):
-            term = term_of(k)
-
-            @pl.when(z < 3)
-            def _():
-                z_copy(k).wait_recv()
-
-            below = jnp.where(z < 3, z_in[k].astype(f32), 0.0)
-            passed = term + below
-
-            @pl.when((z > 1) | ((z == 1) & (k < 6)))
-            def _():
-                z_out[k] = passed.astype(bf16)
-                z_copy(k).start()
-
-            @pl.when(z == 0)
-            def _():
-                keep_late(k, k // 2, passed)
-
-            @pl.when((z == 1) & (k >= 6))
-            def _():
-                up_copy(k).wait_recv()
-                keep_late(k, k // 2 - 3, passed + up_in[k - 6].astype(f32))
-
-        def at_position(p, carry):
-            k = jnp.where(p < 6, p + 6, p - 6)
-
-            @pl.when((z > 0) | (k < 6))
-            def _():
-                pass_on(k)
-
-            return carry
-
-        begin, end = jnp.int32(0), jnp.int32(0)
-        for place, line in enumerate(TAKEN):
-            for at, upto in line:
-                begin = jnp.where((z == place) & (step > at), upto, begin)
-                end = jnp.where((z == place) & (step >= at), upto, end)
-        lax.fori_loop(begin, end, at_position, 0)
-
-        @pl.when((step == 0) & (z == 0))
-        def _():
-            for k in range(6, CHUNKS):
-                z_out[k] = term_of(k).astype(bf16)
-                up_copy(k).start()
 
     @pl.when(step == pl.num_programs(0) - 1)
     def _():
@@ -1057,14 +1083,7 @@
     half = seq // ROWS // 2
     core = lambda: lax.axis_index("tensor") % 2
 
-    def block(i):
-        work = jnp.clip(i - GRAD_STEPS, 0, 2 * half - 1)
-        return lax.rem(work + (1 - core()) * half, 2 * half)
-
     own = lambda i: jnp.clip(i - GRAD_STEPS - half, 0, half - 1)
-    tall = seq // GRAD_STEPS
-    wide = lambda n: pl.BlockSpec((tall, n), lambda i: (jnp.minimum(i, GRAD_STEPS - 1), 0))
-    row = pl.BlockSpec((ROWS, PAIR), lambda i: (block(i), 0))
     mine = pl.BlockSpec((ROWS, D), lambda i: (own(i), 0))
     dma = pltpu.SemaphoreType.DMA
     out_specs = [pl.BlockSpec(memory_space=pl.ANY)] * 2
@@ -1089,19 +1108,14 @@
     else:
         out_specs += [full((16, D)), full((3, SIDE, PAIR)), full((3, SIDE, PAIR))]
         out_shape += [jax.ShapeDtypeStruct((16, D), f32)] + [jax.ShapeDtypeStruct((3, SIDE, PAIR), bf16)] * 2
-    scratch_more = [pltpu.VMEM((2, half, ROWS, D), bf16), pltpu.VMEM((3 * SIDE, D), f32)]
-    scratch_more += [pltpu.VMEM((3, SIDE, PAIR), bf16)] * 2 + [dma((2, half))] * 3
+    scratch_more = [pltpu.VMEM((2, half, ROWS, D), bf16), pltpu.VMEM((seq, D), bf16)]
+    scratch_more += [pltpu.VMEM((seq, PAIR), bf16)] * 3
+    scratch_more += [pltpu.VMEM((3, SIDE, PAIR), bf16)] * 2 + [dma((2, half))] * 3 + [dma((4,))]
     return pl.pallas_call(
         functools.partial(last_kernel, small),
         grid=(GRAD_STEPS + 2 * half + 2,),
         in_specs=[
-            wide(D),
-            wide(PAIR),
-            wide(PAIR),
-            wide(PAIR),
-            row,
-            row,
-            row,
+            *[pl.BlockSpec(memory_space=pl.ANY)] * 4,
             full(cat.shape),
             pl.BlockSpec((ROWS, D), lambda i: (core() * half + own(i), 0)),
             pl.BlockSpec((1, ROWS), lambda i: (0, core() * half + own(i))),
@@ -1120,7 +1134,7 @@
         compiler_params=params(collective_id=2, has_side_effects=True),
         cost_estimate=cost(38),
         name="last",
-    )(norm, dq, dk, dv, dq, dk, dv, cat, tokens, passes, vec, grad_second, sums_two, second, chip, far, mid_near, mid_keep)
+    )(norm, dq, dk, dv, cat, tokens, passes, vec, grad_second, sums_two, second, chip, far, mid_near, mid_keep)
 
 
 def precondition(grad, weight, left, right, left_root, right_root):

time: 249 us -> 238 us (0.956)
  Pallas kernels: 228 us -> 221 us
  starting transfers between devices: 16.6 us -> 13 us
    pallas_call x1, Pallas kernels: 43.3 us -> 35.7 us  [last(): pl.pallas_call(functools.partial(last_kernel, small), grid=(GRAD_STEPS +...]
    ppermute x3, starting transfers between devices: 14.6 us -> 10.9 us  [hop_z(): return lax.ppermute(value, 'dp', pairs)]
  transfers between devices with their start and end apart: 5 -> 5, of which waited for: 0 -> 1; matrix products, arithmetic and copies ran while one was open for 0% -> 0% of each run, Pallas kernels for 14% -> 15%
where the time goes in v10:
time: 238 us
  Pallas kernels  221 us (93%)
  starting transfers between devices  13 us (5%)
    pallas_call x1, Pallas kernels, feed(): pl.pallas_call(functools.partial(feed_kernel, small), grid=(3 * half + 1,...  62.6 us
    pallas_call x1, Pallas kernels, gather(): pl.pallas_call(gather_kernel, in_specs=[vmem, vmem, far, vmem], out_specs...  52.3 us
    pallas_call x1, Pallas kernels, last(): pl.pallas_call(functools.partial(last_kernel, small), grid=(GRAD_STEPS +...  35.7 us
    pallas_call x1, Pallas kernels, attend_back(): pl.pallas_call(attend_back_kernel, grid_spec=pltpu.PrefetchScalarGridSpec...  34.5 us
    pallas_call x1, Pallas kernels, attend(): pl.pallas_call(attend_kernel, grid_spec=pltpu.PrefetchScalarGridSpec(num_...  24 us
    pallas_call x1, Pallas kernels, renew(): pl.pallas_call(renew_kernel, grid=(4,), in_specs=[pair] * 5 + [slot] * 5...  11.4 us
    ppermute x3, starting transfers between devices, hop_z(): return lax.ppermute(value, 'dp', pairs)  10.9 us
  transfers between devices with their start and end apart: 5, of which 1 were waited for; matrix products, arithmetic and copies ran while one was open for 0% of the time, Pallas kernels for 15%

profile of v10, /device:TPU:0, one launch (start us, length us, event | category | flops | bytes accessed | tf_op | source)
XLA Modules:
  0.0 237.5 jit_solution(8080652576531365276)
XLA Ops:
  0.6 52.3 %gather.1 = (bf16[2,24,192,384]{3,2,1,0:T(8,128)(2,1)}, bf16[2,2,192,384]{3,2,1,0:T(8,128)(2,1)}, f32[16,768]{1,0:T(8,128)}, bf16[2048,768]{1,0:T(8,128)(2,1)}, ...) custom-call(f32[1,6,192,192]{3,2,1,0:T(8,128)} %weight.1, ...), custom_call_target="tpu_custom_call" | custom-call | flops 65999998976 | bytes 60000000 | tf_op jit(solution)/shard_map/gather/pallas_call | solution.py:279
  52.9 24.0 %attend.1 = (bf16[2048,384]{1,0:T(8,128)(2,1)}, f32[8,2048]{1,0:T(8,128)}) custom-call(s32[8]{0:T(128)} %bitcast.5, bf16[2048,384]{1,0:T(8,128)(2,1)} %get-tuple-element.51.q, bf16[2048,384]{1,0:T(8,128)(2,1)} %get-tuple-element.52.k, bf16[2048,384]{1,0:T(8,128)(2,1)} %get-tuple-element.53.v), custom_call_target="tpu_custom_call" | custom-call | flops 32999999488 | bytes 30000000 | tf_op jit(solution)/shard_map/attend/pallas_call | solution.py:417
  76.9 62.6 %feed_forward.1 = (bf16[1024,768]{1,0:T(8,128)(2,1)}, f32[1024,768]{1,0:T(8,128)}, f32[1024,768]{1,0:T(8,128)}, bf16[2048,384]{1,0:T(8,128)(2,1)}, f32[8,768]{1,...) custom-call(bf16[2048,768]{1,0:T(8,128)(2,1)} %tok.3, ...), custom_call_target="tpu_custom_call" | custom-call | flops 54999998464 | bytes 50000000 | tf_op jit(solution)/shard_map/feed_forward/pallas_call | solution.py:759
  139.5 0.7 collective-permute-start
  140.2 8.9 %collective-permute-start.1 = (bf16[3,192,384]{2,1,0:T(8,128)(2,1)}, bf16[3,192,384]{2,1,0:T(8,128)(2,1)S(1)}, u32[]{:S(2)}, u32[]{:S(2)}) collective-permute-start(bf16[3,192,384]{2,1,0:T(8,128)(2,1)} %get-tuple-element.58), channel_id=1, source_target_pairs={{0,16},{4,20},{8,24},{12,28},{1,17},{5,21},{9,25},{13,29},{2,18},{... | collective-permute-start | bytes 1327112 | tf_op jit(solution)/shard_map/ppermute | solution.py:1222
  149.1 1.3 collective-permute-start.2
  150.4 1.6 collective-permute-start.4
  152.0 0.5 collective-permute-start.3
  152.5 34.5 %attend_back.1 = (bf16[2048,384]{1,0:T(8,128)(2,1)}, bf16[2048,384]{1,0:T(8,128)(2,1)}, bf16[2048,384]{1,0:T(8,128)(2,1)}) custom-call(s32[8]{0:T(128)} %bitcast.6, bf16[2048,384]{1,0:T(8,128)(2,1)} %get-tuple-element.51.q, bf16[2048,384]{1,0:T(8,128)(2,1)} %get-tuple-element.52.k, bf16[2048,384]{1,0:T(8,128)(2,1)} %get-tuple-element.53.v, ...), custom_call_target="tpu_custom_call" | custom-call | flops 44000002048 | bytes 40000000 | tf_op jit(solution)/shard_map/attend_back/pallas_call | solution.py:498
  187.1 0.0 collective-permute-done.one
  187.1 0.0 copy-start.3
  187.1 0.0 collective-permute-done.1.two
  187.1 0.0 copy-start.4
  187.1 0.0 collective-permute-done.2.three
  187.1 0.0 copy-start.5
  187.1 0.0 collective-permute-done.4.mid_near
  187.1 0.0 copy-start.6
  187.2 0.4 collective-permute-done.3.far
  187.5 0.0 copy-start.2
  187.5 0.5 copy-done.6
  188.0 0.8 copy-done.2
  188.8 0.0 copy-start
  188.8 0.0 copy-start.1
  188.8 35.7 %last.1 = (bf16[2048,768]{1,0:T(8,128)(2,1)}, bf16[2048,768]{1,0:T(8,128)(2,1)}, f32[3,192,384]{2,1,0:T(8,128)}, f32[16,128]{1,0:T(8,128)}) custom-call(bf16[2048,768]{1,0:T(8,128)(2,1)} %get-tuple-element.49.norm_all, bf16[2048,384]{1,0:T(8,128)(2,1)} %get-tuple-element.65.dq_all, bf16[2048,384]{1,0:T(8,128)(2,1)} %get-tuple-element.66.dk_all, ...), custom_call_target="tpu_custom_call" | custom-call | flops 41799999488 | bytes 38000000 | tf_op jit(solution)/shard_map/last/pallas_call | solution.py:1114
  224.5 0.0 copy-done.3
  224.6 0.0 copy-done.4
  224.6 0.0 copy-done.5
  224.6 0.0 copy-done
  224.6 0.0 copy-done.1
  224.6 1.3 divide_subtract_fusion
  225.9 11.4 %renew.1 = (f32[1,6,192,192]{3,2,1,0:T(8,128)}, f32[1,6,192,192]{3,2,1,0:T(8,128)}, f32[1,6,192,192]{3,2,1,0:T(8,128)}, f32[1,6,192,192]{3,2,1,0:T(8,128)}, bf16...) custom-call(f32[3,192,384]{2,1,0:T(8,128)} %get-tuple-element.75.late, bf16[3,192,384]{2,1,0:T(8,128)(2,1)} %get-tuple-element.76.own, ...), custom_call_target="tpu_custom_call" | custom-call | flops 8800000000 | bytes 8000000 | tf_op jit(solution)/shard_map/renew/pallas_call | solution.py:1189
Async XLA Ops:
  139.5 47.6 %collective-permute-start = (bf16[3,192,384]{2,1,0:T(8,128)(2,1)}, bf16[3,192,384]{2,1,0:T(8,128)(2,1)S(1)}, u32[]{:S(2)}, u32[]{:S(2)}) collective-permute-start(bf16[3,192,384]{2,1,0:T(8,128)(2,1)} %get-tuple-element.57), channel_id=1, source_target_pairs={{8,16},{12,20},{16,24},{20,28},{9,17},{13,21},{17,25},{21,29},{10,... | collective-permute-start | bytes 1327112 | tf_op jit(solution)/shard_map/ppermute | solution.py:1222
  140.2 46.9 %collective-permute-start.1 = (bf16[3,192,384]{2,1,0:T(8,128)(2,1)}, bf16[3,192,384]{2,1,0:T(8,128)(2,1)S(1)}, u32[]{:S(2)}, u32[]{:S(2)}) collective-permute-start(bf16[3,192,384]{2,1,0:T(8,128)(2,1)} %get-tuple-element.58), channel_id=1, source_target_pairs={{0,16},{4,20},{8,24},{12,28},{1,17},{5,21},{9,25},{13,29},{2,18},{... | collective-permute-start | bytes 1327112 | tf_op jit(solution)/shard_map/ppermute | solution.py:1222
  149.1 38.0 %collective-permute-start.2 = (bf16[3,192,384]{2,1,0:T(8,128)(2,1)}, bf16[3,192,384]{2,1,0:T(8,128)(2,1)S(1)}, u32[]{:S(2)}, u32[]{:S(2)}) collective-permute-start(bf16[3,192,384]{2,1,0:T(8,128)(2,1)} %get-tuple-element.59), channel_id=1, source_target_pairs={{0,24},{4,28},{24,16},{28,20},{1,25},{5,29},{25,17},{29,21},{2,26}... | collective-permute-start | bytes 1327112 | tf_op jit(solution)/shard_map/ppermute | solution.py:1222
  150.4 36.7 %collective-permute-start.4 = (bf16[3,192,384]{2,1,0:T(8,128)(2,1)}, bf16[3,192,384]{2,1,0:T(8,128)(2,1)S(1)}, u32[]{:S(2)}, u32[]{:S(2)}) collective-permute-start(bf16[3,192,384]{2,1,0:T(8,128)(2,1)} %get-tuple-element.61), channel_id=1, source_target_pairs={{0,4},{4,0},{8,12},{12,8},{16,20},{20,16},{24,28},{28,24},{1,5},{5... | collective-permute-start | bytes 1327112 | tf_op jit(solution)/shard_map/ppermute | solution.py:1217
  152.0 35.5 %collective-permute-start.3 = (bf16[1024,768]{1,0:T(8,128)(2,1)}, bf16[1024,768]{1,0:T(8,128)(2,1)S(1)}, u32[]{:S(2)}, u32[]{:S(2)}) collective-permute-start(bf16[1024,768]{1,0:T(8,128)(2,1)} %get-tuple-element.60.chip), channel_id=1, source_target_pairs={{0,2},{1,3},{2,0},{3,1},{4,6},{5,7},{6,4},{7,5},{8,10},{9,11},{10,... | collective-permute-start | bytes 4718600 | tf_op jit(solution)/shard_map/ppermute | solution.py:1213
  187.1 37.5 %copy-start.3 = (bf16[3,192,384]{2,1,0:T(8,128)(2,1)}, bf16[3,192,384]{2,1,0:T(8,128)(2,1)S(1)}, u32[]{:S(2)}) copy-start(bf16[3,192,384]{2,1,0:T(8,128)(2,1)S(1)} %collective-permute-done.one) | copy-start | bytes 1327108
  187.1 37.5 %copy-start.4 = (bf16[3,192,384]{2,1,0:T(8,128)(2,1)}, bf16[3,192,384]{2,1,0:T(8,128)(2,1)S(1)}, u32[]{:S(2)}) copy-start(bf16[3,192,384]{2,1,0:T(8,128)(2,1)S(1)} %collective-permute-done.1.two) | copy-start | bytes 1327108
  187.1 37.4 %copy-start.5 = (bf16[3,192,384]{2,1,0:T(8,128)(2,1)}, bf16[3,192,384]{2,1,0:T(8,128)(2,1)S(1)}, u32[]{:S(2)}) copy-start(bf16[3,192,384]{2,1,0:T(8,128)(2,1)S(1)} %collective-permute-done.2.three) | copy-start | bytes 1327108
  187.1 0.9 copy-start.6
  187.5 1.3 copy-start.2
  188.8 35.8 %copy-start = (f32[9,96]{1,0:T(8,128)S(1)}, f32[9,96]{1,0:T(8,128)}, u32[]{:S(2)}) copy-start(f32[9,96]{1,0:T(8,128)} %vec_own.1) | copy-start | bytes 10372
  188.8 35.8 %copy-start.1 = (f32[9,96]{1,0:T(8,128)S(1)}, f32[9,96]{1,0:T(8,128)}, u32[]{:S(2)}) copy-start(f32[9,96]{1,0:T(8,128)} %param.17) | copy-start | bytes 10372

commit v11 on v10

--- a/solution.py
+++ b/solution.py
@@ -658,7 +658,7 @@
                     pair = at + 2 * r + m
                     slot, place = (pair // 6 - 1) * 3 + pair % 3, pair // 3 % 2
                     value = total[rows, cols].astype(bf16)
-                    kept, sent, n = (mid_keep, mid_send, slot) if slot < 3 else (g_keep, g_send, slot - 3)
+                    kept, sent, n = (mid_keep, mid_send, slot) if slot < 6 else (g_keep, g_send, slot - 6)
 
                     @pl.when(column == place)
                     def _():
@@ -668,7 +668,7 @@
                     def _():
                         sent[n] = value
         if small:
-            for n in range(6):
+            for n in range(3):
                 x_copy(n).start()
 
     def through_out(grad, block):
@@ -719,15 +719,15 @@
             far_copy(j).wait_send()
             ga_copy(j).wait_send()
         if small:
-            for n in range(6):
+            for n in range(3):
                 x_copy(n).wait_send()
                 x_copy(n).wait_recv()
                 value = (g_keep[n].astype(f32) + g_in[n].astype(f32)).astype(bf16)
                 for turn in range(4):
 
-                    @pl.when(lax.rem(z + turn, 4) == n // 3 + 2)
+                    @pl.when(z + turn == 3)
                     def _():
-                        results[turn][n % 3] = value
+                        results[turn][n] = value
         else:
             results[0][...] = g_send[...]
             results[1][...] = g_keep[...]
@@ -753,7 +753,7 @@
     last = pl.BlockSpec((ROWS, D), lambda i: (jnp.clip(i - 2 * half, 0, half - 1), 0))
     rows = lambda kind: jax.ShapeDtypeStruct((seq // 2, D), kind)
     gr = lambda n: jax.ShapeDtypeStruct((n, SIDE, PAIR), bf16)
-    ends = [(3, SIDE, PAIR)] * 4 if small else [(6, SIDE, PAIR)] * 2
+    ends = [(3, SIDE, PAIR)] * (4 if small else 2)
     buffer = pltpu.VMEM((half, ROWS, D), bf16)
     dma = pltpu.SemaphoreType.DMA((half,))
     return pl.pallas_call(
@@ -776,8 +776,8 @@
             last,
             full((seq, PAIR)),
             full((8, D)),
-            full((3, SIDE, PAIR)),
-            full((3, SIDE, PAIR)),
+            full((6, SIDE, PAIR)),
+            full((6, SIDE, PAIR)),
         ]
         + [full(shape) for shape in ends],
         scratch_shapes=[
@@ -790,9 +790,9 @@
             pltpu.VMEM((PAIR, D), f32),
         ]
         + [buffer] * 8
-        + [pltpu.VMEM((6, SIDE, PAIR), bf16)] * 3
+        + [pltpu.VMEM((3, SIDE, PAIR), bf16)] * 3
         + [dma] * 8
-        + [pltpu.SemaphoreType.DMA((6,))] * 2
+        + [pltpu.SemaphoreType.DMA((3,))] * 2
         + [pltpu.SemaphoreType.DMA((2 * half,))] * 2,
         out_shape=[
             rows(bf16),
@@ -800,8 +800,8 @@
             rows(f32),
             jax.ShapeDtypeStruct((seq, PAIR), bf16),
             jax.ShapeDtypeStruct((8, D), f32),
-            gr(3),
-            gr(3),
+            gr(6),
+            gr(6),
         ]
         + [jax.ShapeDtypeStruct(shape, bf16) for shape in ends],
         compiler_params=params(collective_id=1, has_side_effects=True),
@@ -811,7 +811,7 @@
 
 
 CHUNK = SIDE // 2
-CHUNKS = 12
+CHUNKS = 18
 TAKEN = (
     ((8, 3), (10, 4), (12, 12)),
     ((5, 1), (7, 3), (8, 4), (9, 6), (10, 7), (11, 8), (12, 12)),
@@ -1034,6 +1034,30 @@
                 z_out[k] = term_of(k).astype(bf16)
                 up_copy(k).start()
 
+        for at, first_chunk, upto in ((0, 12, 14), (7, 14, 18)):
+
+            @pl.when((step == at) & (z == 3))
+            def _(first_chunk=first_chunk, upto=upto):
+                for k in range(first_chunk, upto):
+                    z_out[k] = term_of(k).astype(bf16)
+                    z_copy(k).start()
+
+        for at, first_chunk, upto in ((10, 12, 16), (11, 16, 18)):
+
+            @pl.when((step == at) & (z == 1))
+            def _(first_chunk=first_chunk, upto=upto):
+                for k in range(first_chunk, upto):
+                    up_copy(k).wait_recv()
+                    z_out[k] = (term_of(k) + up_in[k - 6].astype(f32)).astype(bf16)
+                    up_copy(k).start()
+
+        @pl.when((step == pl.num_programs(0) - 1) & (z == 2))
+        def _():
+            for k in range(12, CHUNKS):
+                z_copy(k).wait_recv()
+                up_copy(k).wait_recv()
+                keep_late(k, k // 2 - 6, term_of(k) + z_in[k].astype(f32) + up_in[k - 6].astype(f32))
+
     @pl.when(i == 2 * half)
     def _():
         sum_copy().wait_recv()
@@ -1071,9 +1095,12 @@
                 if k < 6:
                     x_copy(k).wait_send()
                     pl.when(z > 0)(z_copy(k).wait_send)
-                else:
+                elif k < 12:
                     pl.when(z > 1)(z_copy(k).wait_send)
                     pl.when(z == 0)(up_copy(k).wait_send)
+                else:
+                    pl.when(z == 3)(z_copy(k).wait_send)
+                    pl.when(z < 2)(up_copy(k).wait_send)
 
 
 def last(
@@ -1102,9 +1129,9 @@
             jax.ShapeDtypeStruct((16, 128), f32),
         ]
         scratch += [pltpu.VMEM((CHUNKS, CHUNK, PAIR), bf16)] * 3
-        scratch += [pltpu.VMEM((6, CHUNK, PAIR), bf16)]
+        scratch += [pltpu.VMEM((12, CHUNK, PAIR), bf16)]
         scratch += [pltpu.VMEM((8, 16, 128), f32)] * 2 + [pltpu.VMEM((CHUNK, PAIR), f32)]
-        sems += [dma((6,))] * 2 + [dma((CHUNKS,))] * 2 + [dma((6,))] * 2 + [dma((7,)), dma((8,))]
+        sems += [dma((6,))] * 2 + [dma((CHUNKS,))] * 2 + [dma((12,))] * 2 + [dma((7,)), dma((8,))]
     else:
         out_specs += [full((16, D)), full((3, SIDE, PAIR)), full((3, SIDE, PAIR))]
         out_shape += [jax.ShapeDtypeStruct((16, D), f32)] + [jax.ShapeDtypeStruct((3, SIDE, PAIR), bf16)] * 2
@@ -1170,7 +1197,7 @@
     def _():
         early = own[0].astype(f32) + one[0].astype(f32) + two[0].astype(f32) + three[0].astype(f32)
         z = lax.axis_index("dp") // 2
-        both = late[0] + jnp.where(z > 1, early, 0.0)
+        both = late[0] + jnp.where(z > 2, early, 0.0)
         for n in range(2):
             grad = both[:, n * SIDE : (n + 1) * SIDE]
             grad = two_part(jnp.where(z == 0, grad.T, grad))
@@ -1193,7 +1220,7 @@
         out_specs=[slot] * 4 + [rows] * 2,
         out_shape=[jax.ShapeDtypeStruct(weight.shape, f32)] * 4
         + [jax.ShapeDtypeStruct(value.shape, value.dtype) for value in (output, input_grad)],
-        compiler_params=params(),
+        compiler_params=params(46),
         cost_estimate=cost(8),
         name="renew",
     )(late, own, *far, weight, left, right, left_root, right_root, output, input_grad)
@@ -1267,7 +1294,7 @@
     )
     out_far = swap(out_chip, 2)
     if small:
-        far = [hop_z(ends[turn], turn, (2, 3)) for turn in (1, 2, 3)]
+        far = [hop_z(ends[turn], turn, (3,)) for turn in (1, 2, 3)]
         mid_send = hop_x(mid_send)
     dq, dk, dv = attend_back(lens, q, k, v, mine, lse, grad_mixed)
     if small:

time: 238 us -> 233 us (0.979); the launches traced: 238 us -> 235 us
  Pallas kernels: 221 us -> 214 us
    pallas_call x1, Pallas kernels: 62.6 us -> 54 us  [feed(): pl.pallas_call(functools.partial(feed_kernel, small), grid=(3 * half + 1,...]
    pallas_call x1, Pallas kernels: 35.7 us -> 40.4 us  [last(): pl.pallas_call(functools.partial(last_kernel, small), grid=(GRAD_STEPS +...]
where the time goes in v11:
time: 233 us; the launch traced here: 235 us
  Pallas kernels  214 us (92%)
  starting transfers between devices  15.2 us (7%)
  local copies, waits for them, and re-layouts  2.34 us (1%)
    pallas_call x1, Pallas kernels, feed(): pl.pallas_call(functools.partial(feed_kernel, small), grid=(3 * half + 1,...  54 us
    pallas_call x1, Pallas kernels, gather(): pl.pallas_call(gather_kernel, in_specs=[vmem, vmem, far, vmem], out_specs...  52.3 us
    pallas_call x1, Pallas kernels, last(): pl.pallas_call(functools.partial(last_kernel, small), grid=(GRAD_STEPS +...  40.4 us
    pallas_call x1, Pallas kernels, attend_back(): pl.pallas_call(attend_back_kernel, grid_spec=pltpu.PrefetchScalarGridSpec...  34.5 us
    pallas_call x1, Pallas kernels, attend(): pl.pallas_call(attend_kernel, grid_spec=pltpu.PrefetchScalarGridSpec(num_...  24 us
    ppermute x3, starting transfers between devices, hop_z(): return lax.ppermute(value, 'dp', pairs)  13.1 us
    pallas_call x1, Pallas kernels, renew(): pl.pallas_call(renew_kernel, grid=(4,), in_specs=[pair] * 5 + [slot] * 5...  9.17 us
  transfers between devices with their start and end apart: 5, of which 1 were waited for; matrix products, arithmetic and copies ran while one was open for 0% of the time, Pallas kernels for 15%

profile of v11, /device:TPU:0, one launch (start us, length us, event | category | flops | bytes accessed | tf_op | source)
XLA Modules:
  0.0 235.3 jit_solution(8925632575493891677)
XLA Ops:
  0.6 52.3 %gather.1 = (bf16[2,24,192,384]{3,2,1,0:T(8,128)(2,1)}, bf16[2,2,192,384]{3,2,1,0:T(8,128)(2,1)}, f32[16,768]{1,0:T(8,128)}, bf16[2048,768]{1,0:T(8,128)(2,1)}, ...) custom-call(f32[1,6,192,192]{3,2,1,0:T(8,128)} %weight.1, ...), custom_call_target="tpu_custom_call" | custom-call | flops 65999998976 | bytes 60000000 | tf_op jit(solution)/shard_map/gather/pallas_call | solution.py:279
  53.0 24.0 %attend.1 = (bf16[2048,384]{1,0:T(8,128)(2,1)}, f32[8,2048]{1,0:T(8,128)}) custom-call(s32[8]{0:T(128)} %bitcast.5, bf16[2048,384]{1,0:T(8,128)(2,1)} %get-tuple-element.51.q, bf16[2048,384]{1,0:T(8,128)(2,1)} %get-tuple-element.52.k, bf16[2048,384]{1,0:T(8,128)(2,1)} %get-tuple-element.53.v), custom_call_target="tpu_custom_call" | custom-call | flops 32999999488 | bytes 30000000 | tf_op jit(solution)/shard_map/attend/pallas_call | solution.py:417
  76.9 54.0 %feed_forward.1 = (bf16[1024,768]{1,0:T(8,128)(2,1)}, f32[1024,768]{1,0:T(8,128)}, f32[1024,768]{1,0:T(8,128)}, bf16[2048,384]{1,0:T(8,128)(2,1)}, f32[8,768]{1,...) custom-call(bf16[2048,768]{1,0:T(8,128)(2,1)} %tok.3, ...), custom_call_target="tpu_custom_call" | custom-call | flops 54999998464 | bytes 50000000 | tf_op jit(solution)/shard_map/feed_forward/pallas_call | solution.py:759
  131.0 0.7 collective-permute-start
  131.6 0.7 collective-permute-start.1
  132.3 11.7 %collective-permute-start.2 = (bf16[3,192,384]{2,1,0:T(8,128)(2,1)}, bf16[3,192,384]{2,1,0:T(8,128)(2,1)S(1)}, u32[]{:S(2)}, u32[]{:S(2)}) collective-permute-start(bf16[3,192,384]{2,1,0:T(8,128)(2,1)} %get-tuple-element.59), channel_id=1, source_target_pairs={{0,24},{4,28},{1,25},{5,29},{2,26},{6,30},{3,27},{7,31}} | collective-permute-start | bytes 1327112 | tf_op jit(solution)/shard_map/ppermute | solution.py:1249
  144.1 1.6 collective-permute-start.4
  145.7 0.5 collective-permute-start.3
  146.2 34.5 %attend_back.1 = (bf16[2048,384]{1,0:T(8,128)(2,1)}, bf16[2048,384]{1,0:T(8,128)(2,1)}, bf16[2048,384]{1,0:T(8,128)(2,1)}) custom-call(s32[8]{0:T(128)} %bitcast.6, bf16[2048,384]{1,0:T(8,128)(2,1)} %get-tuple-element.51.q, bf16[2048,384]{1,0:T(8,128)(2,1)} %get-tuple-element.52.k, bf16[2048,384]{1,0:T(8,128)(2,1)} %get-tuple-element.53.v, ...), custom_call_target="tpu_custom_call" | custom-call | flops 44000002048 | bytes 40000000 | tf_op jit(solution)/shard_map/attend_back/pallas_call | solution.py:498
  180.7 0.0 collective-permute-done.one
  180.7 0.0 collective-permute-done.1.two
  180.7 0.0 collective-permute-done.2.three
  180.8 0.0 collective-permute-done.4.mid_near
  180.8 0.0 copy-start.9
  180.8 1.1 collective-permute-done.3.far
  181.9 0.0 copy-start.8
  181.9 0.0 copy-done.9
  181.9 1.1 copy-done.8
  183.1 0.0 copy-start.6
  183.1 0.0 copy-start.7
  183.1 0.0 copy-start
  183.1 0.0 copy-start.1
  183.1 0.0 copy-start.2
  183.1 0.0 copy-start.3
  183.1 0.0 copy-start.5
  183.1 40.4 %last.1 = (bf16[2048,768]{1,0:T(8,128)(2,1)}, bf16[2048,768]{1,0:T(8,128)(2,1)}, f32[3,192,384]{2,1,0:T(8,128)}, f32[16,128]{1,0:T(8,128)}) custom-call(bf16[2048,768]{1,0:T(8,128)(2,1)} %get-tuple-element.49.norm_all, bf16[2048,384]{1,0:T(8,128)(2,1)} %get-tuple-element.65.dq_all, bf16[2048,384]{1,0:T(8,128)(2,1)} %get-tuple-element.66.dk_all, ...), custom_call_target="tpu_custom_call" | custom-call | flops 41799999488 | bytes 38000000 | tf_op jit(solution)/shard_map/last/pallas_call | solution.py:1141
  223.6 0.0 copy-done.6
  223.6 0.0 copy-done.7
  223.6 1.3 divide_subtract_fusion
  224.9 0.0 copy-done
  224.9 0.0 copy-done.1
  224.9 0.0 copy-done.2
  224.9 0.0 copy-done.3
  224.9 0.0 copy-done.5
  224.9 0.0 copy-start.4
  224.9 1.2 copy-done.4
  226.1 9.2 %renew.1 = (f32[1,6,192,192]{3,2,1,0:T(8,128)}, f32[1,6,192,192]{3,2,1,0:T(8,128)}, f32[1,6,192,192]{3,2,1,0:T(8,128)}, f32[1,6,192,192]{3,2,1,0:T(8,128)}, bf16...) custom-call(f32[3,192,384]{2,1,0:T(8,128)S(1)} %copy-done.4, bf16[3,192,384]{2,1,0:T(8,128)(2,1)S(1)} %copy-done.5, ...), custom_call_target="tpu_custom_call" | custom-call | flops 8800000000 | bytes 8000000 | tf_op jit(solution)/shard_map/renew/pallas_call | solution.py:1216
Async XLA Ops:
  131.0 49.8 %collective-permute-start = (bf16[3,192,384]{2,1,0:T(8,128)(2,1)}, bf16[3,192,384]{2,1,0:T(8,128)(2,1)S(1)}, u32[]{:S(2)}, u32[]{:S(2)}) collective-permute-start(bf16[3,192,384]{2,1,0:T(8,128)(2,1)} %get-tuple-element.57), channel_id=1, source_target_pairs={{16,24},{20,28},{17,25},{21,29},{18,26},{22,30},{19,27},{23,31}} | collective-permute-start | bytes 1327112 | tf_op jit(solution)/shard_map/ppermute | solution.py:1249
  131.6 49.1 %collective-permute-start.1 = (bf16[3,192,384]{2,1,0:T(8,128)(2,1)}, bf16[3,192,384]{2,1,0:T(8,128)(2,1)S(1)}, u32[]{:S(2)}, u32[]{:S(2)}) collective-permute-start(bf16[3,192,384]{2,1,0:T(8,128)(2,1)} %get-tuple-element.58), channel_id=1, source_target_pairs={{8,24},{12,28},{9,25},{13,29},{10,26},{14,30},{11,27},{15,31}} | collective-permute-start | bytes 1327112 | tf_op jit(solution)/shard_map/ppermute | solution.py:1249
  132.3 48.4 %collective-permute-start.2 = (bf16[3,192,384]{2,1,0:T(8,128)(2,1)}, bf16[3,192,384]{2,1,0:T(8,128)(2,1)S(1)}, u32[]{:S(2)}, u32[]{:S(2)}) collective-permute-start(bf16[3,192,384]{2,1,0:T(8,128)(2,1)} %get-tuple-element.59), channel_id=1, source_target_pairs={{0,24},{4,28},{1,25},{5,29},{2,26},{6,30},{3,27},{7,31}} | collective-permute-start | bytes 1327112 | tf_op jit(solution)/shard_map/ppermute | solution.py:1249
  144.1 36.7 %collective-permute-start.4 = (bf16[6,192,384]{2,1,0:T(8,128)(2,1)}, bf16[6,192,384]{2,1,0:T(8,128)(2,1)S(1)}, u32[]{:S(2)}, u32[]{:S(2)}) collective-permute-start(bf16[6,192,384]{2,1,0:T(8,128)(2,1)} %get-tuple-element.61), channel_id=1, source_target_pairs={{0,4},{4,0},{8,12},{12,8},{16,20},{20,16},{24,28},{28,24},{1,5},{5... | collective-permute-start | bytes 2654216 | tf_op jit(solution)/shard_map/ppermute | solution.py:1244
  145.7 36.2 %collective-permute-start.3 = (bf16[1024,768]{1,0:T(8,128)(2,1)}, bf16[1024,768]{1,0:T(8,128)(2,1)S(1)}, u32[]{:S(2)}, u32[]{:S(2)}) collective-permute-start(bf16[1024,768]{1,0:T(8,128)(2,1)} %get-tuple-element.60.chip), channel_id=1, source_target_pairs={{0,2},{1,3},{2,0},{3,1},{4,6},{5,7},{6,4},{7,5},{8,10},{9,11},{10,... | collective-permute-start | bytes 4718600 | tf_op jit(solution)/shard_map/ppermute | solution.py:1240
  180.8 1.2 copy-start.9
  181.9 1.1 copy-start.8
  183.1 40.5 %copy-start.6 = (f32[9,96]{1,0:T(8,128)S(1)}, f32[9,96]{1,0:T(8,128)}, u32[]{:S(2)}) copy-start(f32[9,96]{1,0:T(8,128)} %vec_own.1) | copy-start | bytes 10372
  183.1 40.5 %copy-start.7 = (f32[9,96]{1,0:T(8,128)S(1)}, f32[9,96]{1,0:T(8,128)}, u32[]{:S(2)}) copy-start(f32[9,96]{1,0:T(8,128)} %param.17) | copy-start | bytes 10372
  183.1 41.8 %copy-start = (f32[1,6,192,192]{3,2,1,0:T(8,128)S(1)}, f32[1,6,192,192]{3,2,1,0:T(8,128)}, u32[]{:S(2)}) copy-start(f32[1,6,192,192]{3,2,1,0:T(8,128)} %weight.1) | copy-start | bytes 2654212
  183.1 41.8 %copy-start.1 = (f32[1,6,192,192]{3,2,1,0:T(8,128)S(1)}, f32[1,6,192,192]{3,2,1,0:T(8,128)}, u32[]{:S(2)}) copy-start(f32[1,6,192,192]{3,2,1,0:T(8,128)} %left.1) | copy-start | bytes 2654212
  183.1 41.8 %copy-start.2 = (f32[1,6,192,192]{3,2,1,0:T(8,128)S(1)}, f32[1,6,192,192]{3,2,1,0:T(8,128)}, u32[]{:S(2)}) copy-start(f32[1,6,192,192]{3,2,1,0:T(8,128)} %right.1) | copy-start | bytes 2654212
  183.1 41.8 %copy-start.3 = (f32[1,6,192,192]{3,2,1,0:T(8,128)S(1)}, f32[1,6,192,192]{3,2,1,0:T(8,128)}, u32[]{:S(2)}) copy-start(f32[1,6,192,192]{3,2,1,0:T(8,128)} %left_root.1) | copy-start | bytes 2654212
  183.1 41.8 %copy-start.5 = (bf16[3,192,384]{2,1,0:T(8,128)(2,1)S(1)}, bf16[3,192,384]{2,1,0:T(8,128)(2,1)}, u32[]{:S(2)}) copy-start(bf16[3,192,384]{2,1,0:T(8,128)(2,1)} %get-tuple-element.76.own) | copy-start | bytes 1327108
  224.9 1.2 copy-start.4

commit v12 on v11

--- a/solution.py
+++ b/solution.py
@@ -88,7 +88,7 @@
 
 def gather_kernel(
     own, vec_own, tokens, passes,
-    all_pairs, wo_other, vec_out, norm, q, k_out, v, cat,
+    all_pairs, columns, wo_other, vec_out, norm, q, k_out, v, cat,
     pack, vec_pack, vec_land, wq, tok, norm_s, qkv_s, cat_s, *sems,
 ):
     (
@@ -148,37 +148,46 @@
     def piece(side, column, k):
         return wq.at[side, 3 * column + k // 2, pl.ds((k % 2) * half, half)]
 
+    def at_one(m):
+        return all_pairs.at[y, 6 + 3 * x + m]
+
     def at_z(d, m):
-        return all_pairs.at[y, 3 * dp + 6 * d + m]
-
-    own_copy = pltpu.make_async_copy(pack, all_pairs.at[y, pl.ds(3 * dp, 3)], loc)
-    pl.when(z > 0)(own_copy.start)
+        return columns.at[3 * (z + d - 2) + m]
+
+    own_one = pltpu.make_async_copy(pack, all_pairs.at[y, pl.ds(6 + 3 * x, 3)], loc)
+    own_more = pltpu.make_async_copy(pack, columns.at[pl.ds(3 * (z - 2), 3)], loc)
+    pl.when(z == 1)(own_one.start)
+    pl.when(z > 1)(own_more.start)
 
     for m in range(3):
-        send(pack.at[m], at_z(0, m), s_l.at[0, m], r_l.at[0, m], to_left, z > 0)
+        send(pack.at[m], at_one(m), s_l.at[0, m], r_l.at[0, m], to_left, z == 1)
+        send(pack.at[m], at_z(0, m), s_l.at[0, m], r_l.at[0, m], to_left, z > 1)
     for n, peer in enumerate(peers):
         send(vec_pack, vec_land.at[dp], s_v.at[n], r_v.at[dp], {"dp": peer})
     send(pack.at[0], at_z(0, 0), s_r.at[0, 0], r_r.at[0, 0], to_right, z == 2)
-    for m in range(3):
-        send(pack.at[m], at_z(0, m), s_x2.at[z, m], r_x2.at[z, m], to_x, z > m)
+    send(pack.at[0], at_one(0), s_x2.at[0], r_x2.at[0], to_x, z == 1)
 
     def diagonal(k):
-        arrived(piece(y, 1 - x, k), r_x1.at[k])
-        send(piece(y, 1 - x, k), piece(y, 1 - x, k), s_d1.at[k], r_d1.at[k], to_y)
+        if k % 2 == 0:
+            arrived(piece(y, 1 - x, k), r_x1.at[k])
+            send(piece(y, 1 - x, k), piece(y, 1 - x, k), s_d1.at[k], r_d1.at[k], to_y)
+        else:
+            arrived(piece(1 - y, x, k), r_y1.at[k])
+            send(piece(1 - y, x, k), piece(1 - y, x, k), s_d1.at[k], r_d1.at[k], to_x)
 
     def from_right(d, m):
-        arrived(at_z(d, m), r_l.at[d - 1, m], z + d < 4)
+        arrived(columns.at[m], r_l.at[d - 1, m], z + d < 4)
         if d < 3:
             send(at_z(d, m), at_z(d, m), s_l.at[d, m], r_l.at[d, m], to_left, (z + d < 4) & (z > 0))
 
-    def from_left(d, m, cond):
-        arrived(at_z(-d, m), r_r.at[d - 1, m], cond)
+    def along_x(m, cond):
+        send(at_one(m), at_one(m), s_x2.at[m], r_x2.at[m], to_x, cond)
+
+    def from_left(d, m):
+        arrived(columns.at[m], r_r.at[d - 1, m], z > d)
         if d == 1:
-            send(at_z(-d, m), at_z(-d, m), s_r.at[1, m], r_r.at[1, m], to_right, cond & (z < 3))
-        along_x(-d, m, cond)
-
-    def along_x(d, m, cond):
-        send(at_z(d, m), at_z(d, m), s_x2.at[z + d, m], r_x2.at[z + d, m], to_x, cond)
+            send(at_one(m), at_one(m), s_r.at[1, m], r_r.at[1, m], to_right, z == 2)
+        along_x(m, z == d + 1)
 
     for k in range(6):
         arrived(piece(y, x, k), r_z1.at[k], z > 0)
@@ -187,22 +196,27 @@
         send(piece(y, x, k), piece(y, x, k), s_y1.at[k], r_y1.at[k], to_y)
         if k == 5:
             for m in range(3):
-                send(pack.at[m], at_z(0, m), s_r.at[0, m], r_r.at[0, m], to_right, (z == 1) | ((z == 2) & (m > 0)))
-                send(pack.at[m], at_z(0, m), s_x2.at[z, m], r_x2.at[z, m], to_x, (z > 0) & (z <= m))
+                send(pack.at[m], at_one(m), s_r.at[0, m], r_r.at[0, m], to_right, z == 1)
+                if m > 0:
+                    send(pack.at[m], at_z(0, m), s_r.at[0, m], r_r.at[0, m], to_right, z == 2)
+                    send(pack.at[m], at_one(m), s_x2.at[m], r_x2.at[m], to_x, z == 1)
         if k >= 1:
             diagonal(k - 1)
         if k % 2 == 1:
             from_right(1, k // 2)
     diagonal(5)
-    pl.when(z > 0)(own_copy.wait)
+    pl.when(z == 1)(own_one.wait)
+    pl.when(z > 1)(own_more.wait)
     for m in range(3):
-        along_x(1, m, z + 1 < 4)
+        along_x(m, z == 0)
     for m in range(3):
-        from_left(1, m, z > 1)
+        from_left(1, m)
         from_right(2, m)
-        along_x(2, m, z + 2 < 4)
     for k in range(6):
-        arrived(piece(1 - y, x, k), r_y1.at[k])
+        if k % 2 == 0:
+            arrived(piece(1 - y, x, k), r_y1.at[k])
+        else:
+            arrived(piece(y, 1 - x, k), r_x1.at[k])
         arrived(piece(1 - y, 1 - x, k), r_d1.at[k])
     for peer in peers:
         arrived(vec_land.at[peer], r_v.at[peer])
@@ -235,28 +249,20 @@
         rows_of(b)
         if b == 0:
             for m in range(3):
+                from_left(2, m)
                 from_right(3, m)
-                along_x(3, m, z + 3 < 4)
         if b == 1:
-            for m in range(3):
-                from_left(2, m, z == 3)
-        if b == 2:
             for m in range(2):
                 ref = all_pairs.at[y, 6 + m]
-                arrived(ref, r_x2.at[1, m], x == 1)
+                arrived(ref, r_x2.at[m], x == 1)
                 send(ref, ref, s_y2.at[m], r_y2.at[m], to_y)
                 send(ref, wo_other.at[y, m], s_c.at[0, m], r_c.at[y, m], {"tensor": near})
     for m in range(2):
         ref = all_pairs.at[1 - y, 6 + m]
         arrived(ref, r_y2.at[m])
         send(ref, wo_other.at[1 - y, m], s_c.at[1, m], r_c.at[1 - y, m], {"tensor": near})
-    for w in range(1, 4):
-        for m in range(3):
-            ref = all_pairs.at[y, 6 * w + 3 * (1 - x) + m]
-            if w == 1 and m < 2:
-                arrived(ref, r_x2.at[w, m], x == 0)
-            else:
-                arrived(ref, r_x2.at[w, m])
+    for m in range(3):
+        arrived(all_pairs.at[y, 6 + 3 * (1 - x) + m], r_x2.at[m], None if m == 2 else x == 0)
     for h in range(2):
         for m in range(2):
             arrived(wo_other.at[h, m], r_c.at[h, m])
@@ -272,16 +278,17 @@
 def gather(block_weights, vector_params, tokens, passes):
     seq = tokens.shape[0]
     dma = pltpu.SemaphoreType.DMA
-    sizes = [(6,)] * 8 + [(3, 3)] * 2 + [(2, 3)] * 2 + [(4, 3)] * 2 + [(2,)] * 2 + [(7,), (8,)] + [(2, 2)] * 2
+    sizes = [(6,)] * 8 + [(3, 3)] * 2 + [(2, 3)] * 2 + [(3,)] * 2 + [(2,)] * 2 + [(7,), (8,)] + [(2, 2)] * 2
     sizes += [(seq // WIDE, 4)]
     vmem, far = pl.BlockSpec(memory_space=pltpu.VMEM), pl.BlockSpec(memory_space=pl.ANY)
     wide = jax.ShapeDtypeStruct((seq, PAIR), bf16)
     return pl.pallas_call(
         gather_kernel,
         in_specs=[vmem, vmem, far, vmem],
-        out_specs=[far, far, vmem, far, far, far, far, far],
+        out_specs=[far, far, far, vmem, far, far, far, far, far],
         out_shape=[
             jax.ShapeDtypeStruct((2, 24, SIDE, PAIR), bf16),
+            jax.ShapeDtypeStruct((6, SIDE, PAIR), bf16),
             jax.ShapeDtypeStruct((2, 2, SIDE, PAIR), bf16),
             jax.ShapeDtypeStruct((16, D), f32),
             jax.ShapeDtypeStruct((seq, D), bf16),
@@ -523,7 +530,7 @@
 
 
 def feed_kernel(
-    small, tok, pas, vec, mine, cot, wo_mine, wo_other, w1, w2,
+    small, tok, pas, vec, mine, cot, wo_mine, wo_other, four, columns, columns_x,
     out_chip, second_keep, grad_second, grad_mixed, sums, mid_send, mid_keep, *rest,
 ):
     results, rest = (rest[:4], rest[4:]) if small else (rest[:2], rest[2:])
@@ -591,8 +598,18 @@
         for r in range(4):
             for m in range(2):
                 rows, cols = slice(r * SIDE, (r + 1) * SIDE), slice(m * PAIR, (m + 1) * PAIR)
-                up[rows, cols] = w1[0, 2 * r + m]
-                down[rows, cols] = w2[0, 2 * r + m]
+                for at, weight in ((8, up), (16, down)):
+                    pair = at + 2 * r + m
+                    if pair < 12:
+                        weight[rows, cols] = four[0, pair - 8]
+                        continue
+                    n = (pair // 6 - 2) * 3 + pair % 3
+                    for source, here in ((columns, pair // 3 % 2), (columns_x, 1 - pair // 3 % 2)):
+
+                        @pl.when(column == here)
+                        def _():
+                            weight[rows, cols] = source[n]
+
         pl.semaphore_wait(barrier, 3 if small else 2)
         for j in range(half):
             mixed_copy(core * half + j).start()
@@ -733,7 +750,7 @@
             results[1][...] = g_keep[...]
 
 
-def feed(small, tokens, passes, vec, mine, cotangent, pairs, wo_other):
+def feed(small, tokens, passes, vec, mine, cotangent, pairs, wo_other, columns, columns_x):
     seq = tokens.shape[0]
     half = seq // ROWS // 2
 
@@ -767,8 +784,9 @@
             pl.BlockSpec((ROWS, D), lambda i: (cot_block(i), 0)),
             pl.BlockSpec((2, 2, SIDE, PAIR), lambda i: (0, 3, 0, 0)),
             full(wo_other.shape),
-            pl.BlockSpec((1, 8, SIDE, PAIR), lambda i: (side(), 1, 0, 0)),
-            pl.BlockSpec((1, 8, SIDE, PAIR), lambda i: (side(), 2, 0, 0)),
+            pl.BlockSpec((1, 4, SIDE, PAIR), lambda i: (side(), 2, 0, 0)),
+            full(columns.shape),
+            full(columns.shape),
         ],
         out_specs=[
             keep,
@@ -807,7 +825,7 @@
         compiler_params=params(collective_id=1, has_side_effects=True),
         cost_estimate=cost(50),
         name="feed_forward",
-    )(tokens, passes, vec, mine, cotangent, pairs, wo_other, pairs, pairs)
+    )(tokens, passes, vec, mine, cotangent, pairs, wo_other, pairs, columns, columns_x)
 
 
 CHUNK = SIDE // 2
@@ -1278,7 +1296,10 @@
     slots = block_weights.shape[1] * n_dp
 
     if small:
-        pairs, wo_other, vec, norm, q, k, v, cat = gather(block_weights, vector_params, tokens, passes)
+        pairs, columns, wo_other, vec, norm, q, k, v, cat = gather(
+            block_weights, vector_params, tokens, passes
+        )
+        columns_x = hop_x(columns)
     else:
         every = lax.all_gather(block_weights.astype(bf16), "dp", axis=1, tiled=True)[0]
         near = to_pairs(every[:total_blocks])
@@ -1287,10 +1308,12 @@
         vec = lax.all_gather(vector_params, "dp", axis=1, tiled=True)
         vec = jnp.pad(vec, ((0, 16 - vec.shape[0]), (0, 0)))
         wo_other = swap(pairs[:, 6:8], 1)
+        columns = jnp.concatenate([near[12:15], near[18:21]], axis=0)
+        columns_x = jnp.concatenate([near[15:18], near[21:24]], axis=0)
         norm, q, k, v, cat = project(tokens, passes, vec, pairs)
     mine, lse = attend(lens, q, k, v)
     out_chip, second, grad_second, grad_mixed, sums_two, mid_send, mid_keep, *ends = feed(
-        small, tokens, passes, vec, mine, cotangent, pairs, wo_other
+        small, tokens, passes, vec, mine, cotangent, pairs, wo_other, columns, columns_x
     )
     out_far = swap(out_chip, 2)
     if small:

time: 233 us -> 234 us (level); the launches traced: 235 us -> 234 us
    pallas_call x1, Pallas kernels: 52.3 us -> 49.6 us  [gather(): pl.pallas_call(gather_kernel, in_specs=[vmem, vmem, far, vmem], out_specs...]
  transfers between devices with their start and end apart: 5 -> 6, of which waited for: 1 -> 1; matrix products, arithmetic and copies ran while one was open for 0% -> 0% of each run, Pallas kernels for 15% -> 25%
where the time goes in v12:
time: 234 us
  Pallas kernels  212 us (91%)
  starting transfers between devices  15.7 us (7%)
  local copies, waits for them, and re-layouts  3.24 us (1%)
    pallas_call x1, Pallas kernels, feed(): pl.pallas_call(functools.partial(feed_kernel, small), grid=(3 * half + 1,...  54.2 us
    pallas_call x1, Pallas kernels, gather(): pl.pallas_call(gather_kernel, in_specs=[vmem, vmem, far, vmem], out_specs...  49.6 us
    pallas_call x1, Pallas kernels, last(): pl.pallas_call(functools.partial(last_kernel, small), grid=(GRAD_STEPS +...  40.4 us
    pallas_call x1, Pallas kernels, attend_back(): pl.pallas_call(attend_back_kernel, grid_spec=pltpu.PrefetchScalarGridSpec...  34.5 us
    pallas_call x1, Pallas kernels, attend(): pl.pallas_call(attend_kernel, grid_spec=pltpu.PrefetchScalarGridSpec(num_...  24 us
    ppermute x3, starting transfers between devices, hop_z(): return lax.ppermute(value, 'dp', pairs)  12.9 us
    pallas_call x1, Pallas kernels, renew(): pl.pallas_call(renew_kernel, grid=(4,), in_specs=[pair] * 5 + [slot] * 5...  9.18 us
  transfers between devices with their start and end apart: 6, of which 1 were waited for; matrix products, arithmetic and copies ran while one was open for 0% of the time, Pallas kernels for 25%

profile of v12, /device:TPU:0, one launch (start us, length us, event | category | flops | bytes accessed | tf_op | source)
XLA Modules:
  0.0 233.6 jit_solution(15785330596058030388)
XLA Ops:
  0.6 49.6 %gather.1 = (bf16[2,24,192,384]{3,2,1,0:T(8,128)(2,1)}, bf16[6,192,384]{2,1,0:T(8,128)(2,1)}, bf16[2,2,192,384]{3,2,1,0:T(8,128)(2,1)}, f32[16,768]{1,0:T(8,128)...) custom-call(f32[1,6,192,192]{3,2,1,0:T(8,128)} %weight.1, ...), custom_call_target="tpu_custom_call" | custom-call | flops 65999998976 | bytes 60000000 | tf_op jit(solution)/shard_map/gather/pallas_call | solution.py:285
  50.2 0.7 collective-permute-start
  50.9 24.0 %attend.1 = (bf16[2048,384]{1,0:T(8,128)(2,1)}, f32[8,2048]{1,0:T(8,128)}) custom-call(s32[8]{0:T(128)} %bitcast.5, bf16[2048,384]{1,0:T(8,128)(2,1)} %get-tuple-element.52.q, bf16[2048,384]{1,0:T(8,128)(2,1)} %get-tuple-element.53.k, bf16[2048,384]{1,0:T(8,128)(2,1)} %get-tuple-element.54.v), custom_call_target="tpu_custom_call" | custom-call | flops 32999999488 | bytes 30000000 | tf_op jit(solution)/shard_map/attend/pallas_call | solution.py:424
  74.9 0.0 collective-permute-done.columns_x
  74.9 0.0 copy-start.10
  74.9 0.9 copy-done.10
  75.8 54.2 %feed_forward.1 = (bf16[1024,768]{1,0:T(8,128)(2,1)}, f32[1024,768]{1,0:T(8,128)}, f32[1024,768]{1,0:T(8,128)}, bf16[2048,384]{1,0:T(8,128)(2,1)}, f32[8,768]{1,...) custom-call(bf16[2048,768]{1,0:T(8,128)(2,1)} %tok.3, ...), custom_call_target="tpu_custom_call" | custom-call | flops 54999998464 | bytes 50000000 | tf_op jit(solution)/shard_map/feed_forward/pallas_call | solution.py:776
  130.0 0.7 collective-permute-start.1
  130.7 0.7 collective-permute-start.2
  131.4 11.5 %collective-permute-start.3 = (bf16[3,192,384]{2,1,0:T(8,128)(2,1)}, bf16[3,192,384]{2,1,0:T(8,128)(2,1)S(1)}, u32[]{:S(2)}, u32[]{:S(2)}) collective-permute-start(bf16[3,192,384]{2,1,0:T(8,128)(2,1)} %get-tuple-element.61), channel_id=1, source_target_pairs={{0,24},{4,28},{1,25},{5,29},{2,26},{6,30},{3,27},{7,31}} | collective-permute-start | bytes 1327112 | tf_op jit(solution)/shard_map/ppermute | solution.py:1267
  142.9 1.1 collective-permute-start.5
  144.0 1.0 collective-permute-start.4
  145.0 34.5 %attend_back.1 = (bf16[2048,384]{1,0:T(8,128)(2,1)}, bf16[2048,384]{1,0:T(8,128)(2,1)}, bf16[2048,384]{1,0:T(8,128)(2,1)}) custom-call(s32[8]{0:T(128)} %bitcast.6, bf16[2048,384]{1,0:T(8,128)(2,1)} %get-tuple-element.52.q, bf16[2048,384]{1,0:T(8,128)(2,1)} %get-tuple-element.53.k, bf16[2048,384]{1,0:T(8,128)(2,1)} %get-tuple-element.54.v, ...), custom_call_target="tpu_custom_call" | custom-call | flops 44000002048 | bytes 40000000 | tf_op jit(solution)/shard_map/attend_back/pallas_call | solution.py:505
  179.6 0.0 collective-permute-done.1.one
  179.6 0.0 collective-permute-done.2.two
  179.6 0.0 collective-permute-done.3.three
  179.6 0.0 collective-permute-done.5.mid_near
  179.6 0.0 copy-start.9
  179.6 0.7 collective-permute-done.4.far
  180.3 0.0 copy-start.8
  180.3 0.2 copy-done.9
  180.5 0.9 copy-done.8
  181.4 0.0 copy-start.6
  181.4 0.0 copy-start.7
  181.4 0.0 copy-start
  181.4 0.0 copy-start.1
  181.4 0.0 copy-start.2
  181.4 0.0 copy-start.3
  181.5 0.0 copy-start.5
  181.5 40.4 %last.1 = (bf16[2048,768]{1,0:T(8,128)(2,1)}, bf16[2048,768]{1,0:T(8,128)(2,1)}, f32[3,192,384]{2,1,0:T(8,128)}, f32[16,128]{1,0:T(8,128)}) custom-call(bf16[2048,768]{1,0:T(8,128)(2,1)} %get-tuple-element.50.norm_all, bf16[2048,384]{1,0:T(8,128)(2,1)} %get-tuple-element.67.dq_all, bf16[2048,384]{1,0:T(8,128)(2,1)} %get-tuple-element.68.dk_all, ...), custom_call_target="tpu_custom_call" | custom-call | flops 41799999488 | bytes 38000000 | tf_op jit(solution)/shard_map/last/pallas_call | solution.py:1159
  221.9 0.0 copy-done.6
  221.9 0.0 copy-done.7
  221.9 1.3 divide_subtract_fusion
  223.3 0.0 copy-done
  223.3 0.0 copy-done.1
  223.3 0.0 copy-done.2
  223.3 0.0 copy-done.3
  223.3 0.0 copy-done.5
  223.3 0.0 copy-start.4
  223.3 1.2 copy-done.4
  224.5 9.2 %renew.1 = (f32[1,6,192,192]{3,2,1,0:T(8,128)}, f32[1,6,192,192]{3,2,1,0:T(8,128)}, f32[1,6,192,192]{3,2,1,0:T(8,128)}, f32[1,6,192,192]{3,2,1,0:T(8,128)}, bf16...) custom-call(f32[3,192,384]{2,1,0:T(8,128)S(1)} %copy-done.4, bf16[3,192,384]{2,1,0:T(8,128)(2,1)S(1)} %copy-done.5, ...), custom_call_target="tpu_custom_call" | custom-call | flops 8800000000 | bytes 8000000 | tf_op jit(solution)/shard_map/renew/pallas_call | solution.py:1234
Async XLA Ops:
  50.2 24.7 %collective-permute-start = (bf16[6,192,384]{2,1,0:T(8,128)(2,1)}, bf16[6,192,384]{2,1,0:T(8,128)(2,1)S(1)}, u32[]{:S(2)}, u32[]{:S(2)}) collective-permute-start(bf16[6,192,384]{2,1,0:T(8,128)(2,1)} %get-tuple-element.58.columns), channel_id=1, source_target_pairs={{0,4},{4,0},{8,12},{12,8},{16,20},{20,16},{24,28},{28,24},{1,5},{5... | collective-permute-start | bytes 2654216 | tf_op jit(solution)/shard_map/ppermute | solution.py:1262
  74.9 0.9 copy-start.10
  130.0 49.6 %collective-permute-start.1 = (bf16[3,192,384]{2,1,0:T(8,128)(2,1)}, bf16[3,192,384]{2,1,0:T(8,128)(2,1)S(1)}, u32[]{:S(2)}, u32[]{:S(2)}) collective-permute-start(bf16[3,192,384]{2,1,0:T(8,128)(2,1)} %get-tuple-element.59), channel_id=1, source_target_pairs={{16,24},{20,28},{17,25},{21,29},{18,26},{22,30},{19,27},{23,31}} | collective-permute-start | bytes 1327112 | tf_op jit(solution)/shard_map/ppermute | solution.py:1267
  130.7 48.9 %collective-permute-start.2 = (bf16[3,192,384]{2,1,0:T(8,128)(2,1)}, bf16[3,192,384]{2,1,0:T(8,128)(2,1)S(1)}, u32[]{:S(2)}, u32[]{:S(2)}) collective-permute-start(bf16[3,192,384]{2,1,0:T(8,128)(2,1)} %get-tuple-element.60), channel_id=1, source_target_pairs={{8,24},{12,28},{9,25},{13,29},{10,26},{14,30},{11,27},{15,31}} | collective-permute-start | bytes 1327112 | tf_op jit(solution)/shard_map/ppermute | solution.py:1267
  131.4 48.2 %collective-permute-start.3 = (bf16[3,192,384]{2,1,0:T(8,128)(2,1)}, bf16[3,192,384]{2,1,0:T(8,128)(2,1)S(1)}, u32[]{:S(2)}, u32[]{:S(2)}) collective-permute-start(bf16[3,192,384]{2,1,0:T(8,128)(2,1)} %get-tuple-element.61), channel_id=1, source_target_pairs={{0,24},{4,28},{1,25},{5,29},{2,26},{6,30},{3,27},{7,31}} | collective-permute-start | bytes 1327112 | tf_op jit(solution)/shard_map/ppermute | solution.py:1267
  142.9 36.7 %collective-permute-start.5 = (bf16[6,192,384]{2,1,0:T(8,128)(2,1)}, bf16[6,192,384]{2,1,0:T(8,128)(2,1)S(1)}, u32[]{:S(2)}, u32[]{:S(2)}) collective-permute-start(bf16[6,192,384]{2,1,0:T(8,128)(2,1)} %get-tuple-element.63), channel_id=1, source_target_pairs={{0,4},{4,0},{8,12},{12,8},{16,20},{20,16},{24,28},{28,24},{1,5},{5... | collective-permute-start | bytes 2654216 | tf_op jit(solution)/shard_map/ppermute | solution.py:1262
  144.0 36.3 %collective-permute-start.4 = (bf16[1024,768]{1,0:T(8,128)(2,1)}, bf16[1024,768]{1,0:T(8,128)(2,1)S(1)}, u32[]{:S(2)}, u32[]{:S(2)}) collective-permute-start(bf16[1024,768]{1,0:T(8,128)(2,1)} %get-tuple-element.62.chip), channel_id=1, source_target_pairs={{0,2},{1,3},{2,0},{3,1},{4,6},{5,7},{6,4},{7,5},{8,10},{9,11},{10,... | collective-permute-start | bytes 4718600 | tf_op jit(solution)/shard_map/ppermute | solution.py:1258
  179.6 0.9 copy-start.9
  180.3 1.1 copy-start.8
  181.4 40.5 %copy-start.6 = (f32[9,96]{1,0:T(8,128)S(1)}, f32[9,96]{1,0:T(8,128)}, u32[]{:S(2)}) copy-start(f32[9,96]{1,0:T(8,128)} %vec_own.1) | copy-start | bytes 10372
  181.4 40.5 %copy-start.7 = (f32[9,96]{1,0:T(8,128)S(1)}, f32[9,96]{1,0:T(8,128)}, u32[]{:S(2)}) copy-start(f32[9,96]{1,0:T(8,128)} %param.17) | copy-start | bytes 10372
  181.4 41.8 %copy-start = (f32[1,6,192,192]{3,2,1,0:T(8,128)S(1)}, f32[1,6,192,192]{3,2,1,0:T(8,128)}, u32[]{:S(2)}) copy-start(f32[1,6,192,192]{3,2,1,0:T(8,128)} %weight.1) | copy-start | bytes 2654212
  181.4 41.8 %copy-start.1 = (f32[1,6,192,192]{3,2,1,0:T(8,128)S(1)}, f32[1,6,192,192]{3,2,1,0:T(8,128)}, u32[]{:S(2)}) copy-start(f32[1,6,192,192]{3,2,1,0:T(8,128)} %left.1) | copy-start | bytes 2654212
  181.4 41.8 %copy-start.2 = (f32[1,6,192,192]{3,2,1,0:T(8,128)S(1)}, f32[1,6,192,192]{3,2,1,0:T(8,128)}, u32[]{:S(2)}) copy-start(f32[1,6,192,192]{3,2,1,0:T(8,128)} %right.1) | copy-start | bytes 2654212
  181.4 41.8 %copy-start.3 = (f32[1,6,192,192]{3,2,1,0:T(8,128)S(1)}, f32[1,6,192,192]{3,2,1,0:T(8,128)}, u32[]{:S(2)}) copy-start(f32[1,6,192,192]{3,2,1,0:T(8,128)} %left_root.1) | copy-start | bytes 2654212
  181.5 41.8 %copy-start.5 = (bf16[3,192,384]{2,1,0:T(8,128)(2,1)S(1)}, bf16[3,192,384]{2,1,0:T(8,128)(2,1)}, u32[]{:S(2)}) copy-start(bf16[3,192,384]{2,1,0:T(8,128)(2,1)} %get-tuple-element.78.own) | copy-start | bytes 1327108
  223.3 1.2 copy-start.4

commit v13 on v12

--- a/solution.py
+++ b/solution.py
@@ -832,9 +832,9 @@
 CHUNKS = 18
 TAKEN = (
     ((8, 3), (10, 4), (12, 12)),
-    ((5, 1), (7, 3), (8, 4), (9, 6), (10, 7), (11, 8), (12, 12)),
-    ((2, 2), (4, 3), (5, 4), (7, 6), (8, 8), (9, 9), (10, 11), (12, 12)),
-    ((0, 3), (2, 5), (4, 6), (5, 7), (6, 8), (7, 12)),
+    ((3, 1), (5, 2), (7, 3), (8, 4), (9, 6), (10, 7), (11, 8), (12, 12)),
+    ((1, 2), (2, 3), (5, 4), (6, 5), (7, 6), (8, 8), (9, 9), (10, 11), (12, 12)),
+    ((-1, 3), (2, 5), (4, 6), (5, 7), (6, 8), (7, 12)),
 )
 GRAD_STEPS = 3
 
@@ -910,6 +910,28 @@
         sums[PASSES + 2 : PASSES + 4] = sums_two[0:2]
         pl.semaphore_wait(barrier, 8 if small else 1)
 
+    if small:
+
+        def term_of(k):
+            rows = pl.ds(pl.multiple_of((k % 2) * CHUNK, 16), CHUNK)
+
+            @pl.when(jnp.asarray(k) < 6)
+            def _():
+                x_copy(k).wait_recv()
+                total[...] = g_keep[k // 2, rows, :].astype(f32) + x_in[k].astype(f32)
+
+            @pl.when(jnp.asarray(k) >= 6)
+            def _():
+                total[...] = mid_keep[k // 2 - 3, rows, :].astype(f32) + mid_near[k // 2 - 3, rows, :].astype(f32)
+
+            return total[...]
+
+        @pl.when((step == 0) & (z == 3))
+        def _():
+            for k in (6, 7, 8, 12, 13):
+                z_out[k] = term_of(k).astype(bf16)
+                z_copy(k).start()
+
     def mine_of(grad):
         return jnp.where(side == 0, grad[:, :SIDE], grad[:, SIDE:])
 
@@ -989,20 +1011,6 @@
 
     if small:
 
-        def term_of(k):
-            rows = pl.ds(pl.multiple_of((k % 2) * CHUNK, 16), CHUNK)
-
-            @pl.when(jnp.asarray(k) < 6)
-            def _():
-                x_copy(k).wait_recv()
-                total[...] = g_keep[k // 2, rows, :].astype(f32) + x_in[k].astype(f32)
-
-            @pl.when(jnp.asarray(k) >= 6)
-            def _():
-                total[...] = mid_keep[k // 2 - 3, rows, :].astype(f32) + mid_near[k // 2 - 3, rows, :].astype(f32)
-
-            return total[...]
-
         def keep_late(k, pair, total):
             late[pair, pl.ds(pl.multiple_of((k % 2) * CHUNK, 16), CHUNK), :] = total
 
@@ -1052,13 +1060,11 @@
                 z_out[k] = term_of(k).astype(bf16)
                 up_copy(k).start()
 
-        for at, first_chunk, upto in ((0, 12, 14), (7, 14, 18)):
-
-            @pl.when((step == at) & (z == 3))
-            def _(first_chunk=first_chunk, upto=upto):
-                for k in range(first_chunk, upto):
-                    z_out[k] = term_of(k).astype(bf16)
-                    z_copy(k).start()
+        @pl.when((step == 7) & (z == 3))
+        def _():
+            for k in range(14, CHUNKS):
+                z_out[k] = term_of(k).astype(bf16)
+                z_copy(k).start()
 
         for at, first_chunk, upto in ((10, 12, 16), (11, 16, 18)):
 
@@ -1205,9 +1211,18 @@
 
 
 def renew_kernel(
-    late, own, one, two, three, weight, left, right, left_root, right_root, output, input_grad,
-    left_new, right_new, step, new, output_new, input_grad_new,
+    late, own, one, two, three, weight, left, right, left_root, right_root, output, input_grad, vec_sum, vec, moment,
+    left_new, right_new, step, new, output_new, input_grad_new, vec_grad, moment_new, vec_new,
 ):
+    @pl.when(pl.program_id(0) == 0)
+    def _():
+        rows, wide = vec.shape
+        grad = vec_sum[:rows, :wide]
+        square = decay * moment[...] + (1.0 - decay) * grad * grad
+        vec_grad[...] = grad
+        moment_new[...] = square
+        vec_new[...] = vec[...] - rate_vector * grad / (jnp.sqrt(square) + moment_eps)
+
     output_new[...] = output[...]
     input_grad_new[...] = input_grad[...]
 
@@ -1227,21 +1242,21 @@
             new[0, n] = weight[0, n] - rate_matrix * value
 
 
-def renew(late, own, far, weight, left, right, left_root, right_root, output, input_grad):
+def renew(late, own, far, weight, left, right, left_root, right_root, output, input_grad, vec_sum, vec, moment):
     pair = pl.BlockSpec((1, SIDE, PAIR), lambda i: (jnp.minimum(i, 2), 0, 0))
     slot = pl.BlockSpec((1, 2, SIDE, SIDE), lambda i: (0, jnp.minimum(i, 2), 0, 0))
     rows = pl.BlockSpec((output.shape[0] // 4, D), lambda i: (i, 0))
     return pl.pallas_call(
         renew_kernel,
         grid=(4,),
-        in_specs=[pair] * 5 + [slot] * 5 + [rows] * 2,
-        out_specs=[slot] * 4 + [rows] * 2,
+        in_specs=[pair] * 5 + [slot] * 5 + [rows] * 2 + [full(vec_sum.shape)] + [full(vec.shape)] * 2,
+        out_specs=[slot] * 4 + [rows] * 2 + [full(vec.shape)] * 3,
         out_shape=[jax.ShapeDtypeStruct(weight.shape, f32)] * 4
-        + [jax.ShapeDtypeStruct(value.shape, value.dtype) for value in (output, input_grad)],
+        + [jax.ShapeDtypeStruct(value.shape, value.dtype) for value in (output, input_grad, vec, vec, vec)],
         compiler_params=params(46),
         cost_estimate=cost(8),
         name="renew",
-    )(late, own, *far, weight, left, right, left_root, right_root, output, input_grad)
+    )(late, own, *far, weight, left, right, left_root, right_root, output, input_grad, vec_sum, vec, moment)
 
 
 def to_pairs(blocks):
@@ -1328,11 +1343,11 @@
     )
     if small:
         late, vector_sum = sums
-        left_new, right_new, step, weight_new, output, input_grad = renew(
+        return_blocks = renew(
             late, ends[0], far, block_weights, block_left, block_right, block_left_root, block_right_root,
-            output, input_grad,
+            output, input_grad, vector_sum, vector_params, vector_moment,
         )
-        vector_grad = vector_sum[: PASSES + 4, : vector_params.shape[1]]
+        left_new, right_new, step, weight_new, output, input_grad, vector_grad, moment_new, vector_new = return_blocks
     else:
         vector_part, g_send, g_keep = sums[0][: PASSES + 4], *sums[1:]
         send, keep = ends
@@ -1352,8 +1367,8 @@
         left_new, right_new, step, weight_new = precondition(
             owned, block_weights, block_left, block_right, block_left_root, block_right_root
         )
-    moment_new = decay * vector_moment + (1.0 - decay) * vector_grad * vector_grad
-    vector_new = vector_params - rate_vector * vector_grad / (jnp.sqrt(moment_new) + moment_eps)
+        moment_new = decay * vector_moment + (1.0 - decay) * vector_grad * vector_grad
+        vector_new = vector_params - rate_vector * vector_grad / (jnp.sqrt(moment_new) + moment_eps)
     return (
         output,
         input_grad,

time: 234 us -> 231 us (0.987)
  Pallas kernels: 212 us -> 209 us
  transfers between devices with their start and end apart: 6 -> 6, of which waited for: 1 -> 1; matrix products, arithmetic and copies ran while one was open for 0% -> 0% of each run, Pallas kernels for 25% -> 24%
where the time goes in v13:
time: 231 us
  Pallas kernels  209 us (90%)
  starting transfers between devices  16 us (7%)
  local copies, waits for them, and re-layouts  3.94 us (2%)
    pallas_call x1, Pallas kernels, feed(): pl.pallas_call(functools.partial(feed_kernel, small), grid=(3 * half + 1,...  55 us
    pallas_call x1, Pallas kernels, gather(): pl.pallas_call(gather_kernel, in_specs=[vmem, vmem, far, vmem], out_specs...  49.6 us
    pallas_call x1, Pallas kernels, last(): pl.pallas_call(functools.partial(last_kernel, small), grid=(GRAD_STEPS +...  38.5 us
    pallas_call x1, Pallas kernels, attend_back(): pl.pallas_call(attend_back_kernel, grid_spec=pltpu.PrefetchScalarGridSpec...  33.4 us
    pallas_call x1, Pallas kernels, attend(): pl.pallas_call(attend_kernel, grid_spec=pltpu.PrefetchScalarGridSpec(num_...  23.1 us
    ppermute x3, starting transfers between devices, hop_z(): return lax.ppermute(value, 'dp', pairs)  13.2 us
    pallas_call x1, Pallas kernels, renew(): pl.pallas_call(renew_kernel, grid=(4,), in_specs=[pair] * 5 + [slot] * 5...  9.22 us
  transfers between devices with their start and end apart: 6, of which 1 were waited for; matrix products, arithmetic and copies ran while one was open for 0% of the time, Pallas kernels for 24%

profile of v13, /device:TPU:0, one launch (start us, length us, event | category | flops | bytes accessed | tf_op | source)
XLA Modules:
  0.0 231.3 jit_solution(15653637719596663476)
XLA Ops:
  0.6 49.6 %gather.1 = (bf16[2,24,192,384]{3,2,1,0:T(8,128)(2,1)}, bf16[6,192,384]{2,1,0:T(8,128)(2,1)}, bf16[2,2,192,384]{3,2,1,0:T(8,128)(2,1)}, f32[16,768]{1,0:T(8,128)...) custom-call(f32[1,6,192,192]{3,2,1,0:T(8,128)} %weight.1, ...), custom_call_target="tpu_custom_call" | custom-call | flops 65999998976 | bytes 60000000 | tf_op jit(solution)/shard_map/gather/pallas_call | solution.py:285
  50.2 0.7 collective-permute-start
  50.9 23.1 %attend.1 = (bf16[2048,384]{1,0:T(8,128)(2,1)}, f32[8,2048]{1,0:T(8,128)}) custom-call(s32[8]{0:T(128)} %bitcast.5, bf16[2048,384]{1,0:T(8,128)(2,1)} %get-tuple-element.55.q, bf16[2048,384]{1,0:T(8,128)(2,1)} %get-tuple-element.56.k, bf16[2048,384]{1,0:T(8,128)(2,1)} %get-tuple-element.57.v), custom_call_target="tpu_custom_call" | custom-call | flops 32999999488 | bytes 30000000 | tf_op jit(solution)/shard_map/attend/pallas_call | solution.py:424
  74.0 0.0 collective-permute-done.columns_x
  74.0 0.0 copy-start.11
  74.0 0.9 copy-done.11
  75.0 55.0 %feed_forward.1 = (bf16[1024,768]{1,0:T(8,128)(2,1)}, f32[1024,768]{1,0:T(8,128)}, f32[1024,768]{1,0:T(8,128)}, bf16[2048,384]{1,0:T(8,128)(2,1)}, f32[8,768]{1,...) custom-call(bf16[2048,768]{1,0:T(8,128)(2,1)} %tok.3, ...), custom_call_target="tpu_custom_call" | custom-call | flops 54999998464 | bytes 50000000 | tf_op jit(solution)/shard_map/feed_forward/pallas_call | solution.py:776
  130.0 0.7 collective-permute-start.1
  130.7 0.7 collective-permute-start.2
  131.4 11.8 %collective-permute-start.3 = (bf16[3,192,384]{2,1,0:T(8,128)(2,1)}, bf16[3,192,384]{2,1,0:T(8,128)(2,1)S(1)}, u32[]{:S(2)}, u32[]{:S(2)}) collective-permute-start(bf16[3,192,384]{2,1,0:T(8,128)(2,1)} %get-tuple-element.64), channel_id=1, source_target_pairs={{0,24},{4,28},{1,25},{5,29},{2,26},{6,30},{3,27},{7,31}} | collective-permute-start | bytes 1327112 | tf_op jit(solution)/shard_map/ppermute | solution.py:1282
  143.2 0.8 collective-permute-start.5
  144.0 1.3 collective-permute-start.4
  145.3 33.4 %attend_back.1 = (bf16[2048,384]{1,0:T(8,128)(2,1)}, bf16[2048,384]{1,0:T(8,128)(2,1)}, bf16[2048,384]{1,0:T(8,128)(2,1)}) custom-call(s32[8]{0:T(128)} %bitcast.6, bf16[2048,384]{1,0:T(8,128)(2,1)} %get-tuple-element.55.q, bf16[2048,384]{1,0:T(8,128)(2,1)} %get-tuple-element.56.k, bf16[2048,384]{1,0:T(8,128)(2,1)} %get-tuple-element.57.v, ...), custom_call_target="tpu_custom_call" | custom-call | flops 44000002048 | bytes 40000000 | tf_op jit(solution)/shard_map/attend_back/pallas_call | solution.py:505
  178.7 0.0 collective-permute-done.1.one
  178.7 0.0 collective-permute-done.2.two
  178.7 0.0 collective-permute-done.3.three
  178.7 0.0 collective-permute-done.5.mid_near
  178.7 0.0 copy-start.10
  178.7 1.6 collective-permute-done.4.far
  180.3 0.0 copy-start.9
  180.3 0.0 copy-done.10
  180.3 1.1 copy-done.9
  181.4 0.0 copy-start
  181.4 0.0 copy-start.1
  181.4 0.0 copy-start.2
  181.4 0.0 copy-start.3
  181.4 0.0 copy-start.4
  181.4 0.0 copy-start.5
  181.5 0.0 copy-start.7
  181.5 38.5 %last.1 = (bf16[2048,768]{1,0:T(8,128)(2,1)}, bf16[2048,768]{1,0:T(8,128)(2,1)}, f32[3,192,384]{2,1,0:T(8,128)}, f32[16,128]{1,0:T(8,128)}) custom-call(bf16[2048,768]{1,0:T(8,128)(2,1)} %get-tuple-element.53.norm_all, bf16[2048,384]{1,0:T(8,128)(2,1)} %get-tuple-element.70.dq_all, bf16[2048,384]{1,0:T(8,128)(2,1)} %get-tuple-element.71.dk_all, ...), custom_call_target="tpu_custom_call" | custom-call | flops 41799999488 | bytes 38000000 | tf_op jit(solution)/shard_map/last/pallas_call | solution.py:1165
  220.0 0.0 copy-done
  220.0 0.0 copy-done.1
  220.0 0.0 copy-done.2
  220.0 0.0 copy-done.3
  220.0 0.0 copy-done.4
  220.0 0.0 copy-done.5
  220.0 0.0 copy-done.7
  220.0 0.0 copy-start.6
  220.1 1.2 copy-done.6
  221.2 0.0 copy-start.8
  221.2 0.7 copy-done.8
  221.9 9.2 %renew.1 = (f32[1,6,192,192]{3,2,1,0:T(8,128)}, f32[1,6,192,192]{3,2,1,0:T(8,128)}, f32[1,6,192,192]{3,2,1,0:T(8,128)}, f32[1,6,192,192]{3,2,1,0:T(8,128)}, bf16...) custom-call(f32[3,192,384]{2,1,0:T(8,128)S(1)} %copy-done.6, ...), custom_call_target="tpu_custom_call" | custom-call | flops 8800000000 | bytes 8000000 | tf_op jit(solution)/shard_map/renew/pallas_call | solution.py:1249
Async XLA Ops:
  50.2 23.8 %collective-permute-start = (bf16[6,192,384]{2,1,0:T(8,128)(2,1)}, bf16[6,192,384]{2,1,0:T(8,128)(2,1)S(1)}, u32[]{:S(2)}, u32[]{:S(2)}) collective-permute-start(bf16[6,192,384]{2,1,0:T(8,128)(2,1)} %get-tuple-element.61.columns), channel_id=1, source_target_pairs={{0,4},{4,0},{8,12},{12,8},{16,20},{20,16},{24,28},{28,24},{1,5},{5... | collective-permute-start | bytes 2654216 | tf_op jit(solution)/shard_map/ppermute | solution.py:1277
  74.0 0.9 copy-start.11
  130.0 48.7 %collective-permute-start.1 = (bf16[3,192,384]{2,1,0:T(8,128)(2,1)}, bf16[3,192,384]{2,1,0:T(8,128)(2,1)S(1)}, u32[]{:S(2)}, u32[]{:S(2)}) collective-permute-start(bf16[3,192,384]{2,1,0:T(8,128)(2,1)} %get-tuple-element.62), channel_id=1, source_target_pairs={{16,24},{20,28},{17,25},{21,29},{18,26},{22,30},{19,27},{23,31}} | collective-permute-start | bytes 1327112 | tf_op jit(solution)/shard_map/ppermute | solution.py:1282
  130.7 48.0 %collective-permute-start.2 = (bf16[3,192,384]{2,1,0:T(8,128)(2,1)}, bf16[3,192,384]{2,1,0:T(8,128)(2,1)S(1)}, u32[]{:S(2)}, u32[]{:S(2)}) collective-permute-start(bf16[3,192,384]{2,1,0:T(8,128)(2,1)} %get-tuple-element.63), channel_id=1, source_target_pairs={{8,24},{12,28},{9,25},{13,29},{10,26},{14,30},{11,27},{15,31}} | collective-permute-start | bytes 1327112 | tf_op jit(solution)/shard_map/ppermute | solution.py:1282
  131.4 47.3 %collective-permute-start.3 = (bf16[3,192,384]{2,1,0:T(8,128)(2,1)}, bf16[3,192,384]{2,1,0:T(8,128)(2,1)S(1)}, u32[]{:S(2)}, u32[]{:S(2)}) collective-permute-start(bf16[3,192,384]{2,1,0:T(8,128)(2,1)} %get-tuple-element.64), channel_id=1, source_target_pairs={{0,24},{4,28},{1,25},{5,29},{2,26},{6,30},{3,27},{7,31}} | collective-permute-start | bytes 1327112 | tf_op jit(solution)/shard_map/ppermute | solution.py:1282
  143.2 35.5 %collective-permute-start.5 = (bf16[6,192,384]{2,1,0:T(8,128)(2,1)}, bf16[6,192,384]{2,1,0:T(8,128)(2,1)S(1)}, u32[]{:S(2)}, u32[]{:S(2)}) collective-permute-start(bf16[6,192,384]{2,1,0:T(8,128)(2,1)} %get-tuple-element.66), channel_id=1, source_target_pairs={{0,4},{4,0},{8,12},{12,8},{16,20},{20,16},{24,28},{28,24},{1,5},{5... | collective-permute-start | bytes 2654216 | tf_op jit(solution)/shard_map/ppermute | solution.py:1277
  144.0 36.2 %collective-permute-start.4 = (bf16[1024,768]{1,0:T(8,128)(2,1)}, bf16[1024,768]{1,0:T(8,128)(2,1)S(1)}, u32[]{:S(2)}, u32[]{:S(2)}) collective-permute-start(bf16[1024,768]{1,0:T(8,128)(2,1)} %get-tuple-element.65.chip), channel_id=1, source_target_pairs={{0,2},{1,3},{2,0},{3,1},{4,6},{5,7},{6,4},{7,5},{8,10},{9,11},{10,... | collective-permute-start | bytes 4718600 | tf_op jit(solution)/shard_map/ppermute | solution.py:1273
  178.7 1.6 copy-start.10
  180.3 1.1 copy-start.9
  181.4 38.6 %copy-start = (f32[1,6,192,192]{3,2,1,0:T(8,128)S(1)}, f32[1,6,192,192]{3,2,1,0:T(8,128)}, u32[]{:S(2)}) copy-start(f32[1,6,192,192]{3,2,1,0:T(8,128)} %weight.1) | copy-start | bytes 2654212
  181.4 38.6 %copy-start.1 = (f32[1,6,192,192]{3,2,1,0:T(8,128)S(1)}, f32[1,6,192,192]{3,2,1,0:T(8,128)}, u32[]{:S(2)}) copy-start(f32[1,6,192,192]{3,2,1,0:T(8,128)} %left.1) | copy-start | bytes 2654212
  181.4 38.6 %copy-start.2 = (f32[1,6,192,192]{3,2,1,0:T(8,128)S(1)}, f32[1,6,192,192]{3,2,1,0:T(8,128)}, u32[]{:S(2)}) copy-start(f32[1,6,192,192]{3,2,1,0:T(8,128)} %right.1) | copy-start | bytes 2654212
  181.4 38.6 %copy-start.3 = (f32[1,6,192,192]{3,2,1,0:T(8,128)S(1)}, f32[1,6,192,192]{3,2,1,0:T(8,128)}, u32[]{:S(2)}) copy-start(f32[1,6,192,192]{3,2,1,0:T(8,128)} %left_root.1) | copy-start | bytes 2654212
  181.4 38.6 %copy-start.4 = (f32[9,96]{1,0:T(8,128)S(1)}, f32[9,96]{1,0:T(8,128)}, u32[]{:S(2)}) copy-start(f32[9,96]{1,0:T(8,128)} %vec.1) | copy-start | bytes 10372
  181.4 38.6 %copy-start.5 = (f32[9,96]{1,0:T(8,128)S(1)}, f32[9,96]{1,0:T(8,128)}, u32[]{:S(2)}) copy-start(f32[9,96]{1,0:T(8,128)} %moment.1) | copy-start | bytes 10372
  181.5 38.6 %copy-start.7 = (bf16[3,192,384]{2,1,0:T(8,128)(2,1)S(1)}, bf16[3,192,384]{2,1,0:T(8,128)(2,1)}, u32[]{:S(2)}) copy-start(bf16[3,192,384]{2,1,0:T(8,128)(2,1)} %get-tuple-element.81.own) | copy-start | bytes 1327108
  220.0 1.2 copy-start.6
  221.2 0.7 copy-start.8

commit v14 on v13

--- a/solution.py
+++ b/solution.py
@@ -926,6 +926,12 @@
 
             return total[...]
 
+        @pl.when((step == 0) & (z == 0))
+        def _():
+            for k in range(6, CHUNKS):
+                z_out[k] = term_of(k).astype(bf16)
+                up_copy(k).start()
+
         @pl.when((step == 0) & (z == 3))
         def _():
             for k in (6, 7, 8, 12, 13):
@@ -1054,19 +1060,13 @@
                 end = jnp.where((z == place) & (step >= at), upto, end)
         lax.fori_loop(begin, end, at_position, 0)
 
-        @pl.when((step == 0) & (z == 0))
-        def _():
-            for k in range(6, CHUNKS):
-                z_out[k] = term_of(k).astype(bf16)
-                up_copy(k).start()
-
         @pl.when((step == 7) & (z == 3))
         def _():
             for k in range(14, CHUNKS):
                 z_out[k] = term_of(k).astype(bf16)
                 z_copy(k).start()
 
-        for at, first_chunk, upto in ((10, 12, 16), (11, 16, 18)):
+        for at, first_chunk, upto in ((9, 12, 15), (10, 15, 18)):
 
             @pl.when((step == at) & (z == 1))
             def _(first_chunk=first_chunk, upto=upto):

time: 231 us -> 232 us (level)
  transfers between devices with their start and end apart: 6 -> 6, of which waited for: 1 -> 1; matrix products, arithmetic and copies ran while one was open for 0% -> 0% of each run, Pallas kernels for 24% -> 25%
where the time goes in v14:
time: 232 us; the launch traced here: 231 us
  Pallas kernels  210 us (91%)
  starting transfers between devices  15.3 us (7%)
  local copies, waits for them, and re-layouts  3.94 us (2%)
    pallas_call x1, Pallas kernels, feed(): pl.pallas_call(functools.partial(feed_kernel, small), grid=(3 * half + 1,...  54 us
    pallas_call x1, Pallas kernels, gather(): pl.pallas_call(gather_kernel, in_specs=[vmem, vmem, far, vmem], out_specs...  49.6 us
    pallas_call x1, Pallas kernels, last(): pl.pallas_call(functools.partial(last_kernel, small), grid=(GRAD_STEPS +...  39 us
    pallas_call x1, Pallas kernels, attend_back(): pl.pallas_call(attend_back_kernel, grid_spec=pltpu.PrefetchScalarGridSpec...  34.5 us
    pallas_call x1, Pallas kernels, attend(): pl.pallas_call(attend_kernel, grid_spec=pltpu.PrefetchScalarGridSpec(num_...  24 us
    ppermute x3, starting transfers between devices, hop_z(): return lax.ppermute(value, 'dp', pairs)  12.5 us
    pallas_call x1, Pallas kernels, renew(): pl.pallas_call(renew_kernel, grid=(4,), in_specs=[pair] * 5 + [slot] * 5...  9.22 us
  transfers between devices with their start and end apart: 6, of which 1 were waited for; matrix products, arithmetic and copies ran while one was open for 0% of the time, Pallas kernels for 25%

profile of v14, /device:TPU:0, one launch (start us, length us, event | category | flops | bytes accessed | tf_op | source)
XLA Modules:
  0.0 230.9 jit_solution(11842677098176453352)
XLA Ops:
  0.6 49.6 %gather.1 = (bf16[2,24,192,384]{3,2,1,0:T(8,128)(2,1)}, bf16[6,192,384]{2,1,0:T(8,128)(2,1)}, bf16[2,2,192,384]{3,2,1,0:T(8,128)(2,1)}, f32[16,768]{1,0:T(8,128)...) custom-call(f32[1,6,192,192]{3,2,1,0:T(8,128)} %weight.1, ...), custom_call_target="tpu_custom_call" | custom-call | flops 65999998976 | bytes 60000000 | tf_op jit(solution)/shard_map/gather/pallas_call | solution.py:285
  50.2 0.7 collective-permute-start
  50.9 24.0 %attend.1 = (bf16[2048,384]{1,0:T(8,128)(2,1)}, f32[8,2048]{1,0:T(8,128)}) custom-call(s32[8]{0:T(128)} %bitcast.5, bf16[2048,384]{1,0:T(8,128)(2,1)} %get-tuple-element.55.q, bf16[2048,384]{1,0:T(8,128)(2,1)} %get-tuple-element.56.k, bf16[2048,384]{1,0:T(8,128)(2,1)} %get-tuple-element.57.v), custom_call_target="tpu_custom_call" | custom-call | flops 32999999488 | bytes 30000000 | tf_op jit(solution)/shard_map/attend/pallas_call | solution.py:424
  74.9 0.0 collective-permute-done.columns_x
  74.9 0.0 copy-start.11
  74.9 0.9 copy-done.11
  75.8 54.0 %feed_forward.1 = (bf16[1024,768]{1,0:T(8,128)(2,1)}, f32[1024,768]{1,0:T(8,128)}, f32[1024,768]{1,0:T(8,128)}, bf16[2048,384]{1,0:T(8,128)(2,1)}, f32[8,768]{1,...) custom-call(bf16[2048,768]{1,0:T(8,128)(2,1)} %tok.3, ...), custom_call_target="tpu_custom_call" | custom-call | flops 54999998464 | bytes 50000000 | tf_op jit(solution)/shard_map/feed_forward/pallas_call | solution.py:776
  129.8 0.7 collective-permute-start.1
  130.5 0.7 collective-permute-start.2
  131.2 11.1 %collective-permute-start.3 = (bf16[3,192,384]{2,1,0:T(8,128)(2,1)}, bf16[3,192,384]{2,1,0:T(8,128)(2,1)S(1)}, u32[]{:S(2)}, u32[]{:S(2)}) collective-permute-start(bf16[3,192,384]{2,1,0:T(8,128)(2,1)} %get-tuple-element.64), channel_id=1, source_target_pairs={{0,24},{4,28},{1,25},{5,29},{2,26},{6,30},{3,27},{7,31}} | collective-permute-start | bytes 1327112 | tf_op jit(solution)/shard_map/ppermute | solution.py:1282
  142.3 0.8 collective-permute-start.5
  143.2 1.3 collective-permute-start.4
  144.4 34.5 %attend_back.1 = (bf16[2048,384]{1,0:T(8,128)(2,1)}, bf16[2048,384]{1,0:T(8,128)(2,1)}, bf16[2048,384]{1,0:T(8,128)(2,1)}) custom-call(s32[8]{0:T(128)} %bitcast.6, bf16[2048,384]{1,0:T(8,128)(2,1)} %get-tuple-element.55.q, bf16[2048,384]{1,0:T(8,128)(2,1)} %get-tuple-element.56.k, bf16[2048,384]{1,0:T(8,128)(2,1)} %get-tuple-element.57.v, ...), custom_call_target="tpu_custom_call" | custom-call | flops 44000002048 | bytes 40000000 | tf_op jit(solution)/shard_map/attend_back/pallas_call | solution.py:505
  179.0 0.0 collective-permute-done.1.one
  179.0 0.0 collective-permute-done.2.two
  179.0 0.0 collective-permute-done.3.three
  179.0 0.0 collective-permute-done.5.mid_near
  179.0 0.0 copy-start.10
  179.0 0.4 collective-permute-done.4.far
  179.4 0.0 copy-start.9
  179.4 0.5 copy-done.10
  179.9 0.6 copy-done.9
  180.6 0.0 copy-start
  180.6 0.0 copy-start.1
  180.6 0.0 copy-start.2
  180.6 0.0 copy-start.3
  180.6 0.0 copy-start.4
  180.6 0.0 copy-start.5
  180.6 0.0 copy-start.7
  180.6 39.0 %last.1 = (bf16[2048,768]{1,0:T(8,128)(2,1)}, bf16[2048,768]{1,0:T(8,128)(2,1)}, f32[3,192,384]{2,1,0:T(8,128)}, f32[16,128]{1,0:T(8,128)}) custom-call(bf16[2048,768]{1,0:T(8,128)(2,1)} %get-tuple-element.53.norm_all, bf16[2048,384]{1,0:T(8,128)(2,1)} %get-tuple-element.70.dq_all, bf16[2048,384]{1,0:T(8,128)(2,1)} %get-tuple-element.71.dk_all, ...), custom_call_target="tpu_custom_call" | custom-call | flops 41799999488 | bytes 38000000 | tf_op jit(solution)/shard_map/last/pallas_call | solution.py:1165
  219.6 0.0 copy-done
  219.6 0.0 copy-done.1
  219.6 0.0 copy-done.2
  219.6 0.0 copy-done.3
  219.6 0.0 copy-done.4
  219.7 0.0 copy-done.5
  219.7 0.0 copy-done.7
  219.7 0.0 copy-start.6
  219.7 1.2 copy-done.6
  220.8 0.0 copy-start.8
  220.8 0.7 copy-done.8
  221.5 9.2 %renew.1 = (f32[1,6,192,192]{3,2,1,0:T(8,128)}, f32[1,6,192,192]{3,2,1,0:T(8,128)}, f32[1,6,192,192]{3,2,1,0:T(8,128)}, f32[1,6,192,192]{3,2,1,0:T(8,128)}, bf16...) custom-call(f32[3,192,384]{2,1,0:T(8,128)S(1)} %copy-done.6, ...), custom_call_target="tpu_custom_call" | custom-call | flops 8800000000 | bytes 8000000 | tf_op jit(solution)/shard_map/renew/pallas_call | solution.py:1249
Async XLA Ops:
  50.2 24.7 %collective-permute-start = (bf16[6,192,384]{2,1,0:T(8,128)(2,1)}, bf16[6,192,384]{2,1,0:T(8,128)(2,1)S(1)}, u32[]{:S(2)}, u32[]{:S(2)}) collective-permute-start(bf16[6,192,384]{2,1,0:T(8,128)(2,1)} %get-tuple-element.61.columns), channel_id=1, source_target_pairs={{0,4},{4,0},{8,12},{12,8},{16,20},{20,16},{24,28},{28,24},{1,5},{5... | collective-permute-start | bytes 2654216 | tf_op jit(solution)/shard_map/ppermute | solution.py:1277
  74.9 0.9 copy-start.11
  129.8 49.1 %collective-permute-start.1 = (bf16[3,192,384]{2,1,0:T(8,128)(2,1)}, bf16[3,192,384]{2,1,0:T(8,128)(2,1)S(1)}, u32[]{:S(2)}, u32[]{:S(2)}) collective-permute-start(bf16[3,192,384]{2,1,0:T(8,128)(2,1)} %get-tuple-element.62), channel_id=1, source_target_pairs={{16,24},{20,28},{17,25},{21,29},{18,26},{22,30},{19,27},{23,31}} | collective-permute-start | bytes 1327112 | tf_op jit(solution)/shard_map/ppermute | solution.py:1282
  130.5 48.4 %collective-permute-start.2 = (bf16[3,192,384]{2,1,0:T(8,128)(2,1)}, bf16[3,192,384]{2,1,0:T(8,128)(2,1)S(1)}, u32[]{:S(2)}, u32[]{:S(2)}) collective-permute-start(bf16[3,192,384]{2,1,0:T(8,128)(2,1)} %get-tuple-element.63), channel_id=1, source_target_pairs={{8,24},{12,28},{9,25},{13,29},{10,26},{14,30},{11,27},{15,31}} | collective-permute-start | bytes 1327112 | tf_op jit(solution)/shard_map/ppermute | solution.py:1282
  131.2 47.8 %collective-permute-start.3 = (bf16[3,192,384]{2,1,0:T(8,128)(2,1)}, bf16[3,192,384]{2,1,0:T(8,128)(2,1)S(1)}, u32[]{:S(2)}, u32[]{:S(2)}) collective-permute-start(bf16[3,192,384]{2,1,0:T(8,128)(2,1)} %get-tuple-element.64), channel_id=1, source_target_pairs={{0,24},{4,28},{1,25},{5,29},{2,26},{6,30},{3,27},{7,31}} | collective-permute-start | bytes 1327112 | tf_op jit(solution)/shard_map/ppermute | solution.py:1282
  142.3 36.6 %collective-permute-start.5 = (bf16[6,192,384]{2,1,0:T(8,128)(2,1)}, bf16[6,192,384]{2,1,0:T(8,128)(2,1)S(1)}, u32[]{:S(2)}, u32[]{:S(2)}) collective-permute-start(bf16[6,192,384]{2,1,0:T(8,128)(2,1)} %get-tuple-element.66), channel_id=1, source_target_pairs={{0,4},{4,0},{8,12},{12,8},{16,20},{20,16},{24,28},{28,24},{1,5},{5... | collective-permute-start | bytes 2654216 | tf_op jit(solution)/shard_map/ppermute | solution.py:1277
  143.2 36.2 %collective-permute-start.4 = (bf16[1024,768]{1,0:T(8,128)(2,1)}, bf16[1024,768]{1,0:T(8,128)(2,1)S(1)}, u32[]{:S(2)}, u32[]{:S(2)}) collective-permute-start(bf16[1024,768]{1,0:T(8,128)(2,1)} %get-tuple-element.65.chip), channel_id=1, source_target_pairs={{0,2},{1,3},{2,0},{3,1},{4,6},{5,7},{6,4},{7,5},{8,10},{9,11},{10,... | collective-permute-start | bytes 4718600 | tf_op jit(solution)/shard_map/ppermute | solution.py:1273
  179.0 0.9 copy-start.10
  179.4 1.1 copy-start.9
  180.6 39.1 %copy-start = (f32[1,6,192,192]{3,2,1,0:T(8,128)S(1)}, f32[1,6,192,192]{3,2,1,0:T(8,128)}, u32[]{:S(2)}) copy-start(f32[1,6,192,192]{3,2,1,0:T(8,128)} %weight.1) | copy-start | bytes 2654212
  180.6 39.1 %copy-start.1 = (f32[1,6,192,192]{3,2,1,0:T(8,128)S(1)}, f32[1,6,192,192]{3,2,1,0:T(8,128)}, u32[]{:S(2)}) copy-start(f32[1,6,192,192]{3,2,1,0:T(8,128)} %left.1) | copy-start | bytes 2654212
  180.6 39.1 %copy-start.2 = (f32[1,6,192,192]{3,2,1,0:T(8,128)S(1)}, f32[1,6,192,192]{3,2,1,0:T(8,128)}, u32[]{:S(2)}) copy-start(f32[1,6,192,192]{3,2,1,0:T(8,128)} %right.1) | copy-start | bytes 2654212
  180.6 39.1 %copy-start.3 = (f32[1,6,192,192]{3,2,1,0:T(8,128)S(1)}, f32[1,6,192,192]{3,2,1,0:T(8,128)}, u32[]{:S(2)}) copy-start(f32[1,6,192,192]{3,2,1,0:T(8,128)} %left_root.1) | copy-start | bytes 2654212
  180.6 39.1 %copy-start.4 = (f32[9,96]{1,0:T(8,128)S(1)}, f32[9,96]{1,0:T(8,128)}, u32[]{:S(2)}) copy-start(f32[9,96]{1,0:T(8,128)} %vec.1) | copy-start | bytes 10372
  180.6 39.1 %copy-start.5 = (f32[9,96]{1,0:T(8,128)S(1)}, f32[9,96]{1,0:T(8,128)}, u32[]{:S(2)}) copy-start(f32[9,96]{1,0:T(8,128)} %moment.1) | copy-start | bytes 10372
  180.6 39.1 %copy-start.7 = (bf16[3,192,384]{2,1,0:T(8,128)(2,1)S(1)}, bf16[3,192,384]{2,1,0:T(8,128)(2,1)}, u32[]{:S(2)}) copy-start(bf16[3,192,384]{2,1,0:T(8,128)(2,1)} %get-tuple-element.81.own) | copy-start | bytes 1327108
  219.7 1.2 copy-start.6
  220.8 0.7 copy-start.8

commit v15 on v14

--- a/solution.py
+++ b/solution.py
@@ -1336,7 +1336,7 @@
         mid_send = hop_x(mid_send)
     dq, dk, dv = attend_back(lens, q, k, v, mine, lse, grad_mixed)
     if small:
-        *far, out_far, mid_send, dq = tie(*far, out_far, mid_send, dq)
+        out_far, mid_send, dq = tie(out_far, mid_send, dq)
     output, input_grad, *sums = last(
         small, norm, dq, dk, dv, cat, tokens, passes, vec, grad_second, sums_two, second, out_chip, out_far,
         mid_send, mid_keep,

time: 232 us -> 232 us (level)
  transfers between devices with their start and end apart: 6 -> 6, of which waited for: 1 -> 0; matrix products, arithmetic and copies ran while one was open for 0% -> 0% of each run, Pallas kernels for 25% -> 43%
where the time goes in v15:
time: 232 us
  Pallas kernels  212 us (91%)
  starting transfers between devices  14.4 us (6%)
  local copies, waits for them, and re-layouts  4.2 us (2%)
    pallas_call x1, Pallas kernels, feed(): pl.pallas_call(functools.partial(feed_kernel, small), grid=(3 * half + 1,...  53.9 us
    pallas_call x1, Pallas kernels, gather(): pl.pallas_call(gather_kernel, in_specs=[vmem, vmem, far, vmem], out_specs...  49.6 us
    pallas_call x1, Pallas kernels, last(): pl.pallas_call(functools.partial(last_kernel, small), grid=(GRAD_STEPS +...  39.1 us
    pallas_call x1, Pallas kernels, attend_back(): pl.pallas_call(attend_back_kernel, grid_spec=pltpu.PrefetchScalarGridSpec...  35.7 us
    pallas_call x1, Pallas kernels, attend(): pl.pallas_call(attend_kernel, grid_spec=pltpu.PrefetchScalarGridSpec(num_...  24.8 us
    ppermute x3, starting transfers between devices, hop_z(): return lax.ppermute(value, 'dp', pairs)  11.6 us
    pallas_call x1, Pallas kernels, renew(): pl.pallas_call(renew_kernel, grid=(4,), in_specs=[pair] * 5 + [slot] * 5...  9.23 us
  transfers between devices with their start and end apart: 6, of which 0 were waited for; matrix products, arithmetic and copies ran while one was open for 0% of the time, Pallas kernels for 43%

profile of v15, /device:TPU:0, one launch (start us, length us, event | category | flops | bytes accessed | tf_op | source)
XLA Modules:
  0.0 232.0 jit_solution(1073017076520619746)
XLA Ops:
  0.6 49.6 %gather.1 = (bf16[2,24,192,384]{3,2,1,0:T(8,128)(2,1)}, bf16[6,192,384]{2,1,0:T(8,128)(2,1)}, bf16[2,2,192,384]{3,2,1,0:T(8,128)(2,1)}, f32[16,768]{1,0:T(8,128)...) custom-call(f32[1,6,192,192]{3,2,1,0:T(8,128)} %weight.1, ...), custom_call_target="tpu_custom_call" | custom-call | flops 65999998976 | bytes 60000000 | tf_op jit(solution)/shard_map/gather/pallas_call | solution.py:285
  50.2 0.7 collective-permute-start
  50.9 24.8 %attend.1 = (bf16[2048,384]{1,0:T(8,128)(2,1)}, f32[8,2048]{1,0:T(8,128)}) custom-call(s32[8]{0:T(128)} %bitcast.5, bf16[2048,384]{1,0:T(8,128)(2,1)} %get-tuple-element.52.q, bf16[2048,384]{1,0:T(8,128)(2,1)} %get-tuple-element.53.k, bf16[2048,384]{1,0:T(8,128)(2,1)} %get-tuple-element.54.v), custom_call_target="tpu_custom_call" | custom-call | flops 32999999488 | bytes 30000000 | tf_op jit(solution)/shard_map/attend/pallas_call | solution.py:424
  75.8 0.0 collective-permute-done.columns_x
  75.8 0.0 copy-start.11
  75.8 0.9 copy-done.11
  76.7 53.9 %feed_forward.1 = (bf16[1024,768]{1,0:T(8,128)(2,1)}, f32[1024,768]{1,0:T(8,128)}, f32[1024,768]{1,0:T(8,128)}, bf16[2048,384]{1,0:T(8,128)(2,1)}, f32[8,768]{1,...) custom-call(bf16[2048,768]{1,0:T(8,128)(2,1)} %tok.3, ...), custom_call_target="tpu_custom_call" | custom-call | flops 54999998464 | bytes 50000000 | tf_op jit(solution)/shard_map/feed_forward/pallas_call | solution.py:776
  130.6 0.7 collective-permute-start.3
  131.3 0.7 collective-permute-start.4
  132.0 10.2 %collective-permute-start.5 = (bf16[3,192,384]{2,1,0:T(8,128)(2,1)}, bf16[3,192,384]{2,1,0:T(8,128)(2,1)S(1)}, u32[]{:S(2)}, u32[]{:S(2)}) collective-permute-start(bf16[3,192,384]{2,1,0:T(8,128)(2,1)} %get-tuple-element.78), channel_id=1, source_target_pairs={{0,24},{4,28},{1,25},{5,29},{2,26},{6,30},{3,27},{7,31}} | collective-permute-start | bytes 1327112 | tf_op jit(solution)/shard_map/ppermute | solution.py:1282
  142.3 0.8 collective-permute-start.2
  143.1 1.3 collective-permute-start.1
  144.3 35.7 %attend_back.1 = (bf16[2048,384]{1,0:T(8,128)(2,1)}, bf16[2048,384]{1,0:T(8,128)(2,1)}, bf16[2048,384]{1,0:T(8,128)(2,1)}) custom-call(s32[8]{0:T(128)} %bitcast.6, bf16[2048,384]{1,0:T(8,128)(2,1)} %get-tuple-element.52.q, bf16[2048,384]{1,0:T(8,128)(2,1)} %get-tuple-element.53.k, bf16[2048,384]{1,0:T(8,128)(2,1)} %get-tuple-element.54.v, ...), custom_call_target="tpu_custom_call" | custom-call | flops 44000002048 | bytes 40000000 | tf_op jit(solution)/shard_map/attend_back/pallas_call | solution.py:505
  180.0 0.0 collective-permute-done.2.mid_near
  180.0 0.0 copy-start.10
  180.1 0.0 collective-permute-done.1.far
  180.1 0.0 copy-start.9
  180.1 0.9 copy-done.10
  181.0 0.5 copy-done.9
  181.5 0.0 copy-start
  181.5 0.0 copy-start.1
  181.5 0.0 copy-start.2
  181.5 0.0 copy-start.3
  181.5 0.0 copy-start.4
  181.5 0.0 copy-start.5
  181.5 0.0 copy-start.7
  181.5 39.1 %last.1 = (bf16[2048,768]{1,0:T(8,128)(2,1)}, bf16[2048,768]{1,0:T(8,128)(2,1)}, f32[3,192,384]{2,1,0:T(8,128)}, f32[16,128]{1,0:T(8,128)}) custom-call(bf16[2048,768]{1,0:T(8,128)(2,1)} %get-tuple-element.50.norm_all, bf16[2048,384]{1,0:T(8,128)(2,1)} %get-tuple-element.64.dq_all, bf16[2048,384]{1,0:T(8,128)(2,1)} %get-tuple-element.65.dk_all, ...), custom_call_target="tpu_custom_call" | custom-call | flops 41799999488 | bytes 38000000 | tf_op jit(solution)/shard_map/last/pallas_call | solution.py:1165
  220.6 0.0 collective-permute-done.3.one
  220.6 0.0 collective-permute-done.4.two
  220.6 0.0 collective-permute-done.5.three
  220.7 0.0 copy-done
  220.7 0.0 copy-done.1
  220.7 0.0 copy-done.2
  220.7 0.0 copy-done.3
  220.7 0.0 copy-done.4
  220.7 0.0 copy-done.5
  220.7 0.0 copy-done.7
  220.7 0.0 copy-start.6
  220.7 1.2 copy-done.6
  221.9 0.0 copy-start.8
  221.9 0.7 copy-done.8
  222.6 9.2 %renew.1 = (f32[1,6,192,192]{3,2,1,0:T(8,128)}, f32[1,6,192,192]{3,2,1,0:T(8,128)}, f32[1,6,192,192]{3,2,1,0:T(8,128)}, f32[1,6,192,192]{3,2,1,0:T(8,128)}, bf16...) custom-call(f32[3,192,384]{2,1,0:T(8,128)S(1)} %copy-done.6, ...), custom_call_target="tpu_custom_call" | custom-call | flops 8800000000 | bytes 8000000 | tf_op jit(solution)/shard_map/renew/pallas_call | solution.py:1249
Async XLA Ops:
  50.2 25.5 %collective-permute-start = (bf16[6,192,384]{2,1,0:T(8,128)(2,1)}, bf16[6,192,384]{2,1,0:T(8,128)(2,1)S(1)}, u32[]{:S(2)}, u32[]{:S(2)}) collective-permute-start(bf16[6,192,384]{2,1,0:T(8,128)(2,1)} %get-tuple-element.58.columns), channel_id=1, source_target_pairs={{0,4},{4,0},{8,12},{12,8},{16,20},{20,16},{24,28},{28,24},{1,5},{5... | collective-permute-start | bytes 2654216 | tf_op jit(solution)/shard_map/ppermute | solution.py:1277
  75.8 0.9 copy-start.11
  130.6 90.0 %collective-permute-start.3 = (bf16[3,192,384]{2,1,0:T(8,128)(2,1)}, bf16[3,192,384]{2,1,0:T(8,128)(2,1)S(1)}, u32[]{:S(2)}, u32[]{:S(2)}) collective-permute-start(bf16[3,192,384]{2,1,0:T(8,128)(2,1)} %get-tuple-element.76), channel_id=1, source_target_pairs={{16,24},{20,28},{17,25},{21,29},{18,26},{22,30},{19,27},{23,31}} | collective-permute-start | bytes 1327112 | tf_op jit(solution)/shard_map/ppermute | solution.py:1282
  131.3 89.3 %collective-permute-start.4 = (bf16[3,192,384]{2,1,0:T(8,128)(2,1)}, bf16[3,192,384]{2,1,0:T(8,128)(2,1)S(1)}, u32[]{:S(2)}, u32[]{:S(2)}) collective-permute-start(bf16[3,192,384]{2,1,0:T(8,128)(2,1)} %get-tuple-element.77), channel_id=1, source_target_pairs={{8,24},{12,28},{9,25},{13,29},{10,26},{14,30},{11,27},{15,31}} | collective-permute-start | bytes 1327112 | tf_op jit(solution)/shard_map/ppermute | solution.py:1282
  132.0 88.6 %collective-permute-start.5 = (bf16[3,192,384]{2,1,0:T(8,128)(2,1)}, bf16[3,192,384]{2,1,0:T(8,128)(2,1)S(1)}, u32[]{:S(2)}, u32[]{:S(2)}) collective-permute-start(bf16[3,192,384]{2,1,0:T(8,128)(2,1)} %get-tuple-element.78), channel_id=1, source_target_pairs={{0,24},{4,28},{1,25},{5,29},{2,26},{6,30},{3,27},{7,31}} | collective-permute-start | bytes 1327112 | tf_op jit(solution)/shard_map/ppermute | solution.py:1282
  142.3 37.8 %collective-permute-start.2 = (bf16[6,192,384]{2,1,0:T(8,128)(2,1)}, bf16[6,192,384]{2,1,0:T(8,128)(2,1)S(1)}, u32[]{:S(2)}, u32[]{:S(2)}) collective-permute-start(bf16[6,192,384]{2,1,0:T(8,128)(2,1)} %get-tuple-element.60), channel_id=1, source_target_pairs={{0,4},{4,0},{8,12},{12,8},{16,20},{20,16},{24,28},{28,24},{1,5},{5... | collective-permute-start | bytes 2654216 | tf_op jit(solution)/shard_map/ppermute | solution.py:1277
  143.1 37.0 %collective-permute-start.1 = (bf16[1024,768]{1,0:T(8,128)(2,1)}, bf16[1024,768]{1,0:T(8,128)(2,1)S(1)}, u32[]{:S(2)}, u32[]{:S(2)}) collective-permute-start(bf16[1024,768]{1,0:T(8,128)(2,1)} %get-tuple-element.59.chip), channel_id=1, source_target_pairs={{0,2},{1,3},{2,0},{3,1},{4,6},{5,7},{6,4},{7,5},{8,10},{9,11},{10,... | collective-permute-start | bytes 4718600 | tf_op jit(solution)/shard_map/ppermute | solution.py:1273
  180.0 0.9 copy-start.10
  180.1 1.4 copy-start.9
  181.5 39.2 %copy-start = (f32[1,6,192,192]{3,2,1,0:T(8,128)S(1)}, f32[1,6,192,192]{3,2,1,0:T(8,128)}, u32[]{:S(2)}) copy-start(f32[1,6,192,192]{3,2,1,0:T(8,128)} %weight.1) | copy-start | bytes 2654212
  181.5 39.2 %copy-start.1 = (f32[1,6,192,192]{3,2,1,0:T(8,128)S(1)}, f32[1,6,192,192]{3,2,1,0:T(8,128)}, u32[]{:S(2)}) copy-start(f32[1,6,192,192]{3,2,1,0:T(8,128)} %left.1) | copy-start | bytes 2654212
  181.5 39.2 %copy-start.2 = (f32[1,6,192,192]{3,2,1,0:T(8,128)S(1)}, f32[1,6,192,192]{3,2,1,0:T(8,128)}, u32[]{:S(2)}) copy-start(f32[1,6,192,192]{3,2,1,0:T(8,128)} %right.1) | copy-start | bytes 2654212
  181.5 39.2 %copy-start.3 = (f32[1,6,192,192]{3,2,1,0:T(8,128)S(1)}, f32[1,6,192,192]{3,2,1,0:T(8,128)}, u32[]{:S(2)}) copy-start(f32[1,6,192,192]{3,2,1,0:T(8,128)} %left_root.1) | copy-start | bytes 2654212
  181.5 39.2 %copy-start.4 = (f32[9,96]{1,0:T(8,128)S(1)}, f32[9,96]{1,0:T(8,128)}, u32[]{:S(2)}) copy-start(f32[9,96]{1,0:T(8,128)} %vec.1) | copy-start | bytes 10372
  181.5 39.2 %copy-start.5 = (f32[9,96]{1,0:T(8,128)S(1)}, f32[9,96]{1,0:T(8,128)}, u32[]{:S(2)}) copy-start(f32[9,96]{1,0:T(8,128)} %moment.1) | copy-start | bytes 10372
  181.5 39.2 %copy-start.7 = (bf16[3,192,384]{2,1,0:T(8,128)(2,1)S(1)}, bf16[3,192,384]{2,1,0:T(8,128)(2,1)}, u32[]{:S(2)}) copy-start(bf16[3,192,384]{2,1,0:T(8,128)(2,1)} %get-tuple-element.75.own) | copy-start | bytes 1327108
  220.7 1.2 copy-start.6
  221.9 0.7 copy-start.8

commit v16 on v14

--- a/solution.py
+++ b/solution.py
@@ -175,8 +175,8 @@
             arrived(piece(1 - y, x, k), r_y1.at[k])
             send(piece(1 - y, x, k), piece(1 - y, x, k), s_d1.at[k], r_d1.at[k], to_x)
 
-    def from_right(d, m):
-        arrived(columns.at[m], r_l.at[d - 1, m], z + d < 4)
+    def from_right(d, m, cond=True):
+        arrived(columns.at[m], r_l.at[d - 1, m], (z + d < 4) & cond)
         if d < 3:
             send(at_z(d, m), at_z(d, m), s_l.at[d, m], r_l.at[d, m], to_left, (z + d < 4) & (z > 0))
 
@@ -203,11 +203,12 @@
         if k >= 1:
             diagonal(k - 1)
         if k % 2 == 1:
-            from_right(1, k // 2)
+            from_right(1, k // 2, z > 0)
     diagonal(5)
     pl.when(z == 1)(own_one.wait)
     pl.when(z > 1)(own_more.wait)
     for m in range(3):
+        arrived(columns.at[m], r_l.at[0, m], z == 0)
         along_x(m, z == 0)
     for m in range(3):
         from_left(1, m)

time: 232 us -> 231 us (level)
  Pallas kernels: 210 us -> 204 us
  waiting for transfers between devices: 0.41 us -> 3.89 us
  starting transfers between devices: 15.3 us -> 17.8 us
    ppermute x1, waiting for transfers between devices: 0.4 us -> 3.88 us  [swap(): return lax.ppermute(value, 'tensor', [(t, t ^ bit) for t in range(NT)])]
    pallas_call x1, Pallas kernels: 34.5 us -> 31.1 us  [attend_back(): pl.pallas_call(attend_back_kernel, grid_spec=pltpu.PrefetchScalarGridSpec...]
    pallas_call x1, Pallas kernels: 24 us -> 21.4 us  [attend(): pl.pallas_call(attend_kernel, grid_spec=pltpu.PrefetchScalarGridSpec(num_...]
  transfers between devices with their start and end apart: 6 -> 6, of which waited for: 1 -> 1; matrix products, arithmetic and copies ran while one was open for 0% -> 0% of each run, Pallas kernels for 25% -> 23%
where the time goes in v16:
time: 231 us; the launch traced here: 230 us
  Pallas kernels  204 us (88%)
  starting transfers between devices  17.8 us (8%)
  local copies, waits for them, and re-layouts  3.94 us (2%)
  waiting for transfers between devices  3.89 us (2%)
    pallas_call x1, Pallas kernels, feed(): pl.pallas_call(functools.partial(feed_kernel, small), grid=(3 * half + 1,...  54 us
    pallas_call x1, Pallas kernels, gather(): pl.pallas_call(gather_kernel, in_specs=[vmem, vmem, far, vmem], out_specs...  49.6 us
    pallas_call x1, Pallas kernels, last(): pl.pallas_call(functools.partial(last_kernel, small), grid=(GRAD_STEPS +...  38.5 us
    pallas_call x1, Pallas kernels, attend_back(): pl.pallas_call(attend_back_kernel, grid_spec=pltpu.PrefetchScalarGridSpec...  31.1 us
    pallas_call x1, Pallas kernels, attend(): pl.pallas_call(attend_kernel, grid_spec=pltpu.PrefetchScalarGridSpec(num_...  21.4 us
    ppermute x3, starting transfers between devices, hop_z(): return lax.ppermute(value, 'dp', pairs)  14.7 us
    pallas_call x1, Pallas kernels, renew(): pl.pallas_call(renew_kernel, grid=(4,), in_specs=[pair] * 5 + [slot] * 5...  9.22 us
  transfers between devices with their start and end apart: 6, of which 1 were waited for; matrix products, arithmetic and copies ran while one was open for 0% of the time, Pallas kernels for 23%

profile of v16, /device:TPU:0, one launch (start us, length us, event | category | flops | bytes accessed | tf_op | source)
XLA Modules:
  0.0 230.4 jit_solution(17564305825213903559)
XLA Ops:
  0.6 49.6 %gather.1 = (bf16[2,24,192,384]{3,2,1,0:T(8,128)(2,1)}, bf16[6,192,384]{2,1,0:T(8,128)(2,1)}, bf16[2,2,192,384]{3,2,1,0:T(8,128)(2,1)}, f32[16,768]{1,0:T(8,128)...) custom-call(f32[1,6,192,192]{3,2,1,0:T(8,128)} %weight.1, ...), custom_call_target="tpu_custom_call" | custom-call | flops 65999998976 | bytes 60000000 | tf_op jit(solution)/shard_map/gather/pallas_call | solution.py:286
  50.2 1.0 collective-permute-start
  51.2 21.4 %attend.1 = (bf16[2048,384]{1,0:T(8,128)(2,1)}, f32[8,2048]{1,0:T(8,128)}) custom-call(s32[8]{0:T(128)} %bitcast.5, bf16[2048,384]{1,0:T(8,128)(2,1)} %get-tuple-element.55.q, bf16[2048,384]{1,0:T(8,128)(2,1)} %get-tuple-element.56.k, bf16[2048,384]{1,0:T(8,128)(2,1)} %get-tuple-element.57.v), custom_call_target="tpu_custom_call" | custom-call | flops 32999999488 | bytes 30000000 | tf_op jit(solution)/shard_map/attend/pallas_call | solution.py:425
  72.6 0.0 collective-permute-done.columns_x
  72.6 0.0 copy-start.11
  72.6 0.9 copy-done.11
  73.5 54.0 %feed_forward.1 = (bf16[1024,768]{1,0:T(8,128)(2,1)}, f32[1024,768]{1,0:T(8,128)}, f32[1024,768]{1,0:T(8,128)}, bf16[2048,384]{1,0:T(8,128)(2,1)}, f32[8,768]{1,...) custom-call(bf16[2048,768]{1,0:T(8,128)(2,1)} %tok.3, ...), custom_call_target="tpu_custom_call" | custom-call | flops 54999998464 | bytes 50000000 | tf_op jit(solution)/shard_map/feed_forward/pallas_call | solution.py:777
  127.5 0.7 collective-permute-start.1
  128.2 0.7 collective-permute-start.2
  128.9 13.3 %collective-permute-start.3 = (bf16[3,192,384]{2,1,0:T(8,128)(2,1)}, bf16[3,192,384]{2,1,0:T(8,128)(2,1)S(1)}, u32[]{:S(2)}, u32[]{:S(2)}) collective-permute-start(bf16[3,192,384]{2,1,0:T(8,128)(2,1)} %get-tuple-element.64), channel_id=1, source_target_pairs={{0,24},{4,28},{1,25},{5,29},{2,26},{6,30},{3,27},{7,31}} | collective-permute-start | bytes 1327112 | tf_op jit(solution)/shard_map/ppermute | solution.py:1283
  142.2 0.9 collective-permute-start.5
  143.1 1.2 collective-permute-start.4
  144.3 31.1 %attend_back.1 = (bf16[2048,384]{1,0:T(8,128)(2,1)}, bf16[2048,384]{1,0:T(8,128)(2,1)}, bf16[2048,384]{1,0:T(8,128)(2,1)}) custom-call(s32[8]{0:T(128)} %bitcast.6, bf16[2048,384]{1,0:T(8,128)(2,1)} %get-tuple-element.55.q, bf16[2048,384]{1,0:T(8,128)(2,1)} %get-tuple-element.56.k, bf16[2048,384]{1,0:T(8,128)(2,1)} %get-tuple-element.57.v, ...), custom_call_target="tpu_custom_call" | custom-call | flops 44000002048 | bytes 40000000 | tf_op jit(solution)/shard_map/attend_back/pallas_call | solution.py:506
  175.4 0.0 collective-permute-done.1.one
  175.4 0.0 collective-permute-done.2.two
  175.4 0.0 collective-permute-done.3.three
  175.4 0.0 collective-permute-done.5.mid_near
  175.4 0.0 copy-start.10
  175.5 3.9 %collective-permute-done.4.far = bf16[1024,768]{1,0:T(8,128)(2,1)S(1)} collective-permute-done((bf16[1024,768]{1,0:T(8,128)(2,1)}, bf16[1024,768]{1,0:T(8,128)(2,1)S(1)}, u32[]{:S(2)}, u32[]{:S(2)}) %collective-permute-start.4) | collective-permute-done | bytes 1572896 | tf_op jit(solution)/shard_map/ppermute | solution.py:1274
  179.3 0.0 copy-start.9
  179.3 0.0 copy-done.10
  179.3 1.1 copy-done.9
  180.5 0.0 copy-start
  180.5 0.0 copy-start.1
  180.5 0.0 copy-start.2
  180.5 0.0 copy-start.3
  180.5 0.0 copy-start.4
  180.5 0.0 copy-start.5
  180.5 0.0 copy-start.7
  180.5 38.5 %last.1 = (bf16[2048,768]{1,0:T(8,128)(2,1)}, bf16[2048,768]{1,0:T(8,128)(2,1)}, f32[3,192,384]{2,1,0:T(8,128)}, f32[16,128]{1,0:T(8,128)}) custom-call(bf16[2048,768]{1,0:T(8,128)(2,1)} %get-tuple-element.53.norm_all, bf16[2048,384]{1,0:T(8,128)(2,1)} %get-tuple-element.70.dq_all, bf16[2048,384]{1,0:T(8,128)(2,1)} %get-tuple-element.71.dk_all, ...), custom_call_target="tpu_custom_call" | custom-call | flops 41799999488 | bytes 38000000 | tf_op jit(solution)/shard_map/last/pallas_call | solution.py:1166
  219.1 0.0 copy-done
  219.1 0.0 copy-done.1
  219.1 0.0 copy-done.2
  219.1 0.0 copy-done.3
  219.1 0.0 copy-done.4
  219.1 0.0 copy-done.5
  219.1 0.0 copy-done.7
  219.1 0.0 copy-start.6
  219.1 1.2 copy-done.6
  220.3 0.0 copy-start.8
  220.3 0.7 copy-done.8
  221.0 9.2 %renew.1 = (f32[1,6,192,192]{3,2,1,0:T(8,128)}, f32[1,6,192,192]{3,2,1,0:T(8,128)}, f32[1,6,192,192]{3,2,1,0:T(8,128)}, f32[1,6,192,192]{3,2,1,0:T(8,128)}, bf16...) custom-call(f32[3,192,384]{2,1,0:T(8,128)S(1)} %copy-done.6, ...), custom_call_target="tpu_custom_call" | custom-call | flops 8800000000 | bytes 8000000 | tf_op jit(solution)/shard_map/renew/pallas_call | solution.py:1250
Async XLA Ops:
  50.2 22.4 %collective-permute-start = (bf16[6,192,384]{2,1,0:T(8,128)(2,1)}, bf16[6,192,384]{2,1,0:T(8,128)(2,1)S(1)}, u32[]{:S(2)}, u32[]{:S(2)}) collective-permute-start(bf16[6,192,384]{2,1,0:T(8,128)(2,1)} %get-tuple-element.61.columns), channel_id=1, source_target_pairs={{0,4},{4,0},{8,12},{12,8},{16,20},{20,16},{24,28},{28,24},{1,5},{5... | collective-permute-start | bytes 2654216 | tf_op jit(solution)/shard_map/ppermute | solution.py:1278
  72.6 0.9 copy-start.11
  127.5 47.9 %collective-permute-start.1 = (bf16[3,192,384]{2,1,0:T(8,128)(2,1)}, bf16[3,192,384]{2,1,0:T(8,128)(2,1)S(1)}, u32[]{:S(2)}, u32[]{:S(2)}) collective-permute-start(bf16[3,192,384]{2,1,0:T(8,128)(2,1)} %get-tuple-element.62), channel_id=1, source_target_pairs={{16,24},{20,28},{17,25},{21,29},{18,26},{22,30},{19,27},{23,31}} | collective-permute-start | bytes 1327112 | tf_op jit(solution)/shard_map/ppermute | solution.py:1283
  128.2 47.2 %collective-permute-start.2 = (bf16[3,192,384]{2,1,0:T(8,128)(2,1)}, bf16[3,192,384]{2,1,0:T(8,128)(2,1)S(1)}, u32[]{:S(2)}, u32[]{:S(2)}) collective-permute-start(bf16[3,192,384]{2,1,0:T(8,128)(2,1)} %get-tuple-element.63), channel_id=1, source_target_pairs={{8,24},{12,28},{9,25},{13,29},{10,26},{14,30},{11,27},{15,31}} | collective-permute-start | bytes 1327112 | tf_op jit(solution)/shard_map/ppermute | solution.py:1283
  128.9 46.5 %collective-permute-start.3 = (bf16[3,192,384]{2,1,0:T(8,128)(2,1)}, bf16[3,192,384]{2,1,0:T(8,128)(2,1)S(1)}, u32[]{:S(2)}, u32[]{:S(2)}) collective-permute-start(bf16[3,192,384]{2,1,0:T(8,128)(2,1)} %get-tuple-element.64), channel_id=1, source_target_pairs={{0,24},{4,28},{1,25},{5,29},{2,26},{6,30},{3,27},{7,31}} | collective-permute-start | bytes 1327112 | tf_op jit(solution)/shard_map/ppermute | solution.py:1283
  142.2 33.2 %collective-permute-start.5 = (bf16[6,192,384]{2,1,0:T(8,128)(2,1)}, bf16[6,192,384]{2,1,0:T(8,128)(2,1)S(1)}, u32[]{:S(2)}, u32[]{:S(2)}) collective-permute-start(bf16[6,192,384]{2,1,0:T(8,128)(2,1)} %get-tuple-element.66), channel_id=1, source_target_pairs={{0,4},{4,0},{8,12},{12,8},{16,20},{20,16},{24,28},{28,24},{1,5},{5... | collective-permute-start | bytes 2654216 | tf_op jit(solution)/shard_map/ppermute | solution.py:1278
  143.1 36.3 %collective-permute-start.4 = (bf16[1024,768]{1,0:T(8,128)(2,1)}, bf16[1024,768]{1,0:T(8,128)(2,1)S(1)}, u32[]{:S(2)}, u32[]{:S(2)}) collective-permute-start(bf16[1024,768]{1,0:T(8,128)(2,1)} %get-tuple-element.65.chip), channel_id=1, source_target_pairs={{0,2},{1,3},{2,0},{3,1},{4,6},{5,7},{6,4},{7,5},{8,10},{9,11},{10,... | collective-permute-start | bytes 4718600 | tf_op jit(solution)/shard_map/ppermute | solution.py:1274
  175.4 3.9 %copy-start.10 = (bf16[6,192,384]{2,1,0:T(8,128)(2,1)}, bf16[6,192,384]{2,1,0:T(8,128)(2,1)S(1)}, u32[]{:S(2)}) copy-start(bf16[6,192,384]{2,1,0:T(8,128)(2,1)S(1)} %collective-permute-done.5.mid_near) | copy-start | bytes 2654212
  179.3 1.1 copy-start.9
  180.5 38.6 %copy-start = (f32[1,6,192,192]{3,2,1,0:T(8,128)S(1)}, f32[1,6,192,192]{3,2,1,0:T(8,128)}, u32[]{:S(2)}) copy-start(f32[1,6,192,192]{3,2,1,0:T(8,128)} %weight.1) | copy-start | bytes 2654212
  180.5 38.6 %copy-start.1 = (f32[1,6,192,192]{3,2,1,0:T(8,128)S(1)}, f32[1,6,192,192]{3,2,1,0:T(8,128)}, u32[]{:S(2)}) copy-start(f32[1,6,192,192]{3,2,1,0:T(8,128)} %left.1) | copy-start | bytes 2654212
  180.5 38.6 %copy-start.2 = (f32[1,6,192,192]{3,2,1,0:T(8,128)S(1)}, f32[1,6,192,192]{3,2,1,0:T(8,128)}, u32[]{:S(2)}) copy-start(f32[1,6,192,192]{3,2,1,0:T(8,128)} %right.1) | copy-start | bytes 2654212
  180.5 38.6 %copy-start.3 = (f32[1,6,192,192]{3,2,1,0:T(8,128)S(1)}, f32[1,6,192,192]{3,2,1,0:T(8,128)}, u32[]{:S(2)}) copy-start(f32[1,6,192,192]{3,2,1,0:T(8,128)} %left_root.1) | copy-start | bytes 2654212
  180.5 38.6 %copy-start.4 = (f32[9,96]{1,0:T(8,128)S(1)}, f32[9,96]{1,0:T(8,128)}, u32[]{:S(2)}) copy-start(f32[9,96]{1,0:T(8,128)} %vec.1) | copy-start | bytes 10372
  180.5 38.6 %copy-start.5 = (f32[9,96]{1,0:T(8,128)S(1)}, f32[9,96]{1,0:T(8,128)}, u32[]{:S(2)}) copy-start(f32[9,96]{1,0:T(8,128)} %moment.1) | copy-start | bytes 10372
  180.5 38.6 %copy-start.7 = (bf16[3,192,384]{2,1,0:T(8,128)(2,1)S(1)}, bf16[3,192,384]{2,1,0:T(8,128)(2,1)}, u32[]{:S(2)}) copy-start(bf16[3,192,384]{2,1,0:T(8,128)(2,1)} %get-tuple-element.81.own) | copy-start | bytes 1327108
  219.1 1.2 copy-start.6
  220.3 0.7 copy-start.8
